TPU v7x, 32 devices: a whole 2x2x4 slice. The times are simulated.
32 devices in a mesh: grp: 8 (over z, x), loc: 4 (over y, core).
Axes of the slice: x: 2, y: 2, z: 4, core: 2. Of those that a mesh axis runs over, the one named last changes fastest.
Arguments:
- carried: float32 [2, 2048, 1000], P(None, ('grp', 'loc')), may hold values from -0.9 to 0.9
- session_plan: int32 [2048], P(('grp', 'loc')), may hold values from 0 to 511, as said below
- item_ids: int32 [4, 2048], P(None, ('grp', 'loc')), may hold values from 0 to 4703, as said below
- target_ids: int32 [4, 2048], P(None, ('grp', 'loc')), may hold values from 0 to 4703, as said below
- reset_mask: int32 [4, 2048], P(None, ('grp', 'loc')), may hold values 0 or 1
- valid_counts: int32 [2048], P(('grp', 'loc')), may hold values from 1 to 4
- negative_ids: int32 [2048], replicated, may hold values from 0 to 4703, as said below
- input_table: bfloat16 [4704, 3000], P('grp'), may hold values from -4 to 4
- output_table: bfloat16 [4704, 1000], P('grp'), may hold values from -0.69921875 to 0.69921875
- output_bias: bfloat16 [4704], P('grp'), may hold values from -3 to 3
- hidden_one: bfloat16 [1000, 3000], P(None, 'loc'), may hold values from -0.1875 to 0.1875
- input_two: bfloat16 [1000, 3000], P(None, 'loc'), may hold values from -0.1875 to 0.1875
- hidden_two: bfloat16 [1000, 3000], P(None, 'loc'), may hold values from -0.1875 to 0.1875
- gate_biases: bfloat16 [2, 3000], P(None, 'loc'), may hold values from -2 to 2
Outputs:
- grad_input_table: float32 [4704, 3000], P(('grp', 'loc'))
- grad_output_table: float32 [4704, 1000], P(('grp', 'loc'))
- grad_output_bias: float32 [4704], P(('grp', 'loc'))
- grad_hidden_one: float32 [1000, 3000], P(None, 'loc')
- grad_input_two: float32 [1000, 3000], P(None, 'loc')
- grad_hidden_two: float32 [1000, 3000], P(None, 'loc')
- grad_gate_biases: float32 [2, 3000], P(None, 'loc')
- grad_carried: float32 [2, 2048, 1000], P(None, ('grp', 'loc'))
Inputs may be any that keep to these rules, and one draw needn't show every extreme that they name: `item_ids`: within each device's block of 4 x 64 events, the items of group g's range g * 588 to (g + 1) * 588 - 1 are named at most 48 times, and exactly 48 times for some group. `target_ids`: within each device's block of 4 x 64 events, the items of one group's range are named at most 48 times, and exactly 48 times for some group. `session_plan`: each value is e * 64 + j for a group e and a new slot j; over the devices of one loc index every pair (e, j) is named exactly once; at most 32 of one device's slots name the same group e, and exactly 32 for some group. `negative_ids`: entry j lies in the range of group j // 256, from (j // 256) * 588 to (j // 256 + 1) * 588 - 1.
All inputs are finite; a program needn't handle non-finite values. No bound on the sum of `reset_mask` on one device may be relied on, other than what follows from the above.
Results may differ from a plain program's by a relative error of at most 0.0075.
Values may be sent and summed in bfloat16 or wider, within the bound.
No kernel may reach another device: no remote copies, remote signals or barrier semaphores. Data moves between devices by JAX's collectives and lax.ppermute only.
A program may use at most 256 MiB of HBM per device.

v0:
```python
import jax
import jax.numpy as jnp
from jax import lax
from jax.sharding import PartitionSpec as P

BPREG = 1.0
HIGHEST = lax.Precision.HIGHEST


def gru_cell(gate_input, hidden_part, previous):
    hidden_size = previous.shape[-1]
    update = jax.nn.sigmoid(gate_input[..., :hidden_size] + hidden_part[..., :hidden_size])
    reset_gate = jax.nn.sigmoid(
        gate_input[..., hidden_size : 2 * hidden_size]
        + hidden_part[..., hidden_size : 2 * hidden_size]
    )
    candidate = jnp.tanh(
        gate_input[..., 2 * hidden_size :] + reset_gate * hidden_part[..., 2 * hidden_size :]
    )
    return candidate + update * (previous - candidate)


def bpr_max(score_tgt, score_neg, valid_mask):
    batch_rows = score_tgt.shape[-1]
    diagonal = jnp.eye(batch_rows, dtype=bool)
    positive = jnp.sum(jnp.where(diagonal, score_tgt, 0.0), axis=-1)
    all_scores = jnp.concatenate([score_tgt, score_neg], axis=-1)
    masked = jnp.concatenate([jnp.where(diagonal, -jnp.inf, score_tgt), score_neg], axis=-1)
    highest = jnp.max(masked, axis=-1, keepdims=True)
    exponent = jnp.exp(masked - highest)
    weights = exponent / jnp.sum(exponent, axis=-1, keepdims=True)
    inside = jnp.sum(weights * jax.nn.sigmoid(positive[..., None] - all_scores), axis=-1)
    penalty = jnp.sum(weights * all_scores * all_scores, axis=-1)
    return jnp.sum(valid_mask * (-jnp.log(inside) + BPREG * penalty))


def run_layer(gate_input, initial, keep_mask, weight):

    def advance(state_now, inputs):
        gate_row, keep_row = inputs
        masked = state_now * keep_row[:, None]
        hidden_part = jnp.dot(
            masked.astype(jnp.bfloat16), weight, preferred_element_type=jnp.float32
        )
        updated = gru_cell(gate_row, hidden_part, masked)
        return (updated, (updated, masked, hidden_part))

    _, outputs = lax.scan(advance, initial, (gate_input, keep_mask))
    return outputs


def back_layer(grad_out, gate_input, hidden_parts, masked_states, keep_mask, weight):

    def retreat(grad_state, inputs):
        grad_row, gate_row, part_row, masked_row, keep_row = inputs
        _, pullback = jax.vjp(gru_cell, gate_row, part_row, masked_row)
        grad_gate, grad_part, grad_masked = pullback(grad_state + grad_row)
        part_low = grad_part.astype(jnp.bfloat16)
        grad_masked = grad_masked + lax.dot_general(
            part_low, weight, (((1,), (1,)), ((), ())), preferred_element_type=jnp.float32
        )
        return (grad_masked * keep_row[:, None], (grad_gate.astype(jnp.bfloat16), part_low))

    initial_grad, (gate_grads, part_grads) = lax.scan(
        retreat,
        jnp.zeros_like(grad_out[0]),
        (grad_out, gate_input, hidden_parts, masked_states, keep_mask),
        reverse=True,
    )
    return (initial_grad, gate_grads, part_grads)


def rank_within(owner_of, owners):
    member = (owner_of[:, None] == jnp.arange(owners, dtype=jnp.int32)[None, :]).astype(jnp.int32)
    before = jnp.cumsum(member, axis=0) - member
    return jnp.sum(before * member, axis=1)


def route_rows(identities, rows_owned, owners, capacity):
    owner_of = identities // rows_owned
    rank_of = rank_within(owner_of, owners)
    request = jnp.full((owners, capacity), -1, jnp.int32).at[owner_of, rank_of].set(identities)
    return (owner_of, rank_of, request)


def row_product(left, right):
    return lax.dot_general(
        left, right, (((0,), (0,)), ((), ())), preferred_element_type=jnp.float32
    )


def on_device(
    carried,
    session_plan,
    item_ids,
    target_ids,
    reset_mask,
    valid_counts,
    negative_ids,
    input_table,
    output_table,
    output_bias,
    hidden_one,
    input_two,
    hidden_two,
    gate_biases,
):
    model_width = carried.shape[2]
    step_count, batch_rows = item_ids.shape
    events = step_count * batch_rows
    owners = lax.axis_size("grp")
    my_group = lax.axis_index("grp")
    rows_owned = input_table.shape[0]
    row_base = my_group * rows_owned
    capacity = events // owners + events // (2 * owners)
    carry_cap = 4 * batch_rows // owners
    hidden_one_w, input_two_w, hidden_two_w, biases_all = (
        lax.all_gather(hidden_one, "loc", axis=1, tiled=True),
        lax.all_gather(input_two, "loc", axis=1, tiled=True),
        lax.all_gather(hidden_two, "loc", axis=1, tiled=True),
        lax.all_gather(gate_biases, "loc", axis=1, tiled=True),
    )
    gate_f = biases_all.astype(jnp.float32)
    gate_width = hidden_one_w.shape[1]
    dest_group = session_plan // batch_rows
    dest_slot = session_plan % batch_rows
    carry_rank = rank_within(dest_group, owners)
    send_states = (
        jnp.zeros((2, owners, carry_cap, model_width), jnp.float32)
        .at[:, dest_group, carry_rank]
        .set(carried)
    )
    send_slots = (
        jnp.full((1, owners, carry_cap), -1, jnp.int32).at[0, dest_group, carry_rank].set(dest_slot)
    )
    got_states, got_slots = (
        lax.all_to_all(send_states, "grp", split_axis=1, concat_axis=1, tiled=True),
        lax.all_to_all(send_slots, "grp", split_axis=1, concat_axis=1, tiled=True),
    )
    arrived_slots = got_slots.reshape(owners * carry_cap)
    landing = jnp.where(arrived_slots >= 0, arrived_slots, batch_rows)
    moved = (
        jnp.zeros((2, batch_rows, model_width), jnp.float32)
        .at[:, landing]
        .set(got_states.reshape(2, owners * carry_cap, model_width), mode="drop")
    )
    in_owner, in_rank, in_request = route_rows(
        item_ids.reshape(events), rows_owned, owners, capacity
    )
    tg_owner, tg_rank, tg_request = route_rows(
        target_ids.reshape(events), rows_owned, owners, capacity
    )
    arrived_in, arrived_tg = (
        lax.all_to_all(in_request, "grp", split_axis=0, concat_axis=0, tiled=True),
        lax.all_to_all(tg_request, "grp", split_axis=0, concat_axis=0, tiled=True),
    )
    local_in = jnp.clip(arrived_in - row_base, 0, rows_owned - 1)
    local_tg = jnp.clip(arrived_tg - row_base, 0, rows_owned - 1)
    present_in = arrived_in >= 0
    present_tg = arrived_tg >= 0
    zero_low = jnp.zeros((), jnp.bfloat16)
    reply = (
        jnp.where(present_in[..., None], input_table[local_in], zero_low),
        jnp.where(present_tg[..., None], output_table[local_tg], zero_low),
        jnp.where(present_tg, output_bias[local_tg], zero_low),
    )
    table_back, output_back, bias_back = (
        lax.all_to_all(reply[0], "grp", split_axis=0, concat_axis=0, tiled=True),
        lax.all_to_all(reply[1], "grp", split_axis=0, concat_axis=0, tiled=True),
        lax.all_to_all(reply[2], "grp", split_axis=0, concat_axis=0, tiled=True),
    )
    layer_rows = table_back[in_owner, in_rank]
    target_rows = output_back[tg_owner, tg_rank].reshape(step_count, batch_rows, model_width)
    target_bias = bias_back[tg_owner, tg_rank].reshape(step_count, batch_rows).astype(jnp.float32)
    neg_per = negative_ids.shape[0] // owners
    mine = lax.dynamic_slice_in_dim(negative_ids, my_group * neg_per, neg_per, 0) - row_base
    negative_rows, negative_bias = (
        lax.all_gather(output_table[mine], "grp", axis=0, tiled=True),
        lax.all_gather(output_bias[mine], "grp", axis=0, tiled=True),
    )
    negative_bias_f = negative_bias.astype(jnp.float32)
    keep_all = (1 - reset_mask).astype(jnp.float32)
    layer_one_in = (
        layer_rows.reshape(step_count, batch_rows, gate_width).astype(jnp.float32) + gate_f[0]
    )
    first, masked_one, part_one = run_layer(layer_one_in, moved[0], keep_all, hidden_one_w)
    first_low = first.astype(jnp.bfloat16).reshape(events, model_width)
    layer_two_in = (
        jnp.dot(first_low, input_two_w, preferred_element_type=jnp.float32) + gate_f[1]
    ).reshape(step_count, batch_rows, gate_width)
    second, masked_two, part_two = run_layer(layer_two_in, moved[1], keep_all, hidden_two_w)
    second_low = second.astype(jnp.bfloat16)
    second_flat = second_low.reshape(events, model_width)
    score_tgt = jnp.einsum(
        "tbh,tch->tbc", second_low, target_rows, preferred_element_type=jnp.float32
    )
    score_neg = lax.dot_general(
        second_flat, negative_rows, (((1,), (1,)), ((), ())), preferred_element_type=jnp.float32
    ).reshape(step_count, batch_rows, -1)
    valid_mask = (jnp.arange(step_count, dtype=jnp.int32)[:, None] < valid_counts[None, :]).astype(
        jnp.float32
    )

    def scored(product_tgt, product_neg, bias_tgt, bias_neg):
        return (
            bpr_max(product_tgt + bias_tgt[:, None, :], product_neg + bias_neg, valid_mask)
            / step_count
        )

    _, pullback = jax.vjp(scored, score_tgt, score_neg, target_bias, negative_bias_f)
    grad_tgt, grad_neg, grad_tgt_bias, grad_neg_bias = pullback(jnp.ones((), jnp.float32))
    grad_tgt_low = grad_tgt.astype(jnp.bfloat16)
    grad_neg_low = grad_neg.astype(jnp.bfloat16).reshape(events, -1)
    into_second = jnp.einsum(
        "tbc,tch->tbh", grad_tgt_low, target_rows, preferred_element_type=jnp.float32
    )
    into_second = into_second + jnp.dot(
        grad_neg_low, negative_rows, preferred_element_type=jnp.float32
    ).reshape(step_count, batch_rows, model_width)
    target_row_grad = jnp.einsum(
        "tbc,tbh->tch", grad_tgt_low, second_low, preferred_element_type=jnp.float32
    ).astype(jnp.bfloat16)
    negative_row_grad = row_product(grad_neg_low, second_flat)
    init_two, gate_two_grad, part_two_grad = back_layer(
        into_second, layer_two_in, part_two, masked_two, keep_all, hidden_two_w
    )
    gate_two_flat = gate_two_grad.reshape(events, gate_width)
    into_first = lax.dot_general(
        gate_two_flat, input_two_w, (((1,), (1,)), ((), ())), preferred_element_type=jnp.float32
    ).reshape(step_count, batch_rows, model_width)
    init_one, gate_one_grad, part_one_grad = back_layer(
        into_first, layer_one_in, part_one, masked_one, keep_all, hidden_one_w
    )
    gate_one_flat = gate_one_grad.reshape(events, gate_width)
    carry_grad = jnp.stack([init_one, init_two])
    present_slot = (arrived_slots >= 0)[None, :, None]
    back_rows = jnp.where(
        present_slot, carry_grad[:, jnp.clip(arrived_slots, 0, batch_rows - 1)], 0.0
    ).reshape(2, owners, carry_cap, model_width)
    returned = lax.all_to_all(back_rows, "grp", split_axis=1, concat_axis=1, tiled=True)
    grad_carried = returned[:, dest_group, carry_rank]
    send_in = (
        jnp.zeros((owners, capacity, gate_width), jnp.bfloat16)
        .at[in_owner, in_rank]
        .set(gate_one_flat)
    )
    send_tg = (
        jnp.zeros((owners, capacity, model_width), jnp.bfloat16)
        .at[tg_owner, tg_rank]
        .set(target_row_grad.reshape(events, model_width))
    )
    send_bias = (
        jnp.zeros((owners, capacity), jnp.bfloat16)
        .at[tg_owner, tg_rank]
        .set(grad_tgt_bias.astype(jnp.bfloat16).reshape(events))
    )
    got_in, got_tg, got_bias = (
        lax.all_to_all(send_in, "grp", split_axis=0, concat_axis=0, tiled=True),
        lax.all_to_all(send_tg, "grp", split_axis=0, concat_axis=0, tiled=True),
        lax.all_to_all(send_bias, "grp", split_axis=0, concat_axis=0, tiled=True),
    )
    slots = owners * capacity
    row_range = jnp.arange(rows_owned, dtype=jnp.int32)[None, :]
    match_in = ((arrived_in.reshape(slots) - row_base)[:, None] == row_range).astype(jnp.bfloat16)
    match_tg = ((arrived_tg.reshape(slots) - row_base)[:, None] == row_range).astype(jnp.bfloat16)
    table_in = row_product(match_in, got_in.reshape(slots, gate_width))
    table_out = row_product(match_tg, got_tg.reshape(slots, model_width))
    table_bias = jnp.dot(got_bias.reshape(slots), match_tg, preferred_element_type=jnp.float32)
    neg_rows_sum, neg_bias_sum = (
        lax.psum_scatter(negative_row_grad, "grp", scatter_dimension=0, tiled=True),
        lax.psum_scatter(grad_neg_bias, "grp", scatter_dimension=0, tiled=True),
    )
    match_neg = (mine[:, None] == row_range).astype(jnp.float32)
    table_out = table_out + lax.dot_general(
        match_neg, neg_rows_sum, (((0,), (0,)), ((), ())), precision=HIGHEST
    )
    table_bias = table_bias + jnp.dot(neg_bias_sum, match_neg, precision=HIGHEST)
    grad_input_table, grad_output_table, grad_output_bias = (
        lax.psum_scatter(table_in, "loc", scatter_dimension=0, tiled=True),
        lax.psum_scatter(table_out, "loc", scatter_dimension=0, tiled=True),
        lax.psum_scatter(table_bias, "loc", scatter_dimension=0, tiled=True),
    )
    prev_one = masked_one.astype(jnp.bfloat16).reshape(events, model_width)
    prev_two = masked_two.astype(jnp.bfloat16).reshape(events, model_width)
    part_one_flat = part_one_grad.reshape(events, gate_width)
    part_two_flat = part_two_grad.reshape(events, gate_width)
    whole = (
        row_product(prev_one, part_one_flat),
        row_product(first_low, gate_two_flat),
        row_product(prev_two, part_two_flat),
        jnp.stack(
            [
                jnp.sum(gate_one_flat, axis=0, dtype=jnp.float32),
                jnp.sum(gate_two_flat, axis=0, dtype=jnp.float32),
            ]
        ),
    )
    parts = (
        lax.psum_scatter(
            whole[0].astype(jnp.bfloat16), "loc", scatter_dimension=1, tiled=True
        ).astype(jnp.float32),
        lax.psum_scatter(
            whole[1].astype(jnp.bfloat16), "loc", scatter_dimension=1, tiled=True
        ).astype(jnp.float32),
        lax.psum_scatter(
            whole[2].astype(jnp.bfloat16), "loc", scatter_dimension=1, tiled=True
        ).astype(jnp.float32),
        lax.psum_scatter(
            whole[3].astype(jnp.bfloat16), "loc", scatter_dimension=1, tiled=True
        ).astype(jnp.float32),
    )
    stacked = jnp.concatenate(parts, axis=0)
    total_rows = stacked.shape[0]
    padded_rows = -(-total_rows // owners) * owners
    stacked = jnp.pad(stacked, ((0, padded_rows - total_rows), (0, 0)))
    shares = lax.psum_scatter(stacked, "grp", scatter_dimension=0, tiled=True)
    summed = lax.all_gather(shares, "grp", axis=0, tiled=True)
    grad_hidden_one = summed[:model_width]
    grad_input_two = summed[model_width : 2 * model_width]
    grad_hidden_two = summed[2 * model_width : 3 * model_width]
    grad_gate_biases = summed[3 * model_width : 3 * model_width + 2]
    return (
        grad_input_table,
        grad_output_table,
        grad_output_bias,
        grad_hidden_one,
        grad_input_two,
        grad_hidden_two,
        grad_gate_biases,
        grad_carried,
    )


def solution(mesh):
    in_specs = (
        P(None, ("grp", "loc"), None),
        P(("grp", "loc")),
        P(None, ("grp", "loc")),
        P(None, ("grp", "loc")),
        P(None, ("grp", "loc")),
        P(("grp", "loc")),
        P(),
        P("grp", None),
        P("grp", None),
        P("grp"),
        P(None, "loc"),
        P(None, "loc"),
        P(None, "loc"),
        P(None, "loc"),
    )
    out_specs = (
        P(("grp", "loc"), None),
        P(("grp", "loc"), None),
        P(("grp", "loc")),
        P(None, "loc"),
        P(None, "loc"),
        P(None, "loc"),
        P(None, "loc"),
        P(None, ("grp", "loc"), None),
    )
    return jax.shard_map(
        on_device, mesh=mesh, in_specs=in_specs, out_specs=out_specs, check_vma=False
    )
```

profile of v0, /device:TPU:0, one launch (start us, length us, event | category | flops | bytes accessed | tf_op | source)
XLA Modules:
  0.0 1466.9 jit_solution(14733215820618218376)
XLA Ops:
  10.7 38.7 %scatter_fusion.4 = s32[8,48]{1,0:T(8,128)} fusion(s32[8,48]{1,0:T(8,128)} %broadcast.521.clone, s32[256]{0:T(256)S(1)} %bitcast.285, s32[256]{0:T(256)S(1)} %reshape.632), kind=kCustom, calls=%fused_computation.14 | custom fusion | bytes 5120 | tf_op jit(solution)/shard_map/scatter | solution.py:82
  59.8 38.7 %scatter_fusion = s32[8,48]{1,0:T(8,128)} fusion(s32[8,48]{1,0:T(8,128)} %broadcast.521.clone.1, s32[256]{0:T(256)S(1)} %bitcast.290, s32[256]{0:T(256)S(1)} %reshape.604), kind=kCustom, calls=%fused_computation.10 | custom fusion | bytes 5120 | tf_op jit(solution)/shard_map/scatter | solution.py:82
  105.6 10.2 scatter_fusion.1
  153.8 7.6 all-to-all-done.5
  165.9 9.3 gather_fusion
  178.5 34.0 %all-to-all-done.3 = f32[2,8,32,1000]{3,0,2,1:T(2,128)} async-done(((f32[2,8,32,1000]{3,0,2,1:T(2,128)}), f32[2,8,32,1000]{3,0,2,1:T(2,128)}, u32[]{:S(2)}, u32[]{:S(2)}) %all-to-all-start.3) | async-done | bytes 2048032 | tf_op jit(solution)/shard_map/all_to_all | solution.py:137
  227.8 56.0 %all-gather.6 = bf16[8,1,256]{2,1,0:T(2,128)(2,1)S(1)} all-gather(bf16[1,1,256]{2,1,0:T(2,128)(2,1)S(1)} %reshape.670), channel_id=3, replica_groups=mesh['grp'=8,'loc'=4] {'grp'}, dimensions={0}, use_global_device_ids=true | all-gather | bytes 4608 | tf_op jit(solution)/shard_map/all_gather | solution.py:179
  291.9 17.3 %scatter_fusion.3 = f32[2,64,1000]{2,0,1:T(2,128)S(1)} fusion(f32[2,64,1000]{2,0,1:T(2,128)S(1)} %broadcast_in_dim.220, s32[256]{0:T(256)S(1)} %bitcast.325, f32[256,2,1000]{2,1,0:T(2,128)} %bitcast.35), kind=kCustom, calls=%fused_computation.13 | custom fusion | bytes 6145024 | tf_op jit(solution)/shard_map/scatter | solution.py:145
  319.5 8.6 copy.86
  328.1 8.4 reshape.665
  336.5 8.7 copy.87
  347.3 26.8 %while.70 = (s32[]{:T(128)}, f32[64,1000]{1,0:T(8,128)S(1)}, bf16[4,64,1000]{2,1,0:T(8,128)(2,1)S(1)}, f32[4,64,1000]{2,1,0:T(8,128)S(1)}, f32[4,64,3000]{2,1,0:...) while((s32[]{:T(128)}, f32[64,1000]{1,0:T(8,128)S(1)}, ...), condition=%wide.region_10.11_spmd, body=%wide.region_9.10_spmd.sunk | while | flops 385024000 | bytes 12113769 | solution.py:48
  374.1 9.1 copy.88
  383.2 8.4 reshape.667
  391.7 8.3 reshape.675
  409.8 8.7 copy.90
  418.5 8.3 reshape.669
  426.8 8.7 copy.91
  437.7 26.4 %while.71 = (s32[]{:T(128)}, f32[64,1000]{1,0:T(8,128)S(1)}, bf16[4,64,1000]{2,1,0:T(8,128)(2,1)S(1)}, f32[4,64,1000]{2,1,0:T(8,128)S(1)}, f32[4,64,3000]{2,1,0:...) while((s32[]{:T(128)}, f32[64,1000]{1,0:T(8,128)S(1)}, ...), condition=%wide.region_12.13_spmd, body=%wide.region_11.12_spmd.sunk | while | flops 385024000 | bytes 12113769 | solution.py:48
  485.5 33.6 %while.72 = (s32[]{:T(128)}, f32[64,1000]{1,0:T(8,128)}, bf16[4,64,3000]{2,1,0:T(8,128)(2,1)}, bf16[4,64,3000]{2,1,0:T(8,128)(2,1)}, f32[4,64,3000]{2,1,0:T(8,12...) while((s32[]{:T(128)}, f32[64,1000]{1,0:T(8,128)}, ...), condition=%wide.region_27.28_spmd.clone, body=%wide.region_26.27_spmd.clone.sunk | while | flops 388416000 | bytes 42307392 | solution.py:64
  533.3 31.0 %while.73 = (s32[]{:T(128)}, f32[64,1000]{1,0:T(8,128)S(1)}, bf16[4,64,3000]{2,1,0:T(8,128)(2,1)}, bf16[4,64,3000]{2,1,0:T(8,128)(2,1)}, f32[4,64,3000]{2,1,0:T(...) while((s32[]{:T(128)}, f32[64,1000]{1,0:T(8,128)S(1)}, ...), condition=%wide.region_29.30_spmd.clone, body=%wide.region_28.29_spmd.clone.sunk | while | flops 388416000 | bytes 42307392 | solution.py:64
  579.0 10.1 all-reduce.16
  589.2 322.3 %all-reduce.23.cloned.1.call-done = (bf16[1000,3000]{1,0:T(8,128)(2,1)}, bf16[1000,3000]{1,0:T(8,128)(2,1)}, bf16[1000,3000]{1,0:T(8,128)(2,1)}) async-done(((bf16[1000,3000]{1,0:T(8,128)(2,1)}, bf16[1000,3000]{1,0:T(8,128)(2,1)}, bf16[1000,3000]{1,0:T(8,128)(2,1)}), (bf16[1000,3000]{1,0:T(8,128)(2,1)}, bf16[1000,3000]{1,0:T(8,128)(2,1)}, bf16[1000,3000]{1,0:T(8,128)(2,1)})) %all-reduce.23.cloned.1.call-update) | async-done | bytes 18000016
  927.7 155.6 %reduce-scatter.13.cloned.1.call-done = f32[376,750]{1,0:T(8,128)} async-done(((f32[3008,750]{1,0:T(8,128)}), f32[376,750]{1,0:T(8,128)}) %reduce-scatter.13.cloned.1.call-update) | async-done | bytes 1128016 | tf_op jit(solution)/shard_map/reduce_scatter | solution.py:316
  1083.4 11.5 scatter_fusion.7
  1100.9 54.6 %scatter_fusion.5 = bf16[8,48,3000]{2,1,0:T(8,128)(2,1)} fusion(bf16[8,48,3000]{2,1,0:T(8,128)(2,1)} %broadcast_in_dim.218, s32[256]{0:T(256)S(1)} %bitcast.291, bf16[256,3000]{1,0:T(8,128)(2,1)S(1)} %bitcast.298), kind=kCustom, calls=%fused_computation.15 | custom fusion | bytes 4610048 | tf_op jit(solution)/shard_map/scatter | solution.py:245
  1166.1 37.2 %scatter_fusion.6 = bf16[8,48,1000]{2,1,0:T(8,128)(2,1)} fusion(bf16[8,48,1000]{2,1,0:T(8,128)(2,1)} %broadcast_in_dim.231, s32[256]{0:T(256)S(1)} %bitcast.287, bf16[256,1000]{1,0:T(8,128)(2,1)S(1)} %bitcast.306), kind=kCustom, calls=%fused_computation.16 | custom fusion | bytes 1538048 | tf_op jit(solution)/shard_map/scatter | solution.py:250
  1203.4 12.2 all-to-all-done.7
  1223.1 38.6 %all-reduce.11 = f32[2048]{0:T(1024)S(1)} all-reduce(f32[2048]{0:T(1024)S(1)} %get-tuple-element.838), channel_id=7, replica_groups=mesh['grp'=8,'loc'=4] {'grp'}, use_global_device_ids=true, to_apply=%region_38.39.clone | all-reduce | flops 2048 | bytes 16384
  1278.4 11.1 all-to-all-start.10
  1293.8 86.5 %fusion.126 = (f32[152,3000]{1,0:T(8,128)S(1)}, f32[152,1000]{1,0:T(8,128)S(1)}) fusion(f32[588,3000]{1,0:T(8,128)} %fusion.93, f32[588,1000]{1,0:T(8,128)} %convolution_add_fusion.3), kind=kCustom, calls=%all-reduce-scatter.2 | all-reduce-scatter fusion | flops 2432001 | bytes 11840512
  1411.2 39.6 %all-gather.13.cloned.1.call-done = f32[3008,750]{1,0:T(8,128)} async-done(((f32[376,750]{1,0:T(8,128)}), f32[3008,750]{1,0:T(8,128)}) %all-gather.13.cloned.1.call-update) | async-done | bytes 9024016 | tf_op jit(solution)/shard_map/all_gather | solution.py:317
  (385 shorter events, 379.2 us)
Async XLA Ops:
  7.2 118.3 %copy-start = (bf16[588,1000]{1,0:T(8,128)(2,1)S(1)}, bf16[588,1000]{1,0:T(8,128)(2,1)}, u32[]{:S(2)}) copy-start(bf16[588,1000]{1,0:T(8,128)(2,1)} %param.30) | copy-start | bytes 3528004
  7.2 312.3 %all-gather.17.cloned.1.call-start = ((), (), s32[]{:S(2)}) async-start(), calls=%async_computation.17 | async-start | bytes 7680000 | tf_op jit(solution)/shard_map/all_gather | solution.py:118
  7.9 366.2 %all-gather.19.cloned.1.call-start = ((), (), s32[]{:S(2)}) async-start(), calls=%async_computation.18 | async-start | bytes 7680000 | tf_op jit(solution)/shard_map/all_gather | solution.py:119
  8.7 48.7 %copy-start.31 = (s32[4,64]{1,0:T(4,128)S(1)}, s32[4,64]{1,0:T(4,128)}, u32[]{:S(2)}) copy-start(s32[4,64]{1,0:T(4,128)} %param.24) | copy-start | bytes 3076
  8.7 50.0 %copy-start.41 = (s32[64]{0:T(128)S(1)}, s32[64]{0:T(128)}, u32[]{:S(2)}) copy-start(s32[64]{0:T(128)} %param.23) | copy-start | bytes 772
  10.1 46.6 %copy-start.5 = (s32[256,1]{0,1:T(1,128)}, s32[256,1]{0,1:T(1,128)S(1)}, u32[]{:S(2)}) copy-start(s32[256,1]{0,1:T(1,128)S(1)} %get-tuple-element.809) | copy-start | bytes 3076
  49.4 49.1 %all-to-all-start.4 = ((s32[8,1,48]{2,1,0:T(1,128)}), s32[8,1,48]{2,1,0:T(1,128)S(1)}, u32[]{:S(2)}, u32[]{:S(2)}) async-start(s32[8,1,48]{2,1,0:T(1,128)} %bitcast.52), calls=%async_computation.4 | async-start | bytes 8192 | tf_op jit(solution)/shard_map/all_to_all | solution.py:155
  56.7 353.1 %all-gather.21.cloned.1.call-start = ((), (), s32[]{:S(2)}) async-start(), calls=%async_computation.19 | async-start | bytes 7680000 | tf_op jit(solution)/shard_map/all_gather | solution.py:120
  56.7 65.8 %copy-start.2 = (bf16[588]{0:T(1024)(128)(2,1)S(1)}, bf16[588]{0:T(1024)(128)(2,1)}, u32[]{:S(2)}) copy-start(bf16[588]{0:T(1024)(128)(2,1)} %param.31) | copy-start | bytes 3532
  59.0 66.3 %copy-start.7 = (s32[256,1]{0,1:T(1,128)}, s32[256,1]{0,1:T(1,128)S(1)}, u32[]{:S(2)}) copy-start(s32[256,1]{0,1:T(1,128)S(1)} %get-tuple-element.815) | copy-start | bytes 3076
  98.5 17.3 %all-to-all-start = ((s32[8,1,48]{2,1,0:T(1,128)}), s32[8,1,48]{2,1,0:T(1,128)S(1)}, u32[]{:S(2)}, u32[]{:S(2)}) async-start(s32[8,1,48]{2,1,0:T(1,128)} %bitcast.15), calls=%async_computation | async-start | bytes 8192 | tf_op jit(solution)/shard_map/all_to_all | solution.py:154
  115.8 12.4 all-to-all-start.2
  128.2 156.2 %copy-start.28 = (s32[1,8,32]{2,0,1:T(1,128)}, s32[1,8,32]{2,0,1:T(1,128)S(1)}, u32[]{:S(2)}) copy-start(s32[1,8,32]{2,0,1:T(1,128)S(1)} %all-to-all-done.2) | copy-start | bytes 3076
  128.2 12.3 all-to-all-start.6
  140.5 20.9 %all-to-all-start.5 = ((bf16[8,48,1000]{2,1,0:T(8,128)(2,1)}), bf16[8,48,1000]{2,1,0:T(8,128)(2,1)S(1)}, u32[]{:S(2)}, u32[]{:S(2)}) async-start(bf16[8,48,1000]{2,1,0:T(8,128)(2,1)} %broadcast_select_fusion.2), calls=%async_computation.5 | async-start | bytes 1572864 | tf_op jit(solution)/shard_map/all_to_all | solution.py:169
  161.4 51.0 %all-to-all-start.3 = ((f32[2,8,32,1000]{3,0,2,1:T(2,128)}), f32[2,8,32,1000]{3,0,2,1:T(2,128)}, u32[]{:S(2)}, u32[]{:S(2)}) async-start(f32[2,8,32,1000]{3,0,2,1:T(2,128)} %scatter_fusion.2), calls=%async_computation.3 | async-start | bytes 4194304 | tf_op jit(solution)/shard_map/all_to_all | solution.py:137
  212.4 97.3 %all-to-all-start.1 = ((bf16[8,48,3000]{2,1,0:T(8,128)(2,1)}), bf16[8,48,3000]{2,1,0:T(8,128)(2,1)}, u32[]{:S(2)}, u32[]{:S(2)}) async-start(bf16[8,48,3000]{2,1,0:T(8,128)(2,1)} %broadcast_select_fusion), calls=%async_computation.1 | async-start | bytes 4718592 | tf_op jit(solution)/shard_map/all_to_all | solution.py:168
  216.8 249.0 %all-gather.15.cloned.1.call-start = ((), (), s32[]{:S(2)}) async-start(), calls=%async_computation.16 | async-start | bytes 4608000 | tf_op jit(solution)/shard_map/all_gather | solution.py:178
  219.4 64.4 %copy-start.37 = (s32[4,64]{1,0:T(4,128)S(1)}, s32[4,64]{1,0:T(4,128)}, u32[]{:S(2)}) copy-start(s32[4,64]{1,0:T(4,128)} %param.26) | copy-start | bytes 3076
  220.4 691.0 %all-reduce.23.cloned.1.call-start = ((), (), s32[]{:S(2)}) async-start(), calls=%async_computation.20 | async-start | bytes 36864000
  227.8 64.0 %copy-start.10 = (bf16[4,64,1000]{2,1,0:T(8,128)(2,1)}, bf16[4,64,1000]{2,1,0:T(8,128)(2,1)S(1)}, u32[]{:S(2)}) copy-start(bf16[4,64,1000]{2,1,0:T(8,128)(2,1)S(1)} %fusion.141) | copy-start | bytes 1536004
  575.1 508.2 %reduce-scatter.13.cloned.1.call-start = ((), (), s32[]{:S(2)}) async-start(), calls=%async_computation.14 | async-start | bytes 10395648 | tf_op jit(solution)/shard_map/reduce_scatter | solution.py:316
  921.9 352.5 %reduce-scatter.11.cloned.1.call-start = ((), (), s32[]{:S(2)}) async-start(), calls=%async_computation.13 | async-start | bytes 9216000 | tf_op jit(solution)/shard_map/reduce_scatter | solution.py:270
  927.6 155.8 %copy-start.6 = (s32[256,1]{0,1:T(1,128)S(1)}, s32[256,1]{0,1:T(1,128)}, u32[]{:S(2)}) copy-start(s32[256,1]{0,1:T(1,128)} %copy-done.5) | copy-start | bytes 3076
  927.6 523.2 %all-gather.13.cloned.1.call-start = ((), (), s32[]{:S(2)}) async-start(), calls=%async_computation.15 | async-start | bytes 10395648 | tf_op jit(solution)/shard_map/all_gather | solution.py:317
  1095.5 60.1 %all-to-all-start.9 = ((bf16[8,1,48]{2,1,0:T(2,128)(2,1)}), bf16[8,1,48]{2,1,0:T(2,128)(2,1)S(1)}, u32[]{:S(2)}, u32[]{:S(2)}) async-start(bf16[8,1,48]{2,1,0:T(2,128)(2,1)} %copy.100), calls=%async_computation.10 | async-start | bytes 8192 | tf_op jit(solution)/shard_map/all_to_all | solution.py:260
  1155.6 59.9 %all-to-all-start.7 = ((bf16[8,48,3000]{2,1,0:T(8,128)(2,1)}), bf16[8,48,3000]{2,1,0:T(8,128)(2,1)}, u32[]{:S(2)}, u32[]{:S(2)}) async-start(bf16[8,48,3000]{2,1,0:T(8,128)(2,1)} %scatter_fusion.5), calls=%async_computation.7 | async-start | bytes 4718592 | tf_op jit(solution)/shard_map/all_to_all | solution.py:258
  1215.5 62.9 %all-to-all-start.8 = ((bf16[8,48,1000]{2,1,0:T(8,128)(2,1)}), bf16[8,48,1000]{2,1,0:T(8,128)(2,1)}, u32[]{:S(2)}, u32[]{:S(2)}) async-start(bf16[8,48,1000]{2,1,0:T(8,128)(2,1)} %scatter_fusion.6), calls=%async_computation.8 | async-start | bytes 1572864 | tf_op jit(solution)/shard_map/all_to_all | solution.py:259
  1278.4 114.3 %all-to-all-start.10 = ((f32[2,8,32,1000]{3,0,2,1:T(2,128)}), f32[2,8,32,1000]{3,0,2,1:T(2,128)}, u32[]{:S(2)}, u32[]{:S(2)}) async-start(f32[2,8,32,1000]{3,0,2,1:T(2,128)} %broadcast_select_fusion.1), calls=%async_computation.12 | async-start | bytes 4194304 | tf_op jit(solution)/shard_map/all_to_all | solution.py:240
  1293.8 98.9 %copy-start.25 = (s32[64]{0:T(128)S(1)}, s32[64]{0:T(128)}, u32[]{:S(2)}) copy-start(s32[64]{0:T(128)} %get-tuple-element.849) | copy-start | bytes 772
  1380.3 16.1 %collective-permute-start.1 = (f32[15,1000]{1,0:T(8,128)S(1)}, f32[15,1000]{1,0:T(8,128)}, u32[]{:S(2)}, u32[]{:S(2)}) collective-permute-start(f32[15,1000]{1,0:T(8,128)S(1)} %slice.276), channel_id=1, source_target_pairs={{0,1},{1,2},{2,3},{4,5},{5,6},{6,7},{8,9},{9,10},{10,11},{12,13},{... | collective-permute-start | bytes 180008
  1382.2 20.0 %collective-permute-start = (f32[15,3000]{1,0:T(8,128)S(1)}, f32[15,3000]{1,0:T(8,128)S(1)}, u32[]{:S(2)}, u32[]{:S(2)}) collective-permute-start(f32[15,3000]{1,0:T(8,128)S(1)} %slice.275), channel_id=1, source_target_pairs={{0,1},{1,2},{2,3},{4,5},{5,6},{6,7},{8,9},{9,10},{10,11},{12,13},{... | collective-permute-start | bytes 540008
  (38 other events, 298.3 us)
Sparse Core Ops, SparseCore 0:
  9.6 48.2 all-gather.16
  59.4 45.5 all-gather.18
  106.6 45.5 all-gather.20
  220.5 102.6 all-gather.14
  575.2 336.2 all-reduce.22
  922.0 161.2 reduce-scatter.12
  1087.0 187.2 reduce-scatter.10
  1276.6 174.2 all-gather.12
where the time goes:
time: 1490 us; the launch traced here: 1470 us
  waiting for transfers between devices  582 us (39%)
  local copies, waits for them, and re-layouts  411 us (28%)
  blocking collectives  202 us (14%)
  matrix products  115 us (8%)
  starting transfers between devices  68.2 us (5%)
  other arithmetic  68.1 us (5%)
  between operations  17.9 us (1%)
    unnamed x11, waiting for transfers between devices  324 us
    reduce_scatter x1, waiting for transfers between devices, on_device(): shares = lax.psum_scatter(stacked, 'grp', scatter_dimension=0, tiled=True)  156 us
    unnamed x4, blocking collectives  141 us
    scatter x2, local copies, waits for them, and re-layouts, route_rows(): jnp.full((owners, capacity), -1, jnp.int32).at[owner_of, rank_of]  77.4 us
    unnamed x105, local copies, waits for them, and re-layouts  60.9 us
    all_gather x1, blocking collectives, on_device(): lax.all_gather(output_bias[mine], 'grp', axis=0, tiled=True)  56 us
    scatter x1, local copies, waits for them, and re-layouts, on_device(): send_in = jnp.zeros((owners, capacity, gate_width), jnp.bfloat16).at[in_o...  54.6 us
    dot_general x8, matrix products, advance(): jnp.dot(masked.astype(jnp.bfloat16), weight, preferred_element_type=jnp.f...  40 us
  transfers between devices with their start and end apart: 21, of which 9 were waited for; matrix products, arithmetic and copies ran while one was open for 38% of the time, Pallas kernels for 0%

commit v1 on v0

v1 whole, which is shorter than its diff:
```python
import functools

import jax
import jax.numpy as jnp
from jax import lax
from jax.experimental import pallas as pl
from jax.experimental.pallas import tpu as pltpu
from jax.sharding import PartitionSpec as P

BPREG = 1.0
BF16 = jnp.bfloat16
F32 = jnp.float32
I32 = jnp.int32
LANES = 128
VMEM_LIMIT = 48 << 20


def swap(x, axis, bit):
    n = lax.axis_size(axis)
    return lax.ppermute(x, axis, [(i, i ^ bit) for i in range(n)])


def gather_xor(x, axis):
    blocks = {0: x}
    bit = lax.axis_size(axis) // 2
    while bit:
        for k in list(blocks):
            blocks[k | bit] = swap(blocks[k], axis, bit)
        bit //= 2
    return [blocks[k] for k in range(len(blocks))]


def send_xor(chunks, axis):
    return [chunks[0]] + [swap(chunks[j], axis, j) for j in range(1, len(chunks))]


def kernel_call(body, outs, ins, smem=0, scratch=(), flops=0):
    nbytes = sum(a.size * a.dtype.itemsize for a in ins)
    nbytes += sum(int(functools.reduce(lambda a, b: a * b, o.shape)) * o.dtype.itemsize for o in outs)
    return pl.pallas_call(
        body,
        out_shape=outs,
        in_specs=[pl.BlockSpec(memory_space=pltpu.SMEM)] * smem
        + [pl.BlockSpec(memory_space=pltpu.VMEM)] * (len(ins) - smem),
        scratch_shapes=list(scratch),
        compiler_params=pltpu.CompilerParams(vmem_limit_bytes=VMEM_LIMIT),
        cost_estimate=pl.CostEstimate(flops=flops, bytes_accessed=nbytes, transcendentals=0),
    )(*ins)


def shape(dims, dtype):
    return jax.ShapeDtypeStruct(dims, dtype)


def iota(dims, dim):
    return lax.broadcasted_iota(I32, dims, dim)


def dot(a, b, ca=1, cb=0):
    return lax.dot_general(a, b, (((ca,), (cb,)), ((), ())), preferred_element_type=F32)


def low(cond):
    return jnp.where(cond, 1.0, 0.0).astype(BF16)


def route_kernel(owners, rows, cap, batch, ccap, in_ref, tg_ref, plan_ref, s_in, s_tg, s_pl, req):
    width = 2 * cap + ccap

    def place(ids, span):
        n = ids.shape[0]
        owner_i = iota((n, owners), 1)
        member = (ids >= owner_i * span) & (ids < (owner_i + 1) * span)
        earlier = low(iota((n, n), 1) < iota((n, n), 0))
        before = dot(earlier, low(member))
        rank = jnp.sum(jnp.where(member, before, 0.0), axis=1, keepdims=True).astype(I32)
        owner = jnp.sum(jnp.where(member, owner_i, 0).astype(F32), axis=1, keepdims=True).astype(I32)
        return owner, rank

    def wanted(owner, rank, offset, value):
        n = owner.shape[0]
        hit = iota((n, owners * width), 1) == owner * width + offset + rank
        return jnp.sum(jnp.where(hit, value.astype(F32), 0.0), axis=0, keepdims=True)

    o_in, r_in = place(in_ref[...], rows)
    o_tg, r_tg = place(tg_ref[...], rows)
    o_pl, r_pl = place(plan_ref[...], batch)
    s_in[...] = o_in * cap + r_in
    s_tg[...] = o_tg * cap + r_tg
    s_pl[...] = o_pl * ccap + r_pl
    total = wanted(o_in, r_in, 0, in_ref[...] + 1)
    total += wanted(o_tg, r_tg, cap, tg_ref[...] + 1)
    total += wanted(o_pl, r_pl, 2 * cap, plan_ref[...] - o_pl * batch + 1)
    req[...] = total.astype(I32)


def extend(value, keep, hidden):
    lane = iota(value.shape, 1)
    return jnp.where(lane == hidden, 1.0, jnp.where(lane == hidden + 1, keep, value)).astype(BF16)


def run_steps(steps, batch, hidden, l, keep_ref, w_refs, x_of, start, state_ref, res, q_s):
    n_loc = len(w_refs)
    wide = start.shape[1]
    tail = jnp.zeros((batch, wide), F32)
    lane = iota((batch, wide), 1)
    prev = start
    for t in range(steps):
        at = pl.ds(t * batch, batch)
        keep = keep_ref[at, :]
        state_ref[at, :] = extend(prev, keep, hidden)
        p = prev * keep
        p_low = p.astype(BF16)
        for j in range(n_loc):
            q_s[l ^ j] = dot(p_low, w_refs[j][...])
        q = jnp.concatenate([q_s[i] for i in range(n_loc)] + [tail], axis=1)
        x = x_of(t)
        h2 = 2 * hidden
        z = jax.nn.sigmoid(x[:, :wide] + q[:, :wide])
        r = jax.nn.sigmoid(x[:, hidden : hidden + wide] + q[:, hidden : hidden + wide])
        qn = q[:, h2 : h2 + wide]
        n = jnp.tanh(x[:, h2 : h2 + wide] + r * qn)
        prev = jnp.where(lane < hidden, n + z * (p - n), 0.0)
        for ref, val in zip(res, (z, r, n, qn, p)):
            ref[at, :] = val
    state_ref[pl.ds(steps * batch, batch), :] = extend(prev, 0.0, hidden)


def first_kernel(
    dims, l_ref, keep_ref, slot_ref, land_ref, got_ref, rows_ref, *refs
):
    steps, batch, hidden, bias_row, n_loc = dims
    w_refs, refs = refs[:n_loc], refs[n_loc:]
    state_ref, start2_ref, z_ref, r_ref, n_ref, qn_ref, p_ref, q_s, b_s = refs
    wide = z_ref.shape[1]
    l = l_ref[0]
    for j in range(n_loc):
        b_s[l ^ j] = w_refs[j][bias_row : bias_row + 16, :].astype(F32)
    bias = jnp.concatenate([b_s[i][0:1, :] for i in range(n_loc)], axis=1)
    pad = jnp.zeros((batch, wide), F32)
    land = low(iota((batch, land_ref.shape[1]), 0) == land_ref[...])
    moved = dot(land, got_ref[...])
    start2_ref[...] = moved[:, wide:]

    def x_of(t):
        slot = slot_ref[pl.ds(t * batch, batch), :]
        pick = low(iota((batch, rows_ref.shape[0]), 1) == slot)
        return jnp.concatenate([dot(pick, rows_ref[...]) + bias, pad], axis=1)

    run_steps(
        steps, batch, hidden, l, keep_ref, w_refs, x_of, moved[:, :wide], state_ref,
        (z_ref, r_ref, n_ref, qn_ref, p_ref), q_s,
    )


def second_kernel(dims, l_ref, keep_ref, start_ref, below_ref, *refs):
    steps, batch, hidden, n_loc = dims
    in_refs, w_refs, refs = refs[:n_loc], refs[n_loc : 2 * n_loc], refs[2 * n_loc :]
    state_ref, z_ref, r_ref, n_ref, qn_ref, p_ref, q_s, x_s = refs
    wide = z_ref.shape[1]
    l = l_ref[0]
    below = below_ref[pl.ds(batch, steps * batch), :]
    for j in range(n_loc):
        x_s[l ^ j] = dot(below, in_refs[j][...])
    pad = jnp.zeros((batch, wide), F32)

    def x_of(t):
        return jnp.concatenate(
            [x_s[i][t * batch : (t + 1) * batch, :] for i in range(n_loc)] + [pad], axis=1
        )

    run_steps(
        steps, batch, hidden, l, keep_ref, w_refs, x_of, start_ref[...], state_ref,
        (z_ref, r_ref, n_ref, qn_ref, p_ref), q_s,
    )


def score_kernel(dims, valid_ref, slot_ref, state_ref, tg_ref, *refs):
    steps, batch, n_loc = dims
    neg_refs, refs = refs[:n_loc], refs[n_loc:]
    gn_refs, into_ref, send_ref, tgg_s = refs[:n_loc], refs[n_loc], refs[n_loc + 1], refs[n_loc + 2]
    diag = iota((batch, batch), 0) == iota((batch, batch), 1)
    slots = tg_ref.shape[0]
    for t in range(steps):
        at = pl.ds(t * batch, batch)
        second = state_ref[pl.ds((t + 1) * batch, batch), :]
        pick = low(iota((batch, slots), 1) == slot_ref[at, :])
        targets = dot(pick, tg_ref[...]).astype(BF16)
        st = dot(second, targets, 1, 1)
        sn = [dot(second, ref[...], 1, 1) for ref in neg_refs]
        pos = jnp.sum(jnp.where(diag, st, 0.0), axis=1, keepdims=True)
        top = jnp.max(jnp.where(diag, -jnp.inf, st), axis=1, keepdims=True)
        for s in sn:
            top = jnp.maximum(top, jnp.max(s, axis=1, keepdims=True))
        parts = [(st, jnp.where(diag, 0.0, jnp.exp(st - top)))]
        parts += [(s, jnp.exp(s - top)) for s in sn]
        mass = sum(jnp.sum(e, axis=1, keepdims=True) for _, e in parts)
        scale = 1.0 / mass
        parts = [(s, e * scale, jax.nn.sigmoid(pos - s)) for s, e in parts]
        inside = sum(jnp.sum(w * g, axis=1, keepdims=True) for _, w, g in parts)
        penalty = sum(jnp.sum(w * s * s, axis=1, keepdims=True) for s, w, _ in parts)
        slope = sum(jnp.sum(w * g * (1.0 - g), axis=1, keepdims=True) for _, w, g in parts)
        inv = 1.0 / inside
        weight = valid_ref[at, :]
        grads = [
            weight * w * (1.0 + BPREG * (s * s + 2.0 * s - penalty) - g * g * inv)
            for s, w, g in parts
        ]
        gt = grads[0] - jnp.where(diag, weight * slope * inv, 0.0)
        gt_low = gt.astype(BF16)
        into = dot(gt_low, targets)
        for j in range(n_loc):
            gn_low = grads[j + 1].astype(BF16)
            gn_refs[j][at, :] = gn_low
            into += dot(gn_low, neg_refs[j][...])
        into_ref[at, :] = into
        tgg_s[at, :] = dot(gt_low, second, 0, 0).astype(BF16)
    pick = low(iota((steps * batch, slots), 1) == slot_ref[...])
    send_ref[...] = dot(pick, tgg_s[...], 0, 0).astype(BF16)


def back_steps(steps, batch, hidden, l, keep_ref, w_refs, into_ref, res, dq_s, emit):
    n_loc = len(w_refs)
    chunk = dq_s.shape[2]
    wide = into_ref.shape[1]
    lane = iota((batch, wide), 1)
    z_ref, r_ref, n_ref, qn_ref, p_ref = res
    carry = jnp.zeros((batch, wide), F32)
    for t in reversed(range(steps)):
        at = pl.ds(t * batch, batch)
        g = jnp.where(lane < hidden, into_ref[at, :] + carry, 0.0)
        z, r, n, qn, p = (ref[at, :] for ref in (z_ref, r_ref, n_ref, qn_ref, p_ref))
        dc = g * (1.0 - z) * (1.0 - n * n)
        da_z = (g * (p - n) * z * (1.0 - z))[:, :hidden]
        da_r = (dc * qn * r * (1.0 - r))[:, :hidden]
        da_n = dc[:, :hidden]
        dq_n = (dc * r)[:, :hidden]
        da = jnp.concatenate([da_z, da_r, da_n], axis=1)
        dq = jnp.concatenate([da_z, da_r, dq_n], axis=1)
        emit(t, da, dq)
        for i in range(n_loc):
            dq_s[i] = dq[:, i * chunk : (i + 1) * chunk]
        dp = g * z
        for j in range(n_loc):
            dp += dot(dq_s[l ^ j].astype(BF16), w_refs[j][...], 1, 1)
        carry = dp * keep_ref[at, :]
    return jnp.where(lane < hidden, carry, 0.0)


def back_second_kernel(dims, l_ref, keep_ref, into_ref, *refs):
    steps, batch, hidden, n_loc = dims
    res, refs = refs[:5], refs[5:]
    in_refs, w_refs, refs = refs[:n_loc], refs[n_loc : 2 * n_loc], refs[2 * n_loc :]
    init_ref, first_ref, refs = refs[0], refs[1], refs[2:]
    ch_refs, refs = refs[:n_loc], refs[n_loc:]
    dq_s, da_all, dq_all = refs
    l = l_ref[0]
    chunk = dq_s.shape[2]

    def emit(t, da, dq):
        for i in range(n_loc):
            da_all[i, pl.ds(t * batch, batch), :] = da[:, i * chunk : (i + 1) * chunk]
            dq_all[i, pl.ds(t * batch, batch), :] = dq[:, i * chunk : (i + 1) * chunk]

    init_ref[...] = back_steps(
        steps, batch, hidden, l, keep_ref, w_refs, into_ref, res, dq_s, emit
    )
    rows = steps * batch
    total = None
    for j in range(n_loc):
        da_low = da_all[l ^ j].astype(BF16)
        ch_refs[j][pl.ds(0, rows), :] = da_low
        ch_refs[j][pl.ds(rows, rows), :] = dq_all[l ^ j].astype(BF16)
        part = dot(da_low, in_refs[j][...], 1, 1)
        total = part if total is None else total + part
    first_ref[...] = total


def back_first_kernel(dims, l_ref, keep_ref, slot_ref, land_ref, init2_ref, into_ref, *refs):
    steps, batch, hidden, n_loc = dims
    res, refs = refs[:5], refs[5:]
    w_refs, refs = refs[:n_loc], refs[n_loc:]
    send_ref, back_ref, refs = refs[0], refs[1], refs[2:]
    ch_refs, refs = refs[:n_loc], refs[n_loc:]
    dq_s, da_all, dq_all, bias_s = refs
    l = l_ref[0]
    chunk = dq_s.shape[2]
    wide = into_ref.shape[1]

    def emit(t, da, dq):
        da_all[pl.ds(t * batch, batch), :] = da.astype(BF16)
        for i in range(n_loc):
            dq_all[i, pl.ds(t * batch, batch), :] = dq[:, i * chunk : (i + 1) * chunk]

    init = back_steps(steps, batch, hidden, l, keep_ref, w_refs, into_ref, res, dq_s, emit)
    rows = steps * batch
    da = da_all[...]
    bias = jnp.sum(da.astype(F32), axis=0, keepdims=True)
    for i in range(n_loc):
        part = bias[:, i * chunk : (i + 1) * chunk]
        bias_s[i] = jnp.concatenate([part, jnp.zeros((15, chunk), F32)], axis=0)
    for j in range(n_loc):
        ch_refs[j][pl.ds(0, rows), :] = dq_all[l ^ j].astype(BF16)
        ch_refs[j][pl.ds(rows, 16), :] = bias_s[l ^ j].astype(BF16)
    pick = low(iota((rows, send_ref.shape[0]), 1) == slot_ref[...])
    send_ref[...] = dot(pick, da, 0, 0).astype(BF16)
    land = low(iota((batch, land_ref.shape[1]), 0) == land_ref[...])
    back_ref[:, :wide] = dot(land, init.astype(BF16), 0, 0).astype(BF16)
    back_ref[:, wide:] = dot(land, init2_ref[...].astype(BF16), 0, 0).astype(BF16)


def dense_two_kernel(dims, *refs):
    steps, batch, hidden, n_loc = dims
    rows = steps * batch
    a_refs, b_refs, ch_refs = refs[:n_loc], refs[n_loc : 2 * n_loc], refs[2 * n_loc : 3 * n_loc]
    out_ref = refs[3 * n_loc]
    wide = a_refs[0].shape[1]
    for which in range(2):
        total = None
        for j in range(n_loc):
            if which == 0:
                left = a_refs[j][pl.ds(batch, rows), :]
                right = ch_refs[j][pl.ds(0, rows), :]
            else:
                left = b_refs[j][pl.ds(0, rows), :]
                left = (left.astype(F32) * left[:, hidden + 1 : hidden + 2].astype(F32)).astype(BF16)
                right = ch_refs[j][pl.ds(rows, rows), :]
            part = dot(left, right, 0, 0)
            total = part if total is None else total + part
        out_ref[pl.ds(which * wide, wide), :] = total.astype(BF16)


def dense_one_kernel(dims, *refs):
    steps, batch, hidden, bias_row, n_loc = dims
    rows = steps * batch
    a_refs, ch_refs = refs[:n_loc], refs[n_loc : 2 * n_loc]
    out_ref = refs[2 * n_loc]
    total, bias = None, None
    for j in range(n_loc):
        left = a_refs[j][pl.ds(0, rows), :]
        left = (left.astype(F32) * left[:, hidden + 1 : hidden + 2].astype(F32)).astype(BF16)
        part = dot(left, ch_refs[j][pl.ds(0, rows), :], 0, 0)
        extra = ch_refs[j][pl.ds(rows, 16), :].astype(F32)
        total = part if total is None else total + part
        bias = extra if bias is None else bias + extra
    out_ref[...] = total.astype(BF16)
    out_ref[pl.ds(bias_row, 16), :] = bias.astype(BF16)


def neg_kernel(n_loc, *refs):
    gn_refs, b_refs, out_ref = refs[:n_loc], refs[n_loc : 2 * n_loc], refs[2 * n_loc]
    rows = gn_refs[0].shape[0]
    batch = b_refs[0].shape[0] - rows
    total = None
    for j in range(n_loc):
        part = dot(gn_refs[j][...], b_refs[j][pl.ds(batch, rows), :], 0, 0)
        total = part if total is None else total + part
    out_ref[...] = total.astype(BF16)


def on_device(
    carried,
    session_plan,
    item_ids,
    target_ids,
    reset_mask,
    valid_counts,
    negative_ids,
    input_table,
    output_table,
    output_bias,
    hidden_one,
    input_two,
    hidden_two,
    gate_biases,
):
    hidden = carried.shape[2]
    wide = -(-(hidden + 2) // LANES) * LANES
    bias_row = wide - 16
    steps, batch = item_ids.shape
    events = steps * batch
    owners = lax.axis_size("grp")
    n_loc = lax.axis_size("loc")
    grp = lax.axis_index("grp")
    loc = lax.axis_index("loc")
    rows = input_table.shape[0]
    base = grp * rows
    gates = input_table.shape[1]
    chunk = gates // n_loc
    cap = events // owners + events // (2 * owners)
    ccap = 4 * batch // owners
    slots, cslots = owners * cap, owners * ccap
    width = 2 * cap + ccap
    neg_own = negative_ids.shape[0] // owners // n_loc
    neg_part = owners * neg_own
    l_arr = loc.astype(I32).reshape(1)

    def pad_rows(w, extra, at):
        out = jnp.zeros((wide, w.shape[1]), BF16).at[: w.shape[0]].set(w)
        return out if extra is None else out.at[at].set(extra)

    w_one = gather_xor(pad_rows(hidden_one, gate_biases[0], bias_row), "loc")
    w_in = gather_xor(pad_rows(input_two, gate_biases[1], hidden), "loc")
    w_two = gather_xor(pad_rows(hidden_two, None, 0), "loc")

    slot_in, slot_tg, slot_pl, request = kernel_call(
        functools.partial(route_kernel, owners, rows, cap, batch, ccap),
        [
            shape((events, 1), I32),
            shape((events, 1), I32),
            shape((batch, 1), I32),
            shape((1, owners * width), I32),
        ],
        [item_ids.reshape(events, 1), target_ids.reshape(events, 1), session_plan.reshape(batch, 1)],
    )
    arrived = lax.all_to_all(
        request.reshape(owners, width), "grp", split_axis=0, concat_axis=0, tiled=True
    )
    in_ids = (arrived[:, :cap] - 1 - base).reshape(slots)
    tg_ids = arrived[:, cap : 2 * cap] - 1 - base
    land = (arrived[:, 2 * cap :] - 1).reshape(1, cslots)
    mine = lax.dynamic_slice(
        negative_ids.reshape(owners, n_loc, neg_own), (grp, loc, 0), (1, 1, neg_own)
    ).reshape(1, neg_own) - base
    out_ids = jnp.concatenate(
        [tg_ids, jnp.broadcast_to(mine, (owners, neg_own))], axis=1
    ).reshape(owners * (cap + neg_own))
    row_range = jnp.arange(rows, dtype=I32)

    pair = jnp.pad(carried.astype(BF16), ((0, 0), (0, 0), (0, wide - hidden)))
    pair = jnp.concatenate([pair[0], pair[1]], axis=1)
    pick_pl = (slot_pl == jnp.arange(cslots, dtype=I32)[None, :]).astype(BF16)
    got_c = lax.all_to_all(
        dot(pick_pl, pair, 0, 0).astype(BF16).reshape(owners, ccap, 2 * wide),
        "grp", split_axis=0, concat_axis=0, tiled=True,
    ).reshape(cslots, 2 * wide)

    pick_in = (in_ids[:, None] == row_range[None, :]).astype(BF16)
    got_rows = lax.all_to_all(
        dot(pick_in, input_table).astype(BF16).reshape(owners, cap, gates),
        "grp", split_axis=0, concat_axis=0, tiled=True,
    ).reshape(slots, gates)
    table_ext = jnp.concatenate(
        [output_table, output_bias[:, None], jnp.zeros((rows, wide - hidden - 1), BF16)], axis=1
    )
    pick_out = (out_ids[:, None] == row_range[None, :]).astype(BF16)
    got_out = lax.all_to_all(
        dot(pick_out, table_ext).astype(BF16).reshape(owners, cap + neg_own, wide),
        "grp", split_axis=0, concat_axis=0, tiled=True,
    )
    tg_rows = got_out[:, :cap].reshape(slots, wide)
    negs = gather_xor(got_out[:, cap:].reshape(neg_part, wide), "loc")

    keep = (1 - reset_mask).astype(F32).reshape(events, 1)
    valid = (jnp.arange(steps, dtype=I32)[:, None] < valid_counts[None, :]).astype(F32)
    valid = (valid / steps).reshape(events, 1)

    flop = 2 * events * wide * gates
    res_shapes = [shape((events, wide), F32)] * 5
    state_shape = shape(((steps + 1) * batch, wide), BF16)
    q_scratch = pltpu.VMEM((n_loc, batch, chunk), F32)
    all_scratch = pltpu.VMEM((n_loc, events, chunk), F32)

    state_a, start_two, *res_one = kernel_call(
        functools.partial(first_kernel, (steps, batch, hidden, bias_row, n_loc)),
        [state_shape, shape((batch, wide), F32)] + res_shapes,
        [l_arr, keep, slot_in, land, got_c, got_rows] + w_one,
        1,
        [q_scratch, pltpu.VMEM((n_loc, 16, chunk), F32)],
        flop,
    )
    states_a = gather_xor(state_a, "loc")
    state_b, *res_two = kernel_call(
        functools.partial(second_kernel, (steps, batch, hidden, n_loc)),
        [state_shape] + res_shapes,
        [l_arr, keep, start_two, state_a] + w_in + w_two,
        1,
        [q_scratch, all_scratch],
        2 * flop,
    )
    states_b = gather_xor(state_b, "loc")

    *g_neg, into_second, send_tg = kernel_call(
        functools.partial(score_kernel, (steps, batch, n_loc)),
        [shape((events, neg_part), BF16)] * n_loc
        + [shape((events, wide), F32), shape((slots, wide), BF16)],
        [valid, slot_tg, state_b, tg_rows] + negs,
        0,
        [pltpu.VMEM((events, wide), BF16)],
        flop,
    )
    g_neg = send_xor(g_neg, "loc")
    neg_grad = kernel_call(
        functools.partial(neg_kernel, n_loc), [shape((neg_part, wide), BF16)], g_neg + states_b
    )[0]
    got_out_g = lax.all_to_all(
        jnp.concatenate(
            [send_tg.reshape(owners, cap, wide), neg_grad.reshape(owners, neg_own, wide)], axis=1
        ),
        "grp", split_axis=0, concat_axis=0, tiled=True,
    ).reshape(owners * (cap + neg_own), wide)

    init_two, into_first, *ch_two = kernel_call(
        functools.partial(back_second_kernel, (steps, batch, hidden, n_loc)),
        [shape((batch, wide), F32), shape((events, wide), F32)]
        + [shape((2 * events, chunk), BF16)] * n_loc,
        [l_arr, keep, into_second] + res_two + w_in + w_two,
        1,
        [q_scratch, all_scratch, all_scratch],
        2 * flop,
    )
    ch_two = send_xor(ch_two, "loc")
    send_in, back_c, *ch_one = kernel_call(
        functools.partial(back_first_kernel, (steps, batch, hidden, n_loc)),
        [shape((slots, gates), BF16), shape((cslots, 2 * wide), BF16)]
        + [shape((events + 16, chunk), BF16)] * n_loc,
        [l_arr, keep, slot_in, land, init_two, into_first] + res_one + w_one,
        1,
        [q_scratch, pltpu.VMEM((events, gates), BF16), all_scratch, pltpu.VMEM((n_loc, 16, chunk), F32)],
        flop,
    )
    ch_one = send_xor(ch_one, "loc")

    dense_two = kernel_call(
        functools.partial(dense_two_kernel, (steps, batch, hidden, n_loc)),
        [shape((2 * wide, chunk), BF16)],
        states_a + states_b + ch_two,
        0, (), 2 * flop,
    )[0]
    dense_one = kernel_call(
        functools.partial(dense_one_kernel, (steps, batch, hidden, bias_row, n_loc)),
        [shape((wide, chunk), BF16)],
        states_a + ch_one,
        0, (), flop,
    )[0]

    def all_sum(x):
        share = lax.psum_scatter(x, "grp", scatter_dimension=0, tiled=True)
        return lax.all_gather(share, "grp", axis=0, tiled=True).astype(F32)

    got_in_g = lax.all_to_all(
        send_in.reshape(owners, cap, gates), "grp", split_axis=0, concat_axis=0, tiled=True
    ).reshape(slots, gates)
    got_back = lax.all_to_all(
        back_c.reshape(owners, ccap, 2 * wide), "grp", split_axis=0, concat_axis=0, tiled=True
    ).reshape(cslots, 2 * wide)
    own = rows // n_loc
    own_pad = -(-own // 16) * 16
    row_of = jnp.arange(own_pad, dtype=I32)
    part_of = loc ^ jnp.arange(n_loc, dtype=I32)
    target = jnp.where(row_of[None, :] < own, part_of[:, None] * own + row_of[None, :], rows)
    target = jnp.where(target < rows, target, -rows * (owners + 1)).reshape(n_loc * own_pad)

    def table_sum(ids, grads):
        match = (target[:, None] == ids[None, :]).astype(BF16)
        part = dot(match, grads).astype(BF16).reshape(n_loc, own_pad, grads.shape[1])
        parts = [part[j] for j in range(n_loc)]
        bit = 1
        while bit < n_loc:
            keep_p = [p for j, p in enumerate(parts) if not j & 1]
            send_p = jnp.stack([p for j, p in enumerate(parts) if j & 1])
            got_p = swap(send_p, "loc", bit)
            parts = [p.astype(F32) + got_p[i].astype(F32) for i, p in enumerate(keep_p)]
            bit *= 2
            if bit < n_loc:
                parts = [p.astype(BF16) for p in parts]
        return parts[0][:own]

    table_in = table_sum(in_ids, got_in_g)
    table_out = table_sum(out_ids, got_out_g)

    pair_two = all_sum(dense_two)
    grad_one = all_sum(dense_one)
    back = dot(pick_pl, got_back)
    grad_carried = jnp.stack([back[:, :hidden], back[:, wide : wide + hidden]])
    grad_biases = jnp.stack([grad_one[bias_row], pair_two[hidden]])
    return (
        table_in,
        table_out[:, :hidden],
        table_out[:, hidden],
        grad_one[:hidden],
        pair_two[:hidden],
        pair_two[wide : wide + hidden],
        grad_biases,
        grad_carried,
    )


def solution(mesh):
    in_specs = (
        P(None, ("grp", "loc"), None),
        P(("grp", "loc")),
        P(None, ("grp", "loc")),
        P(None, ("grp", "loc")),
        P(None, ("grp", "loc")),
        P(("grp", "loc")),
        P(),
        P("grp", None),
        P("grp", None),
        P("grp"),
        P(None, "loc"),
        P(None, "loc"),
        P(None, "loc"),
        P(None, "loc"),
    )
    out_specs = (
        P(("grp", "loc"), None),
        P(("grp", "loc"), None),
        P(("grp", "loc")),
        P(None, "loc"),
        P(None, "loc"),
        P(None, "loc"),
        P(None, "loc"),
        P(None, ("grp", "loc"), None),
    )
    return jax.shard_map(
        on_device, mesh=mesh, in_specs=in_specs, out_specs=out_specs, check_vma=False
    )
```

time: 1490 us -> 704 us (0.47); the launches traced: 1470 us -> 696 us
  local copies, waits for them, and re-layouts: 411 us -> 109 us
  waiting for transfers between devices: 582 us -> 347 us
  blocking collectives: 202 us -> 51.8 us
  matrix products: 115 us -> 20.2 us
  Pallas kernels: 0 us -> 91.2 us
  other arithmetic: 68.1 us -> 15.7 us
  starting transfers between devices: 68.2 us -> 46 us
    unnamed x11 -> x4, waiting for transfers between devices: 324 us -> 0.71 us
    scatter x8, local copies, waits for them, and re-layouts: 215 us -> 8.51 us  [the longest x4 4.91 us: pad_rows(): out = jnp.zeros((wide, w.shape[1]), BF16).at[:w.shape[0]].set(w)]
    ppermute x0 -> x31, waiting for transfers between devices: none -> 203 us  [swap(): return lax.ppermute(x, axis, [(i, i ^ bit) for i in range(n)])]
    reduce_scatter x2, waiting for transfers between devices: 159 us -> 0.02 us  [all_sum(): share = lax.psum_scatter(x, 'grp', scatter_dimension=0, tiled=True)]
    unnamed x4 -> x0, blocking collectives: 141 us -> none
    dot_general x32 -> x6, matrix products: 115 us -> 20.2 us  [dot(): lax.dot_general(a, b, (((ca,), (cb,)), ((), ())), preferred_element_type=...]
    pallas_call x0 -> x9, Pallas kernels: none -> 91.2 us  [kernel_call(): pl.pallas_call(body, out_shape=outs, in_specs=[pl.BlockSpec(memory_space=...]
    all_to_all x11 -> x6, waiting for transfers between devices: 59.2 us -> 141 us  [the longest x1 44.3 us: on_device(): lax.all_to_all(send_in.reshape(owners, cap, gates), 'grp', split_axis=0,...]
  transfers between devices with their start and end apart: 21 -> 41, of which waited for: 9 -> 18; matrix products, arithmetic and copies ran while one was open for 38% -> 16% of each run, Pallas kernels for 0% -> 12%
where the time goes in v1:
time: 704 us; the launch traced here: 696 us
  waiting for transfers between devices  347 us (49%)
  local copies, waits for them, and re-layouts  109 us (15%)
  Pallas kernels  91.2 us (13%)
  blocking collectives  51.8 us (7%)
  starting transfers between devices  46 us (7%)
  matrix products  20.2 us (3%)
  other arithmetic  15.7 us (2%)
  between operations  14.6 us (2%)
    ppermute x31, waiting for transfers between devices, swap(): return lax.ppermute(x, axis, [(i, i ^ bit) for i in range(n)])  203 us
    pallas_call x9, Pallas kernels, kernel_call(): pl.pallas_call(body, out_shape=outs, in_specs=[pl.BlockSpec(memory_space=...  91.2 us
    all_to_all x1, blocking collectives, on_device(): lax.all_to_all(back_c.reshape(owners, ccap, 2 * wide), 'grp', split_axis=...  51.8 us
    all_to_all x1, waiting for transfers between devices, on_device(): lax.all_to_all(send_in.reshape(owners, cap, gates), 'grp', split_axis=0,...  44.3 us
    all_to_all x1, waiting for transfers between devices, on_device(): lax.all_to_all(jnp.concatenate([send_tg.reshape(owners, cap, wide), neg_g...  39.7 us
    all_to_all x1, waiting for transfers between devices, on_device(): lax.all_to_all(dot(pick_out, table_ext).astype(BF16).reshape(owners, cap...  32.1 us
    ppermute x13, local copies, waits for them, and re-layouts, swap(): return lax.ppermute(x, axis, [(i, i ^ bit) for i in range(n)])  32 us
    unnamed x105, local copies, waits for them, and re-layouts  29.4 us
  transfers between devices with their start and end apart: 41, of which 18 were waited for; matrix products, arithmetic and copies ran while one was open for 16% of the time, Pallas kernels for 12%

profile of v1, /device:TPU:0, one launch (start us, length us, event | category | flops | bytes accessed | tf_op | source)
XLA Modules:
  0.0 696.0 jit_solution(12639673680353821573)
XLA Ops:
  11.7 7.3 %all-to-all-start = ((s32[8,1,128]{2,1,0:T(1,128)}), s32[8,1,128]{2,1,0:T(1,128)S(1)}, u32[]{:S(2)}, u32[]{:S(2)}) async-start(s32[8,1,128]{2,1,0:T(1,128)} %bitcast.2), calls=%async_computation | async-start | bytes 8192 | tf_op jit(solution)/shard_map/all_to_all | solution.py:416
  32.4 21.3 %all-to-all-done.1 = bf16[8,32,2048]{2,1,0:T(8,128)(2,1)S(1)} async-done(((bf16[8,32,2048]{2,1,0:T(8,128)(2,1)}), bf16[8,32,2048]{2,1,0:T(8,128)(2,1)S(1)}, u32[]{:S(2)}, u32[]{:S(2)}) %all-to-all-start.1) | async-done | bytes 1048608 | tf_op jit(solution)/shard_map/all_to_all | solution.py:433
  58.4 6.1 convolution_convert_fusion.1
  64.5 4.3 copy.40
  68.8 32.1 %all-to-all-done.3 = bf16[8,112,1024]{2,1,0:T(8,128)(2,1)S(1)} async-done(((bf16[8,112,1024]{2,1,0:T(8,128)(2,1)}), bf16[8,112,1024]{2,1,0:T(8,128)(2,1)S(1)}, u32[]{:S(2)}, u32[]{:S(2)}) %all-to-all-start.3) | async-done | bytes 1835040 | tf_op jit(solution)/shard_map/all_to_all | solution.py:447
  102.2 4.4 all-to-all-start.2
  119.5 26.5 %collective-permute-done.1 = bf16[1024,750]{0,1:T(8,128)(2,1)} collective-permute-done((bf16[1024,750]{0,1:T(8,128)(2,1)}, bf16[1024,750]{0,1:T(8,128)(2,1)}, u32[]{:S(2)}, u32[]{:S(2)}) %collective-permute-start.1) | collective-permute-done | bytes 1536032 | tf_op jit(solution)/shard_map/ppermute | solution.py:20
  148.9 30.1 %collective-permute-done.4 = bf16[1024,750]{0,1:T(8,128)(2,1)} collective-permute-done((bf16[1024,750]{0,1:T(8,128)(2,1)}, bf16[1024,750]{0,1:T(8,128)(2,1)}, u32[]{:S(2)}, u32[]{:S(2)}) %collective-permute-start.4) | collective-permute-done | bytes 1536032 | tf_op jit(solution)/shard_map/ppermute | solution.py:20
  179.5 32.5 %collective-permute-done.7 = bf16[1024,750]{0,1:T(8,128)(2,1)} collective-permute-done((bf16[1024,750]{0,1:T(8,128)(2,1)}, bf16[1024,750]{0,1:T(8,128)(2,1)}, u32[]{:S(2)}, u32[]{:S(2)}) %collective-permute-start.7) | collective-permute-done | bytes 1536032 | tf_op jit(solution)/shard_map/ppermute | solution.py:20
  212.5 19.9 %collective-permute-done.10.refs_2_ = bf16[512,1024]{1,0:T(8,128)(2,1)} collective-permute-done((bf16[512,1024]{1,0:T(8,128)(2,1)S(1)}, bf16[512,1024]{1,0:T(8,128)(2,1)}, u32[]{:S(2)}, u32[]{:S(2)}) %collective-permute-start.10) | collective-permute-done | bytes 1048608 | tf_op jit(solution)/shard_map/ppermute | solution.py:20
  240.6 12.8 %shard_map.198 = (bf16[320,1024]{1,0:T(8,128)(2,1)S(1)}, f32[64,1024]{1,0:T(8,128)S(1)}, f32[256,1024]{1,0:T(8,128)S(1)}, f32[256,1024]{1,0:T(8,128)S(1)}, f32[2...) custom-call(s32[1]{0:T(128)} %bitcast.4.l_ref, f32[256,1]{1,0:T(8,128)S(1)} %reshape.337.keep_ref, ...), custom_call_target="tpu_custom_call" | custom-call | flops 1572864000 | bytes 15660036 | tf_op jit(solution)/shard_map/pallas_call | solution.py:40
  277.7 14.6 %shard_map.199 = (bf16[320,1024]{1,0:T(8,128)(2,1)S(1)}, f32[256,1024]{1,0:T(8,128)S(1)}, f32[256,1024]{1,0:T(8,128)S(1)}, f32[256,1024]{1,0:T(8,128)S(1)}, f32[...) custom-call(s32[1]{0:T(128)} %bitcast.4.l_ref, f32[256,1]{1,0:T(8,128)S(1)} %reshape.337.keep_ref, f32[64,1024]{1,0:T(8,128)S(1)} %copy-done.23, ...), custom_call_target="tpu_custom_call" | custom-call | flops 3145728000 | bytes 19104772 | tf_op jit(solution)/shard_map/pallas_call | solution.py:40
  295.6 14.3 %shard_map.200 = (bf16[256,512]{1,0:T(8,128)(2,1)S(1)}, bf16[256,512]{1,0:T(8,128)(2,1)S(1)}, bf16[256,512]{1,0:T(8,128)(2,1)S(1)}, bf16[256,512]{1,0:T(8,128)(2...) custom-call(f32[256,1]{1,0:T(8,128)S(1)} %copy-done.19, s32[256,1]{1,0:T(8,128)S(1)} %copy-done.25, ...), custom_call_target="tpu_custom_call" | custom-call | flops 1572864000 | bytes 8521728 | tf_op jit(solution)/shard_map/pallas_call | solution.py:40
  313.6 17.2 %shard_map.201 = (f32[64,1024]{1,0:T(8,128)S(1)}, f32[256,1024]{1,0:T(8,128)S(1)}, bf16[512,750]{1,0:T(8,128)(2,1)S(1)}, bf16[512,750]{1,0:T(8,128)(2,1)S(1)}, b...) custom-call(s32[1]{0:T(128)} %bitcast.4.l_ref, f32[256,1]{1,0:T(8,128)S(1)} %reshape.337.keep_ref, ...), custom_call_target="tpu_custom_call" | custom-call | flops 3145728000 | bytes 22963204 | tf_op jit(solution)/shard_map/pallas_call | solution.py:40
  333.5 16.1 %shard_map.202 = (bf16[384,3000]{1,0:T(8,128)(2,1)}, bf16[256,2048]{1,0:T(8,128)(2,1)S(1)}, bf16[272,750]{1,0:T(8,128)(2,1)S(1)}, bf16[272,750]{1,0:T(8,128)(2,1...) custom-call(s32[1]{0:T(128)} %bitcast.4.l_ref, f32[256,1]{1,0:T(8,128)S(1)} %reshape.337.keep_ref, ...), custom_call_target="tpu_custom_call" | custom-call | flops 1572864000 | bytes 17685252 | tf_op jit(solution)/shard_map/pallas_call | solution.py:40
  351.5 10.9 %collective-permute-done.26.refs_6_ = bf16[272,750]{1,0:T(8,128)(2,1)S(1)} collective-permute-done((bf16[272,750]{1,0:T(8,128)(2,1)S(1)}, bf16[272,750]{1,0:T(8,128)(2,1)S(1)}, u32[]{:S(2)}, u32[]{:S(2)}) %collective-permute-start.26) | collective-permute-done | bytes 408032 | tf_op jit(solution)/shard_map/ppermute | solution.py:20
  362.4 7.5 %collective-permute-done.27.refs_7_ = bf16[272,750]{1,0:T(8,128)(2,1)S(1)} collective-permute-done((bf16[272,750]{1,0:T(8,128)(2,1)S(1)}, bf16[272,750]{1,0:T(8,128)(2,1)S(1)}, u32[]{:S(2)}, u32[]{:S(2)}) %collective-permute-start.27) | collective-permute-done | bytes 408032 | tf_op jit(solution)/shard_map/ppermute | solution.py:20
  369.9 4.4 shard_map.204
  384.8 9.0 %collective-permute-done.18.refs_6_ = bf16[320,1024]{1,0:T(8,128)(2,1)} collective-permute-done((bf16[320,1024]{1,0:T(8,128)(2,1)S(1)}, bf16[320,1024]{1,0:T(8,128)(2,1)}, u32[]{:S(2)}, u32[]{:S(2)}) %collective-permute-start.18) | collective-permute-done | bytes 655392 | tf_op jit(solution)/shard_map/ppermute | solution.py:20
  396.1 14.2 %collective-permute-done.29 = bf16[512,750]{0,1:T(8,128)(2,1)} collective-permute-done((bf16[512,750]{0,1:T(8,128)(2,1)}, bf16[512,750]{0,1:T(8,128)(2,1)}, u32[]{:S(2)}, u32[]{:S(2)}) %collective-permute-start.29) | collective-permute-done | bytes 768032 | tf_op jit(solution)/shard_map/ppermute | solution.py:20
  412.6 13.5 %collective-permute-done.30 = bf16[512,750]{0,1:T(8,128)(2,1)} collective-permute-done((bf16[512,750]{0,1:T(8,128)(2,1)}, bf16[512,750]{0,1:T(8,128)(2,1)}, u32[]{:S(2)}, u32[]{:S(2)}) %collective-permute-start.30) | collective-permute-done | bytes 768032 | tf_op jit(solution)/shard_map/ppermute | solution.py:20
  431.7 7.6 %shard_map.205 = bf16[2048,750]{1,0:T(8,128)(2,1)} custom-call(bf16[320,1024]{1,0:T(8,128)(2,1)S(1)} %get-tuple-element.108.below_ref.refs_0_, bf16[320,1024]{1,0:T(8,128)(2,1)S(1)} %copy-done.14, bf16[320,1024]{1,0:T(8,128)(2,1)} %collective-permute-done.23.refs_2_, bf16[320,1024]{1,0:T(8,128)(2,1)S(1)} %copy-done.16, ...), custom_call_target="tpu_custom_call" | custom-call | flops 3145728000 | bytes 11386880 | tf_op jit(solution)/shard_map/pallas_call | solution.py:40
  439.4 51.8 %all_to_all.42 = bf16[8,32,2048]{2,1,0:T(8,128)(2,1)} all-to-all(bf16[8,32,2048]{2,1,0:T(8,128)(2,1)S(1)} %bitcast.69), channel_id=1, replica_groups=mesh['grp'=8,'loc'=4] {'grp'}, dimensions={0} | all-to-all | bytes 2097152 | tf_op jit(solution)/shard_map/all_to_all | solution.py:544
  491.1 4.5 all-to-all-start.4
  498.4 7.3 %collective-permute-done.15.refs_2_ = bf16[256,512]{1,0:T(8,128)(2,1)S(1)} collective-permute-done((bf16[256,512]{1,0:T(8,128)(2,1)S(1)}, bf16[256,512]{1,0:T(8,128)(2,1)S(1)}, u32[]{:S(2)}, u32[]{:S(2)}) %collective-permute-start.15) | collective-permute-done | bytes 262176 | tf_op jit(solution)/shard_map/ppermute | solution.py:20
  505.7 4.7 collective-permute-done.16.refs_3_
  514.5 44.3 %all-to-all-done.4 = bf16[8,48,3000]{2,1,0:T(8,128)(2,1)} async-done(((bf16[8,48,3000]{2,1,0:T(8,128)(2,1)}), bf16[8,48,3000]{2,1,0:T(8,128)(2,1)}, u32[]{:S(2)}, u32[]{:S(2)}) %all-to-all-start.4) | async-done | bytes 2304032 | tf_op jit(solution)/shard_map/all_to_all | solution.py:541
  558.8 5.0 all-to-all-start.5
  564.2 4.3 convolution_convert_fusion
  582.2 39.7 %all-to-all-done.5 = bf16[8,112,1024]{2,1,0:T(8,128)(2,1)} async-done(((bf16[8,112,1024]{2,1,0:T(8,128)(2,1)}), bf16[8,112,1024]{2,1,0:T(8,128)(2,1)}, u32[]{:S(2)}, u32[]{:S(2)}) %all-to-all-start.5) | async-done | bytes 1835040 | tf_op jit(solution)/shard_map/all_to_all | solution.py:496
  638.4 27.1 %collective-permute-done.21 = bf16[1,160,1024]{2,1,0:T(8,128)(2,1)S(1)} collective-permute-done((bf16[1,160,1024]{2,1,0:T(8,128)(2,1)S(1)}, bf16[1,160,1024]{2,1,0:T(8,128)(2,1)S(1)}, u32[]{:S(2)}, u32[]{:S(2)}) %collective-permute-start.21) | collective-permute-done | bytes 327712 | tf_op jit(solution)/shard_map/ppermute | solution.py:20
  684.3 5.0 fusion.35
  (251 shorter events, 161.2 us)
Async XLA Ops:
  25.4 28.3 %all-to-all-start.1 = ((bf16[8,32,2048]{2,1,0:T(8,128)(2,1)}), bf16[8,32,2048]{2,1,0:T(8,128)(2,1)S(1)}, u32[]{:S(2)}, u32[]{:S(2)}) async-start(bf16[8,32,2048]{2,1,0:T(8,128)(2,1)} %bitcast.7), calls=%async_computation.1 | async-start | bytes 2097152 | tf_op jit(solution)/shard_map/all_to_all | solution.py:433
  54.7 46.2 %all-to-all-start.3 = ((bf16[8,112,1024]{2,1,0:T(8,128)(2,1)}), bf16[8,112,1024]{2,1,0:T(8,128)(2,1)S(1)}, u32[]{:S(2)}, u32[]{:S(2)}) async-start(bf16[8,112,1024]{2,1,0:T(8,128)(2,1)} %bitcast.76), calls=%async_computation.3 | async-start | bytes 3670016 | tf_op jit(solution)/shard_map/all_to_all | solution.py:447
  102.2 138.4 %all-to-all-start.2 = ((bf16[8,48,3000]{2,1,0:T(8,128)(2,1)}), bf16[8,48,3000]{2,1,0:T(8,128)(2,1)}, u32[]{:S(2)}, u32[]{:S(2)}) async-start(bf16[8,48,3000]{2,1,0:T(8,128)(2,1)} %bitcast.9), calls=%async_computation.2 | async-start | bytes 4718592 | tf_op jit(solution)/shard_map/all_to_all | solution.py:439
  106.6 389.2 %reduce-scatter.3.cloned.1.call-start = ((), (), s32[]{:S(2)}) async-start(), calls=%async_computation.9 | async-start | bytes 1769472 | tf_op jit(solution)/shard_map/reduce_scatter | solution.py:538
  109.0 36.9 %collective-permute-start.1 = (bf16[1024,750]{0,1:T(8,128)(2,1)}, bf16[1024,750]{0,1:T(8,128)(2,1)}, u32[]{:S(2)}, u32[]{:S(2)}) collective-permute-start(bf16[1024,750]{0,1:T(8,128)(2,1)} %copy.41), channel_id=1, source_target_pairs={{0,2},{1,3},{2,0},{3,1},{4,6},{5,7},{6,4},{7,5},{8,10},{9,11},{10,... | collective-permute-start | bytes 4608008 | tf_op jit(solution)/shard_map/ppermute | solution.py:20
  110.5 36.8 %collective-permute-start = (bf16[1024,750]{0,1:T(8,128)(2,1)}, bf16[1024,750]{0,1:T(8,128)(2,1)}, u32[]{:S(2)}, u32[]{:S(2)}) collective-permute-start(bf16[1024,750]{0,1:T(8,128)(2,1)} %copy.41), channel_id=1, source_target_pairs={{0,1},{1,0},{2,3},{3,2},{4,5},{5,4},{6,7},{7,6},{8,9},{9,8},{10,11... | collective-permute-start | bytes 4608008 | tf_op jit(solution)/shard_map/ppermute | solution.py:20
  114.0 65.0 %collective-permute-start.4 = (bf16[1024,750]{0,1:T(8,128)(2,1)}, bf16[1024,750]{0,1:T(8,128)(2,1)}, u32[]{:S(2)}, u32[]{:S(2)}) collective-permute-start(bf16[1024,750]{0,1:T(8,128)(2,1)} %copy.47), channel_id=1, source_target_pairs={{0,2},{1,3},{2,0},{3,1},{4,6},{5,7},{6,4},{7,5},{8,10},{9,11},{10,... | collective-permute-start | bytes 4608008 | tf_op jit(solution)/shard_map/ppermute | solution.py:20
  114.5 64.5 %collective-permute-start.3 = (bf16[1024,750]{0,1:T(8,128)(2,1)}, bf16[1024,750]{0,1:T(8,128)(2,1)}, u32[]{:S(2)}, u32[]{:S(2)}) collective-permute-start(bf16[1024,750]{0,1:T(8,128)(2,1)} %copy.47), channel_id=1, source_target_pairs={{0,1},{1,0},{2,3},{3,2},{4,5},{5,4},{6,7},{7,6},{8,9},{9,8},{10,11... | collective-permute-start | bytes 4608008 | tf_op jit(solution)/shard_map/ppermute | solution.py:20
  118.0 94.0 %collective-permute-start.7 = (bf16[1024,750]{0,1:T(8,128)(2,1)}, bf16[1024,750]{0,1:T(8,128)(2,1)}, u32[]{:S(2)}, u32[]{:S(2)}) collective-permute-start(bf16[1024,750]{0,1:T(8,128)(2,1)} %copy.49), channel_id=1, source_target_pairs={{0,2},{1,3},{2,0},{3,1},{4,6},{5,7},{6,4},{7,5},{8,10},{9,11},{10,... | collective-permute-start | bytes 4608008 | tf_op jit(solution)/shard_map/ppermute | solution.py:20
  146.0 66.0 %collective-permute-start.2 = (bf16[1024,750]{0,1:T(8,128)(2,1)}, bf16[1024,750]{0,1:T(8,128)(2,1)S(1)}, u32[]{:S(2)}, u32[]{:S(2)}) collective-permute-start(bf16[1024,750]{0,1:T(8,128)(2,1)} %collective-permute-done.1), channel_id=1, source_target_pairs={{0,1},{1,0},{2,3},{3,2},{4,5},{5,4},{6,7},{7,6},{8,9},{9,8},{10,11... | collective-permute-start | bytes 4608008 | tf_op jit(solution)/shard_map/ppermute | solution.py:20
  147.3 85.1 %collective-permute-start.10 = (bf16[512,1024]{1,0:T(8,128)(2,1)S(1)}, bf16[512,1024]{1,0:T(8,128)(2,1)}, u32[]{:S(2)}, u32[]{:S(2)}) collective-permute-start(bf16[512,1024]{1,0:T(8,128)(2,1)S(1)} %bitcast.65), channel_id=1, source_target_pairs={{0,2},{1,3},{2,0},{3,1},{4,6},{5,7},{6,4},{7,5},{8,10},{9,11},{10,... | collective-permute-start | bytes 3145736 | tf_op jit(solution)/shard_map/ppermute | solution.py:20
  179.0 78.2 %collective-permute-start.6 = (bf16[1024,750]{0,1:T(8,128)(2,1)}, bf16[1024,750]{0,1:T(8,128)(2,1)}, u32[]{:S(2)}, u32[]{:S(2)}) collective-permute-start(bf16[1024,750]{0,1:T(8,128)(2,1)} %copy.49), channel_id=1, source_target_pairs={{0,1},{1,0},{2,3},{3,2},{4,5},{5,4},{6,7},{7,6},{8,9},{9,8},{10,11... | collective-permute-start | bytes 4608008 | tf_op jit(solution)/shard_map/ppermute | solution.py:20
  179.0 90.8 %collective-permute-start.5 = (bf16[1024,750]{0,1:T(8,128)(2,1)}, bf16[1024,750]{0,1:T(8,128)(2,1)}, u32[]{:S(2)}, u32[]{:S(2)}) collective-permute-start(bf16[1024,750]{0,1:T(8,128)(2,1)} %collective-permute-done.4), channel_id=1, source_target_pairs={{0,1},{1,0},{2,3},{3,2},{4,5},{5,4},{6,7},{7,6},{8,9},{9,8},{10,11... | collective-permute-start | bytes 4608008 | tf_op jit(solution)/shard_map/ppermute | solution.py:20
  212.0 60.4 %collective-permute-start.8 = (bf16[1024,750]{0,1:T(8,128)(2,1)}, bf16[1024,750]{0,1:T(8,128)(2,1)}, u32[]{:S(2)}, u32[]{:S(2)}) collective-permute-start(bf16[1024,750]{0,1:T(8,128)(2,1)} %collective-permute-done.7), channel_id=1, source_target_pairs={{0,1},{1,0},{2,3},{3,2},{4,5},{5,4},{6,7},{7,6},{8,9},{9,8},{10,11... | collective-permute-start | bytes 4608008 | tf_op jit(solution)/shard_map/ppermute | solution.py:20
  212.0 83.6 %collective-permute-start.9 = (bf16[512,1024]{1,0:T(8,128)(2,1)S(1)}, bf16[512,1024]{1,0:T(8,128)(2,1)}, u32[]{:S(2)}, u32[]{:S(2)}) collective-permute-start(bf16[512,1024]{1,0:T(8,128)(2,1)S(1)} %bitcast.66), channel_id=1, source_target_pairs={{0,1},{1,0},{2,3},{3,2},{4,5},{5,4},{6,7},{7,6},{8,9},{9,8},{10,11... | collective-permute-start | bytes 3145736 | tf_op jit(solution)/shard_map/ppermute | solution.py:20
  232.4 63.2 %collective-permute-start.11 = (bf16[512,1024]{1,0:T(8,128)(2,1)}, bf16[512,1024]{1,0:T(8,128)(2,1)}, u32[]{:S(2)}, u32[]{:S(2)}) collective-permute-start(bf16[512,1024]{1,0:T(8,128)(2,1)} %collective-permute-done.10.refs_2_), channel_id=1, source_target_pairs={{0,1},{1,0},{2,3},{3,2},{4,5},{5,4},{6,7},{7,6},{8,9},{9,8},{10,11... | collective-permute-start | bytes 3145736 | tf_op jit(solution)/shard_map/ppermute | solution.py:20
  257.1 38.1 %collective-permute-start.23 = (bf16[320,1024]{1,0:T(8,128)(2,1)S(1)}, bf16[320,1024]{1,0:T(8,128)(2,1)}, u32[]{:S(2)}, u32[]{:S(2)}) collective-permute-start(bf16[320,1024]{1,0:T(8,128)(2,1)S(1)} %get-tuple-element.108.below_ref.refs_0_), channel_id=1, source_target_pairs={{0,2},{1,3},{2,0},{3,1},{4,6},{5,7},{6,4},{7,5},{8,10},{9,11},{10,... | collective-permute-start | bytes 1966088 | tf_op jit(solution)/shard_map/ppermute | solution.py:20
  276.4 75.1 %collective-permute-start.22 = (bf16[320,1024]{1,0:T(8,128)(2,1)S(1)}, bf16[320,1024]{1,0:T(8,128)(2,1)S(1)}, u32[]{:S(2)}, u32[]{:S(2)}) collective-permute-start(bf16[320,1024]{1,0:T(8,128)(2,1)S(1)} %get-tuple-element.108.below_ref.refs_0_), channel_id=1, source_target_pairs={{0,1},{1,0},{2,3},{3,2},{4,5},{5,4},{6,7},{7,6},{8,9},{9,8},{10,11... | collective-permute-start | bytes 1966088 | tf_op jit(solution)/shard_map/ppermute | solution.py:20
  295.3 56.2 %collective-permute-start.24 = (bf16[320,1024]{1,0:T(8,128)(2,1)}, bf16[320,1024]{1,0:T(8,128)(2,1)S(1)}, u32[]{:S(2)}, u32[]{:S(2)}) collective-permute-start(bf16[320,1024]{1,0:T(8,128)(2,1)} %collective-permute-done.23.refs_2_), channel_id=1, source_target_pairs={{0,1},{1,0},{2,3},{3,2},{4,5},{5,4},{6,7},{7,6},{8,9},{9,8},{10,11... | collective-permute-start | bytes 1966088 | tf_op jit(solution)/shard_map/ppermute | solution.py:20
  350.4 19.5 %collective-permute-start.27 = (bf16[272,750]{1,0:T(8,128)(2,1)S(1)}, bf16[272,750]{1,0:T(8,128)(2,1)S(1)}, u32[]{:S(2)}, u32[]{:S(2)}) collective-permute-start(bf16[272,750]{1,0:T(8,128)(2,1)S(1)} %get-tuple-element.132), channel_id=1, source_target_pairs={{0,3},{1,2},{2,1},{3,0},{4,7},{5,6},{6,5},{7,4},{8,11},{9,10},{10,... | collective-permute-start | bytes 1224008 | tf_op jit(solution)/shard_map/ppermute | solution.py:20
  376.0 198.2 %reduce-scatter.5.cloned.1.call-start = ((), (), s32[]{:S(2)}) async-start(), calls=%async_computation.11 | async-start | bytes 3538944 | tf_op jit(solution)/shard_map/reduce_scatter | solution.py:538
  381.5 28.8 %collective-permute-start.29 = (bf16[512,750]{0,1:T(8,128)(2,1)}, bf16[512,750]{0,1:T(8,128)(2,1)}, u32[]{:S(2)}, u32[]{:S(2)}) collective-permute-start(bf16[512,750]{0,1:T(8,128)(2,1)} %copy.77), channel_id=1, source_target_pairs={{0,2},{1,3},{2,0},{3,1},{4,6},{5,7},{6,4},{7,5},{8,10},{9,11},{10,... | collective-permute-start | bytes 2304008 | tf_op jit(solution)/shard_map/ppermute | solution.py:20
  384.2 41.9 %collective-permute-start.30 = (bf16[512,750]{0,1:T(8,128)(2,1)}, bf16[512,750]{0,1:T(8,128)(2,1)}, u32[]{:S(2)}, u32[]{:S(2)}) collective-permute-start(bf16[512,750]{0,1:T(8,128)(2,1)} %copy.78), channel_id=1, source_target_pairs={{0,3},{1,2},{2,1},{3,0},{4,7},{5,6},{6,5},{7,4},{8,11},{9,10},{10,... | collective-permute-start | bytes 2304008 | tf_op jit(solution)/shard_map/ppermute | solution.py:20
  384.3 44.1 %collective-permute-start.17 = (bf16[320,1024]{1,0:T(8,128)(2,1)S(1)}, bf16[320,1024]{1,0:T(8,128)(2,1)S(1)}, u32[]{:S(2)}, u32[]{:S(2)}) collective-permute-start(bf16[320,1024]{1,0:T(8,128)(2,1)S(1)} %get-tuple-element.109.state_ref.refs_4_), channel_id=1, source_target_pairs={{0,1},{1,0},{2,3},{3,2},{4,5},{5,4},{6,7},{7,6},{8,9},{9,8},{10,11... | collective-permute-start | bytes 1966088 | tf_op jit(solution)/shard_map/ppermute | solution.py:20
  393.8 34.6 %collective-permute-start.19 = (bf16[320,1024]{1,0:T(8,128)(2,1)}, bf16[320,1024]{1,0:T(8,128)(2,1)}, u32[]{:S(2)}, u32[]{:S(2)}) collective-permute-start(bf16[320,1024]{1,0:T(8,128)(2,1)} %collective-permute-done.18.refs_6_), channel_id=1, source_target_pairs={{0,1},{1,0},{2,3},{3,2},{4,5},{5,4},{6,7},{7,6},{8,9},{9,8},{10,11... | collective-permute-start | bytes 1966088 | tf_op jit(solution)/shard_map/ppermute | solution.py:20
  491.1 67.7 %all-to-all-start.4 = ((bf16[8,48,3000]{2,1,0:T(8,128)(2,1)}), bf16[8,48,3000]{2,1,0:T(8,128)(2,1)}, u32[]{:S(2)}, u32[]{:S(2)}) async-start(bf16[8,48,3000]{2,1,0:T(8,128)(2,1)} %bitcast.75), calls=%async_computation.4 | async-start | bytes 4718592 | tf_op jit(solution)/shard_map/all_to_all | solution.py:541
  495.7 174.3 %all-gather.3.cloned.1.call-start = ((), (), s32[]{:S(2)}) async-start(), calls=%async_computation.10 | async-start | bytes 1769472 | tf_op jit(solution)/shard_map/all_gather | solution.py:539
  558.8 63.0 %all-to-all-start.5 = ((bf16[8,112,1024]{2,1,0:T(8,128)(2,1)}), bf16[8,112,1024]{2,1,0:T(8,128)(2,1)}, u32[]{:S(2)}, u32[]{:S(2)}) async-start(bf16[8,112,1024]{2,1,0:T(8,128)(2,1)} %pad_maximum_fusion.1), calls=%async_computation.5 | async-start | bytes 3670016 | tf_op jit(solution)/shard_map/all_to_all | solution.py:496
  563.8 119.2 %all-gather.5.cloned.1.call-start = ((), (), s32[]{:S(2)}) async-start(), calls=%async_computation.12 | async-start | bytes 3538944 | tf_op jit(solution)/shard_map/all_gather | solution.py:539
  579.8 46.4 %collective-permute-start.12 = (bf16[2,160,3000]{2,1,0:T(8,128)(2,1)}, bf16[2,160,3000]{2,1,0:T(8,128)(2,1)}, u32[]{:S(2)}, u32[]{:S(2)}) collective-permute-start(bf16[2,160,3000]{2,1,0:T(8,128)(2,1)} %copy.71), channel_id=1, source_target_pairs={{0,1},{1,0},{2,3},{3,2},{4,5},{5,4},{6,7},{7,6},{8,9},{9,8},{10,11... | collective-permute-start | bytes 5760008 | tf_op jit(solution)/shard_map/ppermute | solution.py:20
  634.3 39.7 %collective-permute-start.13 = (bf16[1,160,3000]{2,1,0:T(8,128)(2,1)}, bf16[1,160,3000]{2,1,0:T(8,128)(2,1)S(1)}, u32[]{:S(2)}, u32[]{:S(2)}) collective-permute-start(bf16[1,160,3000]{2,1,0:T(8,128)(2,1)} %copy.74), channel_id=1, source_target_pairs={{0,2},{1,3},{2,0},{3,1},{4,6},{5,7},{6,4},{7,5},{8,10},{9,11},{10,... | collective-permute-start | bytes 2880008 | tf_op jit(solution)/shard_map/ppermute | solution.py:20
  635.4 30.1 %collective-permute-start.21 = (bf16[1,160,1024]{2,1,0:T(8,128)(2,1)S(1)}, bf16[1,160,1024]{2,1,0:T(8,128)(2,1)S(1)}, u32[]{:S(2)}, u32[]{:S(2)}) collective-permute-start(bf16[1,160,1024]{2,1,0:T(8,128)(2,1)S(1)} %fusion.17), channel_id=1, source_target_pairs={{0,2},{1,3},{2,0},{3,1},{4,6},{5,7},{6,4},{7,5},{8,10},{9,11},{10,... | collective-permute-start | bytes 983048 | tf_op jit(solution)/shard_map/ppermute | solution.py:20
  (60 other events, 741.5 us)
Sparse Core Ops, SparseCore 0:
  376.1 65.2 reduce-scatter.2
  445.4 115.0 reduce-scatter.4
  562.9 59.3 all-gather.2
  624.6 58.3 all-gather.4

commit v2 on v1

v2 whole, which is shorter than its diff:
```python
import functools

import jax
import jax.numpy as jnp
from jax import lax
from jax.experimental import pallas as pl
from jax.experimental.pallas import tpu as pltpu
from jax.sharding import PartitionSpec as P

BPREG = 1.0
BF16 = jnp.bfloat16
F32 = jnp.float32
I32 = jnp.int32
LANES = 128
VMEM_LIMIT = 48 << 20


def swap(x, axis, bit):
    n = lax.axis_size(axis)
    return lax.ppermute(x, axis, [(i, i ^ bit) for i in range(n)])


def gather_xor(x, axis):
    blocks = {0: x}
    bit = lax.axis_size(axis) // 2
    while bit:
        for k in list(blocks):
            blocks[k | bit] = swap(blocks[k], axis, bit)
        bit //= 2
    return [blocks[k] for k in range(len(blocks))]


def send_xor(chunks, axis):
    return [chunks[0]] + [swap(chunks[j], axis, j) for j in range(1, len(chunks))]


def kernel_call(body, outs, ins, smem=0, scratch=(), us=1):
    nbytes = sum(a.size * a.dtype.itemsize for a in ins)
    nbytes += sum(int(functools.reduce(lambda a, b: a * b, o.shape)) * o.dtype.itemsize for o in outs)
    return pl.pallas_call(
        body,
        out_shape=outs,
        in_specs=[pl.BlockSpec(memory_space=pltpu.SMEM)] * smem
        + [pl.BlockSpec(memory_space=pltpu.VMEM)] * (len(ins) - smem),
        scratch_shapes=list(scratch),
        compiler_params=pltpu.CompilerParams(vmem_limit_bytes=VMEM_LIMIT),
        cost_estimate=pl.CostEstimate(flops=us * 10**9, bytes_accessed=nbytes, transcendentals=0),
    )(*ins)


def after(x, *deps):
    return lax.optimization_barrier((x,) + deps)[0]


def shape(dims, dtype):
    return jax.ShapeDtypeStruct(dims, dtype)


def iota(dims, dim):
    return lax.broadcasted_iota(I32, dims, dim)


def dot(a, b, ca=1, cb=0):
    return lax.dot_general(a, b, (((ca,), (cb,)), ((), ())), preferred_element_type=F32)


def low(cond):
    return jnp.where(cond, 1.0, 0.0).astype(BF16)


def route_kernel(owners, rows, cap, batch, ccap, in_ref, tg_ref, plan_ref, s_in, s_tg, s_pl, req):
    width = 2 * cap + ccap

    def place(ids, span):
        n = ids.shape[0]
        owner_i = iota((n, owners), 1)
        member = (ids >= owner_i * span) & (ids < (owner_i + 1) * span)
        earlier = low(iota((n, n), 1) < iota((n, n), 0))
        before = dot(earlier, low(member))
        rank = jnp.sum(jnp.where(member, before, 0.0), axis=1, keepdims=True).astype(I32)
        owner = jnp.sum(jnp.where(member, owner_i, 0).astype(F32), axis=1, keepdims=True).astype(I32)
        return owner, rank

    def wanted(owner, rank, offset, value):
        n = owner.shape[0]
        hit = iota((n, owners * width), 1) == owner * width + offset + rank
        return jnp.sum(jnp.where(hit, value.astype(F32), 0.0), axis=0, keepdims=True)

    o_in, r_in = place(in_ref[...], rows)
    o_tg, r_tg = place(tg_ref[...], rows)
    o_pl, r_pl = place(plan_ref[...], batch)
    s_in[...] = o_in * cap + r_in
    s_tg[...] = o_tg * cap + r_tg
    s_pl[...] = o_pl * ccap + r_pl
    total = wanted(o_in, r_in, 0, in_ref[...] + 1)
    total += wanted(o_tg, r_tg, cap, tg_ref[...] + 1)
    total += wanted(o_pl, r_pl, 2 * cap, plan_ref[...] - o_pl * batch + 1)
    req[...] = total.astype(I32)


def extend(value, keep, hidden):
    lane = iota(value.shape, 1)
    return jnp.where(lane == hidden, 1.0, jnp.where(lane == hidden + 1, keep, value)).astype(BF16)


def run_steps(steps, batch, hidden, l, keep_ref, w_refs, x_of, start, state_ref, res, q_s):
    n_loc = len(w_refs)
    wide = start.shape[1]
    tail = jnp.zeros((batch, wide), F32)
    lane = iota((batch, wide), 1)
    prev = start
    for t in range(steps):
        at = pl.ds(t * batch, batch)
        keep = keep_ref[at, :]
        state_ref[at, :] = extend(prev, keep, hidden)
        p = prev * keep
        p_low = p.astype(BF16)
        for j in range(n_loc):
            q_s[l ^ j] = dot(p_low, w_refs[j][...])[:, : q_s.shape[2]]
        q = jnp.concatenate([q_s[i] for i in range(n_loc)] + [tail], axis=1)
        x = x_of(t)
        h2 = 2 * hidden
        z = jax.nn.sigmoid(x[:, :wide] + q[:, :wide])
        r = jax.nn.sigmoid(x[:, hidden : hidden + wide] + q[:, hidden : hidden + wide])
        qn = q[:, h2 : h2 + wide]
        n = jnp.tanh(x[:, h2 : h2 + wide] + r * qn)
        prev = jnp.where(lane < hidden, n + z * (p - n), 0.0)
        for ref, val in zip(res, (z, r, n, qn, p)):
            ref[at, :] = val
    state_ref[pl.ds(steps * batch, batch), :] = extend(prev, 0.0, hidden)


def pad_kernel(at, n_in, l_ref, w_ref, *refs):
    refs, outs = refs[: n_in - 2], refs[n_in - 2 :]
    out_ref = outs[0]
    rows, cols = w_ref.shape
    out_ref[...] = jnp.zeros(out_ref.shape, BF16)
    out_ref[:rows, :cols] = w_ref[...]
    if at is not None:
        which, row = at
        tile = row // 16 * 16
        here = (iota((16, cols), 0) == row - tile).astype(F32)
        old = out_ref[tile : tile + 16, :cols].astype(F32)
        extra = refs[0][which : which + 1, :].astype(F32)
        out_ref[tile : tile + 16, :cols] = (old + here * extra).astype(BF16)
    if len(outs) == 2:
        half = outs[1].shape[0]
        side = l_ref[0] & 1
        outs[1][...] = out_ref[pl.ds(pl.multiple_of(side * half, half), half), :]


def gather_kernel(ids_ref, table_ref, out_ref):
    rows, cols = table_ref.shape
    pick = low(iota((ids_ref.shape[0], rows), 1) == ids_ref[...])
    if out_ref.shape[1] > cols:
        out_ref[...] = jnp.zeros(out_ref.shape, BF16)
    out_ref[:, :cols] = dot(pick, table_ref[...]).astype(BF16)


def gather_biased_kernel(ids_ref, table_ref, bias_ref, out_ref):
    n, wide = out_ref.shape
    rows, cols = table_ref.shape
    pick = low(iota((n, rows), 1) == ids_ref[...])
    parts = [dot(pick, table_ref[...]), dot(pick, bias_ref[...])[:, :1]]
    parts.append(jnp.zeros((n, wide - cols - 1), F32))
    out_ref[...] = jnp.concatenate(parts, axis=1).astype(BF16)


def pack_kernel(slot_ref, carried_ref, one_ref, two_ref):
    pick = low(iota((slot_ref.shape[0], one_ref.shape[0]), 1) == slot_ref[...])
    hidden = carried_ref.shape[2]
    for layer, ref in enumerate((one_ref, two_ref)):
        ref[...] = jnp.zeros(ref.shape, BF16)
        ref[:, :hidden] = dot(pick, carried_ref[layer].astype(BF16), 0, 0).astype(BF16)


def table_kernel(own, pairs, l_ref, *refs):
    mine_ref, far_ref, near_ref = refs[2 * pairs :]
    pad = mine_ref.shape[0]
    l = l_ref[0]
    for j, (ref, at) in enumerate(((mine_ref, None), (near_ref, 0), (far_ref, None), (near_ref, 1))):
        part = None
        for ids_ref, got_ref in zip(refs[:pairs], refs[pairs : 2 * pairs]):
            row = iota((pad, ids_ref.shape[1]), 0)
            hit = (row < own) & (row + (l ^ j) * own == ids_ref[...])
            term = dot(low(hit), got_ref[...])
            part = term if part is None else part + term
        if at is None:
            ref[...] = part
        else:
            ref[at, :, :] = part.astype(BF16)


def table_add_kernel(mine_ref, far_ref, got_ref, sum_ref, send_ref):
    sum_ref[...] = mine_ref[...] + got_ref[0].astype(F32)
    send_ref[...] = (far_ref[...] + got_ref[1].astype(F32)).astype(BF16)


def table_out_kernel(sum_ref, got_ref, out_ref):
    rows, cols = out_ref.shape
    out_ref[...] = (sum_ref[...] + got_ref[...].astype(F32))[:rows, :cols]


def carry_kernel(slot_ref, got_ref, out_ref):
    hidden = out_ref.shape[2]
    wide = got_ref.shape[1] // 2
    pick = low(iota((slot_ref.shape[0], got_ref.shape[0]), 1) == slot_ref[...])
    back = dot(pick, got_ref[...])
    out_ref[0] = back[:, :hidden]
    out_ref[1] = back[:, wide : wide + hidden]


def split_kernel(bit, l_ref, a_ref, b_ref, keep_ref, send_ref):
    half = keep_ref.shape[0]
    side = (l_ref[0] >> bit) & 1
    for ref, at in ((keep_ref, side), (send_ref, 1 - side)):
        rows = pl.ds(pl.multiple_of(at * half, half), half)
        ref[...] = (a_ref[rows, :].astype(F32) + b_ref[rows, :].astype(F32)).astype(BF16)


def add_kernel(a_ref, b_ref, out_ref):
    out_ref[...] = (a_ref[...].astype(F32) + b_ref[...].astype(F32)).astype(BF16)


def join_kernel(bit, l_ref, a_ref, b_ref, out_ref):
    half = a_ref.shape[0]
    side = (l_ref[0] >> bit) & 1
    for ref, at in ((a_ref, side), (b_ref, 1 - side)):
        out_ref[pl.ds(pl.multiple_of(at * half, half), half), :] = ref[...]


def final_kernel(hidden, bias_row, l_ref, a_ref, b_ref, out_ref, bias_ref):
    side = l_ref[0] & 1
    cols = out_ref.shape[1]
    half = a_ref.shape[0]
    at = (bias_row - half) // 16 * 16
    for first, second, when in ((a_ref, b_ref, 0), (b_ref, a_ref, 1)):

        @pl.when(side == when)
        def _():
            out_ref[:half, :] = first[...].astype(F32)[:, :cols]
            out_ref[half:, :] = second[...].astype(F32)[: hidden - half, :cols]
            row = bias_row - half - at
            bias_ref[...] = second[at : at + 16, :].astype(F32)[row : row + 1, :cols]


def first_kernel(
    dims, l_ref, keep_ref, slot_ref, land_ref, got_ref, rows_ref, *refs
):
    steps, batch, hidden, bias_row, n_loc = dims
    w_refs, refs = refs[:n_loc], refs[n_loc:]
    state_ref, z_ref, r_ref, n_ref, qn_ref, p_ref, q_s, b_s, x_s = refs
    wide = z_ref.shape[1]
    l = l_ref[0]
    pick = low(iota((steps * batch, rows_ref.shape[0]), 1) == slot_ref[...])
    x_s[...] = dot(pick, rows_ref[...])
    for j in range(n_loc):
        b_s[l ^ j] = w_refs[j][bias_row : bias_row + 16, :].astype(F32)[:, : b_s.shape[2]]
    bias = jnp.concatenate([b_s[i][0:1, :] for i in range(n_loc)], axis=1)
    pad = jnp.zeros((batch, wide), F32)
    land = low(iota((batch, land_ref.shape[1]), 0) == land_ref[...])
    moved = dot(land, got_ref[...])

    def x_of(t):
        gates = bias.shape[1]
        return jnp.concatenate([x_s[pl.ds(t * batch, batch), :][:, :gates] + bias, pad], axis=1)

    run_steps(
        steps, batch, hidden, l, keep_ref, w_refs, x_of, moved, state_ref,
        (z_ref, r_ref, n_ref, qn_ref, p_ref), q_s,
    )


def second_kernel(dims, l_ref, keep_ref, land_ref, got_ref, below_ref, *refs):
    steps, batch, hidden, n_loc = dims
    in_refs, w_refs, refs = refs[:n_loc], refs[n_loc : 2 * n_loc], refs[2 * n_loc :]
    state_ref, z_ref, r_ref, n_ref, qn_ref, p_ref, q_s, x_s = refs
    wide = z_ref.shape[1]
    l = l_ref[0]
    land = low(iota((batch, land_ref.shape[1]), 0) == land_ref[...])
    moved = dot(land, got_ref[...])
    below = below_ref[pl.ds(batch, steps * batch), :]
    for j in range(n_loc):
        x_s[l ^ j] = dot(below, in_refs[j][...])[:, : x_s.shape[2]]
    pad = jnp.zeros((batch, wide), F32)

    def x_of(t):
        return jnp.concatenate(
            [x_s[i][t * batch : (t + 1) * batch, :] for i in range(n_loc)] + [pad], axis=1
        )

    run_steps(
        steps, batch, hidden, l, keep_ref, w_refs, x_of, moved, state_ref,
        (z_ref, r_ref, n_ref, qn_ref, p_ref), q_s,
    )


def score_kernel(dims, valid_ref, slot_ref, state_ref, tg_ref, *refs):
    steps, batch, n_loc = dims
    rows = steps * batch
    neg_refs, refs = refs[:n_loc], refs[n_loc:]
    gn_refs, into_ref, send_ref = refs[:n_loc], refs[n_loc], refs[n_loc + 1]
    sn_s, tgt_s, tgg_s = refs[n_loc + 2 :]
    diag = iota((batch, batch), 0) == iota((batch, batch), 1)
    slots = tg_ref.shape[0]
    pick = low(iota((rows, slots), 1) == slot_ref[...])
    tgt_s[...] = dot(pick, tg_ref[...]).astype(BF16)
    every = state_ref[pl.ds(batch, rows), :]
    for j in range(n_loc):
        sn_s[j] = dot(every, neg_refs[j][...], 1, 1)
    for t in range(steps):
        at = pl.ds(t * batch, batch)
        second = state_ref[pl.ds((t + 1) * batch, batch), :]
        targets = tgt_s[at, :]
        st = dot(second, targets, 1, 1)
        sn = [sn_s[j, at, :] for j in range(n_loc)]
        pos = jnp.sum(jnp.where(diag, st, 0.0), axis=1, keepdims=True)
        top = jnp.max(jnp.where(diag, -jnp.inf, st), axis=1, keepdims=True)
        for s in sn:
            top = jnp.maximum(top, jnp.max(s, axis=1, keepdims=True))
        parts = [(st, jnp.where(diag, 0.0, jnp.exp(st - top)))]
        parts += [(s, jnp.exp(s - top)) for s in sn]
        mass = sum(jnp.sum(e, axis=1, keepdims=True) for _, e in parts)
        scale = 1.0 / mass
        parts = [(s, e * scale, jax.nn.sigmoid(pos - s)) for s, e in parts]
        inside = sum(jnp.sum(w * g, axis=1, keepdims=True) for _, w, g in parts)
        penalty = sum(jnp.sum(w * s * s, axis=1, keepdims=True) for s, w, _ in parts)
        slope = sum(jnp.sum(w * g * (1.0 - g), axis=1, keepdims=True) for _, w, g in parts)
        inv = 1.0 / inside
        weight = valid_ref[at, :]
        grads = [
            weight * w * (1.0 + BPREG * (s * s + 2.0 * s - penalty) - g * g * inv)
            for s, w, g in parts
        ]
        gt = grads[0] - jnp.where(diag, weight * slope * inv, 0.0)
        gt_low = gt.astype(BF16)
        into_ref[at, :] = dot(gt_low, targets)
        for j in range(n_loc):
            gn_refs[j][at, :] = grads[j + 1].astype(BF16)
        tgg_s[at, :] = dot(gt_low, second, 0, 0).astype(BF16)
    total = into_ref[...]
    for j in range(n_loc):
        total += dot(gn_refs[j][...], neg_refs[j][...])
    into_ref[...] = total
    send_ref[...] = dot(pick, tgg_s[...], 0, 0).astype(BF16)


def back_steps(steps, batch, hidden, chunk, l, keep_ref, w_refs, into_ref, res, dq_s, emit):
    n_loc = len(w_refs)
    dq_s[...] = jnp.zeros(dq_s.shape, F32)
    wide = into_ref.shape[1]
    lane = iota((batch, wide), 1)
    z_ref, r_ref, n_ref, qn_ref, p_ref = res
    carry = jnp.zeros((batch, wide), F32)
    for t in reversed(range(steps)):
        at = pl.ds(t * batch, batch)
        g = jnp.where(lane < hidden, into_ref[at, :] + carry, 0.0)
        z, r, n, qn, p = (ref[at, :] for ref in (z_ref, r_ref, n_ref, qn_ref, p_ref))
        dc = g * (1.0 - z) * (1.0 - n * n)
        da_z = (g * (p - n) * z * (1.0 - z))[:, :hidden]
        da_r = (dc * qn * r * (1.0 - r))[:, :hidden]
        da_n = dc[:, :hidden]
        dq_n = (dc * r)[:, :hidden]
        da = jnp.concatenate([da_z, da_r, da_n], axis=1)
        dq = jnp.concatenate([da_z, da_r, dq_n], axis=1)
        emit(t, da, dq)
        for i in range(n_loc):
            dq_s[i, :, :chunk] = dq[:, i * chunk : (i + 1) * chunk]
        dp = g * z
        for j in range(n_loc):
            dp += dot(dq_s[l ^ j].astype(BF16), w_refs[j][...], 1, 1)
        carry = dp * keep_ref[at, :]
    return jnp.where(lane < hidden, carry, 0.0)


def back_second_kernel(dims, l_ref, keep_ref, into_ref, *refs):
    steps, batch, hidden, chunk, n_loc = dims
    res, refs = refs[:5], refs[5:]
    in_refs, w_refs, refs = refs[:n_loc], refs[n_loc : 2 * n_loc], refs[2 * n_loc :]
    init_ref, first_ref, refs = refs[0], refs[1], refs[2:]
    ch_refs, refs = refs[:n_loc], refs[n_loc:]
    dq_s, da_all, dq_all = refs
    l = l_ref[0]
    da_all[...] = jnp.zeros(da_all.shape, F32)
    dq_all[...] = jnp.zeros(dq_all.shape, F32)

    def emit(t, da, dq):
        for i in range(n_loc):
            da_all[i, pl.ds(t * batch, batch), :chunk] = da[:, i * chunk : (i + 1) * chunk]
            dq_all[i, pl.ds(t * batch, batch), :chunk] = dq[:, i * chunk : (i + 1) * chunk]

    init_ref[...] = back_steps(
        steps, batch, hidden, chunk, l, keep_ref, w_refs, into_ref, res, dq_s, emit
    )
    rows = steps * batch
    total = None
    for j in range(n_loc):
        da_low = da_all[l ^ j].astype(BF16)
        ch_refs[j][pl.ds(0, rows), :] = da_low
        ch_refs[j][pl.ds(rows, rows), :] = dq_all[l ^ j].astype(BF16)
        part = dot(da_low, in_refs[j][...], 1, 1)
        total = part if total is None else total + part
    first_ref[...] = total


def back_first_kernel(dims, l_ref, keep_ref, slot_ref, land_ref, init2_ref, into_ref, *refs):
    steps, batch, hidden, chunk, n_loc = dims
    res, refs = refs[:5], refs[5:]
    w_refs, refs = refs[:n_loc], refs[n_loc:]
    send_ref, back_ref, refs = refs[0], refs[1], refs[2:]
    ch_refs, refs = refs[:n_loc], refs[n_loc:]
    dq_s, da_all, dq_all, bias_s = refs
    l = l_ref[0]
    wide = into_ref.shape[1]
    cols = da_all.shape[1]
    dq_all[...] = jnp.zeros(dq_all.shape, F32)
    bias_s[...] = jnp.zeros(bias_s.shape, F32)

    def emit(t, da, dq):
        da_all[pl.ds(t * batch, batch), :] = da.astype(BF16)
        for i in range(n_loc):
            dq_all[i, pl.ds(t * batch, batch), :chunk] = dq[:, i * chunk : (i + 1) * chunk]

    init = back_steps(steps, batch, hidden, chunk, l, keep_ref, w_refs, into_ref, res, dq_s, emit)
    rows = steps * batch
    da = da_all[...]
    bias = jnp.sum(da.astype(F32), axis=0, keepdims=True)
    for i in range(n_loc):
        part = bias[:, i * chunk : (i + 1) * chunk]
        bias_s[i, 0:1, :chunk] = part
    for j in range(n_loc):
        ch_refs[j][pl.ds(0, rows), :] = dq_all[l ^ j].astype(BF16)
        ch_refs[j][pl.ds(rows, 16), :] = bias_s[l ^ j].astype(BF16)
    pick = low(iota((rows, send_ref.shape[0]), 1) == slot_ref[...])
    if send_ref.shape[1] > cols:
        send_ref[...] = jnp.zeros(send_ref.shape, BF16)
    send_ref[:, :cols] = dot(pick, da, 0, 0).astype(BF16)
    land = low(iota((batch, land_ref.shape[1]), 0) == land_ref[...])
    back_ref[:, :wide] = dot(land, init.astype(BF16), 0, 0).astype(BF16)
    back_ref[:, wide:] = dot(land, init2_ref[...].astype(BF16), 0, 0).astype(BF16)


def scaled(ref, rows, hidden):
    left = ref[pl.ds(0, rows), :].astype(F32)
    return (left * left[:, hidden + 1 : hidden + 2]).astype(BF16)


def dense_kernel(dims, l_ref, *refs):
    steps, batch, hidden, skip, at, bias_row, n_loc = dims
    rows = steps * batch
    left_refs, ch_refs = refs[:n_loc], refs[n_loc : 2 * n_loc]
    keep_ref, send_ref, all_s = refs[2 * n_loc :]
    half = keep_ref.shape[0]
    side = l_ref[0] & 1
    total, bias = None, None
    for j in range(n_loc):
        left = left_refs[j][pl.ds(batch, rows), :] if skip else scaled(left_refs[j], rows, hidden)
        part = dot(left, ch_refs[j][pl.ds(at, rows), :], 0, 0)
        total = part if total is None else total + part
        if bias_row is not None:
            extra = ch_refs[j][pl.ds(rows, 16), :].astype(F32)
            bias = extra if bias is None else bias + extra
    all_s[...] = total.astype(BF16)
    if bias_row is not None:
        all_s[pl.ds(bias_row, 16), :] = bias.astype(BF16)
    keep_ref[...] = all_s[pl.ds(pl.multiple_of(side * half, half), half), :]
    send_ref[...] = all_s[pl.ds(pl.multiple_of((1 - side) * half, half), half), :]


def neg_kernel(n_loc, owners, *refs):
    gn_refs, b_refs, out_ref = refs[:n_loc], refs[n_loc : 2 * n_loc], refs[2 * n_loc]
    rows = gn_refs[0].shape[0]
    batch = b_refs[0].shape[0] - rows
    total = None
    for j in range(n_loc):
        part = dot(gn_refs[j][...], b_refs[j][pl.ds(batch, rows), :], 0, 0)
        total = part if total is None else total + part
    own = out_ref.shape[0] // owners
    places = [(g >> 1) + (g & 1) * (owners // 2) for g in range(owners)]
    blocks = [total[p * own : (p + 1) * own, :] for p in places]
    out_ref[...] = jnp.concatenate(blocks, axis=0).astype(BF16)


def on_device(
    carried,
    session_plan,
    item_ids,
    target_ids,
    reset_mask,
    valid_counts,
    negative_ids,
    input_table,
    output_table,
    output_bias,
    hidden_one,
    input_two,
    hidden_two,
    gate_biases,
):
    hidden = carried.shape[2]
    wide = -(-(hidden + 2) // LANES) * LANES
    bias_row = wide - 16
    steps, batch = item_ids.shape
    events = steps * batch
    owners = lax.axis_size("grp")
    n_loc = lax.axis_size("loc")
    grp = lax.axis_index("grp")
    loc = lax.axis_index("loc")
    rows = input_table.shape[0]
    base = grp * rows
    gates = input_table.shape[1]
    chunk = gates // n_loc
    cap = events // owners + events // (2 * owners)
    ccap = 4 * batch // owners
    slots, cslots = owners * cap, owners * ccap
    width = 2 * cap + ccap
    neg_own = negative_ids.shape[0] // owners // n_loc
    neg_part = owners * neg_own
    l_arr = loc.astype(I32).reshape(1)

    cpad = -(-chunk // LANES) * LANES
    gpad = -(-gates // LANES) * LANES
    w_shape = shape((wide, cpad), BF16)

    g_arr = grp.astype(I32).reshape(1)
    bits = owners.bit_length() - 1

    def padded(w, at, halved):
        ins = [g_arr, w] if at is None else [g_arr, w, gate_biases]
        outs = [w_shape, shape((wide // 2, cpad), BF16)] if halved else [w_shape]
        return kernel_call(functools.partial(pad_kernel, at, len(ins)), outs, ins, 1)

    def near(x):
        return swap(x, "loc", 1)

    def across(x):
        return swap(x, "loc", 2)

    def join(bit, kept, got):
        return kernel_call(
            functools.partial(join_kernel, bit),
            [shape((2 * kept.shape[0],) + kept.shape[1:], BF16)],
            [g_arr, kept, got], 1,
        )[0]

    p_one = padded(hidden_one, (0, bias_row), False)[0]
    y_one = across(p_one)

    bias_col = output_bias[:, None]

    def gathered(ids, table, cols, *bias):
        n = ids.shape[0]
        return kernel_call(
            gather_biased_kernel if bias else gather_kernel,
            [shape((n, cols), BF16)], [ids.reshape(n, 1), table, *bias], 0, (), 2,
        )[0]

    mine = lax.dynamic_slice(
        negative_ids.reshape(owners, n_loc, neg_own), (grp, loc, 0), (1, 1, neg_own)
    ).reshape(neg_own) - base
    negs_by = [gathered(after(mine, p_one), output_table, wide, bias_col)]
    for bit in list(range(1, bits)) + [0]:
        got = swap(negs_by[-1], "grp", 1 << bit)
        negs_by.append(join(bit, negs_by[-1], got))
    negs = negs_by[-1]

    slot_in, slot_tg, slot_pl, request = kernel_call(
        functools.partial(route_kernel, owners, rows, cap, batch, ccap),
        [
            shape((events, 1), I32),
            shape((events, 1), I32),
            shape((batch, 1), I32),
            shape((1, owners * width), I32),
        ],
        [
            after(item_ids, p_one).reshape(events, 1),
            target_ids.reshape(events, 1),
            session_plan.reshape(batch, 1),
        ],
    )

    def to_owners(x):
        got = lax.all_to_all(
            x.reshape((owners, x.shape[0] // owners) + x.shape[1:]),
            "grp", split_axis=0, concat_axis=0, tiled=True,
        )
        return got.reshape(x.shape)

    arrived = to_owners(request.reshape(owners, width))
    in_ids = (arrived[:, :cap] - 1 - base).reshape(slots)
    tg_ids = (arrived[:, cap : 2 * cap] - 1 - base).reshape(slots)
    land = (arrived[:, 2 * cap :] - 1).reshape(1, cslots)

    pack_one, pack_two = kernel_call(
        pack_kernel, [shape((cslots, wide), BF16)] * 2, [slot_pl, carried], 0, (), 2
    )
    p_in, h_in = padded(input_two, (1, hidden), True)
    p_two, h_two = padded(hidden_two, None, True)
    got_c = to_owners(after(pack_one, arrived, negs_by[1]))
    reply_in = gathered(in_ids, input_table, gpad)
    y_in = across(after(h_in, y_one))
    got_rows = to_owners(after(reply_in, got_c, negs_by[-2]))
    y_two = across(after(h_two, y_in))
    got_c2 = to_owners(after(pack_two, got_rows))
    reply_tg = gathered(tg_ids, output_table, wide, bias_col)
    tg_rows = to_owners(after(reply_tg, got_c2))
    y_neg = across(after(negs, y_two))
    y_in = join(0, y_in, swap(y_in, "grp", 1))
    y_two = join(0, y_two, swap(y_two, "grp", 1))

    w_one = [p_one, near(p_one), y_one, near(y_one)]
    w_in = [p_in, near(p_in), y_in, near(y_in)]
    w_two = [p_two, near(p_two), y_two, near(y_two)]
    negs = [negs, near(negs), y_neg, near(y_neg)]

    keep = (1 - reset_mask).astype(F32).reshape(events, 1)
    valid = (jnp.arange(steps, dtype=I32)[:, None] < valid_counts[None, :]).astype(F32)
    valid = (valid / steps).reshape(events, 1)

    res_shapes = [shape((events, wide), F32)] * 5
    state_shape = shape(((steps + 1) * batch, wide), BF16)
    q_scratch = pltpu.VMEM((n_loc, batch, chunk), F32)
    dq_scratch = pltpu.VMEM((n_loc, batch, cpad), F32)
    x_scratch = pltpu.VMEM((n_loc, events, chunk), F32)
    all_scratch = pltpu.VMEM((n_loc, events, cpad), F32)

    state_a, *res_one = kernel_call(
        functools.partial(first_kernel, (steps, batch, hidden, bias_row, n_loc)),
        [state_shape] + res_shapes,
        [l_arr, keep, slot_in, land, got_c, got_rows] + w_one,
        1,
        [q_scratch, pltpu.VMEM((n_loc, 16, chunk), F32), pltpu.VMEM((events, gpad), F32)],
        12,
    )
    state_b, *res_two = kernel_call(
        functools.partial(second_kernel, (steps, batch, hidden, n_loc)),
        [state_shape] + res_shapes,
        [l_arr, keep, land, got_c2, state_a] + w_in + w_two,
        1,
        [q_scratch, x_scratch],
        15,
    )
    y_b = across(after(state_b, y_neg))

    *g_neg, into_second, send_tg = kernel_call(
        functools.partial(score_kernel, (steps, batch, n_loc)),
        [shape((events, neg_part), BF16)] * n_loc
        + [shape((events, wide), F32), shape((slots, wide), BF16)],
        [valid, slot_tg, state_b, tg_rows] + negs,
        0,
        [
            pltpu.VMEM((n_loc, events, neg_part), F32),
            pltpu.VMEM((events, wide), BF16),
            pltpu.VMEM((events, wide), BF16),
        ],
        12,
    )
    g_neg = send_xor(g_neg, "loc")
    init_two, into_first, *ch_two = kernel_call(
        functools.partial(back_second_kernel, (steps, batch, hidden, chunk, n_loc)),
        [shape((batch, wide), F32), shape((events, wide), F32)]
        + [shape((2 * events, cpad), BF16)] * n_loc,
        [l_arr, keep, into_second] + res_two + w_in + w_two,
        1,
        [dq_scratch, all_scratch, all_scratch],
        17,
    )
    ch_two = send_xor(ch_two, "loc")
    y_a = across(after(state_a, into_second))
    got_tg_g = to_owners(send_tg)
    y_b = after(y_b, into_first)
    states_b = [state_b, near(state_b), y_b, near(y_b)]
    neg_grad = kernel_call(
        functools.partial(neg_kernel, n_loc, owners),
        [shape((neg_part, wide), BF16)],
        [after(g_neg[0], into_first)] + g_neg[1:] + states_b,
        0, (), 2,
    )[0]
    got_neg_g = to_owners(after(neg_grad, got_tg_g))
    y_a = after(y_a, neg_grad)
    states_a = [state_a, near(state_a), y_a, near(y_a)]

    send_in, back_c, *ch_one = kernel_call(
        functools.partial(back_first_kernel, (steps, batch, hidden, chunk, n_loc)),
        [shape((slots, gpad), BF16), shape((cslots, 2 * wide), BF16)]
        + [shape((events + 16, cpad), BF16)] * n_loc,
        [l_arr, keep, slot_in, land, init_two, after(into_first, neg_grad)] + res_one + w_one,
        1,
        [
            dq_scratch,
            pltpu.VMEM((events, gates), BF16),
            all_scratch,
            pltpu.VMEM((n_loc, 16, cpad), F32),
        ],
        16,
    )
    got_in_g = to_owners(after(send_in, got_neg_g, *ch_two[2:]))
    got_back = to_owners(after(back_c, got_in_g))
    ch_one = send_xor(ch_one, "loc")

    def all_sum(kept, sent):
        rest = kept.shape[0]
        for bit in range(bits):
            got = swap(sent, "grp", 1 << bit)
            if bit < bits - 2:
                rest //= 2
                kept, sent = kernel_call(
                    functools.partial(split_kernel, bit + 1),
                    [shape((rest, cpad), BF16)] * 2,
                    [g_arr, kept, got],
                    1,
                )
            else:
                kept = kernel_call(add_kernel, [shape((rest, cpad), BF16)], [kept, got])[0]
                sent = kept
        for bit in reversed(range(1, bits - 1)):
            kept = join(bit, kept, swap(kept, "grp", 1 << bit))
        return kept, swap(kept, "grp", 1)

    half_shape = shape((wide // 2, cpad), BF16)

    def dense(lefts, chunks, skip, at, bias_at, bias_row):
        parts = kernel_call(
            functools.partial(dense_kernel, (steps, batch, hidden, skip, at, bias_at, n_loc)),
            [half_shape] * 2,
            [g_arr] + lefts + chunks,
            1, [pltpu.VMEM((wide, cpad), BF16)], 6,
        )
        kept, got = all_sum(*parts)
        return kernel_call(
            functools.partial(final_kernel, hidden, bias_row),
            [shape((hidden, chunk), F32), shape((1, chunk), F32)],
            [g_arr, kept, got],
            1, (), 2,
        )

    grad_in, bias_in = dense(states_a, ch_two, True, 0, None, hidden)
    grad_two, _ = dense(states_b, ch_two, False, events, None, hidden)
    grad_one, bias_one = dense(states_a, ch_one, False, 0, bias_row, bias_row)

    own = rows // n_loc
    own_pad = -(-own // 16) * 16

    def table_sum(ids, grads, cols, *wait):
        across_cols = grads[0].shape[1]
        full = shape((own_pad, across_cols), F32)
        sent = shape((own_pad, across_cols), BF16)
        mine_p, far_p, near_p = kernel_call(
            functools.partial(table_kernel, own, len(ids)),
            [full, full, shape((2, own_pad, across_cols), BF16)],
            [l_arr] + [i.reshape(1, i.shape[0]) for i in ids] + grads,
            1, (), 4,
        )
        total, far_s = kernel_call(
            table_add_kernel, [full, sent], [after(mine_p, *wait), far_p, near(near_p)]
        )
        return kernel_call(table_out_kernel, [shape((own, cols), F32)], [total, across(far_s)])[0]

    table_in = table_sum([in_ids], [got_in_g], gates, got_back)
    neg_ids = jnp.broadcast_to(mine[None, :], (owners, neg_own)).reshape(neg_part)
    table_out = table_sum([tg_ids, neg_ids], [got_tg_g, got_neg_g], wide)
    grad_carried = kernel_call(
        carry_kernel, [shape((2, batch, hidden), F32)], [slot_pl, got_back]
    )[0]
    return (
        table_in,
        table_out[:, :hidden],
        table_out[:, hidden],
        grad_one,
        grad_in,
        grad_two,
        jnp.concatenate([bias_one, bias_in], axis=0),
        grad_carried,
    )


def solution(mesh):
    in_specs = (
        P(None, ("grp", "loc"), None),
        P(("grp", "loc")),
        P(None, ("grp", "loc")),
        P(None, ("grp", "loc")),
        P(None, ("grp", "loc")),
        P(("grp", "loc")),
        P(),
        P("grp", None),
        P("grp", None),
        P("grp"),
        P(None, "loc"),
        P(None, "loc"),
        P(None, "loc"),
        P(None, "loc"),
    )
    out_specs = (
        P(("grp", "loc"), None),
        P(("grp", "loc"), None),
        P(("grp", "loc")),
        P(None, "loc"),
        P(None, "loc"),
        P(None, "loc"),
        P(None, "loc"),
        P(None, ("grp", "loc"), None),
    )
    return jax.shard_map(
        on_device, mesh=mesh, in_specs=in_specs, out_specs=out_specs, check_vma=False
    )
```

time: 704 us -> 531 us (0.75)
  waiting for transfers between devices: 347 us -> 223 us
  local copies, waits for them, and re-layouts: 109 us -> 47.6 us
  starting transfers between devices: 46 us -> 105 us
  Pallas kernels: 91.2 us -> 145 us
  blocking collectives: 51.8 us -> 0 us
  matrix products: 20.2 us -> 0 us
  other arithmetic: 15.7 us -> 0.76 us
  between operations: 14.6 us -> 1.5 us
    all_to_all x6 -> x9, waiting for transfers between devices: 141 us -> 0.02 us  [to_owners(): lax.all_to_all(x.reshape((owners, x.shape[0] // owners) + x.shape[1:]), '...]
    pallas_call x9 -> x44, Pallas kernels: 91.2 us -> 145 us  [kernel_call(): pl.pallas_call(body, out_shape=outs, in_specs=[pl.BlockSpec(memory_space=...]
    all_to_all x1 -> x0, blocking collectives: 51.8 us -> none  [on_device(): lax.all_to_all(back_c.reshape(owners, ccap, 2 * wide), 'grp', split_axis=...]
    ppermute x31 -> x51, starting transfers between devices: 17.4 us -> 50.9 us  [swap(): return lax.ppermute(x, axis, [(i, i ^ bit) for i in range(n)])]
    ppermute x13 -> x0, local copies, waits for them, and re-layouts: 32 us -> none  [swap(): return lax.ppermute(x, axis, [(i, i ^ bit) for i in range(n)])]
    all_to_all x6 -> x9, starting transfers between devices: 28.3 us -> 54.6 us  [to_owners(): lax.all_to_all(x.reshape((owners, x.shape[0] // owners) + x.shape[1:]), '...]
    dot_general x6 -> x0, matrix products: 20.2 us -> none  [dot(): lax.dot_general(a, b, (((ca,), (cb,)), ((), ())), preferred_element_type=...]
    ppermute x31 -> x51, waiting for transfers between devices: 203 us -> 223 us  [swap(): return lax.ppermute(x, axis, [(i, i ^ bit) for i in range(n)])]
  transfers between devices with their start and end apart: 41 -> 60, of which waited for: 18 -> 25; matrix products, arithmetic and copies ran while one was open for 16% -> 1% of each run, Pallas kernels for 12% -> 27%
where the time goes in v2:
time: 531 us; the launch traced here: 523 us
  waiting for transfers between devices  223 us (42%)
  Pallas kernels  145 us (27%)
  starting transfers between devices  105 us (20%)
  local copies, waits for them, and re-layouts  47.6 us (9%)
    ppermute x51, waiting for transfers between devices, swap(): return lax.ppermute(x, axis, [(i, i ^ bit) for i in range(n)])  223 us
    pallas_call x44, Pallas kernels, kernel_call(): pl.pallas_call(body, out_shape=outs, in_specs=[pl.BlockSpec(memory_space=...  145 us
    all_to_all x9, starting transfers between devices, to_owners(): lax.all_to_all(x.reshape((owners, x.shape[0] // owners) + x.shape[1:]), '...  54.6 us
    ppermute x51, starting transfers between devices, swap(): return lax.ppermute(x, axis, [(i, i ^ bit) for i in range(n)])  50.9 us
    unnamed x156, local copies, waits for them, and re-layouts  44.5 us
  transfers between devices with their start and end apart: 60, of which 25 were waited for; matrix products, arithmetic and copies ran while one was open for 1% of the time, Pallas kernels for 27%

profile of v2, /device:TPU:0, one launch (start us, length us, event | category | flops | bytes accessed | tf_op | source)
XLA Modules:
  0.0 523.2 jit_solution(17623377310999543298)
XLA Ops:
  6.0 7.3 %all-to-all-start = ((s32[8,1,128]{2,1,0:T(1,128)}), s32[8,1,128]{2,1,0:T(1,128)S(1)}, u32[]{:S(2)}, u32[]{:S(2)}) async-start(s32[8,1,128]{2,1,0:T(1,128)} %bitcast.4), calls=%async_computation | async-start | bytes 8192 | tf_op jit(solution)/shard_map/all_to_all | solution.py:583
  20.5 6.0 %all-to-all-start.1 = ((bf16[8,32,1024]{2,1,0:T(8,128)(2,1)}), bf16[8,32,1024]{2,1,0:T(8,128)(2,1)S(1)}, u32[]{:S(2)}, u32[]{:S(2)}) async-start(bf16[8,32,1024]{2,1,0:T(8,128)(2,1)} %bitcast.8), calls=%async_computation.1 | async-start | bytes 1048576 | tf_op jit(solution)/shard_map/all_to_all | solution.py:583
  36.6 13.9 %collective-permute-done.1.b_ref = bf16[128,1024]{1,0:T(8,128)(2,1)S(1)} collective-permute-done((bf16[128,1024]{1,0:T(8,128)(2,1)S(1)}, bf16[128,1024]{1,0:T(8,128)(2,1)S(1)}, u32[]{:S(2)}, u32[]{:S(2)}) %collective-permute-start.1) | collective-permute-done | bytes 262176 | tf_op jit(solution)/shard_map/ppermute | solution.py:20
  63.9 14.7 %collective-permute-done.6.a_ref = bf16[512,768]{1,0:T(8,128)(2,1)S(1)} collective-permute-done((bf16[512,768]{1,0:T(8,128)(2,1)S(1)}, bf16[512,768]{1,0:T(8,128)(2,1)S(1)}, u32[]{:S(2)}, u32[]{:S(2)}) %collective-permute-start.6) | collective-permute-done | bytes 786464 | tf_op jit(solution)/shard_map/ppermute | solution.py:20
  82.7 11.7 %collective-permute-done.10.a_ref = bf16[512,768]{1,0:T(8,128)(2,1)} collective-permute-done((bf16[512,768]{1,0:T(8,128)(2,1)S(1)}, bf16[512,768]{1,0:T(8,128)(2,1)}, u32[]{:S(2)}, u32[]{:S(2)}) %collective-permute-start.10) | collective-permute-done | bytes 786464 | tf_op jit(solution)/shard_map/ppermute | solution.py:20
  96.8 9.6 %collective-permute-done.7.b_ref = bf16[512,768]{1,0:T(8,128)(2,1)} collective-permute-done((bf16[512,768]{1,0:T(8,128)(2,1)S(1)}, bf16[512,768]{1,0:T(8,128)(2,1)}, u32[]{:S(2)}, u32[]{:S(2)}) %collective-permute-start.7) | collective-permute-done | bytes 786464 | tf_op jit(solution)/shard_map/ppermute | solution.py:20
  108.7 14.5 %collective-permute-done.11.b_ref = bf16[512,768]{1,0:T(8,128)(2,1)} collective-permute-done((bf16[512,768]{1,0:T(8,128)(2,1)}, bf16[512,768]{1,0:T(8,128)(2,1)}, u32[]{:S(2)}, u32[]{:S(2)}) %collective-permute-start.11) | collective-permute-done | bytes 786464 | tf_op jit(solution)/shard_map/ppermute | solution.py:20
  125.9 8.4 %collective-permute-done.13.b_ref = bf16[256,1024]{1,0:T(8,128)(2,1)} collective-permute-done((bf16[256,1024]{1,0:T(8,128)(2,1)}, bf16[256,1024]{1,0:T(8,128)(2,1)}, u32[]{:S(2)}, u32[]{:S(2)}) %collective-permute-start.13) | collective-permute-done | bytes 524320 | tf_op jit(solution)/shard_map/ppermute | solution.py:20
  139.6 8.0 %all-to-all-start.3 = ((bf16[8,32,1024]{2,1,0:T(8,128)(2,1)}), bf16[8,32,1024]{2,1,0:T(8,128)(2,1)S(1)}, u32[]{:S(2)}, u32[]{:S(2)}) async-start(bf16[8,32,1024]{2,1,0:T(8,128)(2,1)} %bitcast.12), calls=%async_computation.3 | async-start | bytes 1048576 | tf_op jit(solution)/shard_map/all_to_all | solution.py:583
  149.0 12.8 %shard_map.204 = (bf16[320,1024]{1,0:T(8,128)(2,1)S(1)}, f32[256,1024]{1,0:T(8,128)S(1)}, f32[256,1024]{1,0:T(8,128)S(1)}, f32[256,1024]{1,0:T(8,128)S(1)}, f32[...) custom-call(s32[1]{0:T(128)} %bitcast.l_ref, f32[256,1]{1,0:T(8,128)S(1)} %reshape.160.keep_ref, s32[256,1]{1,0:T(8,128)S(1)} %copy-done.43, ...), custom_call_target="tpu_custom_call" | custom-call | flops 12000000000 | bytes 15076356 | tf_op jit(solution)/shard_map/pallas_call | solution.py:40
  166.6 6.3 %all-to-all-start.4 = ((bf16[8,48,1024]{2,1,0:T(8,128)(2,1)}), bf16[8,48,1024]{2,1,0:T(8,128)(2,1)S(1)}, u32[]{:S(2)}, u32[]{:S(2)}) async-start(bf16[8,48,1024]{2,1,0:T(8,128)(2,1)} %bitcast.14), calls=%async_computation.4 | async-start | bytes 1572864 | tf_op jit(solution)/shard_map/all_to_all | solution.py:583
  173.5 15.0 %shard_map.209 = (bf16[320,1024]{1,0:T(8,128)(2,1)}, f32[256,1024]{1,0:T(8,128)S(1)}, f32[256,1024]{1,0:T(8,128)S(1)}, f32[256,1024]{1,0:T(8,128)S(1)}, f32[256,1024]{1,0:T(8,128)S(1)}, /*index=5*/f32[256,1024]{1,0:T(8,128)}) custom-call(s32[1]{0:T(128)} %bitcast.l_ref, f32[256,1]{1,0:T(8,128)S(1)} %reshape.160.keep_ref, s32[1,256]{1,0:T(1,128)S(1)} %reshape.139.land_ref, ...), custom_call_target="tpu_custom_call" | custom-call | flops 15000000512 | bytes 19662852 | tf_op jit(solution)/shard_map/pallas_call | solution.py:40
  194.4 10.8 %shard_map.212 = (bf16[256,512]{1,0:T(8,128)(2,1)S(1)}, bf16[256,512]{1,0:T(8,128)(2,1)S(1)}, bf16[256,512]{1,0:T(8,128)(2,1)S(1)}, bf16[256,512]{1,0:T(8,128)(2...) custom-call(f32[256,1]{1,0:T(8,128)S(1)} %div.11.valid_ref, s32[256,1]{1,0:T(8,128)S(1)} %copy-done.46, ...), custom_call_target="tpu_custom_call" | custom-call | flops 12000000000 | bytes 8521728 | tf_op jit(solution)/shard_map/pallas_call | solution.py:40
  207.6 5.9 %all-to-all-start.5 = ((bf16[8,48,1024]{2,1,0:T(8,128)(2,1)}), bf16[8,48,1024]{2,1,0:T(8,128)(2,1)S(1)}, u32[]{:S(2)}, u32[]{:S(2)}) async-start(bf16[8,48,1024]{2,1,0:T(8,128)(2,1)} %bitcast.16), calls=%async_computation.5 | async-start | bytes 1572864 | tf_op jit(solution)/shard_map/all_to_all | solution.py:583
  214.8 17.3 %shard_map.213 = (f32[64,1024]{1,0:T(8,128)S(1)}, f32[256,1024]{1,0:T(8,128)S(1)}, bf16[512,768]{1,0:T(8,128)(2,1)S(1)}, bf16[512,768]{1,0:T(8,128)(2,1)S(1)}, b...) custom-call(s32[1]{0:T(128)} %bitcast.l_ref, f32[256,1]{1,0:T(8,128)S(1)} %reshape.160.keep_ref, ...), custom_call_target="tpu_custom_call" | custom-call | flops 16999999488 | bytes 23331844 | tf_op jit(solution)/shard_map/pallas_call | solution.py:40
  236.5 7.2 %collective-permute-done.18.refs_2_ = bf16[256,512]{1,0:T(8,128)(2,1)S(1)} collective-permute-done((bf16[256,512]{1,0:T(8,128)(2,1)S(1)}, bf16[256,512]{1,0:T(8,128)(2,1)S(1)}, u32[]{:S(2)}, u32[]{:S(2)}) %collective-permute-start.18) | collective-permute-done | bytes 262176 | tf_op jit(solution)/shard_map/ppermute | solution.py:20
  253.0 6.4 %all-to-all-start.6 = ((bf16[8,64,1024]{2,1,0:T(8,128)(2,1)}), bf16[8,64,1024]{2,1,0:T(8,128)(2,1)S(1)}, u32[]{:S(2)}, u32[]{:S(2)}) async-start(bf16[8,64,1024]{2,1,0:T(8,128)(2,1)} %bitcast.18), calls=%async_computation.6 | async-start | bytes 2097152 | tf_op jit(solution)/shard_map/all_to_all | solution.py:583
  265.6 15.4 %shard_map.215 = (bf16[384,3072]{1,0:T(8,128)(2,1)}, bf16[256,2048]{1,0:T(8,128)(2,1)S(1)}, bf16[272,768]{1,0:T(8,128)(2,1)S(1)}, bf16[272,768]{1,0:T(8,128)(2,1...) custom-call(s32[1]{0:T(128)} %bitcast.l_ref, f32[256,1]{1,0:T(8,128)S(1)} %reshape.160.keep_ref, ...), custom_call_target="tpu_custom_call" | custom-call | flops 16000000000 | bytes 17927172 | tf_op jit(solution)/shard_map/pallas_call | solution.py:40
  283.7 12.2 %collective-permute-done.24.refs_7_ = bf16[512,768]{1,0:T(8,128)(2,1)} collective-permute-done((bf16[512,768]{1,0:T(8,128)(2,1)S(1)}, bf16[512,768]{1,0:T(8,128)(2,1)}, u32[]{:S(2)}, u32[]{:S(2)}) %collective-permute-start.24) | collective-permute-done | bytes 786464 | tf_op jit(solution)/shard_map/ppermute | solution.py:20
  295.9 5.8 %all-to-all-start.7 = ((bf16[8,48,3072]{2,1,0:T(8,128)(2,1)}), bf16[8,48,3072]{2,1,0:T(8,128)(2,1)}, u32[]{:S(2)}, u32[]{:S(2)}) async-start(bf16[8,48,3072]{2,1,0:T(8,128)(2,1)} %bitcast.33), calls=%async_computation.7 | async-start | bytes 4718592 | tf_op jit(solution)/shard_map/all_to_all | solution.py:583
  303.3 15.6 %collective-permute-done.30.refs_2_ = bf16[320,1024]{1,0:T(8,128)(2,1)S(1)} collective-permute-done((bf16[320,1024]{1,0:T(8,128)(2,1)S(1)}, bf16[320,1024]{1,0:T(8,128)(2,1)S(1)}, u32[]{:S(2)}, u32[]{:S(2)}) %collective-permute-start.30) | collective-permute-done | bytes 655392 | tf_op jit(solution)/shard_map/ppermute | solution.py:20
  332.1 7.0 %collective-permute-done.34.refs_7_ = bf16[272,768]{1,0:T(8,128)(2,1)S(1)} collective-permute-done((bf16[272,768]{1,0:T(8,128)(2,1)}, bf16[272,768]{1,0:T(8,128)(2,1)S(1)}, u32[]{:S(2)}, u32[]{:S(2)}) %collective-permute-start.34) | collective-permute-done | bytes 417824 | tf_op jit(solution)/shard_map/ppermute | solution.py:20
  356.8 6.1 %collective-permute-start.47 = (bf16[256,768]{1,0:T(8,128)(2,1)}, bf16[256,768]{1,0:T(8,128)(2,1)}, u32[]{:S(2)}, u32[]{:S(2)}) collective-permute-start(bf16[256,768]{1,0:T(8,128)(2,1)} %get-tuple-element.176), channel_id=1, source_target_pairs={{0,8},{4,12},{8,0},{12,4},{16,24},{20,28},{24,16},{28,20},{1,9},{5... | collective-permute-start | bytes 1179656 | tf_op jit(solution)/shard_map/ppermute | solution.py:20
  362.9 8.8 %collective-permute-done.35.b_ref = bf16[512,768]{1,0:T(8,128)(2,1)} collective-permute-done((bf16[512,768]{1,0:T(8,128)(2,1)}, bf16[512,768]{1,0:T(8,128)(2,1)}, u32[]{:S(2)}, u32[]{:S(2)}) %collective-permute-start.35) | collective-permute-done | bytes 786464 | tf_op jit(solution)/shard_map/ppermute | solution.py:20
  373.8 6.1 %collective-permute-start.36 = (bf16[256,768]{1,0:T(8,128)(2,1)S(1)}, bf16[256,768]{1,0:T(8,128)(2,1)}, u32[]{:S(2)}, u32[]{:S(2)}) collective-permute-start(bf16[256,768]{1,0:T(8,128)(2,1)S(1)} %get-tuple-element.164), channel_id=1, source_target_pairs={{0,8},{4,12},{8,0},{12,4},{16,24},{20,28},{24,16},{28,20},{1,9},{5... | collective-permute-start | bytes 1179656 | tf_op jit(solution)/shard_map/ppermute | solution.py:20
  379.9 5.2 shard_map.216
  400.9 19.4 %collective-permute-done.48.b_ref = bf16[256,768]{1,0:T(8,128)(2,1)} collective-permute-done((bf16[256,768]{1,0:T(8,128)(2,1)}, bf16[256,768]{1,0:T(8,128)(2,1)}, u32[]{:S(2)}, u32[]{:S(2)}) %collective-permute-start.48) | collective-permute-done | bytes 393248 | tf_op jit(solution)/shard_map/ppermute | solution.py:20
  427.6 29.0 %collective-permute-done.37.b_ref = bf16[256,768]{1,0:T(8,128)(2,1)S(1)} collective-permute-done((bf16[256,768]{1,0:T(8,128)(2,1)S(1)}, bf16[256,768]{1,0:T(8,128)(2,1)S(1)}, u32[]{:S(2)}, u32[]{:S(2)}) %collective-permute-start.37) | collective-permute-done | bytes 393248 | tf_op jit(solution)/shard_map/ppermute | solution.py:20
  459.6 5.6 %collective-permute-done.43.b_ref = bf16[256,768]{1,0:T(8,128)(2,1)} collective-permute-done((bf16[256,768]{1,0:T(8,128)(2,1)}, bf16[256,768]{1,0:T(8,128)(2,1)}, u32[]{:S(2)}, u32[]{:S(2)}) %collective-permute-start.43) | collective-permute-done | bytes 393248 | tf_op jit(solution)/shard_map/ppermute | solution.py:20
  466.5 7.1 %collective-permute-done.38.b_ref = bf16[256,768]{1,0:T(8,128)(2,1)} collective-permute-done((bf16[256,768]{1,0:T(8,128)(2,1)}, bf16[256,768]{1,0:T(8,128)(2,1)}, u32[]{:S(2)}, u32[]{:S(2)}) %collective-permute-start.38) | collective-permute-done | bytes 393248 | tf_op jit(solution)/shard_map/ppermute | solution.py:20
  491.2 5.8 %collective-permute-done.39.b_ref = bf16[512,768]{1,0:T(8,128)(2,1)} collective-permute-done((bf16[512,768]{1,0:T(8,128)(2,1)}, bf16[512,768]{1,0:T(8,128)(2,1)}, u32[]{:S(2)}, u32[]{:S(2)}) %collective-permute-start.39) | collective-permute-done | bytes 786464 | tf_op jit(solution)/shard_map/ppermute | solution.py:20
  500.2 12.9 %collective-permute-done.45.b_ref = bf16[512,768]{1,0:T(8,128)(2,1)} collective-permute-done((bf16[512,768]{1,0:T(8,128)(2,1)S(1)}, bf16[512,768]{1,0:T(8,128)(2,1)}, u32[]{:S(2)}, u32[]{:S(2)}) %collective-permute-start.45) | collective-permute-done | bytes 786464 | tf_op jit(solution)/shard_map/ppermute | solution.py:20
  (310 shorter events, 183.7 us)
Async XLA Ops:
  20.5 30.9 %all-to-all-start.1 = ((bf16[8,32,1024]{2,1,0:T(8,128)(2,1)}), bf16[8,32,1024]{2,1,0:T(8,128)(2,1)S(1)}, u32[]{:S(2)}, u32[]{:S(2)}) async-start(bf16[8,32,1024]{2,1,0:T(8,128)(2,1)} %bitcast.8), calls=%async_computation.1 | async-start | bytes 1048576 | tf_op jit(solution)/shard_map/all_to_all | solution.py:583
  26.5 34.6 %collective-permute-start.3 = (bf16[1024,768]{1,0:T(8,128)(2,1)S(1)}, bf16[1024,768]{1,0:T(8,128)(2,1)}, u32[]{:S(2)}, u32[]{:S(2)}) collective-permute-start(bf16[1024,768]{1,0:T(8,128)(2,1)S(1)} %shard_map.197.refs_0_.refs_5_), channel_id=1, source_target_pairs={{0,2},{1,3},{2,0},{3,1},{4,6},{5,7},{6,4},{7,5},{8,10},{9,11},{10,... | collective-permute-start | bytes 4718600 | tf_op jit(solution)/shard_map/ppermute | solution.py:20
  51.4 88.3 %all-to-all-start.2 = ((bf16[8,48,3072]{2,1,0:T(8,128)(2,1)}), bf16[8,48,3072]{2,1,0:T(8,128)(2,1)}, u32[]{:S(2)}, u32[]{:S(2)}) async-start(bf16[8,48,3072]{2,1,0:T(8,128)(2,1)} %bitcast.10), calls=%async_computation.2 | async-start | bytes 4718592 | tf_op jit(solution)/shard_map/all_to_all | solution.py:583
  80.2 54.2 %collective-permute-start.2 = (bf16[1024,768]{1,0:T(8,128)(2,1)S(1)}, bf16[1024,768]{1,0:T(8,128)(2,1)}, u32[]{:S(2)}, u32[]{:S(2)}) collective-permute-start(bf16[1024,768]{1,0:T(8,128)(2,1)S(1)} %shard_map.197.refs_0_.refs_5_), channel_id=1, source_target_pairs={{0,1},{1,0},{2,3},{3,2},{4,5},{5,4},{6,7},{7,6},{8,9},{9,8},{10,11... | collective-permute-start | bytes 4718600 | tf_op jit(solution)/shard_map/ppermute | solution.py:20
  80.2 67.5 %collective-permute-start.4 = (bf16[1024,768]{1,0:T(8,128)(2,1)}, bf16[1024,768]{1,0:T(8,128)(2,1)}, u32[]{:S(2)}, u32[]{:S(2)}) collective-permute-start(bf16[1024,768]{1,0:T(8,128)(2,1)} %collective-permute-done.3.refs_2_.refs_7_), channel_id=1, source_target_pairs={{0,1},{1,0},{2,3},{3,2},{4,5},{5,4},{6,7},{7,6},{8,9},{9,8},{10,11... | collective-permute-start | bytes 4718600 | tf_op jit(solution)/shard_map/ppermute | solution.py:20
  94.4 28.8 %collective-permute-start.11 = (bf16[512,768]{1,0:T(8,128)(2,1)}, bf16[512,768]{1,0:T(8,128)(2,1)}, u32[]{:S(2)}, u32[]{:S(2)}) collective-permute-start(bf16[512,768]{1,0:T(8,128)(2,1)} %collective-permute-done.10.a_ref), channel_id=1, source_target_pairs={{0,4},{4,0},{8,12},{12,8},{16,20},{20,16},{24,28},{28,24},{1,5},{5... | collective-permute-start | bytes 2359304 | tf_op jit(solution)/shard_map/ppermute | solution.py:20
  96.2 38.1 %collective-permute-start.13 = (bf16[256,1024]{1,0:T(8,128)(2,1)}, bf16[256,1024]{1,0:T(8,128)(2,1)}, u32[]{:S(2)}, u32[]{:S(2)}) collective-permute-start(bf16[256,1024]{1,0:T(8,128)(2,1)} %shard_map.203.a_ref), channel_id=1, source_target_pairs={{0,4},{4,0},{8,12},{12,8},{16,20},{20,16},{24,28},{28,24},{1,5},{5... | collective-permute-start | bytes 1572872 | tf_op jit(solution)/shard_map/ppermute | solution.py:20
  106.4 66.5 %collective-permute-start.5 = (bf16[1024,768]{1,0:T(8,128)(2,1)}, bf16[1024,768]{1,0:T(8,128)(2,1)}, u32[]{:S(2)}, u32[]{:S(2)}) collective-permute-start(bf16[1024,768]{1,0:T(8,128)(2,1)} %copy-done.6), channel_id=1, source_target_pairs={{0,1},{1,0},{2,3},{3,2},{4,5},{5,4},{6,7},{7,6},{8,9},{9,8},{10,11... | collective-permute-start | bytes 4718600 | tf_op jit(solution)/shard_map/ppermute | solution.py:20
  123.2 50.3 %collective-permute-start.9 = (bf16[1024,768]{1,0:T(8,128)(2,1)}, bf16[1024,768]{1,0:T(8,128)(2,1)}, u32[]{:S(2)}, u32[]{:S(2)}) collective-permute-start(bf16[1024,768]{1,0:T(8,128)(2,1)} %get-tuple-element.109.refs_4_.refs_9_), channel_id=1, source_target_pairs={{0,1},{1,0},{2,3},{3,2},{4,5},{5,4},{6,7},{7,6},{8,9},{9,8},{10,11... | collective-permute-start | bytes 4718600 | tf_op jit(solution)/shard_map/ppermute | solution.py:20
  134.3 39.2 %collective-permute-start.8 = (bf16[1024,768]{1,0:T(8,128)(2,1)}, bf16[1024,768]{1,0:T(8,128)(2,1)}, u32[]{:S(2)}, u32[]{:S(2)}) collective-permute-start(bf16[1024,768]{1,0:T(8,128)(2,1)} %shard_map.206.refs_2_.refs_7_), channel_id=1, source_target_pairs={{0,1},{1,0},{2,3},{3,2},{4,5},{5,4},{6,7},{7,6},{8,9},{9,8},{10,11... | collective-permute-start | bytes 4718600 | tf_op jit(solution)/shard_map/ppermute | solution.py:20
  134.3 39.2 %collective-permute-start.12 = (bf16[1024,768]{1,0:T(8,128)(2,1)}, bf16[1024,768]{1,0:T(8,128)(2,1)}, u32[]{:S(2)}, u32[]{:S(2)}) collective-permute-start(bf16[1024,768]{1,0:T(8,128)(2,1)} %shard_map.208.refs_6_.refs_11_), channel_id=1, source_target_pairs={{0,1},{1,0},{2,3},{3,2},{4,5},{5,4},{6,7},{7,6},{8,9},{9,8},{10,11... | collective-permute-start | bytes 4718600 | tf_op jit(solution)/shard_map/ppermute | solution.py:20
  139.6 26.9 %all-to-all-start.3 = ((bf16[8,32,1024]{2,1,0:T(8,128)(2,1)}), bf16[8,32,1024]{2,1,0:T(8,128)(2,1)S(1)}, u32[]{:S(2)}, u32[]{:S(2)}) async-start(bf16[8,32,1024]{2,1,0:T(8,128)(2,1)} %bitcast.12), calls=%async_computation.3 | async-start | bytes 1048576 | tf_op jit(solution)/shard_map/all_to_all | solution.py:583
  166.6 27.8 %all-to-all-start.4 = ((bf16[8,48,1024]{2,1,0:T(8,128)(2,1)}), bf16[8,48,1024]{2,1,0:T(8,128)(2,1)S(1)}, u32[]{:S(2)}, u32[]{:S(2)}) async-start(bf16[8,48,1024]{2,1,0:T(8,128)(2,1)} %bitcast.14), calls=%async_computation.4 | async-start | bytes 1572864 | tf_op jit(solution)/shard_map/all_to_all | solution.py:583
  192.5 43.5 %collective-permute-start.20 = (bf16[320,1024]{1,0:T(8,128)(2,1)}, bf16[320,1024]{1,0:T(8,128)(2,1)}, u32[]{:S(2)}, u32[]{:S(2)}) collective-permute-start(bf16[320,1024]{1,0:T(8,128)(2,1)} %get-tuple-element.128.state_ref.refs_4_.refs_0_), channel_id=1, source_target_pairs={{0,1},{1,0},{2,3},{3,2},{4,5},{5,4},{6,7},{7,6},{8,9},{9,8},{10,11... | collective-permute-start | bytes 1966088 | tf_op jit(solution)/shard_map/ppermute | solution.py:20
  192.6 41.4 %collective-permute-start.21 = (bf16[320,1024]{1,0:T(8,128)(2,1)}, bf16[320,1024]{1,0:T(8,128)(2,1)}, u32[]{:S(2)}, u32[]{:S(2)}) collective-permute-start(bf16[320,1024]{1,0:T(8,128)(2,1)} %get-tuple-element.128.state_ref.refs_4_.refs_0_), channel_id=1, source_target_pairs={{0,2},{1,3},{2,0},{3,1},{4,6},{5,7},{6,4},{7,5},{8,10},{9,11},{10,... | collective-permute-start | bytes 1966088 | tf_op jit(solution)/shard_map/ppermute | solution.py:20
  207.6 44.5 %all-to-all-start.5 = ((bf16[8,48,1024]{2,1,0:T(8,128)(2,1)}), bf16[8,48,1024]{2,1,0:T(8,128)(2,1)S(1)}, u32[]{:S(2)}, u32[]{:S(2)}) async-start(bf16[8,48,1024]{2,1,0:T(8,128)(2,1)} %bitcast.16), calls=%async_computation.5 | async-start | bytes 1572864 | tf_op jit(solution)/shard_map/all_to_all | solution.py:583
  253.0 42.9 %all-to-all-start.6 = ((bf16[8,64,1024]{2,1,0:T(8,128)(2,1)}), bf16[8,64,1024]{2,1,0:T(8,128)(2,1)S(1)}, u32[]{:S(2)}, u32[]{:S(2)}) async-start(bf16[8,64,1024]{2,1,0:T(8,128)(2,1)} %bitcast.18), calls=%async_computation.6 | async-start | bytes 2097152 | tf_op jit(solution)/shard_map/all_to_all | solution.py:583
  260.7 35.1 %collective-permute-start.24 = (bf16[512,768]{1,0:T(8,128)(2,1)S(1)}, bf16[512,768]{1,0:T(8,128)(2,1)}, u32[]{:S(2)}, u32[]{:S(2)}) collective-permute-start(bf16[512,768]{1,0:T(8,128)(2,1)S(1)} %get-tuple-element.140), channel_id=1, source_target_pairs={{0,3},{1,2},{2,1},{3,0},{4,7},{5,6},{6,5},{7,4},{8,11},{9,10},{10,... | collective-permute-start | bytes 2359304 | tf_op jit(solution)/shard_map/ppermute | solution.py:20
  295.9 84.1 %all-to-all-start.7 = ((bf16[8,48,3072]{2,1,0:T(8,128)(2,1)}), bf16[8,48,3072]{2,1,0:T(8,128)(2,1)}, u32[]{:S(2)}, u32[]{:S(2)}) async-start(bf16[8,48,3072]{2,1,0:T(8,128)(2,1)} %bitcast.33), calls=%async_computation.7 | async-start | bytes 4718592 | tf_op jit(solution)/shard_map/all_to_all | solution.py:583
  328.1 26.7 %collective-permute-start.46 = (bf16[512,768]{1,0:T(8,128)(2,1)S(1)}, bf16[512,768]{1,0:T(8,128)(2,1)S(1)}, u32[]{:S(2)}, u32[]{:S(2)}) collective-permute-start(bf16[512,768]{1,0:T(8,128)(2,1)S(1)} %get-tuple-element.174), channel_id=1, source_target_pairs={{0,4},{4,0},{8,12},{12,8},{16,20},{20,16},{24,28},{28,24},{1,5},{5... | collective-permute-start | bytes 2359304 | tf_op jit(solution)/shard_map/ppermute | solution.py:20
  343.3 28.5 %collective-permute-start.35 = (bf16[512,768]{1,0:T(8,128)(2,1)}, bf16[512,768]{1,0:T(8,128)(2,1)}, u32[]{:S(2)}, u32[]{:S(2)}) collective-permute-start(bf16[512,768]{1,0:T(8,128)(2,1)} %get-tuple-element.162), channel_id=1, source_target_pairs={{0,4},{4,0},{8,12},{12,8},{16,20},{20,16},{24,28},{28,24},{1,5},{5... | collective-permute-start | bytes 2359304 | tf_op jit(solution)/shard_map/ppermute | solution.py:20
  350.7 42.1 %collective-permute-start.41 = (bf16[512,768]{1,0:T(8,128)(2,1)}, bf16[512,768]{1,0:T(8,128)(2,1)}, u32[]{:S(2)}, u32[]{:S(2)}) collective-permute-start(bf16[512,768]{1,0:T(8,128)(2,1)} %get-tuple-element.169), channel_id=1, source_target_pairs={{0,4},{4,0},{8,12},{12,8},{16,20},{20,16},{24,28},{28,24},{1,5},{5... | collective-permute-start | bytes 2359304 | tf_op jit(solution)/shard_map/ppermute | solution.py:20
  356.8 29.7 %collective-permute-start.47 = (bf16[256,768]{1,0:T(8,128)(2,1)}, bf16[256,768]{1,0:T(8,128)(2,1)}, u32[]{:S(2)}, u32[]{:S(2)}) collective-permute-start(bf16[256,768]{1,0:T(8,128)(2,1)} %get-tuple-element.176), channel_id=1, source_target_pairs={{0,8},{4,12},{8,0},{12,4},{16,24},{20,28},{24,16},{28,20},{1,9},{5... | collective-permute-start | bytes 1179656 | tf_op jit(solution)/shard_map/ppermute | solution.py:20
  386.4 95.6 %collective-permute-start.25 = (bf16[2,160,3072]{2,1,0:T(8,128)(2,1)}, bf16[2,160,3072]{2,1,0:T(8,128)(2,1)}, u32[]{:S(2)}, u32[]{:S(2)}) collective-permute-start(bf16[2,160,3072]{2,1,0:T(8,128)(2,1)} %get-tuple-element.147), channel_id=1, source_target_pairs={{0,1},{1,0},{2,3},{3,2},{4,5},{5,4},{6,7},{7,6},{8,9},{9,8},{10,11... | collective-permute-start | bytes 5898248 | tf_op jit(solution)/shard_map/ppermute | solution.py:20
  388.2 32.0 %collective-permute-start.48 = (bf16[256,768]{1,0:T(8,128)(2,1)}, bf16[256,768]{1,0:T(8,128)(2,1)}, u32[]{:S(2)}, u32[]{:S(2)}) collective-permute-start(bf16[256,768]{1,0:T(8,128)(2,1)} %shard_map.236.a_ref), channel_id=1, source_target_pairs={{0,16},{4,20},{8,24},{12,28},{16,0},{20,4},{24,8},{28,12},{1,17},{... | collective-permute-start | bytes 1179656 | tf_op jit(solution)/shard_map/ppermute | solution.py:20
  388.3 93.8 %all-to-all-start.8 = ((bf16[8,32,2048]{2,1,0:T(8,128)(2,1)}), bf16[8,32,2048]{2,1,0:T(8,128)(2,1)}, u32[]{:S(2)}, u32[]{:S(2)}) async-start(bf16[8,32,2048]{2,1,0:T(8,128)(2,1)} %bitcast.28), calls=%async_computation.8 | async-start | bytes 2097152 | tf_op jit(solution)/shard_map/all_to_all | solution.py:583
  395.2 28.7 %collective-permute-start.42 = (bf16[256,768]{1,0:T(8,128)(2,1)S(1)}, bf16[256,768]{1,0:T(8,128)(2,1)S(1)}, u32[]{:S(2)}, u32[]{:S(2)}) collective-permute-start(bf16[256,768]{1,0:T(8,128)(2,1)S(1)} %get-tuple-element.171), channel_id=1, source_target_pairs={{0,8},{4,12},{8,0},{12,4},{16,24},{20,28},{24,16},{28,20},{1,9},{5... | collective-permute-start | bytes 1179656 | tf_op jit(solution)/shard_map/ppermute | solution.py:20
  398.4 58.2 %collective-permute-start.37 = (bf16[256,768]{1,0:T(8,128)(2,1)S(1)}, bf16[256,768]{1,0:T(8,128)(2,1)S(1)}, u32[]{:S(2)}, u32[]{:S(2)}) collective-permute-start(bf16[256,768]{1,0:T(8,128)(2,1)S(1)} %shard_map.224.a_ref), channel_id=1, source_target_pairs={{0,16},{4,20},{8,24},{12,28},{16,0},{20,4},{24,8},{28,12},{1,17},{... | collective-permute-start | bytes 1179656 | tf_op jit(solution)/shard_map/ppermute | solution.py:20
  421.5 36.2 %collective-permute-start.49 = (bf16[256,768]{1,0:T(8,128)(2,1)S(1)}, bf16[256,768]{1,0:T(8,128)(2,1)}, u32[]{:S(2)}, u32[]{:S(2)}) collective-permute-start(bf16[256,768]{1,0:T(8,128)(2,1)S(1)} %shard_map.237.a_ref), channel_id=1, source_target_pairs={{0,8},{4,12},{8,0},{12,4},{16,24},{20,28},{24,16},{28,20},{1,9},{5... | collective-permute-start | bytes 1179656 | tf_op jit(solution)/shard_map/ppermute | solution.py:20
  424.8 40.5 %collective-permute-start.43 = (bf16[256,768]{1,0:T(8,128)(2,1)}, bf16[256,768]{1,0:T(8,128)(2,1)}, u32[]{:S(2)}, u32[]{:S(2)}) collective-permute-start(bf16[256,768]{1,0:T(8,128)(2,1)} %shard_map.230.a_ref), channel_id=1, source_target_pairs={{0,16},{4,20},{8,24},{12,28},{16,0},{20,4},{24,8},{28,12},{1,17},{... | collective-permute-start | bytes 1179656 | tf_op jit(solution)/shard_map/ppermute | solution.py:20
  482.0 31.1 %collective-permute-start.45 = (bf16[512,768]{1,0:T(8,128)(2,1)S(1)}, bf16[512,768]{1,0:T(8,128)(2,1)}, u32[]{:S(2)}, u32[]{:S(2)}) collective-permute-start(bf16[512,768]{1,0:T(8,128)(2,1)S(1)} %shard_map.232.a_ref), channel_id=1, source_target_pairs={{0,4},{4,0},{8,12},{12,8},{16,20},{20,16},{24,28},{28,24},{1,5},{5... | collective-permute-start | bytes 2359304 | tf_op jit(solution)/shard_map/ppermute | solution.py:20
  484.6 36.9 %collective-permute-start.26 = (bf16[160,3072]{1,0:T(8,128)(2,1)S(1)}, bf16[160,3072]{1,0:T(8,128)(2,1)S(1)}, u32[]{:S(2)}, u32[]{:S(2)}) collective-permute-start(bf16[160,3072]{1,0:T(8,128)(2,1)S(1)} %get-tuple-element.149), channel_id=1, source_target_pairs={{0,2},{1,3},{2,0},{3,1},{4,6},{5,7},{6,4},{7,5},{8,10},{9,11},{10,... | collective-permute-start | bytes 2949128 | tf_op jit(solution)/shard_map/ppermute | solution.py:20
  (106 other events, 992.6 us)

commit v3 on v2

v3 whole, which is shorter than its diff:
```python
import functools

import jax
import jax.numpy as jnp
import numpy as np
from jax import lax
from jax.experimental import pallas as pl
from jax.experimental.pallas import tpu as pltpu
from jax.sharding import PartitionSpec as P

BPREG = 1.0
BF16 = jnp.bfloat16
F32 = jnp.float32
I32 = jnp.int32
LANES = 128
VMEM_LIMIT = 48 << 20


def swap(x, axis, bit):
    n = lax.axis_size(axis)
    return lax.ppermute(x, axis, [(i, i ^ bit) for i in range(n)])


def gather_xor(x, axis):
    blocks = {0: x}
    bit = lax.axis_size(axis) // 2
    while bit:
        for k in list(blocks):
            blocks[k | bit] = swap(blocks[k], axis, bit)
        bit //= 2
    return [blocks[k] for k in range(len(blocks))]


def send_xor(chunks, axis):
    return [chunks[0]] + [swap(chunks[j], axis, j) for j in range(1, len(chunks))]


def kernel_call(body, outs, ins, smem=0, scratch=(), us=1, left=0, left_outs=0):
    vmem, place = pl.BlockSpec(memory_space=pltpu.VMEM), pl.BlockSpec(memory_space=pl.ANY)
    nbytes = sum(a.size * a.dtype.itemsize for a in ins)
    nbytes += sum(int(functools.reduce(lambda a, b: a * b, o.shape)) * o.dtype.itemsize for o in outs)
    return pl.pallas_call(
        body,
        out_shape=outs,
        in_specs=[pl.BlockSpec(memory_space=pltpu.SMEM)] * smem
        + [vmem] * (len(ins) - smem - left)
        + [place] * left,
        out_specs=[vmem] * (len(outs) - left_outs) + [place] * left_outs,
        scratch_shapes=list(scratch),
        compiler_params=pltpu.CompilerParams(vmem_limit_bytes=VMEM_LIMIT),
        cost_estimate=pl.CostEstimate(flops=us * 10**9, bytes_accessed=nbytes, transcendentals=0),
    )(*ins)


def after(x, *deps):
    return lax.optimization_barrier((x,) + deps)[0]


def shape(dims, dtype):
    return jax.ShapeDtypeStruct(dims, dtype)


def iota(dims, dim):
    return lax.broadcasted_iota(I32, dims, dim)


def dot(a, b, ca=1, cb=0):
    return lax.dot_general(a, b, (((ca,), (cb,)), ((), ())), preferred_element_type=F32)


class Loader:
    def __init__(self, copies):
        self.copies = copies
        self.waited = set()
        for group in copies.values():
            for copy in group:
                copy.start()

    def ready(self, slot):
        if slot not in self.waited:
            self.waited.add(slot)
            for copy in self.copies[slot]:
                copy.wait()


class Weights(Loader):
    def __init__(self, refs, buf, sem, side=None):
        n = buf.shape[0]
        pieces = (len(refs) - n // 2) // (n // 2)
        copies, k = {}, 0
        for j in range(n):
            row, copies[j] = 0, []
            for _ in range(1 if j < n // 2 else pieces):
                size = refs[k].shape[0]
                at = row
                if side is not None and j >= n // 2:
                    at = pl.multiple_of((side if row == 0 else 1 - side) * size, size)
                part = buf.at[j, pl.ds(at, size), :]
                copies[j].append(pltpu.make_async_copy(refs[k], part, sem.at[k]))
                row, k = row + size, k + 1
        self.buf = buf
        super().__init__(copies)

    def __getitem__(self, j):
        self.ready(j)
        return self.buf[j]


def step_copies(ref, buf, sem, steps, batch, out):
    copies = {}
    for t in reversed(range(steps)):
        at = (slice(None), pl.ds(t * batch, batch), slice(None))
        pair = (buf.at[at], ref.at[at]) if out else (ref.at[at], buf.at[at])
        copies[t] = [pltpu.make_async_copy(*pair, sem.at[t])]
    return copies


def low(cond):
    return jnp.where(cond, 1.0, 0.0).astype(BF16)


def start_kernel(dims, in_ref, tg_ref, plan_ref, carried_ref, s_in, s_tg, s_pl, out_ref):
    owners, rows, cap, batch, ccap = dims
    hidden = carried_ref.shape[2]
    wide = out_ref.shape[1] // 2
    spare = wide - hidden

    def place(ids, span):
        n = ids.shape[0]
        owner_i = iota((n, owners), 1)
        member = (ids >= owner_i * span) & (ids < (owner_i + 1) * span)
        earlier = low(iota((n, n), 1) < iota((n, n), 0))
        before = dot(earlier, low(member))
        rank = jnp.sum(jnp.where(member, before, 0.0), axis=1, keepdims=True).astype(I32)
        owner = jnp.sum(jnp.where(member, owner_i, 0).astype(F32), axis=1, keepdims=True).astype(I32)
        return owner, rank

    def digits(owner, rank, first, value):
        n = owner.shape[0]
        turn = sum((rank >= k * ccap).astype(I32) for k in range(1, -(-cap // ccap)))
        row = owner * ccap + rank - turn * ccap
        hit = low(iota((n, owners * ccap), 1) == row)
        lane = iota((n, LANES), 1)
        high, rest = (value >> 8).astype(F32), (value & 255).astype(F32)
        at = first + 2 * turn
        code = jnp.where(lane == at, high, jnp.where(lane == at + 1, rest, 0.0))
        return dot(hit, code.astype(BF16), 0, 0)

    o_in, r_in = place(in_ref[...], rows)
    o_tg, r_tg = place(tg_ref[...], rows)
    o_pl, r_pl = place(plan_ref[...], batch)
    s_in[...] = o_in * cap + r_in
    s_tg[...] = o_tg * cap + r_tg
    s_pl[...] = o_pl * ccap + r_pl
    turns = -(-cap // ccap)
    code = digits(o_in, r_in, 0, in_ref[...] + 1)
    code += digits(o_tg, r_tg, 2 * turns, tg_ref[...] + 1)
    code += digits(o_pl, r_pl, 4 * turns, plan_ref[...] - o_pl * batch + 1)
    pick = low(iota((batch, owners * ccap), 1) == o_pl * ccap + r_pl)
    parts = [dot(pick, carried_ref[k].astype(BF16), 0, 0) for k in range(2)]
    parts = [parts[0], code[:, :spare], parts[1], jnp.zeros((owners * ccap, spare), F32)]
    out_ref[...] = jnp.concatenate(parts, axis=1).astype(BF16)


def decode(got_ref, row_ref, turn_ref, hidden, first):
    wide = got_ref.shape[1] // 2
    block = got_ref[:, wide - LANES : wide]
    n = row_ref.shape[0]
    found = dot(low(iota((n, block.shape[0]), 1) == row_ref[...]), block)
    at = hidden - wide + LANES + first + 2 * turn_ref[...]
    lane = iota((n, LANES), 1)
    worth = jnp.where(lane == at, 256.0, jnp.where(lane == at + 1, 1.0, 0.0))
    return jnp.sum(found * worth, axis=1, keepdims=True).astype(I32)


def landing(land_ref, got_ref, layer, batch, hidden):
    wide = got_ref.shape[1] // 2
    land = low(iota((land_ref.shape[0], batch), 1) == land_ref[...])
    moved = dot(land, got_ref[:, layer * wide : (layer + 1) * wide], 0, 0)
    return jnp.where(iota(moved.shape, 1) < hidden, moved, 0.0)


def extend(value, keep, hidden):
    lane = iota(value.shape, 1)
    return jnp.where(lane == hidden, 1.0, jnp.where(lane == hidden + 1, keep, value)).astype(BF16)


def run_steps(steps, batch, hidden, l, keep_ref, weights, x_of, start, state_ref, res, q_s):
    res_ref, res_s, res_sem = res
    n_loc = q_s.shape[0]
    wide = start.shape[1]
    tail = jnp.zeros((batch, wide), F32)
    lane = iota((batch, wide), 1)
    prev = start
    writes = step_copies(res_ref, res_s, res_sem, steps, batch, True)
    for t in range(steps):
        at = pl.ds(t * batch, batch)
        keep = keep_ref[at, :]
        state_ref[at, :] = extend(prev, keep, hidden)
        p = prev * keep
        p_low = p.astype(BF16)
        for j in range(n_loc):
            q_s[l ^ j] = dot(p_low, weights[j])[:, : q_s.shape[2]]
        q = jnp.concatenate([q_s[i] for i in range(n_loc)] + [tail], axis=1)
        x = x_of(t)
        h2 = 2 * hidden
        z = jax.nn.sigmoid(x[:, :wide] + q[:, :wide])
        r = jax.nn.sigmoid(x[:, hidden : hidden + wide] + q[:, hidden : hidden + wide])
        qn = q[:, h2 : h2 + wide]
        n = jnp.tanh(x[:, h2 : h2 + wide] + r * qn)
        prev = jnp.where(lane < hidden, n + z * (p - n), 0.0)
        for k, val in enumerate((z, r, n, qn, p)):
            res_s[k, at, :] = val
        writes[t][0].start()
    state_ref[pl.ds(steps * batch, batch), :] = extend(prev, 0.0, hidden)
    for t in range(steps):
        writes[t][0].wait()


def pad_kernel(at, n_in, l_ref, w_ref, *refs):
    refs, outs = refs[: n_in - 2], refs[n_in - 2 :]
    out_ref = outs[0]
    rows, cols = w_ref.shape
    out_ref[...] = jnp.zeros(out_ref.shape, BF16)
    out_ref[:rows, :cols] = w_ref[...]
    if at is not None:
        which, row = at
        tile = row // 16 * 16
        here = (iota((16, cols), 0) == row - tile).astype(F32)
        old = out_ref[tile : tile + 16, :cols].astype(F32)
        extra = refs[0][which : which + 1, :].astype(F32)
        out_ref[tile : tile + 16, :cols] = (old + here * extra).astype(BF16)
    if len(outs) == 2:
        half = outs[1].shape[0]
        side = l_ref[1] & 1
        outs[1][...] = out_ref[pl.ds(pl.multiple_of(side * half, half), half), :]
    else:
        first = outs[1].shape[0]
        outs[1][...] = out_ref[:first, :]
        outs[2][...] = out_ref[first:, :]


def gather_in_kernel(dims, base_ref, got_ref, row_ref, turn_ref, table_ref, out_ref, ids_ref, land_ref):
    hidden, turns = dims
    rows, cols = table_ref.shape
    wide = got_ref.shape[1] // 2
    ids = decode(got_ref, row_ref, turn_ref, hidden, 0) - 1 - base_ref[0]
    ids_ref[...] = ids
    at = hidden - wide + LANES + 4 * turns + 1
    land = got_ref[:, wide - LANES : wide].astype(F32)[:, at : at + 1]
    land_ref[...] = land.astype(I32) - 1
    pick = low(iota((ids.shape[0], rows), 1) == ids)
    if out_ref.shape[1] > cols:
        out_ref[...] = jnp.zeros(out_ref.shape, BF16)
    out_ref[:, :cols] = dot(pick, table_ref[...]).astype(BF16)


def biased_rows(ids, table_ref, bias_ref, wide):
    n = ids.shape[0]
    rows, cols = table_ref.shape
    pick = low(iota((n, rows), 1) == ids)
    parts = [dot(pick, table_ref[...]), dot(pick, bias_ref[...])[:, :1]]
    parts.append(jnp.zeros((n, wide - cols - 1), F32))
    return jnp.concatenate(parts, axis=1).astype(BF16)


def gather_tg_kernel(dims, base_ref, got_ref, row_ref, turn_ref, table_ref, bias_ref, out_ref, ids_ref):
    hidden, turns = dims
    ids = decode(got_ref, row_ref, turn_ref, hidden, 2 * turns) - 1 - base_ref[0]
    ids_ref[...] = ids
    out_ref[...] = biased_rows(ids, table_ref, bias_ref, out_ref.shape[1])


def gather_neg_kernel(ids_ref, table_ref, bias_ref, out_ref):
    out_ref[...] = biased_rows(ids_ref[...], table_ref, bias_ref, out_ref.shape[1])


def table_kernel(own, pairs, l_ref, *refs):
    mine_ref, far_ref, near_ref = refs[2 * pairs :]
    pad = mine_ref.shape[0]
    l = l_ref[0]
    for j, (ref, at) in enumerate(((mine_ref, None), (near_ref, 0), (far_ref, None), (near_ref, 1))):
        part = None
        for ids_ref, got_ref in zip(refs[:pairs], refs[pairs : 2 * pairs]):
            row = iota((pad, ids_ref.shape[1]), 0)
            hit = (row < own) & (row + (l ^ j) * own == ids_ref[...])
            term = dot(low(hit), got_ref[...])
            part = term if part is None else part + term
        if at is None:
            ref[...] = part
        else:
            ref[at, :, :] = part.astype(BF16)


def table_add_kernel(mine_ref, far_ref, got_ref, sum_ref, send_ref):
    sum_ref[...] = mine_ref[...] + got_ref[0].astype(F32)
    send_ref[...] = (far_ref[...] + got_ref[1].astype(F32)).astype(BF16)


def table_out_kernel(sum_ref, got_ref, out_ref):
    rows, cols = out_ref.shape
    out_ref[...] = (sum_ref[...] + got_ref[...].astype(F32))[:rows, :cols]


def carry_kernel(slot_ref, got_ref, out_ref):
    hidden = out_ref.shape[2]
    wide = got_ref.shape[1] // 2
    pick = low(iota((slot_ref.shape[0], got_ref.shape[0]), 1) == slot_ref[...])
    back = dot(pick, got_ref[...])
    out_ref[0] = back[:, :hidden]
    out_ref[1] = back[:, wide : wide + hidden]


def split_kernel(bit, l_ref, a_ref, b_ref, keep_ref, send_ref):
    half = keep_ref.shape[0]
    side = (l_ref[0] >> bit) & 1
    for ref, at in ((keep_ref, side), (send_ref, 1 - side)):
        rows = pl.ds(pl.multiple_of(at * half, half), half)
        ref[...] = (a_ref[rows, :].astype(F32) + b_ref[rows, :].astype(F32)).astype(BF16)


def add_kernel(a_ref, b_ref, out_ref):
    out_ref[...] = (a_ref[...].astype(F32) + b_ref[...].astype(F32)).astype(BF16)


def join_kernel(bit, l_ref, a_ref, b_ref, out_ref):
    half = a_ref.shape[0]
    side = (l_ref[0] >> bit) & 1
    for ref, at in ((a_ref, side), (b_ref, 1 - side)):
        out_ref[pl.ds(pl.multiple_of(at * half, half), half), :] = ref[...]


def final_kernel(hidden, bias_row, l_ref, a_ref, b_ref, out_ref, bias_ref):
    side = l_ref[0] & 1
    cols = out_ref.shape[1]
    half = a_ref.shape[0]
    at = (bias_row - half) // 16 * 16
    for first, second, when in ((a_ref, b_ref, 0), (b_ref, a_ref, 1)):

        @pl.when(side == when)
        def _():
            out_ref[:half, :] = first[...].astype(F32)[:, :cols]
            out_ref[half:, :] = second[...].astype(F32)[: hidden - half, :cols]
            row = bias_row - half - at
            bias_ref[...] = second[at : at + 16, :].astype(F32)[row : row + 1, :cols]


def first_kernel(dims, n_w, l_ref, keep_ref, slot_ref, land_ref, got_ref, rows_ref, *refs):
    steps, batch, hidden, bias_row, n_loc = dims
    w_refs, refs = refs[:n_w], refs[n_w:]
    state_ref, res_ref, w_buf, w_sem, res_s, res_sem, q_s, b_s, x_s = refs
    wide = res_s.shape[2]
    l = l_ref[0]
    weights = Weights(w_refs, w_buf, w_sem)
    pick = low(iota((steps * batch, rows_ref.shape[0]), 1) == slot_ref[...])
    x_s[...] = dot(pick, rows_ref[...])
    moved = landing(land_ref, got_ref, 0, batch, hidden)
    for j in range(n_loc):
        weights.ready(j)
        b_s[l ^ j] = w_buf[j, bias_row : bias_row + 16, :].astype(F32)[:, : b_s.shape[2]]
    bias = jnp.concatenate([b_s[i][0:1, :] for i in range(n_loc)], axis=1)
    pad = jnp.zeros((batch, wide), F32)

    def x_of(t):
        gates = bias.shape[1]
        return jnp.concatenate([x_s[pl.ds(t * batch, batch), :][:, :gates] + bias, pad], axis=1)

    run_steps(
        steps, batch, hidden, l, keep_ref, weights, x_of, moved, state_ref,
        (res_ref, res_s, res_sem), q_s,
    )


def second_kernel(dims, n_in, n_w, l_ref, keep_ref, land_ref, got_ref, below_ref, *refs):
    steps, batch, hidden, n_loc = dims
    in_refs, w_refs, refs = refs[:n_in], refs[n_in : n_in + n_w], refs[n_in + n_w :]
    state_ref, res_ref, in_buf, in_sem, w_buf, w_sem, res_s, res_sem, q_s, x_s = refs
    wide = res_s.shape[2]
    l = l_ref[0]
    inputs = Weights(in_refs, in_buf, in_sem, l_ref[1] & 1)
    weights = Weights(w_refs, w_buf, w_sem, l_ref[1] & 1)
    moved = landing(land_ref, got_ref, 1, batch, hidden)
    below = below_ref[pl.ds(batch, steps * batch), :]
    for j in range(n_loc):
        x_s[l ^ j] = dot(below, inputs[j])[:, : x_s.shape[2]]
    pad = jnp.zeros((batch, wide), F32)

    def x_of(t):
        return jnp.concatenate(
            [x_s[i][t * batch : (t + 1) * batch, :] for i in range(n_loc)] + [pad], axis=1
        )

    run_steps(
        steps, batch, hidden, l, keep_ref, weights, x_of, moved, state_ref,
        (res_ref, res_s, res_sem), q_s,
    )


def score_kernel(dims, valid_ref, slot_ref, state_ref, tg_ref, *refs):
    steps, batch, n_loc = dims
    rows = steps * batch
    neg_refs, refs = refs[:n_loc], refs[n_loc:]
    gn_refs, into_ref, send_ref = refs[:n_loc], refs[n_loc], refs[n_loc + 1]
    sn_s, tgt_s, tgg_s, neg_buf, neg_sem = refs[n_loc + 2 :]
    negs = Loader(
        {
            j: [pltpu.make_async_copy(neg_refs[j], neg_buf.at[j], neg_sem.at[j])]
            for j in range(n_loc)
        }
    )
    diag = iota((batch, batch), 0) == iota((batch, batch), 1)
    slots = tg_ref.shape[0]
    pick = low(iota((rows, slots), 1) == slot_ref[...])
    tgt_s[...] = dot(pick, tg_ref[...]).astype(BF16)
    every = state_ref[pl.ds(batch, rows), :]
    for j in range(n_loc):
        negs.ready(j)
        sn_s[j] = dot(every, neg_buf[j], 1, 1)
    for t in range(steps):
        at = pl.ds(t * batch, batch)
        second = state_ref[pl.ds((t + 1) * batch, batch), :]
        targets = tgt_s[at, :]
        st = dot(second, targets, 1, 1)
        sn = [sn_s[j, at, :] for j in range(n_loc)]
        pos = jnp.sum(jnp.where(diag, st, 0.0), axis=1, keepdims=True)
        top = jnp.max(jnp.where(diag, -jnp.inf, st), axis=1, keepdims=True)
        for s in sn:
            top = jnp.maximum(top, jnp.max(s, axis=1, keepdims=True))
        parts = [(st, jnp.where(diag, 0.0, jnp.exp(st - top)))]
        parts += [(s, jnp.exp(s - top)) for s in sn]
        mass = sum(jnp.sum(e, axis=1, keepdims=True) for _, e in parts)
        scale = 1.0 / mass
        parts = [(s, e * scale, jax.nn.sigmoid(pos - s)) for s, e in parts]
        inside = sum(jnp.sum(w * g, axis=1, keepdims=True) for _, w, g in parts)
        penalty = sum(jnp.sum(w * s * s, axis=1, keepdims=True) for s, w, _ in parts)
        slope = sum(jnp.sum(w * g * (1.0 - g), axis=1, keepdims=True) for _, w, g in parts)
        inv = 1.0 / inside
        weight = valid_ref[at, :]
        grads = [
            weight * w * (1.0 + BPREG * (s * s + 2.0 * s - penalty) - g * g * inv)
            for s, w, g in parts
        ]
        gt = grads[0] - jnp.where(diag, weight * slope * inv, 0.0)
        gt_low = gt.astype(BF16)
        into_ref[at, :] = dot(gt_low, targets)
        for j in range(n_loc):
            gn_refs[j][at, :] = grads[j + 1].astype(BF16)
        tgg_s[at, :] = dot(gt_low, second, 0, 0).astype(BF16)
    total = into_ref[...]
    for j in range(n_loc):
        total += dot(gn_refs[j][...], neg_buf[j])
    into_ref[...] = total
    send_ref[...] = dot(pick, tgg_s[...], 0, 0).astype(BF16)


def back_steps(steps, batch, hidden, chunk, l, keep_ref, weights, into_ref, res, dq_s, emit):
    loader, res_s = res
    n_loc = dq_s.shape[0]
    dq_s[...] = jnp.zeros(dq_s.shape, F32)
    wide = into_ref.shape[1]
    lane = iota((batch, wide), 1)
    carry = jnp.zeros((batch, wide), F32)
    for t in reversed(range(steps)):
        at = pl.ds(t * batch, batch)
        g = jnp.where(lane < hidden, into_ref[at, :] + carry, 0.0)
        loader.ready(t)
        z, r, n, qn, p = (res_s[k, at, :] for k in range(5))
        dc = g * (1.0 - z) * (1.0 - n * n)
        da_z = (g * (p - n) * z * (1.0 - z))[:, :hidden]
        da_r = (dc * qn * r * (1.0 - r))[:, :hidden]
        da_n = dc[:, :hidden]
        dq_n = (dc * r)[:, :hidden]
        da = jnp.concatenate([da_z, da_r, da_n], axis=1)
        dq = jnp.concatenate([da_z, da_r, dq_n], axis=1)
        emit(t, da, dq)
        for i in range(n_loc):
            dq_s[i, :, :chunk] = dq[:, i * chunk : (i + 1) * chunk]
        dp = g * z
        for j in range(n_loc):
            dp += dot(dq_s[l ^ j].astype(BF16), weights[j], 1, 1)
        carry = dp * keep_ref[at, :]
    return jnp.where(lane < hidden, carry, 0.0)


def back_second_kernel(dims, n_in, n_w, l_ref, keep_ref, into_ref, *refs):
    steps, batch, hidden, chunk, n_loc = dims
    res_ref, refs = refs[0], refs[1:]
    in_refs, w_refs, refs = refs[:n_in], refs[n_in : n_in + n_w], refs[n_in + n_w :]
    init_ref, first_ref, refs = refs[0], refs[1], refs[2:]
    ch_refs, refs = refs[: 2 * n_loc], refs[2 * n_loc :]
    dq_s, da_all, dq_all, in_buf, in_sem, w_buf, w_sem, res_s, res_sem = refs
    l = l_ref[0]
    loader = Loader(step_copies(res_ref, res_s, res_sem, steps, batch, False))
    weights = Weights(w_refs, w_buf, w_sem, l_ref[1] & 1)
    inputs = Weights(in_refs, in_buf, in_sem, l_ref[1] & 1)
    da_all[...] = jnp.zeros(da_all.shape, F32)
    dq_all[...] = jnp.zeros(dq_all.shape, F32)

    def emit(t, da, dq):
        for i in range(n_loc):
            da_all[i, pl.ds(t * batch, batch), :chunk] = da[:, i * chunk : (i + 1) * chunk]
            dq_all[i, pl.ds(t * batch, batch), :chunk] = dq[:, i * chunk : (i + 1) * chunk]

    init_ref[...] = back_steps(
        steps, batch, hidden, chunk, l, keep_ref, weights, into_ref, (loader, res_s), dq_s, emit
    )
    rows = steps * batch
    total = None
    for j in range(n_loc):
        da_low = da_all[l ^ j].astype(BF16)
        ch_refs[j][...] = da_low
        ch_refs[n_loc + j][...] = dq_all[l ^ j].astype(BF16)
        part = dot(da_low, inputs[j], 1, 1)
        total = part if total is None else total + part
    first_ref[...] = total


def back_first_kernel(dims, n_w, l_ref, keep_ref, into_ref, *refs):
    steps, batch, hidden, chunk, n_loc = dims
    res_ref, refs = refs[0], refs[1:]
    w_refs, refs = refs[:n_w], refs[n_w:]
    init_ref, da_all, refs = refs[0], refs[1], refs[2:]
    ch_refs, refs = refs[:n_loc], refs[n_loc:]
    dq_s, dq_all, bias_s, w_buf, w_sem, res_s, res_sem = refs
    l = l_ref[0]
    loader = Loader(step_copies(res_ref, res_s, res_sem, steps, batch, False))
    weights = Weights(w_refs, w_buf, w_sem)
    dq_all[...] = jnp.zeros(dq_all.shape, F32)
    bias_s[...] = jnp.zeros(bias_s.shape, F32)

    def emit(t, da, dq):
        da_all[pl.ds(t * batch, batch), :] = da.astype(BF16)
        for i in range(n_loc):
            dq_all[i, pl.ds(t * batch, batch), :chunk] = dq[:, i * chunk : (i + 1) * chunk]

    init_ref[...] = back_steps(
        steps, batch, hidden, chunk, l, keep_ref, weights, into_ref, (loader, res_s), dq_s, emit
    )
    rows = steps * batch
    bias = jnp.sum(da_all[...].astype(F32), axis=0, keepdims=True)
    for i in range(n_loc):
        bias_s[i, 0:1, :chunk] = bias[:, i * chunk : (i + 1) * chunk]
    for j in range(n_loc):
        ch_refs[j][pl.ds(0, rows), :] = dq_all[l ^ j].astype(BF16)
        ch_refs[j][pl.ds(rows, 16), :] = bias_s[l ^ j].astype(BF16)


def return_kernel(slot_ref, land_ref, da_ref, init_ref, init2_ref, send_ref, back_ref):
    rows, cols = da_ref.shape
    wide = init_ref.shape[1]
    pick = low(iota((rows, send_ref.shape[0]), 1) == slot_ref[...])
    sent = dot(pick, da_ref[...], 0, 0).astype(BF16)
    send_ref[:, :cols] = sent
    if send_ref.shape[1] > cols:
        rest = send_ref.shape[1] - cols
        send_ref[:, cols:] = jnp.zeros((send_ref.shape[0], rest), BF16)
    land = low(iota((land_ref.shape[0], init_ref.shape[0]), 1) == land_ref[...])
    back_ref[:, :wide] = dot(land, init_ref[...].astype(BF16)).astype(BF16)
    back_ref[:, wide:] = dot(land, init2_ref[...].astype(BF16)).astype(BF16)


def scaled(ref, rows, hidden):
    left = ref[pl.ds(0, rows), :].astype(F32)
    return (left * left[:, hidden + 1 : hidden + 2]).astype(BF16)


def dense_kernel(dims, l_ref, *refs):
    steps, batch, hidden, skip, bias_row, n_loc = dims
    rows = steps * batch
    left_refs, ch_refs = refs[:n_loc], refs[n_loc : 2 * n_loc]
    keep_ref, send_ref, all_s = refs[2 * n_loc :]
    half = keep_ref.shape[0]
    side = l_ref[0] & 1
    total, bias = None, None
    for j in range(n_loc):
        left = left_refs[j][pl.ds(batch, rows), :] if skip else scaled(left_refs[j], rows, hidden)
        part = dot(left, ch_refs[j][pl.ds(0, rows), :], 0, 0)
        total = part if total is None else total + part
        if bias_row is not None:
            extra = ch_refs[j][pl.ds(rows, 16), :].astype(F32)
            bias = extra if bias is None else bias + extra
    all_s[...] = total.astype(BF16)
    if bias_row is not None:
        all_s[pl.ds(bias_row, 16), :] = bias.astype(BF16)
    keep_ref[...] = all_s[pl.ds(pl.multiple_of(side * half, half), half), :]
    send_ref[...] = all_s[pl.ds(pl.multiple_of((1 - side) * half, half), half), :]


def neg_kernel(n_loc, owners, *refs):
    gn_refs, b_refs, out_ref = refs[:n_loc], refs[n_loc : 2 * n_loc], refs[2 * n_loc]
    rows = gn_refs[0].shape[0]
    batch = b_refs[0].shape[0] - rows
    total = None
    for j in range(n_loc):
        part = dot(gn_refs[j][...], b_refs[j][pl.ds(batch, rows), :], 0, 0)
        total = part if total is None else total + part
    own = out_ref.shape[0] // owners
    places = [(g >> 1) + (g & 1) * (owners // 2) for g in range(owners)]
    blocks = [total[p * own : (p + 1) * own, :] for p in places]
    out_ref[...] = jnp.concatenate(blocks, axis=0).astype(BF16)


def on_device(
    carried,
    session_plan,
    item_ids,
    target_ids,
    reset_mask,
    valid_counts,
    negative_ids,
    input_table,
    output_table,
    output_bias,
    hidden_one,
    input_two,
    hidden_two,
    gate_biases,
):
    hidden = carried.shape[2]
    wide = -(-(hidden + 2) // LANES) * LANES
    bias_row = wide - 16
    steps, batch = item_ids.shape
    events = steps * batch
    owners = lax.axis_size("grp")
    n_loc = lax.axis_size("loc")
    grp = lax.axis_index("grp")
    loc = lax.axis_index("loc")
    rows = input_table.shape[0]
    base = grp * rows
    gates = input_table.shape[1]
    chunk = gates // n_loc
    cap = events // owners + events // (2 * owners)
    ccap = 4 * batch // owners
    slots, cslots = owners * cap, owners * ccap
    neg_own = negative_ids.shape[0] // owners // n_loc
    neg_part = owners * neg_own
    l_arr = jnp.stack([loc, grp]).astype(I32)

    cpad = -(-chunk // LANES) * LANES
    gpad = -(-gates // LANES) * LANES
    w_shape = shape((wide, cpad), BF16)

    g_arr = grp.astype(I32).reshape(1)
    bits = owners.bit_length() - 1

    def padded(w, at, first):
        ins = [l_arr, w] if at is None else [l_arr, w, gate_biases]
        outs = [w_shape, shape((first, cpad), BF16)]
        if 2 * first < wide:
            outs.append(shape((wide - first, cpad), BF16))
        return kernel_call(functools.partial(pad_kernel, at, len(ins)), outs, ins, 1)

    def near(x):
        return swap(x, "loc", 1)

    def across(x):
        return swap(x, "loc", 2)

    def join(bit, kept, got, index=g_arr):
        return kernel_call(
            functools.partial(join_kernel, bit),
            [shape((2 * kept.shape[0],) + kept.shape[1:], BF16)],
            [index, kept, got], 1,
        )[0]

    p_one, *one_pieces = padded(hidden_one, (0, bias_row), wide // 8)
    y_one = [across(one_pieces[0])]
    y_one.append(across(after(one_pieces[1], y_one[0])))

    slot_in, slot_tg, slot_pl, packed = kernel_call(
        functools.partial(start_kernel, (owners, rows, cap, batch, ccap)),
        [
            shape((events, 1), I32),
            shape((events, 1), I32),
            shape((batch, 1), I32),
            shape((cslots, 2 * wide), BF16),
        ],
        [
            after(item_ids, p_one).reshape(events, 1),
            target_ids.reshape(events, 1),
            session_plan.reshape(batch, 1),
            carried,
        ],
        0, (), 3,
    )

    def to_owners(x):
        got = lax.all_to_all(
            x.reshape((owners, x.shape[0] // owners) + x.shape[1:]),
            "grp", split_axis=0, concat_axis=0, tiled=True,
        )
        return got.reshape(x.shape)

    got_c = to_owners(after(packed, y_one[0]))

    bias_col = output_bias[:, None]
    mine = lax.dynamic_slice(
        negative_ids.reshape(owners, n_loc, neg_own), (grp, loc, 0), (1, 1, neg_own)
    ).reshape(neg_own) - base
    negs_own = kernel_call(
        gather_neg_kernel,
        [shape((neg_own, wide), BF16)],
        [after(mine, p_one).reshape(neg_own, 1), output_table, bias_col],
    )[0]
    negs_half = negs_own
    for bit in range(1, bits):
        negs_half = join(bit, negs_half, swap(negs_half, "grp", 1 << bit))
    negs = join(0, negs_half, swap(negs_half, "grp", 1))

    place = np.arange(slots)
    turns = -(-cap // ccap)
    place_row = jnp.asarray((place // cap * ccap + place % cap % ccap)[:, None], I32)
    place_turn = jnp.asarray((place % cap // ccap)[:, None], I32)
    base_arr = base.astype(I32).reshape(1)
    ids_shape = shape((slots, 1), I32)
    reply_in, in_ids, land = kernel_call(
        functools.partial(gather_in_kernel, (hidden, turns)),
        [shape((slots, gpad), BF16), ids_shape, shape((cslots, 1), I32)],
        [base_arr, got_c, place_row, place_turn, input_table],
        1, (), 4,
    )
    p_in, h_in = padded(input_two, (1, hidden), wide // 2)
    p_two, h_two = padded(hidden_two, None, wide // 2)
    y_in = across(after(h_in, y_one[1]))
    got_rows = to_owners(after(reply_in, negs_half, y_one[1]))
    y_two = across(after(h_two, y_in))
    y_in = [y_in, swap(y_in, "grp", 1)]
    y_neg = across(after(negs, y_two))
    y_two = [y_two, swap(y_two, "grp", 1)]
    reply_tg, tg_ids = kernel_call(
        functools.partial(gather_tg_kernel, (hidden, turns)),
        [shape((slots, wide), BF16), ids_shape],
        [base_arr, got_c, place_row, place_turn, output_table, bias_col],
        1, (), 3,
    )
    tg_rows = to_owners(after(reply_tg, got_rows))

    def four(own, pieces):
        return [own, near(own), *pieces, *(near(p) for p in pieces)]

    w_one = four(p_one, y_one)

    keep = (1 - reset_mask).astype(F32).reshape(events, 1)
    valid = (jnp.arange(steps, dtype=I32)[:, None] < valid_counts[None, :]).astype(F32)
    valid = (valid / steps).reshape(events, 1)

    res_shape = shape((5, events, wide), F32)
    n_w = 2 + n_loc
    w_scratch = [pltpu.VMEM((n_loc, wide, cpad), BF16), pltpu.SemaphoreType.DMA((n_w,))]
    res_scratch = [pltpu.VMEM((5, events, wide), F32), pltpu.SemaphoreType.DMA((steps,))]
    state_shape = shape(((steps + 1) * batch, wide), BF16)
    q_scratch = pltpu.VMEM((n_loc, batch, chunk), F32)
    dq_scratch = pltpu.VMEM((n_loc, batch, cpad), F32)
    x_scratch = pltpu.VMEM((n_loc, events, chunk), F32)
    all_scratch = pltpu.VMEM((n_loc, events, cpad), F32)

    state_a, res_one = kernel_call(
        functools.partial(first_kernel, (steps, batch, hidden, bias_row, n_loc), n_w),
        [state_shape, res_shape],
        [l_arr, keep, slot_in, land, got_c, after(got_rows, reply_tg, negs, y_two[0], y_in[1])] + w_one,
        1,
        w_scratch
        + res_scratch
        + [q_scratch, pltpu.VMEM((n_loc, 16, chunk), F32), pltpu.VMEM((events, gpad), F32)],
        12, n_w, 1,
    )
    w_in = four(p_in, [after(y, state_a) for y in y_in])
    w_two = four(p_two, [after(y, state_a) for y in y_two])
    state_b, res_two = kernel_call(
        functools.partial(second_kernel, (steps, batch, hidden, n_loc), n_w, n_w),
        [state_shape, res_shape],
        [l_arr, keep, land, got_c, after(state_a, y_neg)] + w_in + w_two,
        1,
        w_scratch + w_scratch + res_scratch + [q_scratch, x_scratch],
        15, 2 * n_w, 1,
    )
    y_b = across(after(state_b, y_neg))

    y_neg = after(y_neg, state_b)
    negs = [negs, near(negs), y_neg, near(y_neg)]
    *g_neg, into_second, send_tg = kernel_call(
        functools.partial(score_kernel, (steps, batch, n_loc)),
        [shape((events, neg_part), BF16)] * n_loc
        + [shape((events, wide), F32), shape((slots, wide), BF16)],
        [valid, slot_tg, state_b, tg_rows] + negs,
        0,
        [
            pltpu.VMEM((n_loc, events, neg_part), F32),
            pltpu.VMEM((events, wide), BF16),
            pltpu.VMEM((events, wide), BF16),
            pltpu.VMEM((n_loc, neg_part, wide), BF16),
            pltpu.SemaphoreType.DMA((n_loc,)),
        ],
        12, n_loc,
    )
    init_two, into_first, *ch_two = kernel_call(
        functools.partial(back_second_kernel, (steps, batch, hidden, chunk, n_loc), n_w, n_w),
        [shape((batch, wide), F32), shape((events, wide), F32)]
        + [shape((events, cpad), BF16)] * (2 * n_loc),
        [l_arr, keep, after(into_second, y_b), res_two] + w_in + w_two,
        1,
        [dq_scratch, all_scratch, all_scratch] + w_scratch + w_scratch + res_scratch,
        17, 2 * n_w + 1,
    )
    def send_after(chunks, *deps):
        return send_xor([after(c, *deps) for c in chunks], "loc")

    ch_in, ch_two = send_xor(ch_two[:n_loc], "loc"), send_xor(ch_two[n_loc:], "loc")
    y_a = across(after(state_a, into_second))
    got_tg_g = to_owners(send_tg)
    init_one, da_one, *ch_one = kernel_call(
        functools.partial(back_first_kernel, (steps, batch, hidden, chunk, n_loc), n_w),
        [shape((batch, wide), F32), shape((events, gates), BF16)]
        + [shape((events + 16, cpad), BF16)] * n_loc,
        [l_arr, keep, after(into_first, y_a), res_one] + w_one,
        1,
        [dq_scratch, all_scratch, pltpu.VMEM((n_loc, 16, cpad), F32)] + w_scratch + res_scratch,
        13, n_w + 1,
    )
    send_in, back_c = kernel_call(
        return_kernel,
        [shape((slots, gpad), BF16), shape((cslots, 2 * wide), BF16)],
        [slot_in, land, after(da_one, *ch_in[2:]), init_one, init_two],
        0, (), 3,
    )
    got_in_g = to_owners(after(send_in, got_tg_g))
    ch_one = send_xor(ch_one, "loc")
    g_neg = send_after(g_neg, *ch_one[2:])

    y_a, y_b = after(y_a, send_in), after(y_b, send_in)
    states_a = [state_a, near(state_a), y_a, near(y_a)]
    states_b = [state_b, near(state_b), y_b, near(y_b)]

    neg_grad = kernel_call(
        functools.partial(neg_kernel, n_loc, owners),
        [shape((neg_part, wide), BF16)],
        g_neg + states_b,
        0, (), 2,
    )[0]

    def all_sums(makers, waits):
        def one(make):
            kept, sent = make()
            rest = kept.shape[0]
            for bit in range(bits):
                got = yield sent, 1 << bit
                if bit < bits - 2:
                    rest //= 2
                    kept, sent = kernel_call(
                        functools.partial(split_kernel, bit + 1),
                        [shape((rest, cpad), BF16)] * 2,
                        [g_arr, kept, got],
                        1,
                    )
                else:
                    kept = kernel_call(add_kernel, [shape((rest, cpad), BF16)], [kept, got])[0]
                    sent = kept
            for bit in reversed(range(1, bits - 1)):
                kept = join(bit, kept, (yield kept, 1 << bit))
            got = yield kept, 1
            return kept, got

        chains = [one(make) for make in makers]
        results, asks, before, step = [None] * len(chains), {}, (), 0
        while None in results:
            if step < len(chains):
                asks[step] = next(chains[step])
            wait = tuple(before) + tuple(waits.get(step, lambda: ())())
            answers = {
                k: swap(after(ask[0], *wait) if wait else ask[0], "grp", ask[1])
                for k, ask in asks.items()
            }
            asks, before = {}, list(answers.values())
            for k, answer in answers.items():
                try:
                    asks[k] = chains[k].send(answer)
                except StopIteration as done:
                    results[k] = done.value
            step += 1
        return results

    half_shape = shape((wide // 2, cpad), BF16)

    def product(lefts, chunks, skip, bias_at):
        return kernel_call(
            functools.partial(dense_kernel, (steps, batch, hidden, skip, bias_at, n_loc)),
            [half_shape] * 2,
            [g_arr] + lefts + chunks,
            1, [pltpu.VMEM((wide, cpad), BF16)], 5,
        )

    def finish(parts, bias_row):
        return kernel_call(
            functools.partial(final_kernel, hidden, bias_row),
            [shape((hidden, chunk), F32), shape((1, chunk), F32)],
            [g_arr, *parts],
            1, (), 2,
        )

    sums = {}

    def made(name, *args):
        def make():
            sums[name] = product(*args)
            return sums[name]

        return make

    def start_back():
        sums["back"] = to_owners(after(back_c, got_in_g, sums["one"][0]))
        return ()

    def bring_back():
        return (sums["back"],)

    in_parts, two_parts, one_parts = all_sums(
        [
            made("in", states_a, ch_in, True, None),
            made("two", states_b, ch_two, False, None),
            made("one", states_a, ch_one, False, bias_row),
        ],
        {1: lambda: tuple(ch_one[2:]), 2: start_back, 3: lambda: (got_in_g,), 5: bring_back},
    )
    got_back = sums["back"]
    got_neg_g = to_owners(after(neg_grad, got_back))
    grad_in, bias_in = finish(in_parts, hidden)
    grad_two, _ = finish(two_parts, hidden)
    grad_one, bias_one = finish(one_parts, bias_row)

    own = rows // n_loc
    own_pad = -(-own // 16) * 16

    def table_sum(ids, grads, cols, *wait):
        across_cols = grads[0].shape[1]
        full = shape((own_pad, across_cols), F32)
        sent = shape((own_pad, across_cols), BF16)
        mine_p, far_p, near_p = kernel_call(
            functools.partial(table_kernel, own, len(ids)),
            [full, full, shape((2, own_pad, across_cols), BF16)],
            [l_arr] + [i.reshape(1, i.size) for i in ids] + grads,
            1, (), 4,
        )
        total, far_s = kernel_call(
            table_add_kernel, [full, sent], [after(mine_p, *wait), far_p, near(near_p)]
        )
        return kernel_call(table_out_kernel, [shape((own, cols), F32)], [total, across(far_s)])[0]

    table_in = table_sum([in_ids], [got_in_g], gates, got_back)
    neg_ids = jnp.broadcast_to(mine[None, :], (owners, neg_own)).reshape(neg_part)
    table_out = table_sum([tg_ids, neg_ids], [got_tg_g, got_neg_g], wide)
    grad_carried = kernel_call(
        carry_kernel, [shape((2, batch, hidden), F32)], [slot_pl, got_back]
    )[0]
    return (
        table_in,
        table_out[:, :hidden],
        table_out[:, hidden],
        grad_one,
        grad_in,
        grad_two,
        jnp.concatenate([bias_one, bias_in], axis=0),
        grad_carried,
    )


def solution(mesh):
    in_specs = (
        P(None, ("grp", "loc"), None),
        P(("grp", "loc")),
        P(None, ("grp", "loc")),
        P(None, ("grp", "loc")),
        P(None, ("grp", "loc")),
        P(("grp", "loc")),
        P(),
        P("grp", None),
        P("grp", None),
        P("grp"),
        P(None, "loc"),
        P(None, "loc"),
        P(None, "loc"),
        P(None, "loc"),
    )
    out_specs = (
        P(("grp", "loc"), None),
        P(("grp", "loc"), None),
        P(("grp", "loc")),
        P(None, "loc"),
        P(None, "loc"),
        P(None, "loc"),
        P(None, "loc"),
        P(None, ("grp", "loc"), None),
    )
    return jax.shard_map(
        on_device, mesh=mesh, in_specs=in_specs, out_specs=out_specs, check_vma=False
    )
```

time: 531 us -> 478 us (0.900)
  waiting for transfers between devices: 223 us -> 189 us
  starting transfers between devices: 105 us -> 89.7 us
  Pallas kernels: 145 us -> 136 us
  local copies, waits for them, and re-layouts: 47.6 us -> 54.2 us
    ppermute x51 -> x58, waiting for transfers between devices: 223 us -> 162 us  [swap(): return lax.ppermute(x, axis, [(i, i ^ bit) for i in range(n)])]
    all_to_all x9 -> x7, waiting for transfers between devices: 0.02 us -> 26.8 us  [to_owners(): lax.all_to_all(x.reshape((owners, x.shape[0] // owners) + x.shape[1:]), '...]
    all_to_all x9 -> x7, starting transfers between devices: 54.6 us -> 35.6 us  [to_owners(): lax.all_to_all(x.reshape((owners, x.shape[0] // owners) + x.shape[1:]), '...]
    pallas_call x44 -> x42, Pallas kernels: 145 us -> 136 us  [kernel_call(): pl.pallas_call(body, out_shape=outs, in_specs=[pl.BlockSpec(memory_space=...]
    unnamed x156 -> x180, local copies, waits for them, and re-layouts: 44.5 us -> 51.5 us
    ppermute x51 -> x58, starting transfers between devices: 50.9 us -> 54.1 us  [swap(): return lax.ppermute(x, axis, [(i, i ^ bit) for i in range(n)])]
  transfers between devices with their start and end apart: 60 -> 65, of which waited for: 25 -> 24; matrix products, arithmetic and copies ran while one was open for 1% -> 0% of each run, Pallas kernels for 27% -> 29%
where the time goes in v3:
time: 478 us; the launch traced here: 472 us
  waiting for transfers between devices  189 us (40%)
  Pallas kernels  136 us (28%)
  starting transfers between devices  89.7 us (19%)
  local copies, waits for them, and re-layouts  54.2 us (11%)
    ppermute x58, waiting for transfers between devices, swap(): return lax.ppermute(x, axis, [(i, i ^ bit) for i in range(n)])  162 us
    pallas_call x42, Pallas kernels, kernel_call(): pl.pallas_call(body, out_shape=outs, in_specs=[pl.BlockSpec(memory_space=...  136 us
    ppermute x58, starting transfers between devices, swap(): return lax.ppermute(x, axis, [(i, i ^ bit) for i in range(n)])  54.1 us
    unnamed x180, local copies, waits for them, and re-layouts  51.5 us
    all_to_all x7, starting transfers between devices, to_owners(): lax.all_to_all(x.reshape((owners, x.shape[0] // owners) + x.shape[1:]), '...  35.6 us
    all_to_all x7, waiting for transfers between devices, to_owners(): lax.all_to_all(x.reshape((owners, x.shape[0] // owners) + x.shape[1:]), '...  26.8 us
  transfers between devices with their start and end apart: 65, of which 24 were waited for; matrix products, arithmetic and copies ran while one was open for 0% of the time, Pallas kernels for 29%

profile of v3, /device:TPU:0, one launch (start us, length us, event | category | flops | bytes accessed | tf_op | source)
XLA Modules:
  0.0 471.9 jit_solution(17374501585337993679)
XLA Ops:
  12.6 6.0 %all-to-all-start = ((bf16[8,32,2048]{2,1,0:T(8,128)(2,1)}), bf16[8,32,2048]{2,1,0:T(8,128)(2,1)S(1)}, u32[]{:S(2)}, u32[]{:S(2)}) async-start(bf16[8,32,2048]{2,1,0:T(8,128)(2,1)} %bitcast.4), calls=%async_computation | async-start | bytes 2097152 | tf_op jit(solution)/shard_map/all_to_all | solution.py:688
  24.3 13.4 %collective-permute-done.1.b_ref = bf16[64,1024]{1,0:T(8,128)(2,1)S(1)} collective-permute-done((bf16[64,1024]{1,0:T(8,128)(2,1)S(1)}, bf16[64,1024]{1,0:T(8,128)(2,1)S(1)}, u32[]{:S(2)}, u32[]{:S(2)}) %collective-permute-start.1) | collective-permute-done | bytes 131104 | tf_op jit(solution)/shard_map/ppermute | solution.py:21
  37.7 5.2 %collective-permute-start.2 = (bf16[128,1024]{1,0:T(8,128)(2,1)S(1)}, bf16[128,1024]{1,0:T(8,128)(2,1)S(1)}, u32[]{:S(2)}, u32[]{:S(2)}) collective-permute-start(bf16[128,1024]{1,0:T(8,128)(2,1)S(1)} %shard_map.219.a_ref), channel_id=1, source_target_pairs={{0,16},{4,20},{8,24},{12,28},{16,0},{20,4},{24,8},{28,12},{1,17},{... | collective-permute-start | bytes 786440 | tf_op jit(solution)/shard_map/ppermute | solution.py:21
  42.9 12.1 %collective-permute-done.2.b_ref = bf16[128,1024]{1,0:T(8,128)(2,1)S(1)} collective-permute-done((bf16[128,1024]{1,0:T(8,128)(2,1)S(1)}, bf16[128,1024]{1,0:T(8,128)(2,1)S(1)}, u32[]{:S(2)}, u32[]{:S(2)}) %collective-permute-start.2) | collective-permute-done | bytes 262176 | tf_op jit(solution)/shard_map/ppermute | solution.py:21
  56.9 5.9 %shard_map.217 = (bf16[384,3072]{1,0:T(8,128)(2,1)}, s32[384,1]{1,0:T(8,128)S(1)}, s32[256,1]{1,0:T(8,128)S(1)}) custom-call(s32[1]{0:T(128)} %bitcast.2.base_ref, bf16[256,2048]{1,0:T(8,128)(2,1)S(1)} %bitcast.23, s32[384,1]{1,0:T(8,128)S(1)} %copy-done.48, s32[384,1]{1,0:T(8,128)S(1)} %copy-done.50, bf16[588,3000]{1,0:T(8,128)(2,1)} %table_ref.3), custom_call_target="tpu_custom_call" | custom-call | flops 4000000000 | bytes 6941508 | tf_op jit(solution)/shard_map/pallas_call | solution.py:42
  63.5 4.8 %all-to-all-start.1 = ((bf16[8,48,3072]{2,1,0:T(8,128)(2,1)}), bf16[8,48,3072]{2,1,0:T(8,128)(2,1)}, u32[]{:S(2)}, u32[]{:S(2)}) async-start(bf16[8,48,3072]{2,1,0:T(8,128)(2,1)} %bitcast.8), calls=%async_computation.1 | async-start | bytes 4718592 | tf_op jit(solution)/shard_map/all_to_all | solution.py:688
  77.6 12.2 %collective-permute-done.5.refs_2_.refs_3_ = bf16[512,768]{1,0:T(8,128)(2,1)} collective-permute-done((bf16[512,768]{1,0:T(8,128)(2,1)S(1)}, bf16[512,768]{1,0:T(8,128)(2,1)}, u32[]{:S(2)}, u32[]{:S(2)}) %collective-permute-start.5) | collective-permute-done | bytes 786464 | tf_op jit(solution)/shard_map/ppermute | solution.py:21
  93.1 13.8 %collective-permute-done.4.b_ref = bf16[256,1024]{1,0:T(8,128)(2,1)S(1)} collective-permute-done((bf16[256,1024]{1,0:T(8,128)(2,1)S(1)}, bf16[256,1024]{1,0:T(8,128)(2,1)S(1)}, u32[]{:S(2)}, u32[]{:S(2)}) %collective-permute-start.4) | collective-permute-done | bytes 524320 | tf_op jit(solution)/shard_map/ppermute | solution.py:21
  115.7 7.5 %collective-permute-done.7.refs_3_.refs_4_ = bf16[512,768]{1,0:T(8,128)(2,1)} collective-permute-done((bf16[512,768]{1,0:T(8,128)(2,1)}, bf16[512,768]{1,0:T(8,128)(2,1)}, u32[]{:S(2)}, u32[]{:S(2)}) %collective-permute-start.7) | collective-permute-done | bytes 786464 | tf_op jit(solution)/shard_map/ppermute | solution.py:21
  127.0 14.4 %shard_map.225 = (bf16[320,1024]{1,0:T(8,128)(2,1)}, f32[5,256,1024]{2,1,0:T(8,128)}) custom-call(s32[2]{0:T(128)S(1)} %pad_add_fusion.l_ref, f32[256,1]{1,0:T(8,128)S(1)} %reshape.149.keep_ref, s32[256,1]{1,0:T(8,128)S(1)} %copy-done.74, s32[256,1]{1,0:T(8,128)S(1)} %copy-done.77, bf16[256,2048]{1,0:T(8,128)(2,1)S(1)} %bitcast.25, ...), custom_call_target="tpu_custom_call" | custom-call | flops 12000000000 | bytes 15600648 | tf_op jit(solution)/shard_map/pallas_call | solution.py:42
  145.2 3.9 collective-permute-done.11.refs_2_
  149.1 5.0 %all-to-all-start.2 = ((bf16[8,48,1024]{2,1,0:T(8,128)(2,1)}), bf16[8,48,1024]{2,1,0:T(8,128)(2,1)S(1)}, u32[]{:S(2)}, u32[]{:S(2)}) async-start(bf16[8,48,1024]{2,1,0:T(8,128)(2,1)} %bitcast.10), calls=%async_computation.2 | async-start | bytes 1572864 | tf_op jit(solution)/shard_map/all_to_all | solution.py:688
  156.4 15.6 %shard_map.226 = (bf16[320,1024]{1,0:T(8,128)(2,1)S(1)}, f32[5,256,1024]{2,1,0:T(8,128)}) custom-call(s32[2]{0:T(128)S(1)} %pad_add_fusion.l_ref, f32[256,1]{1,0:T(8,128)S(1)} %reshape.149.keep_ref, s32[256,1]{1,0:T(8,128)S(1)} %copy-done.77, bf16[256,2048]{1,0:T(8,128)(2,1)} %bitcast.26, bf16[320,1024]{1,0:T(8,128)(2,1)} %get-tuple-element.161.below_ref.refs_0_, ...), custom_call_target="tpu_custom_call" | custom-call | flops 15000000512 | bytes 20187144 | tf_op jit(solution)/shard_map/pallas_call | solution.py:42
  177.0 10.1 %shard_map.227 = (bf16[256,512]{1,0:T(8,128)(2,1)S(1)}, bf16[256,512]{1,0:T(8,128)(2,1)}, bf16[256,512]{1,0:T(8,128)(2,1)S(1)}, bf16[256,512]{1,0:T(8,128)(2,1)S...) custom-call(f32[256,1]{1,0:T(8,128)S(1)} %div.11.valid_ref, s32[256,1]{1,0:T(8,128)S(1)} %copy-done.80, ...), custom_call_target="tpu_custom_call" | custom-call | flops 12000000000 | bytes 8521728 | tf_op jit(solution)/shard_map/pallas_call | solution.py:42
  192.1 17.7 %shard_map.228 = (f32[64,1024]{1,0:T(8,128)S(1)}, f32[256,1024]{1,0:T(8,128)}, bf16[256,768]{1,0:T(8,128)(2,1)S(1)}, bf16[256,768]{1,0:T(8,128)(2,1)S(1)}, bf16[...) custom-call(s32[2]{0:T(128)S(1)} %pad_add_fusion.l_ref, ...), custom_call_target="tpu_custom_call" | custom-call | flops 16999999488 | bytes 23331848 | tf_op jit(solution)/shard_map/pallas_call | solution.py:42
  213.7 6.2 %all-to-all-start.3 = ((bf16[8,48,1024]{2,1,0:T(8,128)(2,1)}), bf16[8,48,1024]{2,1,0:T(8,128)(2,1)S(1)}, u32[]{:S(2)}, u32[]{:S(2)}) async-start(bf16[8,48,1024]{2,1,0:T(8,128)(2,1)} %bitcast.12), calls=%async_computation.3 | async-start | bytes 1572864 | tf_op jit(solution)/shard_map/all_to_all | solution.py:688
  222.3 13.0 %shard_map.229 = (f32[64,1024]{1,0:T(8,128)S(1)}, bf16[256,3000]{1,0:T(8,128)(2,1)}, bf16[272,768]{1,0:T(8,128)(2,1)S(1)}, bf16[272,768]{1,0:T(8,128)(2,1)S(1)},...) custom-call(s32[2]{0:T(128)S(1)} %pad_add_fusion.l_ref, f32[256,1]{1,0:T(8,128)S(1)} %reshape.149.keep_ref, ...), custom_call_target="tpu_custom_call" | custom-call | flops 12999999488 | bytes 16053256 | tf_op jit(solution)/shard_map/pallas_call | solution.py:42
  242.1 5.5 %all-to-all-start.4 = ((bf16[8,48,3072]{2,1,0:T(8,128)(2,1)}), bf16[8,48,3072]{2,1,0:T(8,128)(2,1)}, u32[]{:S(2)}, u32[]{:S(2)}) async-start(bf16[8,48,3072]{2,1,0:T(8,128)(2,1)} %bitcast.14), calls=%async_computation.4 | async-start | bytes 4718592 | tf_op jit(solution)/shard_map/all_to_all | solution.py:688
  262.4 7.4 %collective-permute-done.29.refs_7_ = bf16[272,768]{1,0:T(8,128)(2,1)S(1)} collective-permute-done((bf16[272,768]{1,0:T(8,128)(2,1)S(1)}, bf16[272,768]{1,0:T(8,128)(2,1)S(1)}, u32[]{:S(2)}, u32[]{:S(2)}) %collective-permute-start.29) | collective-permute-done | bytes 417824 | tf_op jit(solution)/shard_map/ppermute | solution.py:21
  276.1 25.9 %all-to-all-done.4 = bf16[8,48,3072]{2,1,0:T(8,128)(2,1)} async-done(((bf16[8,48,3072]{2,1,0:T(8,128)(2,1)}), bf16[8,48,3072]{2,1,0:T(8,128)(2,1)}, u32[]{:S(2)}, u32[]{:S(2)}) %all-to-all-start.4) | async-done | bytes 2359328 | tf_op jit(solution)/shard_map/all_to_all | solution.py:688
  302.1 3.6 all-to-all-start.5
  308.9 4.8 %shard_map.241 = (bf16[512,768]{1,0:T(8,128)(2,1)S(1)}, bf16[512,768]{1,0:T(8,128)(2,1)}) custom-call(s32[1]{0:T(128)} %bitcast.1.l_ref, bf16[320,1024]{1,0:T(8,128)(2,1)S(1)} %copy-done.27, bf16[320,1024]{1,0:T(8,128)(2,1)S(1)} %copy-done.30, bf16[320,1024]{1,0:T(8,128)(2,1)} %collective-permute-done.21.refs_6_.refs_2_, ...), custom_call_target="tpu_custom_call" | custom-call | flops 5000000000 | bytes 5767172 | tf_op jit(solution)/shard_map/pallas_call | solution.py:42
  321.3 13.1 %collective-permute-done.41.b_ref = bf16[256,768]{1,0:T(8,128)(2,1)} collective-permute-done((bf16[256,768]{1,0:T(8,128)(2,1)S(1)}, bf16[256,768]{1,0:T(8,128)(2,1)}, u32[]{:S(2)}, u32[]{:S(2)}) %collective-permute-start.41) | collective-permute-done | bytes 393248 | tf_op jit(solution)/shard_map/ppermute | solution.py:21
  338.6 3.6 collective-permute-start.47
  346.2 5.2 %shard_map.231 = (f32[160,3072]{1,0:T(8,128)S(1)}, f32[160,3072]{1,0:T(8,128)S(1)}, bf16[2,160,3072]{2,1,0:T(8,128)(2,1)}) custom-call(s32[2]{0:T(128)S(1)} %pad_add_fusion.l_ref, s32[1,384]{1,0:T(1,128)S(1)} %reshape.130.refs_0_, bf16[384,3072]{1,0:T(8,128)(2,1)} %bitcast.15.refs_1_), custom_call_target="tpu_custom_call" | custom-call | flops 4000000000 | bytes 8259080 | tf_op jit(solution)/shard_map/pallas_call | solution.py:42
  353.9 3.7 shard_map.235
  357.6 4.6 all-to-all-start.6
  369.6 29.8 %collective-permute-done.50.b_ref = bf16[256,768]{1,0:T(8,128)(2,1)S(1)} collective-permute-done((bf16[256,768]{1,0:T(8,128)(2,1)S(1)}, bf16[256,768]{1,0:T(8,128)(2,1)S(1)}, u32[]{:S(2)}, u32[]{:S(2)}) %collective-permute-start.50) | collective-permute-done | bytes 393248 | tf_op jit(solution)/shard_map/ppermute | solution.py:21
  399.5 8.0 %collective-permute-done.49.b_ref = bf16[256,768]{1,0:T(8,128)(2,1)S(1)} collective-permute-done((bf16[256,768]{1,0:T(8,128)(2,1)S(1)}, bf16[256,768]{1,0:T(8,128)(2,1)S(1)}, u32[]{:S(2)}, u32[]{:S(2)}) %collective-permute-start.49) | collective-permute-done | bytes 393248 | tf_op jit(solution)/shard_map/ppermute | solution.py:21
  412.2 15.8 %collective-permute-done.54.b_ref = bf16[256,768]{1,0:T(8,128)(2,1)S(1)} collective-permute-done((bf16[256,768]{1,0:T(8,128)(2,1)S(1)}, bf16[256,768]{1,0:T(8,128)(2,1)S(1)}, u32[]{:S(2)}, u32[]{:S(2)}) %collective-permute-start.54) | collective-permute-done | bytes 393248 | tf_op jit(solution)/shard_map/ppermute | solution.py:21
  444.5 4.5 collective-permute-done.56.b_ref
  455.5 8.3 %collective-permute-done.31.got_ref = bf16[160,3072]{1,0:T(8,128)(2,1)} collective-permute-done((bf16[160,3072]{1,0:T(8,128)(2,1)}, bf16[160,3072]{1,0:T(8,128)(2,1)}, u32[]{:S(2)}, u32[]{:S(2)}) %collective-permute-start.31) | collective-permute-done | bytes 983072 | tf_op jit(solution)/shard_map/ppermute | solution.py:21
  (340 shorter events, 159.8 us)
Async XLA Ops:
  12.6 43.2 %all-to-all-start = ((bf16[8,32,2048]{2,1,0:T(8,128)(2,1)}), bf16[8,32,2048]{2,1,0:T(8,128)(2,1)S(1)}, u32[]{:S(2)}, u32[]{:S(2)}) async-start(bf16[8,32,2048]{2,1,0:T(8,128)(2,1)} %bitcast.4), calls=%async_computation | async-start | bytes 2097152 | tf_op jit(solution)/shard_map/all_to_all | solution.py:688
  18.6 44.9 %collective-permute-start.3 = (bf16[896,768]{1,0:T(8,128)(2,1)}, bf16[896,768]{1,0:T(8,128)(2,1)}, u32[]{:S(2)}, u32[]{:S(2)}) collective-permute-start(bf16[896,768]{1,0:T(8,128)(2,1)} %copy-done.10), channel_id=1, source_target_pairs={{0,2},{1,3},{2,0},{3,1},{4,6},{5,7},{6,4},{7,5},{8,10},{9,11},{10,... | collective-permute-start | bytes 4128776 | tf_op jit(solution)/shard_map/ppermute | solution.py:21
  63.5 59.7 %all-to-all-start.1 = ((bf16[8,48,3072]{2,1,0:T(8,128)(2,1)}), bf16[8,48,3072]{2,1,0:T(8,128)(2,1)}, u32[]{:S(2)}, u32[]{:S(2)}) async-start(bf16[8,48,3072]{2,1,0:T(8,128)(2,1)} %bitcast.8), calls=%async_computation.1 | async-start | bytes 4718592 | tf_op jit(solution)/shard_map/all_to_all | solution.py:688
  73.0 51.8 %collective-permute-start.8 = (bf16[1024,768]{1,0:T(8,128)(2,1)S(1)}, bf16[1024,768]{1,0:T(8,128)(2,1)}, u32[]{:S(2)}, u32[]{:S(2)}) collective-permute-start(bf16[1024,768]{1,0:T(8,128)(2,1)S(1)} %get-tuple-element.124.refs_0_.refs_1_), channel_id=1, source_target_pairs={{0,1},{1,0},{2,3},{3,2},{4,5},{5,4},{6,7},{7,6},{8,9},{9,8},{10,11... | collective-permute-start | bytes 4718600 | tf_op jit(solution)/shard_map/ppermute | solution.py:21
  73.0 52.1 %collective-permute-start.10 = (bf16[896,768]{1,0:T(8,128)(2,1)}, bf16[896,768]{1,0:T(8,128)(2,1)}, u32[]{:S(2)}, u32[]{:S(2)}) collective-permute-start(bf16[896,768]{1,0:T(8,128)(2,1)} %collective-permute-done.3.refs_3_.refs_4_), channel_id=1, source_target_pairs={{0,1},{1,0},{2,3},{3,2},{4,5},{5,4},{6,7},{7,6},{8,9},{9,8},{10,11... | collective-permute-start | bytes 4128776 | tf_op jit(solution)/shard_map/ppermute | solution.py:21
  73.5 33.3 %collective-permute-start.4 = (bf16[256,1024]{1,0:T(8,128)(2,1)S(1)}, bf16[256,1024]{1,0:T(8,128)(2,1)S(1)}, u32[]{:S(2)}, u32[]{:S(2)}) collective-permute-start(bf16[256,1024]{1,0:T(8,128)(2,1)S(1)} %copy-done.36), channel_id=1, source_target_pairs={{0,4},{4,0},{8,12},{12,8},{16,20},{20,16},{24,28},{28,24},{1,5},{5... | collective-permute-start | bytes 1572872 | tf_op jit(solution)/shard_map/ppermute | solution.py:21
  91.3 31.9 %collective-permute-start.7 = (bf16[512,768]{1,0:T(8,128)(2,1)}, bf16[512,768]{1,0:T(8,128)(2,1)}, u32[]{:S(2)}, u32[]{:S(2)}) collective-permute-start(bf16[512,768]{1,0:T(8,128)(2,1)} %collective-permute-done.5.refs_2_.refs_3_), channel_id=1, source_target_pairs={{0,4},{4,0},{8,12},{12,8},{16,20},{20,16},{24,28},{28,24},{1,5},{5... | collective-permute-start | bytes 2359304 | tf_op jit(solution)/shard_map/ppermute | solution.py:21
  107.6 37.1 %collective-permute-start.12 = (bf16[1024,768]{1,0:T(8,128)(2,1)}, bf16[1024,768]{1,0:T(8,128)(2,1)}, u32[]{:S(2)}, u32[]{:S(2)}) collective-permute-start(bf16[1024,768]{1,0:T(8,128)(2,1)} %get-tuple-element.147.refs_0_.refs_1_), channel_id=1, source_target_pairs={{0,1},{1,0},{2,3},{3,2},{4,5},{5,4},{6,7},{7,6},{8,9},{9,8},{10,11... | collective-permute-start | bytes 4718600 | tf_op jit(solution)/shard_map/ppermute | solution.py:21
  123.2 30.9 %collective-permute-start.15 = (bf16[1024,768]{1,0:T(8,128)(2,1)}, bf16[1024,768]{1,0:T(8,128)(2,1)}, u32[]{:S(2)}, u32[]{:S(2)}) collective-permute-start(bf16[1024,768]{1,0:T(8,128)(2,1)} %get-tuple-element.150.refs_6_.refs_7_), channel_id=1, source_target_pairs={{0,1},{1,0},{2,3},{3,2},{4,5},{5,4},{6,7},{7,6},{8,9},{9,8},{10,11... | collective-permute-start | bytes 4718600 | tf_op jit(solution)/shard_map/ppermute | solution.py:21
  123.2 25.9 %collective-permute-start.11 = (bf16[512,1024]{1,0:T(8,128)(2,1)}, bf16[512,1024]{1,0:T(8,128)(2,1)}, u32[]{:S(2)}, u32[]{:S(2)}) collective-permute-start(bf16[512,1024]{1,0:T(8,128)(2,1)} %copy-done.13), channel_id=1, source_target_pairs={{0,2},{1,3},{2,0},{3,1},{4,6},{5,7},{6,4},{7,5},{8,10},{9,11},{10,... | collective-permute-start | bytes 3145736 | tf_op jit(solution)/shard_map/ppermute | solution.py:21
  149.1 25.9 %all-to-all-start.2 = ((bf16[8,48,1024]{2,1,0:T(8,128)(2,1)}), bf16[8,48,1024]{2,1,0:T(8,128)(2,1)S(1)}, u32[]{:S(2)}, u32[]{:S(2)}) async-start(bf16[8,48,1024]{2,1,0:T(8,128)(2,1)} %bitcast.10), calls=%async_computation.2 | async-start | bytes 1572864 | tf_op jit(solution)/shard_map/all_to_all | solution.py:688
  190.6 29.4 %collective-permute-start.22 = (bf16[320,1024]{1,0:T(8,128)(2,1)}, bf16[320,1024]{1,0:T(8,128)(2,1)S(1)}, u32[]{:S(2)}, u32[]{:S(2)}) collective-permute-start(bf16[320,1024]{1,0:T(8,128)(2,1)} %get-tuple-element.161.below_ref.refs_0_), channel_id=1, source_target_pairs={{0,2},{1,3},{2,0},{3,1},{4,6},{5,7},{6,4},{7,5},{8,10},{9,11},{10,... | collective-permute-start | bytes 1966088 | tf_op jit(solution)/shard_map/ppermute | solution.py:21
  213.7 27.5 %all-to-all-start.3 = ((bf16[8,48,1024]{2,1,0:T(8,128)(2,1)}), bf16[8,48,1024]{2,1,0:T(8,128)(2,1)S(1)}, u32[]{:S(2)}, u32[]{:S(2)}) async-start(bf16[8,48,1024]{2,1,0:T(8,128)(2,1)} %bitcast.12), calls=%async_computation.3 | async-start | bytes 1572864 | tf_op jit(solution)/shard_map/all_to_all | solution.py:688
  242.1 60.0 %all-to-all-start.4 = ((bf16[8,48,3072]{2,1,0:T(8,128)(2,1)}), bf16[8,48,3072]{2,1,0:T(8,128)(2,1)}, u32[]{:S(2)}, u32[]{:S(2)}) async-start(bf16[8,48,3072]{2,1,0:T(8,128)(2,1)} %bitcast.14), calls=%async_computation.4 | async-start | bytes 4718592 | tf_op jit(solution)/shard_map/all_to_all | solution.py:688
  251.7 54.0 %collective-permute-start.36 = (bf16[320,1024]{1,0:T(8,128)(2,1)}, bf16[320,1024]{1,0:T(8,128)(2,1)}, u32[]{:S(2)}, u32[]{:S(2)}) collective-permute-start(bf16[320,1024]{1,0:T(8,128)(2,1)} %collective-permute-done.21.refs_6_.refs_2_), channel_id=1, source_target_pairs={{0,1},{1,0},{2,3},{3,2},{4,5},{5,4},{6,7},{7,6},{8,9},{9,8},{10,11... | collective-permute-start | bytes 1966088 | tf_op jit(solution)/shard_map/ppermute | solution.py:21
  259.5 46.3 %collective-permute-start.42 = (bf16[256,768]{1,0:T(8,128)(2,1)}, bf16[256,768]{1,0:T(8,128)(2,1)}, u32[]{:S(2)}, u32[]{:S(2)}) collective-permute-start(bf16[256,768]{1,0:T(8,128)(2,1)} %get-tuple-element.211), channel_id=1, source_target_pairs={{0,1},{1,0},{2,3},{3,2},{4,5},{5,4},{6,7},{7,6},{8,9},{9,8},{10,11... | collective-permute-start | bytes 1179656 | tf_op jit(solution)/shard_map/ppermute | solution.py:21
  259.6 46.1 %collective-permute-start.43 = (bf16[256,768]{1,0:T(8,128)(2,1)}, bf16[256,768]{1,0:T(8,128)(2,1)}, u32[]{:S(2)}, u32[]{:S(2)}) collective-permute-start(bf16[256,768]{1,0:T(8,128)(2,1)} %get-tuple-element.212), channel_id=1, source_target_pairs={{0,2},{1,3},{2,0},{3,1},{4,6},{5,7},{6,4},{7,5},{8,10},{9,11},{10,... | collective-permute-start | bytes 1179656 | tf_op jit(solution)/shard_map/ppermute | solution.py:21
  262.4 43.3 %collective-permute-start.44 = (bf16[256,768]{1,0:T(8,128)(2,1)}, bf16[256,768]{1,0:T(8,128)(2,1)S(1)}, u32[]{:S(2)}, u32[]{:S(2)}) collective-permute-start(bf16[256,768]{1,0:T(8,128)(2,1)} %get-tuple-element.213), channel_id=1, source_target_pairs={{0,3},{1,2},{2,1},{3,0},{4,7},{5,6},{6,5},{7,4},{8,11},{9,10},{10,... | collective-permute-start | bytes 1179656 | tf_op jit(solution)/shard_map/ppermute | solution.py:21
  269.8 43.9 %collective-permute-start.40 = (bf16[512,768]{1,0:T(8,128)(2,1)S(1)}, bf16[512,768]{1,0:T(8,128)(2,1)}, u32[]{:S(2)}, u32[]{:S(2)}) collective-permute-start(bf16[512,768]{1,0:T(8,128)(2,1)S(1)} %get-tuple-element.207), channel_id=1, source_target_pairs={{0,4},{4,0},{8,12},{12,8},{16,20},{20,16},{24,28},{28,24},{1,5},{5... | collective-permute-start | bytes 2359304 | tf_op jit(solution)/shard_map/ppermute | solution.py:21
  302.1 55.5 %all-to-all-start.5 = ((bf16[8,32,2048]{2,1,0:T(8,128)(2,1)}), bf16[8,32,2048]{2,1,0:T(8,128)(2,1)S(1)}, u32[]{:S(2)}, u32[]{:S(2)}) async-start(bf16[8,32,2048]{2,1,0:T(8,128)(2,1)} %bitcast.16), calls=%async_computation.5 | async-start | bytes 2097152 | tf_op jit(solution)/shard_map/all_to_all | solution.py:688
  313.7 24.0 %collective-permute-start.45 = (bf16[512,768]{1,0:T(8,128)(2,1)}, bf16[512,768]{1,0:T(8,128)(2,1)S(1)}, u32[]{:S(2)}, u32[]{:S(2)}) collective-permute-start(bf16[512,768]{1,0:T(8,128)(2,1)} %get-tuple-element.215), channel_id=1, source_target_pairs={{0,4},{4,0},{8,12},{12,8},{16,20},{20,16},{24,28},{28,24},{1,5},{5... | collective-permute-start | bytes 2359304 | tf_op jit(solution)/shard_map/ppermute | solution.py:21
  319.2 25.7 %collective-permute-start.32 = (bf16[256,512]{1,0:T(8,128)(2,1)}, bf16[256,512]{1,0:T(8,128)(2,1)}, u32[]{:S(2)}, u32[]{:S(2)}) collective-permute-start(bf16[256,512]{1,0:T(8,128)(2,1)} %get-tuple-element.191), channel_id=1, source_target_pairs={{0,1},{1,0},{2,3},{3,2},{4,5},{5,4},{6,7},{7,6},{8,9},{9,8},{10,11... | collective-permute-start | bytes 786440 | tf_op jit(solution)/shard_map/ppermute | solution.py:21
  319.4 34.5 %collective-permute-start.33 = (bf16[256,512]{1,0:T(8,128)(2,1)}, bf16[256,512]{1,0:T(8,128)(2,1)S(1)}, u32[]{:S(2)}, u32[]{:S(2)}) collective-permute-start(bf16[256,512]{1,0:T(8,128)(2,1)} %copy-done.43), channel_id=1, source_target_pairs={{0,2},{1,3},{2,0},{3,1},{4,6},{5,7},{6,4},{7,5},{8,10},{9,11},{10,... | collective-permute-start | bytes 786440 | tf_op jit(solution)/shard_map/ppermute | solution.py:21
  320.0 33.9 %collective-permute-start.34 = (bf16[256,512]{1,0:T(8,128)(2,1)}, bf16[256,512]{1,0:T(8,128)(2,1)S(1)}, u32[]{:S(2)}, u32[]{:S(2)}) collective-permute-start(bf16[256,512]{1,0:T(8,128)(2,1)} %copy-done.42), channel_id=1, source_target_pairs={{0,3},{1,2},{2,1},{3,0},{4,7},{5,6},{6,5},{7,4},{8,11},{9,10},{10,... | collective-permute-start | bytes 786440 | tf_op jit(solution)/shard_map/ppermute | solution.py:21
  338.5 25.9 %collective-permute-start.46 = (bf16[512,768]{1,0:T(8,128)(2,1)S(1)}, bf16[512,768]{1,0:T(8,128)(2,1)S(1)}, u32[]{:S(2)}, u32[]{:S(2)}) collective-permute-start(bf16[512,768]{1,0:T(8,128)(2,1)S(1)} %get-tuple-element.216), channel_id=1, source_target_pairs={{0,4},{4,0},{8,12},{12,8},{16,20},{20,16},{24,28},{28,24},{1,5},{5... | collective-permute-start | bytes 2359304 | tf_op jit(solution)/shard_map/ppermute | solution.py:21
  353.9 80.0 %collective-permute-start.30 = (bf16[2,160,3072]{2,1,0:T(8,128)(2,1)}, bf16[2,160,3072]{2,1,0:T(8,128)(2,1)}, u32[]{:S(2)}, u32[]{:S(2)}) collective-permute-start(bf16[2,160,3072]{2,1,0:T(8,128)(2,1)} %get-tuple-element.184), channel_id=1, source_target_pairs={{0,1},{1,0},{2,3},{3,2},{4,5},{5,4},{6,7},{7,6},{8,9},{9,8},{10,11... | collective-permute-start | bytes 5898248 | tf_op jit(solution)/shard_map/ppermute | solution.py:21
  357.6 81.7 %all-to-all-start.6 = ((bf16[8,64,1024]{2,1,0:T(8,128)(2,1)}), bf16[8,64,1024]{2,1,0:T(8,128)(2,1)}, u32[]{:S(2)}, u32[]{:S(2)}) async-start(bf16[8,64,1024]{2,1,0:T(8,128)(2,1)} %bitcast.18), calls=%async_computation.6 | async-start | bytes 2097152 | tf_op jit(solution)/shard_map/all_to_all | solution.py:688
  364.5 35.0 %collective-permute-start.50 = (bf16[256,768]{1,0:T(8,128)(2,1)S(1)}, bf16[256,768]{1,0:T(8,128)(2,1)S(1)}, u32[]{:S(2)}, u32[]{:S(2)}) collective-permute-start(bf16[256,768]{1,0:T(8,128)(2,1)S(1)} %shard_map.246.a_ref), channel_id=1, source_target_pairs={{0,8},{4,12},{8,0},{12,4},{16,24},{20,28},{24,16},{28,20},{1,9},{5... | collective-permute-start | bytes 1179656 | tf_op jit(solution)/shard_map/ppermute | solution.py:21
  366.6 40.8 %collective-permute-start.49 = (bf16[256,768]{1,0:T(8,128)(2,1)S(1)}, bf16[256,768]{1,0:T(8,128)(2,1)S(1)}, u32[]{:S(2)}, u32[]{:S(2)}) collective-permute-start(bf16[256,768]{1,0:T(8,128)(2,1)S(1)} %get-tuple-element.224), channel_id=1, source_target_pairs={{0,8},{4,12},{8,0},{12,4},{16,24},{20,28},{24,16},{28,20},{1,9},{5... | collective-permute-start | bytes 1179656 | tf_op jit(solution)/shard_map/ppermute | solution.py:21
  366.8 40.6 %collective-permute-start.51 = (bf16[256,768]{1,0:T(8,128)(2,1)S(1)}, bf16[256,768]{1,0:T(8,128)(2,1)S(1)}, u32[]{:S(2)}, u32[]{:S(2)}) collective-permute-start(bf16[256,768]{1,0:T(8,128)(2,1)S(1)} %shard_map.247.a_ref), channel_id=1, source_target_pairs={{0,16},{4,20},{8,24},{12,28},{16,0},{20,4},{24,8},{28,12},{1,17},{... | collective-permute-start | bytes 1179656 | tf_op jit(solution)/shard_map/ppermute | solution.py:21
  407.5 23.8 %collective-permute-start.53 = (bf16[512,768]{1,0:T(8,128)(2,1)S(1)}, bf16[512,768]{1,0:T(8,128)(2,1)S(1)}, u32[]{:S(2)}, u32[]{:S(2)}) collective-permute-start(bf16[512,768]{1,0:T(8,128)(2,1)S(1)} %shard_map.249.a_ref), channel_id=1, source_target_pairs={{0,4},{4,0},{8,12},{12,8},{16,20},{20,16},{24,28},{28,24},{1,5},{5... | collective-permute-start | bytes 2359304 | tf_op jit(solution)/shard_map/ppermute | solution.py:21
  438.8 25.0 %collective-permute-start.31 = (bf16[160,3072]{1,0:T(8,128)(2,1)}, bf16[160,3072]{1,0:T(8,128)(2,1)}, u32[]{:S(2)}, u32[]{:S(2)}) collective-permute-start(bf16[160,3072]{1,0:T(8,128)(2,1)} %get-tuple-element.186), channel_id=1, source_target_pairs={{0,2},{1,3},{2,0},{3,1},{4,6},{5,7},{6,4},{7,5},{8,10},{9,11},{10,... | collective-permute-start | bytes 2949128 | tf_op jit(solution)/shard_map/ppermute | solution.py:21
  (123 other events, 1158.2 us)

commit v4 on v3

--- a/solution.py
+++ b/solution.py
@@ -180,16 +180,44 @@
     return jnp.where(iota(moved.shape, 1) < hidden, moved, 0.0)
 
 
+def cut(hidden, chunk, n_loc):
+    gates = []
+    for g in range(3):
+        parts = []
+        for i in range(n_loc):
+            lo, hi = max(g * hidden, i * chunk), min((g + 1) * hidden, (i + 1) * chunk)
+            if lo < hi:
+                parts.append((i, lo - i * chunk, hi - i * chunk))
+        gates.append(parts)
+    return gates
+
+
+def gate_of(g, chunks, hidden, chunk, wide):
+    parts = [chunks[i][:, lo:hi] for i, lo, hi in cut(hidden, chunk, len(chunks))[g]]
+    pad = jnp.zeros((parts[0].shape[0], wide - hidden), parts[0].dtype)
+    return jnp.concatenate(parts + [pad], axis=1)
+
+
+def chunk_of(i, gates, hidden, chunk, n_loc, cpad):
+    parts = []
+    for g, places in enumerate(cut(hidden, chunk, n_loc)):
+        for k, lo, hi in places:
+            if k == i:
+                at = i * chunk + lo - g * hidden
+                parts.append(gates[g][:, at : at + hi - lo])
+    pad = jnp.zeros((parts[0].shape[0], cpad - chunk), parts[0].dtype)
+    return jnp.concatenate(parts + [pad], axis=1)
+
+
 def extend(value, keep, hidden):
     lane = iota(value.shape, 1)
     return jnp.where(lane == hidden, 1.0, jnp.where(lane == hidden + 1, keep, value)).astype(BF16)
 
 
-def run_steps(steps, batch, hidden, l, keep_ref, weights, x_of, start, state_ref, res, q_s):
+def run_steps(steps, batch, hidden, l, keep_ref, weights, gates_of, start, state_ref, res, q_s):
     res_ref, res_s, res_sem = res
     n_loc = q_s.shape[0]
     wide = start.shape[1]
-    tail = jnp.zeros((batch, wide), F32)
     lane = iota((batch, wide), 1)
     prev = start
     writes = step_copies(res_ref, res_s, res_sem, steps, batch, True)
@@ -200,14 +228,11 @@
         p = prev * keep
         p_low = p.astype(BF16)
         for j in range(n_loc):
-            q_s[l ^ j] = dot(p_low, weights[j])[:, : q_s.shape[2]]
-        q = jnp.concatenate([q_s[i] for i in range(n_loc)] + [tail], axis=1)
-        x = x_of(t)
-        h2 = 2 * hidden
-        z = jax.nn.sigmoid(x[:, :wide] + q[:, :wide])
-        r = jax.nn.sigmoid(x[:, hidden : hidden + wide] + q[:, hidden : hidden + wide])
-        qn = q[:, h2 : h2 + wide]
-        n = jnp.tanh(x[:, h2 : h2 + wide] + r * qn)
+            q_s[l ^ j] = dot(p_low, weights[j])
+        in_z, in_r, in_n, qn = gates_of(t, [q_s[i] for i in range(n_loc)])
+        z = jax.nn.sigmoid(in_z)
+        r = jax.nn.sigmoid(in_r)
+        n = jnp.tanh(in_n + r * qn)
         prev = jnp.where(lane < hidden, n + z * (p - n), 0.0)
         for k, val in enumerate((z, r, n, qn, p)):
             res_s[k, at, :] = val
@@ -250,9 +275,11 @@
     land = got_ref[:, wide - LANES : wide].astype(F32)[:, at : at + 1]
     land_ref[...] = land.astype(I32) - 1
     pick = low(iota((ids.shape[0], rows), 1) == ids)
-    if out_ref.shape[1] > cols:
-        out_ref[...] = jnp.zeros(out_ref.shape, BF16)
-    out_ref[:, :cols] = dot(pick, table_ref[...]).astype(BF16)
+    found = dot(pick, table_ref[...])
+    for g in range(3):
+        part = found[:, g * hidden : (g + 1) * hidden]
+        pad = jnp.zeros((part.shape[0], wide - hidden), F32)
+        out_ref[:, g * wide : (g + 1) * wide] = jnp.concatenate([part, pad], axis=1).astype(BF16)
 
 
 def biased_rows(ids, table_ref, bias_ref, wide):
@@ -297,9 +324,13 @@
     send_ref[...] = (far_ref[...] + got_ref[1].astype(F32)).astype(BF16)
 
 
-def table_out_kernel(sum_ref, got_ref, out_ref):
+def table_out_kernel(parts, sum_ref, got_ref, out_ref):
     rows, cols = out_ref.shape
-    out_ref[...] = (sum_ref[...] + got_ref[...].astype(F32))[:rows, :cols]
+    total = (sum_ref[...] + got_ref[...].astype(F32))[:rows]
+    wide = total.shape[1] // parts
+    size = cols // parts
+    split = [total[:, g * wide : g * wide + size] for g in range(parts)]
+    out_ref[...] = jnp.concatenate(split, axis=1)
 
 
 def carry_kernel(slot_ref, got_ref, out_ref):
@@ -352,27 +383,30 @@
     wide = res_s.shape[2]
     l = l_ref[0]
     weights = Weights(w_refs, w_buf, w_sem)
+    chunk = b_s.shape[2]
     pick = low(iota((steps * batch, rows_ref.shape[0]), 1) == slot_ref[...])
-    x_s[...] = dot(pick, rows_ref[...])
+    rows = dot(pick, rows_ref[...])
     moved = landing(land_ref, got_ref, 0, batch, hidden)
     for j in range(n_loc):
         weights.ready(j)
-        b_s[l ^ j] = w_buf[j, bias_row : bias_row + 16, :].astype(F32)[:, : b_s.shape[2]]
-    bias = jnp.concatenate([b_s[i][0:1, :] for i in range(n_loc)], axis=1)
-    pad = jnp.zeros((batch, wide), F32)
-
-    def x_of(t):
-        gates = bias.shape[1]
-        return jnp.concatenate([x_s[pl.ds(t * batch, batch), :][:, :gates] + bias, pad], axis=1)
+        b_s[l ^ j] = w_buf[j, bias_row : bias_row + 16, :].astype(F32)[:, :chunk]
+    bias = [b_s[i][0:1, :] for i in range(n_loc)]
+    bias = [gate_of(g, bias, hidden, chunk, wide) for g in range(3)]
+    x_s[...] = rows + jnp.concatenate(bias, axis=1)
+
+    def gates_of(t, q):
+        x = x_s[pl.ds(t * batch, batch), :]
+        gates = [gate_of(g, q, hidden, chunk, wide) for g in range(3)]
+        return x[:, :wide] + gates[0], x[:, wide : 2 * wide] + gates[1], x[:, 2 * wide :], gates[2]
 
     run_steps(
-        steps, batch, hidden, l, keep_ref, weights, x_of, moved, state_ref,
+        steps, batch, hidden, l, keep_ref, weights, gates_of, moved, state_ref,
         (res_ref, res_s, res_sem), q_s,
     )
 
 
 def second_kernel(dims, n_in, n_w, l_ref, keep_ref, land_ref, got_ref, below_ref, *refs):
-    steps, batch, hidden, n_loc = dims
+    steps, batch, hidden, chunk, n_loc = dims
     in_refs, w_refs, refs = refs[:n_in], refs[n_in : n_in + n_w], refs[n_in + n_w :]
     state_ref, res_ref, in_buf, in_sem, w_buf, w_sem, res_s, res_sem, q_s, x_s = refs
     wide = res_s.shape[2]
@@ -382,16 +416,18 @@
     moved = landing(land_ref, got_ref, 1, batch, hidden)
     below = below_ref[pl.ds(batch, steps * batch), :]
     for j in range(n_loc):
-        x_s[l ^ j] = dot(below, inputs[j])[:, : x_s.shape[2]]
-    pad = jnp.zeros((batch, wide), F32)
-
-    def x_of(t):
-        return jnp.concatenate(
-            [x_s[i][t * batch : (t + 1) * batch, :] for i in range(n_loc)] + [pad], axis=1
+        x_s[l ^ j] = dot(below, inputs[j])
+
+    def gates_of(t, q):
+        x = [x_s[i, pl.ds(t * batch, batch), :] for i in range(n_loc)]
+        both = [x[i] + q[i] for i in range(n_loc)]
+        sizes = (hidden, chunk, wide)
+        return (
+            gate_of(0, both, *sizes), gate_of(1, both, *sizes), gate_of(2, x, *sizes), gate_of(2, q, *sizes)
         )
 
     run_steps(
-        steps, batch, hidden, l, keep_ref, weights, x_of, moved, state_ref,
+        steps, batch, hidden, l, keep_ref, weights, gates_of, moved, state_ref,
         (res_ref, res_s, res_sem), q_s,
     )
 
@@ -453,10 +489,9 @@
     send_ref[...] = dot(pick, tgg_s[...], 0, 0).astype(BF16)
 
 
-def back_steps(steps, batch, hidden, chunk, l, keep_ref, weights, into_ref, res, dq_s, emit):
+def back_steps(steps, batch, hidden, l, keep_ref, weights, into_ref, res, dq_s, chunks_of):
     loader, res_s = res
     n_loc = dq_s.shape[0]
-    dq_s[...] = jnp.zeros(dq_s.shape, F32)
     wide = into_ref.shape[1]
     lane = iota((batch, wide), 1)
     carry = jnp.zeros((batch, wide), F32)
@@ -466,18 +501,13 @@
         loader.ready(t)
         z, r, n, qn, p = (res_s[k, at, :] for k in range(5))
         dc = g * (1.0 - z) * (1.0 - n * n)
-        da_z = (g * (p - n) * z * (1.0 - z))[:, :hidden]
-        da_r = (dc * qn * r * (1.0 - r))[:, :hidden]
-        da_n = dc[:, :hidden]
-        dq_n = (dc * r)[:, :hidden]
-        da = jnp.concatenate([da_z, da_r, da_n], axis=1)
-        dq = jnp.concatenate([da_z, da_r, dq_n], axis=1)
-        emit(t, da, dq)
-        for i in range(n_loc):
-            dq_s[i, :, :chunk] = dq[:, i * chunk : (i + 1) * chunk]
+        da_z = g * (p - n) * z * (1.0 - z)
+        da_r = dc * qn * r * (1.0 - r)
+        for i, value in enumerate(chunks_of(t, da_z, da_r, dc, dc * r)):
+            dq_s[i] = value.astype(BF16)
         dp = g * z
         for j in range(n_loc):
-            dp += dot(dq_s[l ^ j].astype(BF16), weights[j], 1, 1)
+            dp += dot(dq_s[l ^ j], weights[j], 1, 1)
         carry = dp * keep_ref[at, :]
     return jnp.where(lane < hidden, carry, 0.0)
 
@@ -493,23 +523,29 @@
     loader = Loader(step_copies(res_ref, res_s, res_sem, steps, batch, False))
     weights = Weights(w_refs, w_buf, w_sem, l_ref[1] & 1)
     inputs = Weights(in_refs, in_buf, in_sem, l_ref[1] & 1)
-    da_all[...] = jnp.zeros(da_all.shape, F32)
-    dq_all[...] = jnp.zeros(dq_all.shape, F32)
-
-    def emit(t, da, dq):
+    sizes = (hidden, chunk, n_loc, dq_s.shape[2])
+
+    def chunks_of(t, da_z, da_r, da_n, dq_n):
+        at = pl.ds(t * batch, batch)
+        out = []
         for i in range(n_loc):
-            da_all[i, pl.ds(t * batch, batch), :chunk] = da[:, i * chunk : (i + 1) * chunk]
-            dq_all[i, pl.ds(t * batch, batch), :chunk] = dq[:, i * chunk : (i + 1) * chunk]
+            dq = chunk_of(i, (da_z, da_r, dq_n), *sizes)
+            same = (i + 1) * chunk <= 2 * hidden
+            da = dq if same else chunk_of(i, (da_z, da_r, da_n), *sizes)
+            da_all[i, at, :] = da.astype(BF16)
+            dq_all[i, at, :] = dq.astype(BF16)
+            out.append(dq)
+        return out
 
     init_ref[...] = back_steps(
-        steps, batch, hidden, chunk, l, keep_ref, weights, into_ref, (loader, res_s), dq_s, emit
+        steps, batch, hidden, l, keep_ref, weights, into_ref, (loader, res_s), dq_s, chunks_of
     )
     rows = steps * batch
     total = None
     for j in range(n_loc):
-        da_low = da_all[l ^ j].astype(BF16)
+        da_low = da_all[l ^ j]
         ch_refs[j][...] = da_low
-        ch_refs[n_loc + j][...] = dq_all[l ^ j].astype(BF16)
+        ch_refs[n_loc + j][...] = dq_all[l ^ j]
         part = dot(da_low, inputs[j], 1, 1)
         total = part if total is None else total + part
     first_ref[...] = total
@@ -525,23 +561,29 @@
     l = l_ref[0]
     loader = Loader(step_copies(res_ref, res_s, res_sem, steps, batch, False))
     weights = Weights(w_refs, w_buf, w_sem)
-    dq_all[...] = jnp.zeros(dq_all.shape, F32)
+    wide = into_ref.shape[1]
+    sizes = (hidden, chunk, n_loc, dq_s.shape[2])
     bias_s[...] = jnp.zeros(bias_s.shape, F32)
 
-    def emit(t, da, dq):
-        da_all[pl.ds(t * batch, batch), :] = da.astype(BF16)
-        for i in range(n_loc):
-            dq_all[i, pl.ds(t * batch, batch), :chunk] = dq[:, i * chunk : (i + 1) * chunk]
+    def chunks_of(t, da_z, da_r, da_n, dq_n):
+        at = pl.ds(t * batch, batch)
+        for g, da in enumerate((da_z, da_r, da_n)):
+            da_all[at, g * wide : (g + 1) * wide] = da.astype(BF16)
+        out = [chunk_of(i, (da_z, da_r, dq_n), *sizes) for i in range(n_loc)]
+        for i, dq in enumerate(out):
+            dq_all[i, at, :] = dq.astype(BF16)
+        return out
 
     init_ref[...] = back_steps(
-        steps, batch, hidden, chunk, l, keep_ref, weights, into_ref, (loader, res_s), dq_s, emit
+        steps, batch, hidden, l, keep_ref, weights, into_ref, (loader, res_s), dq_s, chunks_of
     )
     rows = steps * batch
     bias = jnp.sum(da_all[...].astype(F32), axis=0, keepdims=True)
+    bias = [bias[:, g * wide : (g + 1) * wide] for g in range(3)]
     for i in range(n_loc):
-        bias_s[i, 0:1, :chunk] = bias[:, i * chunk : (i + 1) * chunk]
+        bias_s[i, 0:1, :] = chunk_of(i, bias, *sizes)
     for j in range(n_loc):
-        ch_refs[j][pl.ds(0, rows), :] = dq_all[l ^ j].astype(BF16)
+        ch_refs[j][pl.ds(0, rows), :] = dq_all[l ^ j]
         ch_refs[j][pl.ds(rows, 16), :] = bias_s[l ^ j].astype(BF16)
 
 
@@ -549,11 +591,7 @@
     rows, cols = da_ref.shape
     wide = init_ref.shape[1]
     pick = low(iota((rows, send_ref.shape[0]), 1) == slot_ref[...])
-    sent = dot(pick, da_ref[...], 0, 0).astype(BF16)
-    send_ref[:, :cols] = sent
-    if send_ref.shape[1] > cols:
-        rest = send_ref.shape[1] - cols
-        send_ref[:, cols:] = jnp.zeros((send_ref.shape[0], rest), BF16)
+    send_ref[...] = dot(pick, da_ref[...], 0, 0).astype(BF16)
     land = low(iota((land_ref.shape[0], init_ref.shape[0]), 1) == land_ref[...])
     back_ref[:, :wide] = dot(land, init_ref[...].astype(BF16)).astype(BF16)
     back_ref[:, wide:] = dot(land, init2_ref[...].astype(BF16)).astype(BF16)
@@ -637,7 +675,7 @@
     l_arr = jnp.stack([loc, grp]).astype(I32)
 
     cpad = -(-chunk // LANES) * LANES
-    gpad = -(-gates // LANES) * LANES
+    gpad = 3 * wide
     w_shape = shape((wide, cpad), BF16)
 
     g_arr = grp.astype(I32).reshape(1)
@@ -749,10 +787,10 @@
     w_scratch = [pltpu.VMEM((n_loc, wide, cpad), BF16), pltpu.SemaphoreType.DMA((n_w,))]
     res_scratch = [pltpu.VMEM((5, events, wide), F32), pltpu.SemaphoreType.DMA((steps,))]
     state_shape = shape(((steps + 1) * batch, wide), BF16)
-    q_scratch = pltpu.VMEM((n_loc, batch, chunk), F32)
-    dq_scratch = pltpu.VMEM((n_loc, batch, cpad), F32)
-    x_scratch = pltpu.VMEM((n_loc, events, chunk), F32)
-    all_scratch = pltpu.VMEM((n_loc, events, cpad), F32)
+    q_scratch = pltpu.VMEM((n_loc, batch, cpad), F32)
+    dq_scratch = pltpu.VMEM((n_loc, batch, cpad), BF16)
+    x_scratch = pltpu.VMEM((n_loc, events, cpad), F32)
+    all_scratch = pltpu.VMEM((n_loc, events, cpad), BF16)
 
     state_a, res_one = kernel_call(
         functools.partial(first_kernel, (steps, batch, hidden, bias_row, n_loc), n_w),
@@ -767,7 +805,7 @@
     w_in = four(p_in, [after(y, state_a) for y in y_in])
     w_two = four(p_two, [after(y, state_a) for y in y_two])
     state_b, res_two = kernel_call(
-        functools.partial(second_kernel, (steps, batch, hidden, n_loc), n_w, n_w),
+        functools.partial(second_kernel, (steps, batch, hidden, chunk, n_loc), n_w, n_w),
         [state_shape, res_shape],
         [l_arr, keep, land, got_c, after(state_a, y_neg)] + w_in + w_two,
         1,
@@ -810,7 +848,7 @@
     got_tg_g = to_owners(send_tg)
     init_one, da_one, *ch_one = kernel_call(
         functools.partial(back_first_kernel, (steps, batch, hidden, chunk, n_loc), n_w),
-        [shape((batch, wide), F32), shape((events, gates), BF16)]
+        [shape((batch, wide), F32), shape((events, gpad), BF16)]
         + [shape((events + 16, cpad), BF16)] * n_loc,
         [l_arr, keep, after(into_first, y_a), res_one] + w_one,
         1,
@@ -930,7 +968,7 @@
     own = rows // n_loc
     own_pad = -(-own // 16) * 16
 
-    def table_sum(ids, grads, cols, *wait):
+    def table_sum(ids, grads, cols, parts, *wait):
         across_cols = grads[0].shape[1]
         full = shape((own_pad, across_cols), F32)
         sent = shape((own_pad, across_cols), BF16)
@@ -943,11 +981,15 @@
         total, far_s = kernel_call(
             table_add_kernel, [full, sent], [after(mine_p, *wait), far_p, near(near_p)]
         )
-        return kernel_call(table_out_kernel, [shape((own, cols), F32)], [total, across(far_s)])[0]
-
-    table_in = table_sum([in_ids], [got_in_g], gates, got_back)
+        return kernel_call(
+            functools.partial(table_out_kernel, parts),
+            [shape((own, cols), F32)],
+            [total, across(far_s)],
+        )[0]
+
+    table_in = table_sum([in_ids], [got_in_g], gates, 3, got_back)
     neg_ids = jnp.broadcast_to(mine[None, :], (owners, neg_own)).reshape(neg_part)
-    table_out = table_sum([tg_ids, neg_ids], [got_tg_g, got_neg_g], wide)
+    table_out = table_sum([tg_ids, neg_ids], [got_tg_g, got_neg_g], wide, 1)
     grad_carried = kernel_call(
         carry_kernel, [shape((2, batch, hidden), F32)], [slot_pl, got_back]
     )[0]

time: 478 us -> 475 us (level)
  transfers between devices with their start and end apart: 65 -> 65, of which waited for: 24 -> 22; matrix products, arithmetic and copies ran while one was open for 0% -> 0% of each run, Pallas kernels for 29% -> 28%
where the time goes in v4:
time: 475 us; the launch traced here: 469 us
  waiting for transfers between devices  191 us (40%)
  Pallas kernels  133 us (28%)
  starting transfers between devices  89 us (19%)
  local copies, waits for them, and re-layouts  54.2 us (11%)
    ppermute x58, waiting for transfers between devices, swap(): return lax.ppermute(x, axis, [(i, i ^ bit) for i in range(n)])  162 us
    pallas_call x42, Pallas kernels, kernel_call(): pl.pallas_call(body, out_shape=outs, in_specs=[pl.BlockSpec(memory_space=...  133 us
    ppermute x58, starting transfers between devices, swap(): return lax.ppermute(x, axis, [(i, i ^ bit) for i in range(n)])  54.2 us
    unnamed x180, local copies, waits for them, and re-layouts  51.5 us
    all_to_all x7, starting transfers between devices, to_owners(): lax.all_to_all(x.reshape((owners, x.shape[0] // owners) + x.shape[1:]), '...  34.8 us
    all_to_all x7, waiting for transfers between devices, to_owners(): lax.all_to_all(x.reshape((owners, x.shape[0] // owners) + x.shape[1:]), '...  28.9 us
  transfers between devices with their start and end apart: 65, of which 22 were waited for; matrix products, arithmetic and copies ran while one was open for 0% of the time, Pallas kernels for 28%

profile of v4, /device:TPU:0, one launch (start us, length us, event | category | flops | bytes accessed | tf_op | source)
XLA Modules:
  0.0 469.3 jit_solution(7310011504972194781)
XLA Ops:
  12.6 6.0 %all-to-all-start = ((bf16[8,32,2048]{2,1,0:T(8,128)(2,1)}), bf16[8,32,2048]{2,1,0:T(8,128)(2,1)S(1)}, u32[]{:S(2)}, u32[]{:S(2)}) async-start(bf16[8,32,2048]{2,1,0:T(8,128)(2,1)} %bitcast.4), calls=%async_computation | async-start | bytes 2097152 | tf_op jit(solution)/shard_map/all_to_all | solution.py:726
  24.3 13.4 %collective-permute-done.1.b_ref = bf16[64,1024]{1,0:T(8,128)(2,1)S(1)} collective-permute-done((bf16[64,1024]{1,0:T(8,128)(2,1)S(1)}, bf16[64,1024]{1,0:T(8,128)(2,1)S(1)}, u32[]{:S(2)}, u32[]{:S(2)}) %collective-permute-start.1) | collective-permute-done | bytes 131104 | tf_op jit(solution)/shard_map/ppermute | solution.py:21
  37.7 5.2 %collective-permute-start.2 = (bf16[128,1024]{1,0:T(8,128)(2,1)S(1)}, bf16[128,1024]{1,0:T(8,128)(2,1)S(1)}, u32[]{:S(2)}, u32[]{:S(2)}) collective-permute-start(bf16[128,1024]{1,0:T(8,128)(2,1)S(1)} %shard_map.219.a_ref), channel_id=1, source_target_pairs={{0,16},{4,20},{8,24},{12,28},{16,0},{20,4},{24,8},{28,12},{1,17},{... | collective-permute-start | bytes 786440 | tf_op jit(solution)/shard_map/ppermute | solution.py:21
  42.9 12.1 %collective-permute-done.2.b_ref = bf16[128,1024]{1,0:T(8,128)(2,1)S(1)} collective-permute-done((bf16[128,1024]{1,0:T(8,128)(2,1)S(1)}, bf16[128,1024]{1,0:T(8,128)(2,1)S(1)}, u32[]{:S(2)}, u32[]{:S(2)}) %collective-permute-start.2) | collective-permute-done | bytes 262176 | tf_op jit(solution)/shard_map/ppermute | solution.py:21
  56.9 6.0 %shard_map.217 = (bf16[384,3072]{1,0:T(8,128)(2,1)}, s32[384,1]{1,0:T(8,128)S(1)}, s32[256,1]{1,0:T(8,128)S(1)}) custom-call(s32[1]{0:T(128)} %bitcast.2.base_ref, bf16[256,2048]{1,0:T(8,128)(2,1)S(1)} %bitcast.23, s32[384,1]{1,0:T(8,128)S(1)} %copy-done.48, s32[384,1]{1,0:T(8,128)S(1)} %copy-done.50, bf16[588,3000]{1,0:T(8,128)(2,1)} %table_ref.3), custom_call_target="tpu_custom_call" | custom-call | flops 4000000000 | bytes 6941508 | tf_op jit(solution)/shard_map/pallas_call | solution.py:42
  63.6 4.7 %all-to-all-start.1 = ((bf16[8,48,3072]{2,1,0:T(8,128)(2,1)}), bf16[8,48,3072]{2,1,0:T(8,128)(2,1)}, u32[]{:S(2)}, u32[]{:S(2)}) async-start(bf16[8,48,3072]{2,1,0:T(8,128)(2,1)} %bitcast.8), calls=%async_computation.1 | async-start | bytes 4718592 | tf_op jit(solution)/shard_map/all_to_all | solution.py:726
  77.7 12.2 %collective-permute-done.5.refs_2_.refs_3_ = bf16[512,768]{1,0:T(8,128)(2,1)} collective-permute-done((bf16[512,768]{1,0:T(8,128)(2,1)S(1)}, bf16[512,768]{1,0:T(8,128)(2,1)}, u32[]{:S(2)}, u32[]{:S(2)}) %collective-permute-start.5) | collective-permute-done | bytes 786464 | tf_op jit(solution)/shard_map/ppermute | solution.py:21
  93.1 13.8 %collective-permute-done.4.b_ref = bf16[256,1024]{1,0:T(8,128)(2,1)S(1)} collective-permute-done((bf16[256,1024]{1,0:T(8,128)(2,1)S(1)}, bf16[256,1024]{1,0:T(8,128)(2,1)S(1)}, u32[]{:S(2)}, u32[]{:S(2)}) %collective-permute-start.4) | collective-permute-done | bytes 524320 | tf_op jit(solution)/shard_map/ppermute | solution.py:21
  115.8 7.5 %collective-permute-done.7.refs_3_.refs_4_ = bf16[512,768]{1,0:T(8,128)(2,1)} collective-permute-done((bf16[512,768]{1,0:T(8,128)(2,1)}, bf16[512,768]{1,0:T(8,128)(2,1)}, u32[]{:S(2)}, u32[]{:S(2)}) %collective-permute-start.7) | collective-permute-done | bytes 786464 | tf_op jit(solution)/shard_map/ppermute | solution.py:21
  127.0 12.8 %shard_map.225 = (bf16[320,1024]{1,0:T(8,128)(2,1)}, f32[5,256,1024]{2,1,0:T(8,128)}) custom-call(s32[2]{0:T(128)S(1)} %pad_add_fusion.l_ref, f32[256,1]{1,0:T(8,128)S(1)} %reshape.149.keep_ref, s32[256,1]{1,0:T(8,128)S(1)} %copy-done.74, s32[256,1]{1,0:T(8,128)S(1)} %copy-done.77, bf16[256,2048]{1,0:T(8,128)(2,1)S(1)} %bitcast.25, ...), custom_call_target="tpu_custom_call" | custom-call | flops 12000000000 | bytes 15600648 | tf_op jit(solution)/shard_map/pallas_call | solution.py:42
  139.9 4.8 %collective-permute-done.16.refs_9_.refs_10_ = bf16[512,768]{1,0:T(8,128)(2,1)} collective-permute-done((bf16[512,768]{1,0:T(8,128)(2,1)}, bf16[512,768]{1,0:T(8,128)(2,1)}, u32[]{:S(2)}, u32[]{:S(2)}) %collective-permute-start.16) | collective-permute-done | bytes 786464 | tf_op jit(solution)/shard_map/ppermute | solution.py:21
  145.3 3.9 collective-permute-done.11.refs_2_
  149.2 4.9 %all-to-all-start.2 = ((bf16[8,48,1024]{2,1,0:T(8,128)(2,1)}), bf16[8,48,1024]{2,1,0:T(8,128)(2,1)S(1)}, u32[]{:S(2)}, u32[]{:S(2)}) async-start(bf16[8,48,1024]{2,1,0:T(8,128)(2,1)} %bitcast.10), calls=%async_computation.2 | async-start | bytes 1572864 | tf_op jit(solution)/shard_map/all_to_all | solution.py:726
  156.4 13.6 %shard_map.226 = (bf16[320,1024]{1,0:T(8,128)(2,1)S(1)}, f32[5,256,1024]{2,1,0:T(8,128)}) custom-call(s32[2]{0:T(128)S(1)} %pad_add_fusion.l_ref, f32[256,1]{1,0:T(8,128)S(1)} %reshape.149.keep_ref, s32[256,1]{1,0:T(8,128)S(1)} %copy-done.77, bf16[256,2048]{1,0:T(8,128)(2,1)} %bitcast.26, bf16[320,1024]{1,0:T(8,128)(2,1)} %get-tuple-element.161.below_ref.refs_0_, ...), custom_call_target="tpu_custom_call" | custom-call | flops 15000000512 | bytes 20187144 | tf_op jit(solution)/shard_map/pallas_call | solution.py:42
  176.0 9.9 %shard_map.227 = (bf16[256,512]{1,0:T(8,128)(2,1)S(1)}, bf16[256,512]{1,0:T(8,128)(2,1)}, bf16[256,512]{1,0:T(8,128)(2,1)S(1)}, bf16[256,512]{1,0:T(8,128)(2,1)S...) custom-call(f32[256,1]{1,0:T(8,128)S(1)} %div.11.valid_ref, s32[256,1]{1,0:T(8,128)S(1)} %copy-done.80, ...), custom_call_target="tpu_custom_call" | custom-call | flops 12000000000 | bytes 8521728 | tf_op jit(solution)/shard_map/pallas_call | solution.py:42
  190.4 17.1 %shard_map.228 = (f32[64,1024]{1,0:T(8,128)S(1)}, f32[256,1024]{1,0:T(8,128)}, bf16[256,768]{1,0:T(8,128)(2,1)S(1)}, bf16[256,768]{1,0:T(8,128)(2,1)S(1)}, bf16[...) custom-call(s32[2]{0:T(128)S(1)} %pad_add_fusion.l_ref, ...), custom_call_target="tpu_custom_call" | custom-call | flops 16999999488 | bytes 23331848 | tf_op jit(solution)/shard_map/pallas_call | solution.py:42
  211.0 6.1 %all-to-all-start.3 = ((bf16[8,48,1024]{2,1,0:T(8,128)(2,1)}), bf16[8,48,1024]{2,1,0:T(8,128)(2,1)S(1)}, u32[]{:S(2)}, u32[]{:S(2)}) async-start(bf16[8,48,1024]{2,1,0:T(8,128)(2,1)} %bitcast.12), calls=%async_computation.3 | async-start | bytes 1572864 | tf_op jit(solution)/shard_map/all_to_all | solution.py:726
  219.5 13.4 %shard_map.229 = (f32[64,1024]{1,0:T(8,128)S(1)}, bf16[256,3072]{1,0:T(8,128)(2,1)}, bf16[272,768]{1,0:T(8,128)(2,1)S(1)}, bf16[272,768]{1,0:T(8,128)(2,1)S(1)},...) custom-call(s32[2]{0:T(128)S(1)} %pad_add_fusion.l_ref, f32[256,1]{1,0:T(8,128)S(1)} %reshape.149.keep_ref, ...), custom_call_target="tpu_custom_call" | custom-call | flops 12999999488 | bytes 16090120 | tf_op jit(solution)/shard_map/pallas_call | solution.py:42
  239.8 5.0 %all-to-all-start.4 = ((bf16[8,48,3072]{2,1,0:T(8,128)(2,1)}), bf16[8,48,3072]{2,1,0:T(8,128)(2,1)}, u32[]{:S(2)}, u32[]{:S(2)}) async-start(bf16[8,48,3072]{2,1,0:T(8,128)(2,1)} %bitcast.14), calls=%async_computation.4 | async-start | bytes 4718592 | tf_op jit(solution)/shard_map/all_to_all | solution.py:726
  259.6 7.8 %collective-permute-done.29.refs_7_ = bf16[272,768]{1,0:T(8,128)(2,1)S(1)} collective-permute-done((bf16[272,768]{1,0:T(8,128)(2,1)S(1)}, bf16[272,768]{1,0:T(8,128)(2,1)S(1)}, u32[]{:S(2)}, u32[]{:S(2)}) %collective-permute-start.29) | collective-permute-done | bytes 417824 | tf_op jit(solution)/shard_map/ppermute | solution.py:21
  273.7 25.9 %all-to-all-done.4 = bf16[8,48,3072]{2,1,0:T(8,128)(2,1)} async-done(((bf16[8,48,3072]{2,1,0:T(8,128)(2,1)}), bf16[8,48,3072]{2,1,0:T(8,128)(2,1)}, u32[]{:S(2)}, u32[]{:S(2)}) %all-to-all-start.4) | async-done | bytes 2359328 | tf_op jit(solution)/shard_map/all_to_all | solution.py:726
  299.6 3.9 all-to-all-start.5
  306.7 4.8 %shard_map.241 = (bf16[512,768]{1,0:T(8,128)(2,1)S(1)}, bf16[512,768]{1,0:T(8,128)(2,1)}) custom-call(s32[1]{0:T(128)} %bitcast.1.l_ref, bf16[320,1024]{1,0:T(8,128)(2,1)S(1)} %copy-done.27, bf16[320,1024]{1,0:T(8,128)(2,1)S(1)} %copy-done.30, bf16[320,1024]{1,0:T(8,128)(2,1)} %collective-permute-done.21.refs_6_.refs_2_, ...), custom_call_target="tpu_custom_call" | custom-call | flops 5000000000 | bytes 5767172 | tf_op jit(solution)/shard_map/pallas_call | solution.py:42
  319.1 13.1 %collective-permute-done.41.b_ref = bf16[256,768]{1,0:T(8,128)(2,1)} collective-permute-done((bf16[256,768]{1,0:T(8,128)(2,1)S(1)}, bf16[256,768]{1,0:T(8,128)(2,1)}, u32[]{:S(2)}, u32[]{:S(2)}) %collective-permute-start.41) | collective-permute-done | bytes 393248 | tf_op jit(solution)/shard_map/ppermute | solution.py:21
  343.9 5.2 %shard_map.231 = (f32[160,3072]{1,0:T(8,128)S(1)}, f32[160,3072]{1,0:T(8,128)S(1)}, bf16[2,160,3072]{2,1,0:T(8,128)(2,1)}) custom-call(s32[2]{0:T(128)S(1)} %pad_add_fusion.l_ref, s32[1,384]{1,0:T(1,128)S(1)} %reshape.130.refs_0_, bf16[384,3072]{1,0:T(8,128)(2,1)} %bitcast.15.refs_1_), custom_call_target="tpu_custom_call" | custom-call | flops 4000000000 | bytes 8259080 | tf_op jit(solution)/shard_map/pallas_call | solution.py:42
  351.7 3.7 shard_map.235
  355.3 4.3 all-to-all-start.6
  367.1 29.8 %collective-permute-done.50.b_ref = bf16[256,768]{1,0:T(8,128)(2,1)S(1)} collective-permute-done((bf16[256,768]{1,0:T(8,128)(2,1)S(1)}, bf16[256,768]{1,0:T(8,128)(2,1)S(1)}, u32[]{:S(2)}, u32[]{:S(2)}) %collective-permute-start.50) | collective-permute-done | bytes 393248 | tf_op jit(solution)/shard_map/ppermute | solution.py:21
  397.0 8.0 %collective-permute-done.49.b_ref = bf16[256,768]{1,0:T(8,128)(2,1)S(1)} collective-permute-done((bf16[256,768]{1,0:T(8,128)(2,1)S(1)}, bf16[256,768]{1,0:T(8,128)(2,1)S(1)}, u32[]{:S(2)}, u32[]{:S(2)}) %collective-permute-start.49) | collective-permute-done | bytes 393248 | tf_op jit(solution)/shard_map/ppermute | solution.py:21
  409.6 15.8 %collective-permute-done.54.b_ref = bf16[256,768]{1,0:T(8,128)(2,1)S(1)} collective-permute-done((bf16[256,768]{1,0:T(8,128)(2,1)S(1)}, bf16[256,768]{1,0:T(8,128)(2,1)S(1)}, u32[]{:S(2)}, u32[]{:S(2)}) %collective-permute-start.54) | collective-permute-done | bytes 393248 | tf_op jit(solution)/shard_map/ppermute | solution.py:21
  442.0 4.5 collective-permute-done.56.b_ref
  453.0 8.3 %collective-permute-done.31.got_ref = bf16[160,3072]{1,0:T(8,128)(2,1)} collective-permute-done((bf16[160,3072]{1,0:T(8,128)(2,1)}, bf16[160,3072]{1,0:T(8,128)(2,1)}, u32[]{:S(2)}, u32[]{:S(2)}) %collective-permute-start.31) | collective-permute-done | bytes 983072 | tf_op jit(solution)/shard_map/ppermute | solution.py:21
  (340 shorter events, 160.6 us)
Async XLA Ops:
  12.6 43.2 %all-to-all-start = ((bf16[8,32,2048]{2,1,0:T(8,128)(2,1)}), bf16[8,32,2048]{2,1,0:T(8,128)(2,1)S(1)}, u32[]{:S(2)}, u32[]{:S(2)}) async-start(bf16[8,32,2048]{2,1,0:T(8,128)(2,1)} %bitcast.4), calls=%async_computation | async-start | bytes 2097152 | tf_op jit(solution)/shard_map/all_to_all | solution.py:726
  18.6 45.0 %collective-permute-start.3 = (bf16[896,768]{1,0:T(8,128)(2,1)}, bf16[896,768]{1,0:T(8,128)(2,1)}, u32[]{:S(2)}, u32[]{:S(2)}) collective-permute-start(bf16[896,768]{1,0:T(8,128)(2,1)} %copy-done.10), channel_id=1, source_target_pairs={{0,2},{1,3},{2,0},{3,1},{4,6},{5,7},{6,4},{7,5},{8,10},{9,11},{10,... | collective-permute-start | bytes 4128776 | tf_op jit(solution)/shard_map/ppermute | solution.py:21
  63.6 59.7 %all-to-all-start.1 = ((bf16[8,48,3072]{2,1,0:T(8,128)(2,1)}), bf16[8,48,3072]{2,1,0:T(8,128)(2,1)}, u32[]{:S(2)}, u32[]{:S(2)}) async-start(bf16[8,48,3072]{2,1,0:T(8,128)(2,1)} %bitcast.8), calls=%async_computation.1 | async-start | bytes 4718592 | tf_op jit(solution)/shard_map/all_to_all | solution.py:726
  73.1 51.8 %collective-permute-start.8 = (bf16[1024,768]{1,0:T(8,128)(2,1)S(1)}, bf16[1024,768]{1,0:T(8,128)(2,1)}, u32[]{:S(2)}, u32[]{:S(2)}) collective-permute-start(bf16[1024,768]{1,0:T(8,128)(2,1)S(1)} %get-tuple-element.124.refs_0_.refs_1_), channel_id=1, source_target_pairs={{0,1},{1,0},{2,3},{3,2},{4,5},{5,4},{6,7},{7,6},{8,9},{9,8},{10,11... | collective-permute-start | bytes 4718600 | tf_op jit(solution)/shard_map/ppermute | solution.py:21
  73.1 52.1 %collective-permute-start.10 = (bf16[896,768]{1,0:T(8,128)(2,1)}, bf16[896,768]{1,0:T(8,128)(2,1)}, u32[]{:S(2)}, u32[]{:S(2)}) collective-permute-start(bf16[896,768]{1,0:T(8,128)(2,1)} %collective-permute-done.3.refs_3_.refs_4_), channel_id=1, source_target_pairs={{0,1},{1,0},{2,3},{3,2},{4,5},{5,4},{6,7},{7,6},{8,9},{9,8},{10,11... | collective-permute-start | bytes 4128776 | tf_op jit(solution)/shard_map/ppermute | solution.py:21
  73.6 33.3 %collective-permute-start.4 = (bf16[256,1024]{1,0:T(8,128)(2,1)S(1)}, bf16[256,1024]{1,0:T(8,128)(2,1)S(1)}, u32[]{:S(2)}, u32[]{:S(2)}) collective-permute-start(bf16[256,1024]{1,0:T(8,128)(2,1)S(1)} %copy-done.36), channel_id=1, source_target_pairs={{0,4},{4,0},{8,12},{12,8},{16,20},{20,16},{24,28},{28,24},{1,5},{5... | collective-permute-start | bytes 1572872 | tf_op jit(solution)/shard_map/ppermute | solution.py:21
  91.4 31.9 %collective-permute-start.7 = (bf16[512,768]{1,0:T(8,128)(2,1)}, bf16[512,768]{1,0:T(8,128)(2,1)}, u32[]{:S(2)}, u32[]{:S(2)}) collective-permute-start(bf16[512,768]{1,0:T(8,128)(2,1)} %collective-permute-done.5.refs_2_.refs_3_), channel_id=1, source_target_pairs={{0,4},{4,0},{8,12},{12,8},{16,20},{20,16},{24,28},{28,24},{1,5},{5... | collective-permute-start | bytes 2359304 | tf_op jit(solution)/shard_map/ppermute | solution.py:21
  107.7 37.1 %collective-permute-start.12 = (bf16[1024,768]{1,0:T(8,128)(2,1)}, bf16[1024,768]{1,0:T(8,128)(2,1)}, u32[]{:S(2)}, u32[]{:S(2)}) collective-permute-start(bf16[1024,768]{1,0:T(8,128)(2,1)} %get-tuple-element.147.refs_0_.refs_1_), channel_id=1, source_target_pairs={{0,1},{1,0},{2,3},{3,2},{4,5},{5,4},{6,7},{7,6},{8,9},{9,8},{10,11... | collective-permute-start | bytes 4718600 | tf_op jit(solution)/shard_map/ppermute | solution.py:21
  123.3 30.8 %collective-permute-start.15 = (bf16[1024,768]{1,0:T(8,128)(2,1)}, bf16[1024,768]{1,0:T(8,128)(2,1)}, u32[]{:S(2)}, u32[]{:S(2)}) collective-permute-start(bf16[1024,768]{1,0:T(8,128)(2,1)} %get-tuple-element.150.refs_6_.refs_7_), channel_id=1, source_target_pairs={{0,1},{1,0},{2,3},{3,2},{4,5},{5,4},{6,7},{7,6},{8,9},{9,8},{10,11... | collective-permute-start | bytes 4718600 | tf_op jit(solution)/shard_map/ppermute | solution.py:21
  123.3 25.9 %collective-permute-start.11 = (bf16[512,1024]{1,0:T(8,128)(2,1)}, bf16[512,1024]{1,0:T(8,128)(2,1)}, u32[]{:S(2)}, u32[]{:S(2)}) collective-permute-start(bf16[512,1024]{1,0:T(8,128)(2,1)} %copy-done.13), channel_id=1, source_target_pairs={{0,2},{1,3},{2,0},{3,1},{4,6},{5,7},{6,4},{7,5},{8,10},{9,11},{10,... | collective-permute-start | bytes 3145736 | tf_op jit(solution)/shard_map/ppermute | solution.py:21
  149.2 25.7 %all-to-all-start.2 = ((bf16[8,48,1024]{2,1,0:T(8,128)(2,1)}), bf16[8,48,1024]{2,1,0:T(8,128)(2,1)S(1)}, u32[]{:S(2)}, u32[]{:S(2)}) async-start(bf16[8,48,1024]{2,1,0:T(8,128)(2,1)} %bitcast.10), calls=%async_computation.2 | async-start | bytes 1572864 | tf_op jit(solution)/shard_map/all_to_all | solution.py:726
  188.9 28.2 %collective-permute-start.22 = (bf16[320,1024]{1,0:T(8,128)(2,1)}, bf16[320,1024]{1,0:T(8,128)(2,1)S(1)}, u32[]{:S(2)}, u32[]{:S(2)}) collective-permute-start(bf16[320,1024]{1,0:T(8,128)(2,1)} %get-tuple-element.161.below_ref.refs_0_), channel_id=1, source_target_pairs={{0,2},{1,3},{2,0},{3,1},{4,6},{5,7},{6,4},{7,5},{8,10},{9,11},{10,... | collective-permute-start | bytes 1966088 | tf_op jit(solution)/shard_map/ppermute | solution.py:21
  211.0 28.0 %all-to-all-start.3 = ((bf16[8,48,1024]{2,1,0:T(8,128)(2,1)}), bf16[8,48,1024]{2,1,0:T(8,128)(2,1)S(1)}, u32[]{:S(2)}, u32[]{:S(2)}) async-start(bf16[8,48,1024]{2,1,0:T(8,128)(2,1)} %bitcast.12), calls=%async_computation.3 | async-start | bytes 1572864 | tf_op jit(solution)/shard_map/all_to_all | solution.py:726
  239.8 59.8 %all-to-all-start.4 = ((bf16[8,48,3072]{2,1,0:T(8,128)(2,1)}), bf16[8,48,3072]{2,1,0:T(8,128)(2,1)}, u32[]{:S(2)}, u32[]{:S(2)}) async-start(bf16[8,48,3072]{2,1,0:T(8,128)(2,1)} %bitcast.14), calls=%async_computation.4 | async-start | bytes 4718592 | tf_op jit(solution)/shard_map/all_to_all | solution.py:726
  249.1 54.4 %collective-permute-start.36 = (bf16[320,1024]{1,0:T(8,128)(2,1)}, bf16[320,1024]{1,0:T(8,128)(2,1)}, u32[]{:S(2)}, u32[]{:S(2)}) collective-permute-start(bf16[320,1024]{1,0:T(8,128)(2,1)} %collective-permute-done.21.refs_6_.refs_2_), channel_id=1, source_target_pairs={{0,1},{1,0},{2,3},{3,2},{4,5},{5,4},{6,7},{7,6},{8,9},{9,8},{10,11... | collective-permute-start | bytes 1966088 | tf_op jit(solution)/shard_map/ppermute | solution.py:21
  256.9 46.6 %collective-permute-start.42 = (bf16[256,768]{1,0:T(8,128)(2,1)}, bf16[256,768]{1,0:T(8,128)(2,1)}, u32[]{:S(2)}, u32[]{:S(2)}) collective-permute-start(bf16[256,768]{1,0:T(8,128)(2,1)} %get-tuple-element.211), channel_id=1, source_target_pairs={{0,1},{1,0},{2,3},{3,2},{4,5},{5,4},{6,7},{7,6},{8,9},{9,8},{10,11... | collective-permute-start | bytes 1179656 | tf_op jit(solution)/shard_map/ppermute | solution.py:21
  257.0 46.4 %collective-permute-start.43 = (bf16[256,768]{1,0:T(8,128)(2,1)}, bf16[256,768]{1,0:T(8,128)(2,1)}, u32[]{:S(2)}, u32[]{:S(2)}) collective-permute-start(bf16[256,768]{1,0:T(8,128)(2,1)} %get-tuple-element.212), channel_id=1, source_target_pairs={{0,2},{1,3},{2,0},{3,1},{4,6},{5,7},{6,4},{7,5},{8,10},{9,11},{10,... | collective-permute-start | bytes 1179656 | tf_op jit(solution)/shard_map/ppermute | solution.py:21
  259.6 43.9 %collective-permute-start.44 = (bf16[256,768]{1,0:T(8,128)(2,1)}, bf16[256,768]{1,0:T(8,128)(2,1)S(1)}, u32[]{:S(2)}, u32[]{:S(2)}) collective-permute-start(bf16[256,768]{1,0:T(8,128)(2,1)} %get-tuple-element.213), channel_id=1, source_target_pairs={{0,3},{1,2},{2,1},{3,0},{4,7},{5,6},{6,5},{7,4},{8,11},{9,10},{10,... | collective-permute-start | bytes 1179656 | tf_op jit(solution)/shard_map/ppermute | solution.py:21
  267.4 44.1 %collective-permute-start.40 = (bf16[512,768]{1,0:T(8,128)(2,1)S(1)}, bf16[512,768]{1,0:T(8,128)(2,1)}, u32[]{:S(2)}, u32[]{:S(2)}) collective-permute-start(bf16[512,768]{1,0:T(8,128)(2,1)S(1)} %get-tuple-element.207), channel_id=1, source_target_pairs={{0,4},{4,0},{8,12},{12,8},{16,20},{20,16},{24,28},{28,24},{1,5},{5... | collective-permute-start | bytes 2359304 | tf_op jit(solution)/shard_map/ppermute | solution.py:21
  299.6 55.7 %all-to-all-start.5 = ((bf16[8,32,2048]{2,1,0:T(8,128)(2,1)}), bf16[8,32,2048]{2,1,0:T(8,128)(2,1)S(1)}, u32[]{:S(2)}, u32[]{:S(2)}) async-start(bf16[8,32,2048]{2,1,0:T(8,128)(2,1)} %bitcast.16), calls=%async_computation.5 | async-start | bytes 2097152 | tf_op jit(solution)/shard_map/all_to_all | solution.py:726
  311.5 24.0 %collective-permute-start.45 = (bf16[512,768]{1,0:T(8,128)(2,1)}, bf16[512,768]{1,0:T(8,128)(2,1)S(1)}, u32[]{:S(2)}, u32[]{:S(2)}) collective-permute-start(bf16[512,768]{1,0:T(8,128)(2,1)} %get-tuple-element.215), channel_id=1, source_target_pairs={{0,4},{4,0},{8,12},{12,8},{16,20},{20,16},{24,28},{28,24},{1,5},{5... | collective-permute-start | bytes 2359304 | tf_op jit(solution)/shard_map/ppermute | solution.py:21
  317.0 25.7 %collective-permute-start.32 = (bf16[256,512]{1,0:T(8,128)(2,1)}, bf16[256,512]{1,0:T(8,128)(2,1)}, u32[]{:S(2)}, u32[]{:S(2)}) collective-permute-start(bf16[256,512]{1,0:T(8,128)(2,1)} %get-tuple-element.191), channel_id=1, source_target_pairs={{0,1},{1,0},{2,3},{3,2},{4,5},{5,4},{6,7},{7,6},{8,9},{9,8},{10,11... | collective-permute-start | bytes 786440 | tf_op jit(solution)/shard_map/ppermute | solution.py:21
  317.2 34.4 %collective-permute-start.33 = (bf16[256,512]{1,0:T(8,128)(2,1)}, bf16[256,512]{1,0:T(8,128)(2,1)S(1)}, u32[]{:S(2)}, u32[]{:S(2)}) collective-permute-start(bf16[256,512]{1,0:T(8,128)(2,1)} %copy-done.43), channel_id=1, source_target_pairs={{0,2},{1,3},{2,0},{3,1},{4,6},{5,7},{6,4},{7,5},{8,10},{9,11},{10,... | collective-permute-start | bytes 786440 | tf_op jit(solution)/shard_map/ppermute | solution.py:21
  317.8 33.9 %collective-permute-start.34 = (bf16[256,512]{1,0:T(8,128)(2,1)}, bf16[256,512]{1,0:T(8,128)(2,1)S(1)}, u32[]{:S(2)}, u32[]{:S(2)}) collective-permute-start(bf16[256,512]{1,0:T(8,128)(2,1)} %copy-done.42), channel_id=1, source_target_pairs={{0,3},{1,2},{2,1},{3,0},{4,7},{5,6},{6,5},{7,4},{8,11},{9,10},{10,... | collective-permute-start | bytes 786440 | tf_op jit(solution)/shard_map/ppermute | solution.py:21
  336.3 25.6 %collective-permute-start.46 = (bf16[512,768]{1,0:T(8,128)(2,1)S(1)}, bf16[512,768]{1,0:T(8,128)(2,1)S(1)}, u32[]{:S(2)}, u32[]{:S(2)}) collective-permute-start(bf16[512,768]{1,0:T(8,128)(2,1)S(1)} %get-tuple-element.216), channel_id=1, source_target_pairs={{0,4},{4,0},{8,12},{12,8},{16,20},{20,16},{24,28},{28,24},{1,5},{5... | collective-permute-start | bytes 2359304 | tf_op jit(solution)/shard_map/ppermute | solution.py:21
  351.6 79.7 %collective-permute-start.30 = (bf16[2,160,3072]{2,1,0:T(8,128)(2,1)}, bf16[2,160,3072]{2,1,0:T(8,128)(2,1)}, u32[]{:S(2)}, u32[]{:S(2)}) collective-permute-start(bf16[2,160,3072]{2,1,0:T(8,128)(2,1)} %get-tuple-element.184), channel_id=1, source_target_pairs={{0,1},{1,0},{2,3},{3,2},{4,5},{5,4},{6,7},{7,6},{8,9},{9,8},{10,11... | collective-permute-start | bytes 5898248 | tf_op jit(solution)/shard_map/ppermute | solution.py:21
  355.3 81.4 %all-to-all-start.6 = ((bf16[8,64,1024]{2,1,0:T(8,128)(2,1)}), bf16[8,64,1024]{2,1,0:T(8,128)(2,1)}, u32[]{:S(2)}, u32[]{:S(2)}) async-start(bf16[8,64,1024]{2,1,0:T(8,128)(2,1)} %bitcast.18), calls=%async_computation.6 | async-start | bytes 2097152 | tf_op jit(solution)/shard_map/all_to_all | solution.py:726
  361.9 35.0 %collective-permute-start.50 = (bf16[256,768]{1,0:T(8,128)(2,1)S(1)}, bf16[256,768]{1,0:T(8,128)(2,1)S(1)}, u32[]{:S(2)}, u32[]{:S(2)}) collective-permute-start(bf16[256,768]{1,0:T(8,128)(2,1)S(1)} %shard_map.246.a_ref), channel_id=1, source_target_pairs={{0,8},{4,12},{8,0},{12,4},{16,24},{20,28},{24,16},{28,20},{1,9},{5... | collective-permute-start | bytes 1179656 | tf_op jit(solution)/shard_map/ppermute | solution.py:21
  364.1 40.8 %collective-permute-start.49 = (bf16[256,768]{1,0:T(8,128)(2,1)S(1)}, bf16[256,768]{1,0:T(8,128)(2,1)S(1)}, u32[]{:S(2)}, u32[]{:S(2)}) collective-permute-start(bf16[256,768]{1,0:T(8,128)(2,1)S(1)} %get-tuple-element.224), channel_id=1, source_target_pairs={{0,8},{4,12},{8,0},{12,4},{16,24},{20,28},{24,16},{28,20},{1,9},{5... | collective-permute-start | bytes 1179656 | tf_op jit(solution)/shard_map/ppermute | solution.py:21
  364.3 40.6 %collective-permute-start.51 = (bf16[256,768]{1,0:T(8,128)(2,1)S(1)}, bf16[256,768]{1,0:T(8,128)(2,1)S(1)}, u32[]{:S(2)}, u32[]{:S(2)}) collective-permute-start(bf16[256,768]{1,0:T(8,128)(2,1)S(1)} %shard_map.247.a_ref), channel_id=1, source_target_pairs={{0,16},{4,20},{8,24},{12,28},{16,0},{20,4},{24,8},{28,12},{1,17},{... | collective-permute-start | bytes 1179656 | tf_op jit(solution)/shard_map/ppermute | solution.py:21
  404.9 23.8 %collective-permute-start.53 = (bf16[512,768]{1,0:T(8,128)(2,1)S(1)}, bf16[512,768]{1,0:T(8,128)(2,1)S(1)}, u32[]{:S(2)}, u32[]{:S(2)}) collective-permute-start(bf16[512,768]{1,0:T(8,128)(2,1)S(1)} %shard_map.249.a_ref), channel_id=1, source_target_pairs={{0,4},{4,0},{8,12},{12,8},{16,20},{20,16},{24,28},{28,24},{1,5},{5... | collective-permute-start | bytes 2359304 | tf_op jit(solution)/shard_map/ppermute | solution.py:21
  436.3 25.0 %collective-permute-start.31 = (bf16[160,3072]{1,0:T(8,128)(2,1)}, bf16[160,3072]{1,0:T(8,128)(2,1)}, u32[]{:S(2)}, u32[]{:S(2)}) collective-permute-start(bf16[160,3072]{1,0:T(8,128)(2,1)} %get-tuple-element.186), channel_id=1, source_target_pairs={{0,2},{1,3},{2,0},{3,1},{4,6},{5,7},{6,4},{7,5},{8,10},{9,11},{10,... | collective-permute-start | bytes 2949128 | tf_op jit(solution)/shard_map/ppermute | solution.py:21
  (123 other events, 1155.6 us)

commit v5 on v4

--- a/solution.py
+++ b/solution.py
@@ -255,7 +255,9 @@
         old = out_ref[tile : tile + 16, :cols].astype(F32)
         extra = refs[0][which : which + 1, :].astype(F32)
         out_ref[tile : tile + 16, :cols] = (old + here * extra).astype(BF16)
-    if len(outs) == 2:
+    if len(outs) == 1:
+        pass
+    elif len(outs) == 2:
         half = outs[1].shape[0]
         side = l_ref[1] & 1
         outs[1][...] = out_ref[pl.ds(pl.multiple_of(side * half, half), half), :]
@@ -412,7 +414,7 @@
     wide = res_s.shape[2]
     l = l_ref[0]
     inputs = Weights(in_refs, in_buf, in_sem, l_ref[1] & 1)
-    weights = Weights(w_refs, w_buf, w_sem, l_ref[1] & 1)
+    weights = Weights(w_refs, w_buf, w_sem)
     moved = landing(land_ref, got_ref, 1, batch, hidden)
     below = below_ref[pl.ds(batch, steps * batch), :]
     for j in range(n_loc):
@@ -521,7 +523,7 @@
     dq_s, da_all, dq_all, in_buf, in_sem, w_buf, w_sem, res_s, res_sem = refs
     l = l_ref[0]
     loader = Loader(step_copies(res_ref, res_s, res_sem, steps, batch, False))
-    weights = Weights(w_refs, w_buf, w_sem, l_ref[1] & 1)
+    weights = Weights(w_refs, w_buf, w_sem)
     inputs = Weights(in_refs, in_buf, in_sem, l_ref[1] & 1)
     sizes = (hidden, chunk, n_loc, dq_s.shape[2])
 
@@ -683,9 +685,11 @@
 
     def padded(w, at, first):
         ins = [l_arr, w] if at is None else [l_arr, w, gate_biases]
-        outs = [w_shape, shape((first, cpad), BF16)]
-        if 2 * first < wide:
-            outs.append(shape((wide - first, cpad), BF16))
+        outs = [w_shape]
+        if first:
+            outs.append(shape((first, cpad), BF16))
+            if 2 * first < wide:
+                outs.append(shape((wide - first, cpad), BF16))
         return kernel_call(functools.partial(pad_kernel, at, len(ins)), outs, ins, 1)
 
     def near(x):
@@ -758,13 +762,12 @@
         1, (), 4,
     )
     p_in, h_in = padded(input_two, (1, hidden), wide // 2)
-    p_two, h_two = padded(hidden_two, None, wide // 2)
+    p_two = padded(hidden_two, None, 0)[0]
     y_in = across(after(h_in, y_one[1]))
     got_rows = to_owners(after(reply_in, negs_half, y_one[1]))
-    y_two = across(after(h_two, y_in))
+    y_two = across(after(p_two, y_in))
     y_in = [y_in, swap(y_in, "grp", 1)]
     y_neg = across(after(negs, y_two))
-    y_two = [y_two, swap(y_two, "grp", 1)]
     reply_tg, tg_ids = kernel_call(
         functools.partial(gather_tg_kernel, (hidden, turns)),
         [shape((slots, wide), BF16), ids_shape],
@@ -795,7 +798,7 @@
     state_a, res_one = kernel_call(
         functools.partial(first_kernel, (steps, batch, hidden, bias_row, n_loc), n_w),
         [state_shape, res_shape],
-        [l_arr, keep, slot_in, land, got_c, after(got_rows, reply_tg, negs, y_two[0], y_in[1])] + w_one,
+        [l_arr, keep, slot_in, land, got_c, after(got_rows, reply_tg, negs, y_in[1])] + w_one,
         1,
         w_scratch
         + res_scratch
@@ -803,14 +806,14 @@
         12, n_w, 1,
     )
     w_in = four(p_in, [after(y, state_a) for y in y_in])
-    w_two = four(p_two, [after(y, state_a) for y in y_two])
+    w_two = four(p_two, [after(y_two, state_a)])
     state_b, res_two = kernel_call(
-        functools.partial(second_kernel, (steps, batch, hidden, chunk, n_loc), n_w, n_w),
+        functools.partial(second_kernel, (steps, batch, hidden, chunk, n_loc), n_w, n_loc),
         [state_shape, res_shape],
-        [l_arr, keep, land, got_c, after(state_a, y_neg)] + w_in + w_two,
+        [l_arr, keep, land, got_c, state_a] + w_in + w_two,
         1,
         w_scratch + w_scratch + res_scratch + [q_scratch, x_scratch],
-        15, 2 * n_w, 1,
+        0, n_w + n_loc, 1,
     )
     y_b = across(after(state_b, y_neg))
 
@@ -832,13 +835,13 @@
         12, n_loc,
     )
     init_two, into_first, *ch_two = kernel_call(
-        functools.partial(back_second_kernel, (steps, batch, hidden, chunk, n_loc), n_w, n_w),
+        functools.partial(back_second_kernel, (steps, batch, hidden, chunk, n_loc), n_w, n_loc),
         [shape((batch, wide), F32), shape((events, wide), F32)]
         + [shape((events, cpad), BF16)] * (2 * n_loc),
         [l_arr, keep, after(into_second, y_b), res_two] + w_in + w_two,
         1,
         [dq_scratch, all_scratch, all_scratch] + w_scratch + w_scratch + res_scratch,
-        17, 2 * n_w + 1,
+        17, n_w + n_loc + 1,
     )
     def send_after(chunks, *deps):
         return send_xor([after(c, *deps) for c in chunks], "loc")
@@ -935,40 +938,10 @@
             1, (), 2,
         )
 
-    sums = {}
-
-    def made(name, *args):
-        def make():
-            sums[name] = product(*args)
-            return sums[name]
-
-        return make
-
-    def start_back():
-        sums["back"] = to_owners(after(back_c, got_in_g, sums["one"][0]))
-        return ()
-
-    def bring_back():
-        return (sums["back"],)
-
-    in_parts, two_parts, one_parts = all_sums(
-        [
-            made("in", states_a, ch_in, True, None),
-            made("two", states_b, ch_two, False, None),
-            made("one", states_a, ch_one, False, bias_row),
-        ],
-        {1: lambda: tuple(ch_one[2:]), 2: start_back, 3: lambda: (got_in_g,), 5: bring_back},
-    )
-    got_back = sums["back"]
-    got_neg_g = to_owners(after(neg_grad, got_back))
-    grad_in, bias_in = finish(in_parts, hidden)
-    grad_two, _ = finish(two_parts, hidden)
-    grad_one, bias_one = finish(one_parts, bias_row)
-
     own = rows // n_loc
     own_pad = -(-own // 16) * 16
 
-    def table_sum(ids, grads, cols, parts, *wait):
+    def table_start(ids, grads, *wait):
         across_cols = grads[0].shape[1]
         full = shape((own_pad, across_cols), F32)
         sent = shape((own_pad, across_cols), BF16)
@@ -981,15 +954,53 @@
         total, far_s = kernel_call(
             table_add_kernel, [full, sent], [after(mine_p, *wait), far_p, near(near_p)]
         )
+        return total, across(far_s)
+
+    def table_end(pair, cols, parts):
         return kernel_call(
-            functools.partial(table_out_kernel, parts),
-            [shape((own, cols), F32)],
-            [total, across(far_s)],
+            functools.partial(table_out_kernel, parts), [shape((own, cols), F32)], list(pair)
         )[0]
 
-    table_in = table_sum([in_ids], [got_in_g], gates, 3, got_back)
+    sums = {}
+
+    def made(name, *args):
+        def make():
+            sums[name] = product(*args)
+            return sums[name]
+
+        return make
+
+    def start_back():
+        sums["back"] = to_owners(after(back_c, got_in_g, sums["one"][0]))
+        return ()
+
+    def table_first():
+        sums["table"] = table_start([in_ids], [got_in_g], sums["back"])
+        return ()
+
+    def table_moved():
+        return (sums["table"][1],)
+
+    def bring_back():
+        return (sums["back"],)
+
+    in_parts, two_parts, one_parts = all_sums(
+        [
+            made("in", states_a, ch_in, True, None),
+            made("two", states_b, ch_two, False, None),
+            made("one", states_a, ch_one, False, bias_row),
+        ],
+        {1: lambda: tuple(ch_one[2:]), 2: start_back, 3: lambda: (got_in_g,), 4: table_first, 5: bring_back, 6: table_moved},
+    )
+    got_back = sums["back"]
+    got_neg_g = to_owners(after(neg_grad, got_back))
+    grad_in, bias_in = finish(in_parts, hidden)
+    grad_two, _ = finish(two_parts, hidden)
+    grad_one, bias_one = finish(one_parts, bias_row)
+
+    table_in = table_end(sums["table"], gates, 3)
     neg_ids = jnp.broadcast_to(mine[None, :], (owners, neg_own)).reshape(neg_part)
-    table_out = table_sum([tg_ids, neg_ids], [got_tg_g, got_neg_g], wide, 1)
+    table_out = table_end(table_start([tg_ids, neg_ids], [got_tg_g, got_neg_g]), wide, 1)
     grad_carried = kernel_call(
         carry_kernel, [shape((2, batch, hidden), F32)], [slot_pl, got_back]
     )[0]

time: 475 us -> 470 us (0.989)
  waiting for transfers between devices: 191 us -> 173 us
  starting transfers between devices: 89 us -> 106 us
    ppermute x58 -> x56, waiting for transfers between devices: 162 us -> 146 us  [swap(): return lax.ppermute(x, axis, [(i, i ^ bit) for i in range(n)])]
    ppermute x58 -> x56, starting transfers between devices: 54.2 us -> 68.2 us  [swap(): return lax.ppermute(x, axis, [(i, i ^ bit) for i in range(n)])]
    unnamed x180 -> x200, local copies, waits for them, and re-layouts: 51.5 us -> 48.6 us
  transfers between devices with their start and end apart: 65 -> 63, of which waited for: 22 -> 25; matrix products, arithmetic and copies ran while one was open for 0% -> 0% of each run, Pallas kernels for 28% -> 28%
where the time goes in v5:
time: 470 us; the launch traced here: 464 us
  waiting for transfers between devices  173 us (37%)
  Pallas kernels  131 us (28%)
  starting transfers between devices  106 us (23%)
  local copies, waits for them, and re-layouts  51.3 us (11%)
    ppermute x56, waiting for transfers between devices, swap(): return lax.ppermute(x, axis, [(i, i ^ bit) for i in range(n)])  146 us
    pallas_call x42, Pallas kernels, kernel_call(): pl.pallas_call(body, out_shape=outs, in_specs=[pl.BlockSpec(memory_space=...  131 us
    ppermute x56, starting transfers between devices, swap(): return lax.ppermute(x, axis, [(i, i ^ bit) for i in range(n)])  68.2 us
    unnamed x200, local copies, waits for them, and re-layouts  48.6 us
    all_to_all x7, starting transfers between devices, to_owners(): lax.all_to_all(x.reshape((owners, x.shape[0] // owners) + x.shape[1:]), '...  37.6 us
    all_to_all x7, waiting for transfers between devices, to_owners(): lax.all_to_all(x.reshape((owners, x.shape[0] // owners) + x.shape[1:]), '...  27 us
  transfers between devices with their start and end apart: 63, of which 25 were waited for; matrix products, arithmetic and copies ran while one was open for 0% of the time, Pallas kernels for 28%

profile of v5, /device:TPU:0, one launch (start us, length us, event | category | flops | bytes accessed | tf_op | source)
XLA Modules:
  0.0 463.8 jit_solution(4365502710264188812)
XLA Ops:
  12.6 6.0 %all-to-all-start = ((bf16[8,32,2048]{2,1,0:T(8,128)(2,1)}), bf16[8,32,2048]{2,1,0:T(8,128)(2,1)S(1)}, u32[]{:S(2)}, u32[]{:S(2)}) async-start(bf16[8,32,2048]{2,1,0:T(8,128)(2,1)} %bitcast.4), calls=%async_computation | async-start | bytes 2097152 | tf_op jit(solution)/shard_map/all_to_all | solution.py:730
  24.3 13.4 %collective-permute-done.1.b_ref = bf16[64,1024]{1,0:T(8,128)(2,1)S(1)} collective-permute-done((bf16[64,1024]{1,0:T(8,128)(2,1)S(1)}, bf16[64,1024]{1,0:T(8,128)(2,1)S(1)}, u32[]{:S(2)}, u32[]{:S(2)}) %collective-permute-start.1) | collective-permute-done | bytes 131104 | tf_op jit(solution)/shard_map/ppermute | solution.py:21
  37.7 5.2 %collective-permute-start.2 = (bf16[128,1024]{1,0:T(8,128)(2,1)S(1)}, bf16[128,1024]{1,0:T(8,128)(2,1)S(1)}, u32[]{:S(2)}, u32[]{:S(2)}) collective-permute-start(bf16[128,1024]{1,0:T(8,128)(2,1)S(1)} %shard_map.219.a_ref), channel_id=1, source_target_pairs={{0,16},{4,20},{8,24},{12,28},{16,0},{20,4},{24,8},{28,12},{1,17},{... | collective-permute-start | bytes 786440 | tf_op jit(solution)/shard_map/ppermute | solution.py:21
  42.9 12.1 %collective-permute-done.2.b_ref = bf16[128,1024]{1,0:T(8,128)(2,1)S(1)} collective-permute-done((bf16[128,1024]{1,0:T(8,128)(2,1)S(1)}, bf16[128,1024]{1,0:T(8,128)(2,1)S(1)}, u32[]{:S(2)}, u32[]{:S(2)}) %collective-permute-start.2) | collective-permute-done | bytes 262176 | tf_op jit(solution)/shard_map/ppermute | solution.py:21
  55.8 6.0 %shard_map.217 = (bf16[384,3072]{1,0:T(8,128)(2,1)}, s32[384,1]{1,0:T(8,128)S(1)}, s32[256,1]{1,0:T(8,128)S(1)}) custom-call(s32[1]{0:T(128)} %bitcast.2.base_ref, bf16[256,2048]{1,0:T(8,128)(2,1)S(1)} %bitcast.22, s32[384,1]{1,0:T(8,128)S(1)} %copy-done.60, s32[384,1]{1,0:T(8,128)S(1)} %copy-done.62, bf16[588,3000]{1,0:T(8,128)(2,1)} %table_ref.3), custom_call_target="tpu_custom_call" | custom-call | flops 4000000000 | bytes 6941508 | tf_op jit(solution)/shard_map/pallas_call | solution.py:42
  63.1 4.7 %all-to-all-start.1 = ((bf16[8,48,3072]{2,1,0:T(8,128)(2,1)}), bf16[8,48,3072]{2,1,0:T(8,128)(2,1)}, u32[]{:S(2)}, u32[]{:S(2)}) async-start(bf16[8,48,3072]{2,1,0:T(8,128)(2,1)} %bitcast.8), calls=%async_computation.1 | async-start | bytes 4718592 | tf_op jit(solution)/shard_map/all_to_all | solution.py:730
  74.1 14.2 %collective-permute-done.5.refs_2_.refs_3_ = bf16[512,768]{1,0:T(8,128)(2,1)S(1)} collective-permute-done((bf16[512,768]{1,0:T(8,128)(2,1)S(1)}, bf16[512,768]{1,0:T(8,128)(2,1)S(1)}, u32[]{:S(2)}, u32[]{:S(2)}) %collective-permute-start.5) | collective-permute-done | bytes 786464 | tf_op jit(solution)/shard_map/ppermute | solution.py:21
  93.6 13.8 %collective-permute-done.4.b_ref = bf16[256,1024]{1,0:T(8,128)(2,1)} collective-permute-done((bf16[256,1024]{1,0:T(8,128)(2,1)}, bf16[256,1024]{1,0:T(8,128)(2,1)}, u32[]{:S(2)}, u32[]{:S(2)}) %collective-permute-start.4) | collective-permute-done | bytes 524320 | tf_op jit(solution)/shard_map/ppermute | solution.py:21
  112.7 10.1 %collective-permute-done.6.refs_3_.refs_4_ = bf16[512,768]{1,0:T(8,128)(2,1)} collective-permute-done((bf16[512,768]{1,0:T(8,128)(2,1)S(1)}, bf16[512,768]{1,0:T(8,128)(2,1)}, u32[]{:S(2)}, u32[]{:S(2)}) %collective-permute-start.6) | collective-permute-done | bytes 786464 | tf_op jit(solution)/shard_map/ppermute | solution.py:21
  126.1 12.0 %shard_map.224 = (bf16[320,1024]{1,0:T(8,128)(2,1)S(1)}, f32[5,256,1024]{2,1,0:T(8,128)}) custom-call(s32[2]{0:T(128)S(1)} %pad_add_fusion.l_ref, f32[256,1]{1,0:T(8,128)S(1)} %reshape.149.keep_ref, s32[256,1]{1,0:T(8,128)S(1)} %copy-done.86, s32[256,1]{1,0:T(8,128)S(1)} %copy-done.18, bf16[256,2048]{1,0:T(8,128)(2,1)S(1)} %bitcast.24, ...), custom_call_target="tpu_custom_call" | custom-call | flops 12000000000 | bytes 15600648 | tf_op jit(solution)/shard_map/pallas_call | solution.py:42
  142.2 4.7 %all-to-all-start.2 = ((bf16[8,48,1024]{2,1,0:T(8,128)(2,1)}), bf16[8,48,1024]{2,1,0:T(8,128)(2,1)S(1)}, u32[]{:S(2)}, u32[]{:S(2)}) async-start(bf16[8,48,1024]{2,1,0:T(8,128)(2,1)} %bitcast.28), calls=%async_computation.2 | async-start | bytes 1572864 | tf_op jit(solution)/shard_map/all_to_all | solution.py:730
  149.2 12.0 %shard_map.226 = (bf16[320,1024]{1,0:T(8,128)(2,1)S(1)}, f32[5,256,1024]{2,1,0:T(8,128)}) custom-call(s32[2]{0:T(128)S(1)} %pad_add_fusion.l_ref, f32[256,1]{1,0:T(8,128)S(1)} %reshape.149.keep_ref, s32[256,1]{1,0:T(8,128)S(1)} %copy-done.19, bf16[256,2048]{1,0:T(8,128)(2,1)S(1)} %bitcast.25, bf16[320,1024]{1,0:T(8,128)(2,1)S(1)} %copy-done.9, ...), custom_call_target="tpu_custom_call" | custom-call | bytes 20187144 | tf_op jit(solution)/shard_map/pallas_call | solution.py:42
  169.8 10.7 %shard_map.227 = (bf16[256,512]{1,0:T(8,128)(2,1)S(1)}, bf16[256,512]{1,0:T(8,128)(2,1)S(1)}, bf16[256,512]{1,0:T(8,128)(2,1)S(1)}, bf16[256,512]{1,0:T(8,128)(2...) custom-call(f32[256,1]{1,0:T(8,128)S(1)} %div.11.valid_ref, s32[256,1]{1,0:T(8,128)S(1)} %copy-done.89, ...), custom_call_target="tpu_custom_call" | custom-call | flops 12000000000 | bytes 8521728 | tf_op jit(solution)/shard_map/pallas_call | solution.py:42
  185.8 16.3 %shard_map.228 = (f32[64,1024]{1,0:T(8,128)S(1)}, f32[256,1024]{1,0:T(8,128)}, bf16[256,768]{1,0:T(8,128)(2,1)S(1)}, bf16[256,768]{1,0:T(8,128)(2,1)S(1)}, bf16[...) custom-call(s32[2]{0:T(128)S(1)} %pad_add_fusion.l_ref, ...), custom_call_target="tpu_custom_call" | custom-call | flops 16999999488 | bytes 23331848 | tf_op jit(solution)/shard_map/pallas_call | solution.py:42
  205.6 4.7 %all-to-all-start.3 = ((bf16[8,48,1024]{2,1,0:T(8,128)(2,1)}), bf16[8,48,1024]{2,1,0:T(8,128)(2,1)S(1)}, u32[]{:S(2)}, u32[]{:S(2)}) async-start(bf16[8,48,1024]{2,1,0:T(8,128)(2,1)} %bitcast.12), calls=%async_computation.3 | async-start | bytes 1572864 | tf_op jit(solution)/shard_map/all_to_all | solution.py:730
  212.8 13.4 %shard_map.229 = (f32[64,1024]{1,0:T(8,128)S(1)}, bf16[256,3072]{1,0:T(8,128)(2,1)}, bf16[272,768]{1,0:T(8,128)(2,1)S(1)}, bf16[272,768]{1,0:T(8,128)(2,1)S(1)},...) custom-call(s32[2]{0:T(128)S(1)} %pad_add_fusion.l_ref, f32[256,1]{1,0:T(8,128)S(1)} %reshape.149.keep_ref, ...), custom_call_target="tpu_custom_call" | custom-call | flops 12999999488 | bytes 16090120 | tf_op jit(solution)/shard_map/pallas_call | solution.py:42
  234.6 6.0 %all-to-all-start.4 = ((bf16[8,48,3072]{2,1,0:T(8,128)(2,1)}), bf16[8,48,3072]{2,1,0:T(8,128)(2,1)}, u32[]{:S(2)}, u32[]{:S(2)}) async-start(bf16[8,48,3072]{2,1,0:T(8,128)(2,1)} %bitcast.14), calls=%async_computation.4 | async-start | bytes 4718592 | tf_op jit(solution)/shard_map/all_to_all | solution.py:730
  255.4 7.4 %collective-permute-done.27.refs_7_ = bf16[272,768]{1,0:T(8,128)(2,1)S(1)} collective-permute-done((bf16[272,768]{1,0:T(8,128)(2,1)}, bf16[272,768]{1,0:T(8,128)(2,1)S(1)}, u32[]{:S(2)}, u32[]{:S(2)}) %collective-permute-start.27) | collective-permute-done | bytes 417824 | tf_op jit(solution)/shard_map/ppermute | solution.py:21
  268.9 26.2 %all-to-all-done.4 = bf16[8,48,3072]{2,1,0:T(8,128)(2,1)} async-done(((bf16[8,48,3072]{2,1,0:T(8,128)(2,1)}), bf16[8,48,3072]{2,1,0:T(8,128)(2,1)}, u32[]{:S(2)}, u32[]{:S(2)}) %all-to-all-start.4) | async-done | bytes 2359328 | tf_op jit(solution)/shard_map/all_to_all | solution.py:730
  295.1 3.9 all-to-all-start.5
  301.1 4.6 shard_map.241
  312.8 3.9 shard_map.231
  319.8 7.8 %collective-permute-done.39.b_ref = bf16[256,768]{1,0:T(8,128)(2,1)S(1)} collective-permute-done((bf16[256,768]{1,0:T(8,128)(2,1)S(1)}, bf16[256,768]{1,0:T(8,128)(2,1)S(1)}, u32[]{:S(2)}, u32[]{:S(2)}) %collective-permute-start.39) | collective-permute-done | bytes 393248 | tf_op jit(solution)/shard_map/ppermute | solution.py:21
  342.8 3.5 shard_map.235
  346.3 7.5 %all-to-all-start.6 = ((bf16[8,64,1024]{2,1,0:T(8,128)(2,1)}), bf16[8,64,1024]{2,1,0:T(8,128)(2,1)}, u32[]{:S(2)}, u32[]{:S(2)}) async-start(bf16[8,64,1024]{2,1,0:T(8,128)(2,1)} %bitcast.18), calls=%async_computation.6 | async-start | bytes 2097152 | tf_op jit(solution)/shard_map/all_to_all | solution.py:730
  361.9 12.1 %collective-permute-start.49 = (bf16[256,768]{1,0:T(8,128)(2,1)S(1)}, bf16[256,768]{1,0:T(8,128)(2,1)S(1)}, u32[]{:S(2)}, u32[]{:S(2)}) collective-permute-start(bf16[256,768]{1,0:T(8,128)(2,1)S(1)} %shard_map.247.a_ref), channel_id=1, source_target_pairs={{0,16},{4,20},{8,24},{12,28},{16,0},{20,4},{24,8},{28,12},{1,17},{... | collective-permute-start | bytes 1179656 | tf_op jit(solution)/shard_map/ppermute | solution.py:21
  374.0 17.2 %collective-permute-done.48.b_ref = bf16[256,768]{1,0:T(8,128)(2,1)S(1)} collective-permute-done((bf16[256,768]{1,0:T(8,128)(2,1)S(1)}, bf16[256,768]{1,0:T(8,128)(2,1)S(1)}, u32[]{:S(2)}, u32[]{:S(2)}) %collective-permute-start.48) | collective-permute-done | bytes 393248 | tf_op jit(solution)/shard_map/ppermute | solution.py:21
  391.2 8.4 %collective-permute-done.47.b_ref = bf16[256,768]{1,0:T(8,128)(2,1)S(1)} collective-permute-done((bf16[256,768]{1,0:T(8,128)(2,1)S(1)}, bf16[256,768]{1,0:T(8,128)(2,1)S(1)}, u32[]{:S(2)}, u32[]{:S(2)}) %collective-permute-start.47) | collective-permute-done | bytes 393248 | tf_op jit(solution)/shard_map/ppermute | solution.py:21
  410.6 9.2 %collective-permute-done.52.b_ref = bf16[256,768]{1,0:T(8,128)(2,1)S(1)} collective-permute-done((bf16[256,768]{1,0:T(8,128)(2,1)S(1)}, bf16[256,768]{1,0:T(8,128)(2,1)S(1)}, u32[]{:S(2)}, u32[]{:S(2)}) %collective-permute-start.52) | collective-permute-done | bytes 393248 | tf_op jit(solution)/shard_map/ppermute | solution.py:21
  429.8 5.5 %collective-permute-done.53.b_ref = bf16[256,768]{1,0:T(8,128)(2,1)} collective-permute-done((bf16[256,768]{1,0:T(8,128)(2,1)}, bf16[256,768]{1,0:T(8,128)(2,1)}, u32[]{:S(2)}, u32[]{:S(2)}) %collective-permute-start.53) | collective-permute-done | bytes 393248 | tf_op jit(solution)/shard_map/ppermute | solution.py:21
  436.4 4.9 %collective-permute-done.54.b_ref = bf16[512,768]{1,0:T(8,128)(2,1)} collective-permute-done((bf16[512,768]{1,0:T(8,128)(2,1)}, bf16[512,768]{1,0:T(8,128)(2,1)}, u32[]{:S(2)}, u32[]{:S(2)}) %collective-permute-start.54) | collective-permute-done | bytes 786464 | tf_op jit(solution)/shard_map/ppermute | solution.py:21
  453.2 5.4 %collective-permute-done.55.b_ref = bf16[512,768]{1,0:T(8,128)(2,1)S(1)} collective-permute-done((bf16[512,768]{1,0:T(8,128)(2,1)S(1)}, bf16[512,768]{1,0:T(8,128)(2,1)S(1)}, u32[]{:S(2)}, u32[]{:S(2)}) %collective-permute-start.55) | collective-permute-done | bytes 786464 | tf_op jit(solution)/shard_map/ppermute | solution.py:21
  (356 shorter events, 169.3 us)
Async XLA Ops:
  12.6 43.2 %all-to-all-start = ((bf16[8,32,2048]{2,1,0:T(8,128)(2,1)}), bf16[8,32,2048]{2,1,0:T(8,128)(2,1)S(1)}, u32[]{:S(2)}, u32[]{:S(2)}) async-start(bf16[8,32,2048]{2,1,0:T(8,128)(2,1)} %bitcast.4), calls=%async_computation | async-start | bytes 2097152 | tf_op jit(solution)/shard_map/all_to_all | solution.py:730
  18.6 44.5 %collective-permute-start.3 = (bf16[896,768]{1,0:T(8,128)(2,1)S(1)}, bf16[896,768]{1,0:T(8,128)(2,1)}, u32[]{:S(2)}, u32[]{:S(2)}) collective-permute-start(bf16[896,768]{1,0:T(8,128)(2,1)S(1)} %get-tuple-element.132), channel_id=1, source_target_pairs={{0,2},{1,3},{2,0},{3,1},{4,6},{5,7},{6,4},{7,5},{8,10},{9,11},{10,... | collective-permute-start | bytes 4128776 | tf_op jit(solution)/shard_map/ppermute | solution.py:21
  63.1 59.7 %all-to-all-start.1 = ((bf16[8,48,3072]{2,1,0:T(8,128)(2,1)}), bf16[8,48,3072]{2,1,0:T(8,128)(2,1)}, u32[]{:S(2)}, u32[]{:S(2)}) async-start(bf16[8,48,3072]{2,1,0:T(8,128)(2,1)} %bitcast.8), calls=%async_computation.1 | async-start | bytes 4718592 | tf_op jit(solution)/shard_map/all_to_all | solution.py:730
  71.6 51.7 %collective-permute-start.7 = (bf16[1024,768]{1,0:T(8,128)(2,1)}, bf16[1024,768]{1,0:T(8,128)(2,1)}, u32[]{:S(2)}, u32[]{:S(2)}) collective-permute-start(bf16[1024,768]{1,0:T(8,128)(2,1)} %get-tuple-element.120.refs_0_.refs_1_), channel_id=1, source_target_pairs={{0,1},{1,0},{2,3},{3,2},{4,5},{5,4},{6,7},{7,6},{8,9},{9,8},{10,11... | collective-permute-start | bytes 4718600 | tf_op jit(solution)/shard_map/ppermute | solution.py:21
  71.6 51.7 %collective-permute-start.9 = (bf16[896,768]{1,0:T(8,128)(2,1)}, bf16[896,768]{1,0:T(8,128)(2,1)}, u32[]{:S(2)}, u32[]{:S(2)}) collective-permute-start(bf16[896,768]{1,0:T(8,128)(2,1)} %collective-permute-done.3.refs_3_.refs_4_), channel_id=1, source_target_pairs={{0,1},{1,0},{2,3},{3,2},{4,5},{5,4},{6,7},{7,6},{8,9},{9,8},{10,11... | collective-permute-start | bytes 4128776 | tf_op jit(solution)/shard_map/ppermute | solution.py:21
  72.2 35.2 %collective-permute-start.4 = (bf16[256,1024]{1,0:T(8,128)(2,1)}, bf16[256,1024]{1,0:T(8,128)(2,1)}, u32[]{:S(2)}, u32[]{:S(2)}) collective-permute-start(bf16[256,1024]{1,0:T(8,128)(2,1)} %shard_map.220.a_ref), channel_id=1, source_target_pairs={{0,4},{4,0},{8,12},{12,8},{16,20},{20,16},{24,28},{28,24},{1,5},{5... | collective-permute-start | bytes 1572872 | tf_op jit(solution)/shard_map/ppermute | solution.py:21
  88.3 34.5 %collective-permute-start.6 = (bf16[512,768]{1,0:T(8,128)(2,1)S(1)}, bf16[512,768]{1,0:T(8,128)(2,1)}, u32[]{:S(2)}, u32[]{:S(2)}) collective-permute-start(bf16[512,768]{1,0:T(8,128)(2,1)S(1)} %collective-permute-done.5.refs_2_.refs_3_), channel_id=1, source_target_pairs={{0,4},{4,0},{8,12},{12,8},{16,20},{20,16},{24,28},{28,24},{1,5},{5... | collective-permute-start | bytes 2359304 | tf_op jit(solution)/shard_map/ppermute | solution.py:21
  91.9 47.1 %collective-permute-start.14 = (bf16[1024,768]{1,0:T(8,128)(2,1)}, bf16[1024,768]{1,0:T(8,128)(2,1)}, u32[]{:S(2)}, u32[]{:S(2)}) collective-permute-start(bf16[1024,768]{1,0:T(8,128)(2,1)} %shard_map.225.refs_6_.refs_7_), channel_id=1, source_target_pairs={{0,2},{1,3},{2,0},{3,1},{4,6},{5,7},{6,4},{7,5},{8,10},{9,11},{10,... | collective-permute-start | bytes 4718600 | tf_op jit(solution)/shard_map/ppermute | solution.py:21
  122.8 24.0 %collective-permute-start.13 = (bf16[1024,768]{1,0:T(8,128)(2,1)}, bf16[1024,768]{1,0:T(8,128)(2,1)}, u32[]{:S(2)}, u32[]{:S(2)}) collective-permute-start(bf16[1024,768]{1,0:T(8,128)(2,1)} %shard_map.225.refs_6_.refs_7_), channel_id=1, source_target_pairs={{0,1},{1,0},{2,3},{3,2},{4,5},{5,4},{6,7},{7,6},{8,9},{9,8},{10,11... | collective-permute-start | bytes 4718600 | tf_op jit(solution)/shard_map/ppermute | solution.py:21
  139.0 25.9 %collective-permute-start.17 = (bf16[512,1024]{1,0:T(8,128)(2,1)}, bf16[512,1024]{1,0:T(8,128)(2,1)}, u32[]{:S(2)}, u32[]{:S(2)}) collective-permute-start(bf16[512,1024]{1,0:T(8,128)(2,1)} %shard_map.222.refs_0_), channel_id=1, source_target_pairs={{0,2},{1,3},{2,0},{3,1},{4,6},{5,7},{6,4},{7,5},{8,10},{9,11},{10,... | collective-permute-start | bytes 3145736 | tf_op jit(solution)/shard_map/ppermute | solution.py:21
  142.2 25.2 %all-to-all-start.2 = ((bf16[8,48,1024]{2,1,0:T(8,128)(2,1)}), bf16[8,48,1024]{2,1,0:T(8,128)(2,1)S(1)}, u32[]{:S(2)}, u32[]{:S(2)}) async-start(bf16[8,48,1024]{2,1,0:T(8,128)(2,1)} %bitcast.28), calls=%async_computation.2 | async-start | bytes 1572864 | tf_op jit(solution)/shard_map/all_to_all | solution.py:730
  184.3 26.0 %collective-permute-start.20 = (bf16[320,1024]{1,0:T(8,128)(2,1)S(1)}, bf16[320,1024]{1,0:T(8,128)(2,1)S(1)}, u32[]{:S(2)}, u32[]{:S(2)}) collective-permute-start(bf16[320,1024]{1,0:T(8,128)(2,1)S(1)} %copy-done.10), channel_id=1, source_target_pairs={{0,2},{1,3},{2,0},{3,1},{4,6},{5,7},{6,4},{7,5},{8,10},{9,11},{10,... | collective-permute-start | bytes 1966088 | tf_op jit(solution)/shard_map/ppermute | solution.py:21
  204.4 24.9 %collective-permute-start.21 = (bf16[256,768]{1,0:T(8,128)(2,1)}, bf16[256,768]{1,0:T(8,128)(2,1)S(1)}, u32[]{:S(2)}, u32[]{:S(2)}) collective-permute-start(bf16[256,768]{1,0:T(8,128)(2,1)} %get-tuple-element.157), channel_id=1, source_target_pairs={{0,2},{1,3},{2,0},{3,1},{4,6},{5,7},{6,4},{7,5},{8,10},{9,11},{10,... | collective-permute-start | bytes 1179656 | tf_op jit(solution)/shard_map/ppermute | solution.py:21
  204.9 24.4 %collective-permute-start.22 = (bf16[256,768]{1,0:T(8,128)(2,1)}, bf16[256,768]{1,0:T(8,128)(2,1)S(1)}, u32[]{:S(2)}, u32[]{:S(2)}) collective-permute-start(bf16[256,768]{1,0:T(8,128)(2,1)} %get-tuple-element.158), channel_id=1, source_target_pairs={{0,3},{1,2},{2,1},{3,0},{4,7},{5,6},{6,5},{7,4},{8,11},{9,10},{10,... | collective-permute-start | bytes 1179656 | tf_op jit(solution)/shard_map/ppermute | solution.py:21
  205.6 28.1 %all-to-all-start.3 = ((bf16[8,48,1024]{2,1,0:T(8,128)(2,1)}), bf16[8,48,1024]{2,1,0:T(8,128)(2,1)S(1)}, u32[]{:S(2)}, u32[]{:S(2)}) async-start(bf16[8,48,1024]{2,1,0:T(8,128)(2,1)} %bitcast.12), calls=%async_computation.3 | async-start | bytes 1572864 | tf_op jit(solution)/shard_map/all_to_all | solution.py:730
  234.6 60.5 %all-to-all-start.4 = ((bf16[8,48,3072]{2,1,0:T(8,128)(2,1)}), bf16[8,48,3072]{2,1,0:T(8,128)(2,1)}, u32[]{:S(2)}, u32[]{:S(2)}) async-start(bf16[8,48,3072]{2,1,0:T(8,128)(2,1)} %bitcast.14), calls=%async_computation.4 | async-start | bytes 4718592 | tf_op jit(solution)/shard_map/all_to_all | solution.py:730
  244.6 54.5 %collective-permute-start.34 = (bf16[320,1024]{1,0:T(8,128)(2,1)}, bf16[320,1024]{1,0:T(8,128)(2,1)}, u32[]{:S(2)}, u32[]{:S(2)}) collective-permute-start(bf16[320,1024]{1,0:T(8,128)(2,1)} %collective-permute-done.19.refs_6_.refs_2_), channel_id=1, source_target_pairs={{0,1},{1,0},{2,3},{3,2},{4,5},{5,4},{6,7},{7,6},{8,9},{9,8},{10,11... | collective-permute-start | bytes 1966088 | tf_op jit(solution)/shard_map/ppermute | solution.py:21
  252.9 46.1 %collective-permute-start.40 = (bf16[256,768]{1,0:T(8,128)(2,1)}, bf16[256,768]{1,0:T(8,128)(2,1)S(1)}, u32[]{:S(2)}, u32[]{:S(2)}) collective-permute-start(bf16[256,768]{1,0:T(8,128)(2,1)} %get-tuple-element.203), channel_id=1, source_target_pairs={{0,1},{1,0},{2,3},{3,2},{4,5},{5,4},{6,7},{7,6},{8,9},{9,8},{10,11... | collective-permute-start | bytes 1179656 | tf_op jit(solution)/shard_map/ppermute | solution.py:21
  253.1 45.9 %collective-permute-start.41 = (bf16[256,768]{1,0:T(8,128)(2,1)}, bf16[256,768]{1,0:T(8,128)(2,1)S(1)}, u32[]{:S(2)}, u32[]{:S(2)}) collective-permute-start(bf16[256,768]{1,0:T(8,128)(2,1)} %get-tuple-element.204), channel_id=1, source_target_pairs={{0,2},{1,3},{2,0},{3,1},{4,6},{5,7},{6,4},{7,5},{8,10},{9,11},{10,... | collective-permute-start | bytes 1179656 | tf_op jit(solution)/shard_map/ppermute | solution.py:21
  255.4 43.6 %collective-permute-start.42 = (bf16[256,768]{1,0:T(8,128)(2,1)}, bf16[256,768]{1,0:T(8,128)(2,1)}, u32[]{:S(2)}, u32[]{:S(2)}) collective-permute-start(bf16[256,768]{1,0:T(8,128)(2,1)} %get-tuple-element.205), channel_id=1, source_target_pairs={{0,3},{1,2},{2,1},{3,0},{4,7},{5,6},{6,5},{7,4},{8,11},{9,10},{10,... | collective-permute-start | bytes 1179656 | tf_op jit(solution)/shard_map/ppermute | solution.py:21
  262.8 43.9 %collective-permute-start.38 = (bf16[512,768]{1,0:T(8,128)(2,1)S(1)}, bf16[512,768]{1,0:T(8,128)(2,1)}, u32[]{:S(2)}, u32[]{:S(2)}) collective-permute-start(bf16[512,768]{1,0:T(8,128)(2,1)S(1)} %get-tuple-element.199), channel_id=1, source_target_pairs={{0,4},{4,0},{8,12},{12,8},{16,20},{20,16},{24,28},{28,24},{1,5},{5... | collective-permute-start | bytes 2359304 | tf_op jit(solution)/shard_map/ppermute | solution.py:21
  295.1 51.2 %all-to-all-start.5 = ((bf16[8,32,2048]{2,1,0:T(8,128)(2,1)}), bf16[8,32,2048]{2,1,0:T(8,128)(2,1)S(1)}, u32[]{:S(2)}, u32[]{:S(2)}) async-start(bf16[8,32,2048]{2,1,0:T(8,128)(2,1)} %bitcast.16), calls=%async_computation.5 | async-start | bytes 2097152 | tf_op jit(solution)/shard_map/all_to_all | solution.py:730
  306.7 24.2 %collective-permute-start.43 = (bf16[512,768]{1,0:T(8,128)(2,1)}, bf16[512,768]{1,0:T(8,128)(2,1)}, u32[]{:S(2)}, u32[]{:S(2)}) collective-permute-start(bf16[512,768]{1,0:T(8,128)(2,1)} %get-tuple-element.207), channel_id=1, source_target_pairs={{0,4},{4,0},{8,12},{12,8},{16,20},{20,16},{24,28},{28,24},{1,5},{5... | collective-permute-start | bytes 2359304 | tf_op jit(solution)/shard_map/ppermute | solution.py:21
  319.3 87.5 %collective-permute-start.28 = (bf16[2,160,3072]{2,1,0:T(8,128)(2,1)S(1)}, bf16[2,160,3072]{2,1,0:T(8,128)(2,1)}, u32[]{:S(2)}, u32[]{:S(2)}) collective-permute-start(bf16[2,160,3072]{2,1,0:T(8,128)(2,1)S(1)} %get-tuple-element.176), channel_id=1, source_target_pairs={{0,1},{1,0},{2,3},{3,2},{4,5},{5,4},{6,7},{7,6},{8,9},{9,8},{10,11... | collective-permute-start | bytes 5898248 | tf_op jit(solution)/shard_map/ppermute | solution.py:21
  330.9 27.5 %collective-permute-start.44 = (bf16[512,768]{1,0:T(8,128)(2,1)}, bf16[512,768]{1,0:T(8,128)(2,1)}, u32[]{:S(2)}, u32[]{:S(2)}) collective-permute-start(bf16[512,768]{1,0:T(8,128)(2,1)} %get-tuple-element.208), channel_id=1, source_target_pairs={{0,4},{4,0},{8,12},{12,8},{16,20},{20,16},{24,28},{28,24},{1,5},{5... | collective-permute-start | bytes 2359304 | tf_op jit(solution)/shard_map/ppermute | solution.py:21
  331.8 22.0 %collective-permute-start.45 = (bf16[256,768]{1,0:T(8,128)(2,1)S(1)}, bf16[256,768]{1,0:T(8,128)(2,1)}, u32[]{:S(2)}, u32[]{:S(2)}) collective-permute-start(bf16[256,768]{1,0:T(8,128)(2,1)S(1)} %shard_map.243.a_ref), channel_id=1, source_target_pairs={{0,16},{4,20},{8,24},{12,28},{16,0},{20,4},{24,8},{28,12},{1,17},{... | collective-permute-start | bytes 1179656 | tf_op jit(solution)/shard_map/ppermute | solution.py:21
  346.3 79.4 %all-to-all-start.6 = ((bf16[8,64,1024]{2,1,0:T(8,128)(2,1)}), bf16[8,64,1024]{2,1,0:T(8,128)(2,1)}, u32[]{:S(2)}, u32[]{:S(2)}) async-start(bf16[8,64,1024]{2,1,0:T(8,128)(2,1)} %bitcast.18), calls=%async_computation.6 | async-start | bytes 2097152 | tf_op jit(solution)/shard_map/all_to_all | solution.py:730
  358.4 32.7 %collective-permute-start.48 = (bf16[256,768]{1,0:T(8,128)(2,1)S(1)}, bf16[256,768]{1,0:T(8,128)(2,1)S(1)}, u32[]{:S(2)}, u32[]{:S(2)}) collective-permute-start(bf16[256,768]{1,0:T(8,128)(2,1)S(1)} %shard_map.246.a_ref), channel_id=1, source_target_pairs={{0,8},{4,12},{8,0},{12,4},{16,24},{20,28},{24,16},{28,20},{1,9},{5... | collective-permute-start | bytes 1179656 | tf_op jit(solution)/shard_map/ppermute | solution.py:21
  359.8 39.7 %collective-permute-start.47 = (bf16[256,768]{1,0:T(8,128)(2,1)S(1)}, bf16[256,768]{1,0:T(8,128)(2,1)S(1)}, u32[]{:S(2)}, u32[]{:S(2)}) collective-permute-start(bf16[256,768]{1,0:T(8,128)(2,1)S(1)} %get-tuple-element.216), channel_id=1, source_target_pairs={{0,8},{4,12},{8,0},{12,4},{16,24},{20,28},{24,16},{28,20},{1,9},{5... | collective-permute-start | bytes 1179656 | tf_op jit(solution)/shard_map/ppermute | solution.py:21
  361.9 37.7 %collective-permute-start.49 = (bf16[256,768]{1,0:T(8,128)(2,1)S(1)}, bf16[256,768]{1,0:T(8,128)(2,1)S(1)}, u32[]{:S(2)}, u32[]{:S(2)}) collective-permute-start(bf16[256,768]{1,0:T(8,128)(2,1)S(1)} %shard_map.247.a_ref), channel_id=1, source_target_pairs={{0,16},{4,20},{8,24},{12,28},{16,0},{20,4},{24,8},{28,12},{1,17},{... | collective-permute-start | bytes 1179656 | tf_op jit(solution)/shard_map/ppermute | solution.py:21
  399.6 24.2 %collective-permute-start.51 = (bf16[512,768]{1,0:T(8,128)(2,1)S(1)}, bf16[512,768]{1,0:T(8,128)(2,1)S(1)}, u32[]{:S(2)}, u32[]{:S(2)}) collective-permute-start(bf16[512,768]{1,0:T(8,128)(2,1)S(1)} %shard_map.249.a_ref), channel_id=1, source_target_pairs={{0,4},{4,0},{8,12},{12,8},{16,20},{20,16},{24,28},{28,24},{1,5},{5... | collective-permute-start | bytes 2359304 | tf_op jit(solution)/shard_map/ppermute | solution.py:21
  410.2 31.2 %collective-permute-start.29 = (bf16[160,3072]{1,0:T(8,128)(2,1)}, bf16[160,3072]{1,0:T(8,128)(2,1)}, u32[]{:S(2)}, u32[]{:S(2)}) collective-permute-start(bf16[160,3072]{1,0:T(8,128)(2,1)} %get-tuple-element.178), channel_id=1, source_target_pairs={{0,2},{1,3},{2,0},{3,1},{4,6},{5,7},{6,4},{7,5},{8,10},{9,11},{10,... | collective-permute-start | bytes 2949128 | tf_op jit(solution)/shard_map/ppermute | solution.py:21
  (131 other events, 1080.3 us)

commit v6 on v5

--- a/solution.py
+++ b/solution.py
@@ -832,7 +832,7 @@
             pltpu.VMEM((n_loc, neg_part, wide), BF16),
             pltpu.SemaphoreType.DMA((n_loc,)),
         ],
-        12, n_loc,
+        3, n_loc,
     )
     init_two, into_first, *ch_two = kernel_call(
         functools.partial(back_second_kernel, (steps, batch, hidden, chunk, n_loc), n_w, n_loc),

time: 470 us -> 467 us (level)
  waiting for transfers between devices: 173 us -> 182 us
  local copies, waits for them, and re-layouts: 51.3 us -> 42.4 us
  starting transfers between devices: 106 us -> 101 us
    unnamed x200 -> x174, local copies, waits for them, and re-layouts: 48.6 us -> 39.7 us
    ppermute x56, waiting for transfers between devices: 146 us -> 153 us  [swap(): return lax.ppermute(x, axis, [(i, i ^ bit) for i in range(n)])]
  transfers between devices with their start and end apart: 63 -> 63, of which waited for: 25 -> 28; matrix products, arithmetic and copies ran while one was open for 0% -> 0% of each run, Pallas kernels for 28% -> 28%
where the time goes in v6:
time: 467 us; the launch traced here: 461 us
  waiting for transfers between devices  182 us (39%)
  Pallas kernels  134 us (29%)
  starting transfers between devices  101 us (22%)
  local copies, waits for them, and re-layouts  42.4 us (9%)
    ppermute x56, waiting for transfers between devices, swap(): return lax.ppermute(x, axis, [(i, i ^ bit) for i in range(n)])  153 us
    pallas_call x42, Pallas kernels, kernel_call(): pl.pallas_call(body, out_shape=outs, in_specs=[pl.BlockSpec(memory_space=...  134 us
    ppermute x56, starting transfers between devices, swap(): return lax.ppermute(x, axis, [(i, i ^ bit) for i in range(n)])  65.2 us
    unnamed x174, local copies, waits for them, and re-layouts  39.7 us
    all_to_all x7, starting transfers between devices, to_owners(): lax.all_to_all(x.reshape((owners, x.shape[0] // owners) + x.shape[1:]), '...  35.3 us
    all_to_all x7, waiting for transfers between devices, to_owners(): lax.all_to_all(x.reshape((owners, x.shape[0] // owners) + x.shape[1:]), '...  28.3 us
  transfers between devices with their start and end apart: 63, of which 28 were waited for; matrix products, arithmetic and copies ran while one was open for 0% of the time, Pallas kernels for 28%

profile of v6, /device:TPU:0, one launch (start us, length us, event | category | flops | bytes accessed | tf_op | source)
XLA Modules:
  0.0 461.1 jit_solution(15538571072977681951)
XLA Ops:
  12.7 6.0 %all-to-all-start = ((bf16[8,32,2048]{2,1,0:T(8,128)(2,1)}), bf16[8,32,2048]{2,1,0:T(8,128)(2,1)S(1)}, u32[]{:S(2)}, u32[]{:S(2)}) async-start(bf16[8,32,2048]{2,1,0:T(8,128)(2,1)} %bitcast.4), calls=%async_computation | async-start | bytes 2097152 | tf_op jit(solution)/shard_map/all_to_all | solution.py:730
  24.4 13.3 %collective-permute-done.1.b_ref = bf16[64,1024]{1,0:T(8,128)(2,1)S(1)} collective-permute-done((bf16[64,1024]{1,0:T(8,128)(2,1)S(1)}, bf16[64,1024]{1,0:T(8,128)(2,1)S(1)}, u32[]{:S(2)}, u32[]{:S(2)}) %collective-permute-start.1) | collective-permute-done | bytes 131104 | tf_op jit(solution)/shard_map/ppermute | solution.py:21
  37.8 5.2 %collective-permute-start.2 = (bf16[128,1024]{1,0:T(8,128)(2,1)S(1)}, bf16[128,1024]{1,0:T(8,128)(2,1)S(1)}, u32[]{:S(2)}, u32[]{:S(2)}) collective-permute-start(bf16[128,1024]{1,0:T(8,128)(2,1)S(1)} %shard_map.219.a_ref), channel_id=1, source_target_pairs={{0,16},{4,20},{8,24},{12,28},{16,0},{20,4},{24,8},{28,12},{1,17},{... | collective-permute-start | bytes 786440 | tf_op jit(solution)/shard_map/ppermute | solution.py:21
  43.0 12.1 %collective-permute-done.2.b_ref = bf16[128,1024]{1,0:T(8,128)(2,1)S(1)} collective-permute-done((bf16[128,1024]{1,0:T(8,128)(2,1)S(1)}, bf16[128,1024]{1,0:T(8,128)(2,1)S(1)}, u32[]{:S(2)}, u32[]{:S(2)}) %collective-permute-start.2) | collective-permute-done | bytes 262176 | tf_op jit(solution)/shard_map/ppermute | solution.py:21
  55.9 6.0 %shard_map.217 = (bf16[384,3072]{1,0:T(8,128)(2,1)}, s32[384,1]{1,0:T(8,128)S(1)}, s32[256,1]{1,0:T(8,128)S(1)}) custom-call(s32[1]{0:T(128)} %bitcast.2.base_ref, bf16[256,2048]{1,0:T(8,128)(2,1)S(1)} %bitcast.22, s32[384,1]{1,0:T(8,128)S(1)} %copy-done.46, s32[384,1]{1,0:T(8,128)S(1)} %copy-done.48, bf16[588,3000]{1,0:T(8,128)(2,1)} %table_ref.3), custom_call_target="tpu_custom_call" | custom-call | flops 4000000000 | bytes 6941508 | tf_op jit(solution)/shard_map/pallas_call | solution.py:42
  63.2 4.7 %all-to-all-start.1 = ((bf16[8,48,3072]{2,1,0:T(8,128)(2,1)}), bf16[8,48,3072]{2,1,0:T(8,128)(2,1)}, u32[]{:S(2)}, u32[]{:S(2)}) async-start(bf16[8,48,3072]{2,1,0:T(8,128)(2,1)} %bitcast.8), calls=%async_computation.1 | async-start | bytes 4718592 | tf_op jit(solution)/shard_map/all_to_all | solution.py:730
  74.2 14.2 %collective-permute-done.5.refs_2_.refs_3_ = bf16[512,768]{1,0:T(8,128)(2,1)S(1)} collective-permute-done((bf16[512,768]{1,0:T(8,128)(2,1)S(1)}, bf16[512,768]{1,0:T(8,128)(2,1)S(1)}, u32[]{:S(2)}, u32[]{:S(2)}) %collective-permute-start.5) | collective-permute-done | bytes 786464 | tf_op jit(solution)/shard_map/ppermute | solution.py:21
  93.7 13.8 %collective-permute-done.4.b_ref = bf16[256,1024]{1,0:T(8,128)(2,1)} collective-permute-done((bf16[256,1024]{1,0:T(8,128)(2,1)}, bf16[256,1024]{1,0:T(8,128)(2,1)}, u32[]{:S(2)}, u32[]{:S(2)}) %collective-permute-start.4) | collective-permute-done | bytes 524320 | tf_op jit(solution)/shard_map/ppermute | solution.py:21
  112.9 10.0 %collective-permute-done.6.refs_3_.refs_4_ = bf16[512,768]{1,0:T(8,128)(2,1)} collective-permute-done((bf16[512,768]{1,0:T(8,128)(2,1)S(1)}, bf16[512,768]{1,0:T(8,128)(2,1)}, u32[]{:S(2)}, u32[]{:S(2)}) %collective-permute-start.6) | collective-permute-done | bytes 786464 | tf_op jit(solution)/shard_map/ppermute | solution.py:21
  125.3 11.9 %shard_map.224 = (bf16[320,1024]{1,0:T(8,128)(2,1)S(1)}, f32[5,256,1024]{2,1,0:T(8,128)}) custom-call(s32[2]{0:T(128)S(1)} %pad_add_fusion.l_ref, f32[256,1]{1,0:T(8,128)S(1)} %reshape.149.keep_ref, s32[256,1]{1,0:T(8,128)S(1)} %copy-done.75, s32[256,1]{1,0:T(8,128)S(1)} %copy-done.18, bf16[256,2048]{1,0:T(8,128)(2,1)S(1)} %bitcast.24, ...), custom_call_target="tpu_custom_call" | custom-call | flops 12000000000 | bytes 15600648 | tf_op jit(solution)/shard_map/pallas_call | solution.py:42
  141.3 4.7 %all-to-all-start.2 = ((bf16[8,48,1024]{2,1,0:T(8,128)(2,1)}), bf16[8,48,1024]{2,1,0:T(8,128)(2,1)S(1)}, u32[]{:S(2)}, u32[]{:S(2)}) async-start(bf16[8,48,1024]{2,1,0:T(8,128)(2,1)} %bitcast.28), calls=%async_computation.2 | async-start | bytes 1572864 | tf_op jit(solution)/shard_map/all_to_all | solution.py:730
  148.3 13.0 %shard_map.226 = (bf16[320,1024]{1,0:T(8,128)(2,1)}, f32[5,256,1024]{2,1,0:T(8,128)}) custom-call(s32[2]{0:T(128)S(1)} %pad_add_fusion.l_ref, f32[256,1]{1,0:T(8,128)S(1)} %reshape.149.keep_ref, s32[256,1]{1,0:T(8,128)S(1)} %copy-done.19, bf16[256,2048]{1,0:T(8,128)(2,1)S(1)} %bitcast.25, bf16[320,1024]{1,0:T(8,128)(2,1)S(1)} %copy-done.9, ...), custom_call_target="tpu_custom_call" | custom-call | bytes 20187144 | tf_op jit(solution)/shard_map/pallas_call | solution.py:42
  168.8 11.8 %shard_map.227 = (bf16[256,512]{1,0:T(8,128)(2,1)S(1)}, bf16[256,512]{1,0:T(8,128)(2,1)S(1)}, bf16[256,512]{1,0:T(8,128)(2,1)S(1)}, bf16[256,512]{1,0:T(8,128)(2...) custom-call(f32[256,1]{1,0:T(8,128)S(1)} %div.11.valid_ref, s32[256,1]{1,0:T(8,128)S(1)} %copy-done.65, ...), custom_call_target="tpu_custom_call" | custom-call | flops 3000000000 | bytes 8521728 | tf_op jit(solution)/shard_map/pallas_call | solution.py:42
  185.3 16.3 %shard_map.228 = (f32[64,1024]{1,0:T(8,128)S(1)}, f32[256,1024]{1,0:T(8,128)}, bf16[256,768]{1,0:T(8,128)(2,1)S(1)}, bf16[256,768]{1,0:T(8,128)(2,1)S(1)}, bf16[...) custom-call(s32[2]{0:T(128)S(1)} %pad_add_fusion.l_ref, ...), custom_call_target="tpu_custom_call" | custom-call | flops 16999999488 | bytes 23331848 | tf_op jit(solution)/shard_map/pallas_call | solution.py:42
  205.9 4.7 %all-to-all-start.3 = ((bf16[8,48,1024]{2,1,0:T(8,128)(2,1)}), bf16[8,48,1024]{2,1,0:T(8,128)(2,1)S(1)}, u32[]{:S(2)}, u32[]{:S(2)}) async-start(bf16[8,48,1024]{2,1,0:T(8,128)(2,1)} %bitcast.12), calls=%async_computation.3 | async-start | bytes 1572864 | tf_op jit(solution)/shard_map/all_to_all | solution.py:730
  212.2 13.1 %shard_map.229 = (f32[64,1024]{1,0:T(8,128)S(1)}, bf16[256,3072]{1,0:T(8,128)(2,1)}, bf16[272,768]{1,0:T(8,128)(2,1)S(1)}, bf16[272,768]{1,0:T(8,128)(2,1)S(1)},...) custom-call(s32[2]{0:T(128)S(1)} %pad_add_fusion.l_ref, f32[256,1]{1,0:T(8,128)S(1)} %reshape.149.keep_ref, ...), custom_call_target="tpu_custom_call" | custom-call | flops 12999999488 | bytes 16090120 | tf_op jit(solution)/shard_map/pallas_call | solution.py:42
  232.8 5.0 %all-to-all-start.4 = ((bf16[8,48,3072]{2,1,0:T(8,128)(2,1)}), bf16[8,48,3072]{2,1,0:T(8,128)(2,1)}, u32[]{:S(2)}, u32[]{:S(2)}) async-start(bf16[8,48,3072]{2,1,0:T(8,128)(2,1)} %bitcast.14), calls=%async_computation.4 | async-start | bytes 4718592 | tf_op jit(solution)/shard_map/all_to_all | solution.py:730
  252.4 7.3 %collective-permute-done.27.refs_7_ = bf16[272,768]{1,0:T(8,128)(2,1)S(1)} collective-permute-done((bf16[272,768]{1,0:T(8,128)(2,1)S(1)}, bf16[272,768]{1,0:T(8,128)(2,1)S(1)}, u32[]{:S(2)}, u32[]{:S(2)}) %collective-permute-start.27) | collective-permute-done | bytes 417824 | tf_op jit(solution)/shard_map/ppermute | solution.py:21
  265.9 26.5 %all-to-all-done.4 = bf16[8,48,3072]{2,1,0:T(8,128)(2,1)} async-done(((bf16[8,48,3072]{2,1,0:T(8,128)(2,1)}), bf16[8,48,3072]{2,1,0:T(8,128)(2,1)}, u32[]{:S(2)}, u32[]{:S(2)}) %all-to-all-start.4) | async-done | bytes 2359328 | tf_op jit(solution)/shard_map/all_to_all | solution.py:730
  292.3 3.9 all-to-all-start.5
  296.3 5.0 %shard_map.241 = (bf16[512,768]{1,0:T(8,128)(2,1)S(1)}, bf16[512,768]{1,0:T(8,128)(2,1)}) custom-call(s32[1]{0:T(128)} %bitcast.1.l_ref, bf16[320,1024]{1,0:T(8,128)(2,1)} %get-tuple-element.149.state_ref.refs_4_.refs_0_, bf16[320,1024]{1,0:T(8,128)(2,1)S(1)} %copy-done.31, bf16[320,1024]{1,0:T(8,128)(2,1)} %collective-permute-done.19.refs_6_.refs_2_, ...), custom_call_target="tpu_custom_call" | custom-call | flops 5000000000 | bytes 5767172 | tf_op jit(solution)/shard_map/pallas_call | solution.py:42
  308.4 3.9 shard_map.231
  315.4 9.0 %collective-permute-done.39.b_ref = bf16[256,768]{1,0:T(8,128)(2,1)S(1)} collective-permute-done((bf16[256,768]{1,0:T(8,128)(2,1)S(1)}, bf16[256,768]{1,0:T(8,128)(2,1)S(1)}, u32[]{:S(2)}, u32[]{:S(2)}) %collective-permute-start.39) | collective-permute-done | bytes 393248 | tf_op jit(solution)/shard_map/ppermute | solution.py:21
  340.1 3.7 shard_map.235
  343.8 6.3 %all-to-all-start.6 = ((bf16[8,64,1024]{2,1,0:T(8,128)(2,1)}), bf16[8,64,1024]{2,1,0:T(8,128)(2,1)}, u32[]{:S(2)}, u32[]{:S(2)}) async-start(bf16[8,64,1024]{2,1,0:T(8,128)(2,1)} %bitcast.18), calls=%async_computation.6 | async-start | bytes 2097152 | tf_op jit(solution)/shard_map/all_to_all | solution.py:730
  358.5 11.4 %collective-permute-start.49 = (bf16[256,768]{1,0:T(8,128)(2,1)S(1)}, bf16[256,768]{1,0:T(8,128)(2,1)S(1)}, u32[]{:S(2)}, u32[]{:S(2)}) collective-permute-start(bf16[256,768]{1,0:T(8,128)(2,1)S(1)} %shard_map.247.a_ref), channel_id=1, source_target_pairs={{0,16},{4,20},{8,24},{12,28},{16,0},{20,4},{24,8},{28,12},{1,17},{... | collective-permute-start | bytes 1179656 | tf_op jit(solution)/shard_map/ppermute | solution.py:21
  369.9 17.2 %collective-permute-done.48.b_ref = bf16[256,768]{1,0:T(8,128)(2,1)S(1)} collective-permute-done((bf16[256,768]{1,0:T(8,128)(2,1)S(1)}, bf16[256,768]{1,0:T(8,128)(2,1)S(1)}, u32[]{:S(2)}, u32[]{:S(2)}) %collective-permute-start.48) | collective-permute-done | bytes 393248 | tf_op jit(solution)/shard_map/ppermute | solution.py:21
  387.2 8.4 %collective-permute-done.47.b_ref = bf16[256,768]{1,0:T(8,128)(2,1)S(1)} collective-permute-done((bf16[256,768]{1,0:T(8,128)(2,1)S(1)}, bf16[256,768]{1,0:T(8,128)(2,1)S(1)}, u32[]{:S(2)}, u32[]{:S(2)}) %collective-permute-start.47) | collective-permute-done | bytes 393248 | tf_op jit(solution)/shard_map/ppermute | solution.py:21
  406.8 9.0 %collective-permute-done.52.b_ref = bf16[256,768]{1,0:T(8,128)(2,1)S(1)} collective-permute-done((bf16[256,768]{1,0:T(8,128)(2,1)S(1)}, bf16[256,768]{1,0:T(8,128)(2,1)S(1)}, u32[]{:S(2)}, u32[]{:S(2)}) %collective-permute-start.52) | collective-permute-done | bytes 393248 | tf_op jit(solution)/shard_map/ppermute | solution.py:21
  426.1 5.8 %collective-permute-done.53.b_ref = bf16[256,768]{1,0:T(8,128)(2,1)} collective-permute-done((bf16[256,768]{1,0:T(8,128)(2,1)}, bf16[256,768]{1,0:T(8,128)(2,1)}, u32[]{:S(2)}, u32[]{:S(2)}) %collective-permute-start.53) | collective-permute-done | bytes 393248 | tf_op jit(solution)/shard_map/ppermute | solution.py:21
  433.1 5.5 %collective-permute-done.54.b_ref = bf16[512,768]{1,0:T(8,128)(2,1)} collective-permute-done((bf16[512,768]{1,0:T(8,128)(2,1)}, bf16[512,768]{1,0:T(8,128)(2,1)}, u32[]{:S(2)}, u32[]{:S(2)}) %collective-permute-start.54) | collective-permute-done | bytes 786464 | tf_op jit(solution)/shard_map/ppermute | solution.py:21
  449.9 6.1 %collective-permute-done.55.b_ref = bf16[512,768]{1,0:T(8,128)(2,1)S(1)} collective-permute-done((bf16[512,768]{1,0:T(8,128)(2,1)S(1)}, bf16[512,768]{1,0:T(8,128)(2,1)S(1)}, u32[]{:S(2)}, u32[]{:S(2)}) %collective-permute-start.55) | collective-permute-done | bytes 786464 | tf_op jit(solution)/shard_map/ppermute | solution.py:21
  (330 shorter events, 164.6 us)
Async XLA Ops:
  12.7 43.2 %all-to-all-start = ((bf16[8,32,2048]{2,1,0:T(8,128)(2,1)}), bf16[8,32,2048]{2,1,0:T(8,128)(2,1)S(1)}, u32[]{:S(2)}, u32[]{:S(2)}) async-start(bf16[8,32,2048]{2,1,0:T(8,128)(2,1)} %bitcast.4), calls=%async_computation | async-start | bytes 2097152 | tf_op jit(solution)/shard_map/all_to_all | solution.py:730
  18.7 44.5 %collective-permute-start.3 = (bf16[896,768]{1,0:T(8,128)(2,1)S(1)}, bf16[896,768]{1,0:T(8,128)(2,1)}, u32[]{:S(2)}, u32[]{:S(2)}) collective-permute-start(bf16[896,768]{1,0:T(8,128)(2,1)S(1)} %get-tuple-element.132), channel_id=1, source_target_pairs={{0,2},{1,3},{2,0},{3,1},{4,6},{5,7},{6,4},{7,5},{8,10},{9,11},{10,... | collective-permute-start | bytes 4128776 | tf_op jit(solution)/shard_map/ppermute | solution.py:21
  63.2 59.7 %all-to-all-start.1 = ((bf16[8,48,3072]{2,1,0:T(8,128)(2,1)}), bf16[8,48,3072]{2,1,0:T(8,128)(2,1)}, u32[]{:S(2)}, u32[]{:S(2)}) async-start(bf16[8,48,3072]{2,1,0:T(8,128)(2,1)} %bitcast.8), calls=%async_computation.1 | async-start | bytes 4718592 | tf_op jit(solution)/shard_map/all_to_all | solution.py:730
  71.7 51.8 %collective-permute-start.7 = (bf16[1024,768]{1,0:T(8,128)(2,1)}, bf16[1024,768]{1,0:T(8,128)(2,1)}, u32[]{:S(2)}, u32[]{:S(2)}) collective-permute-start(bf16[1024,768]{1,0:T(8,128)(2,1)} %get-tuple-element.120.refs_0_.refs_1_), channel_id=1, source_target_pairs={{0,1},{1,0},{2,3},{3,2},{4,5},{5,4},{6,7},{7,6},{8,9},{9,8},{10,11... | collective-permute-start | bytes 4718600 | tf_op jit(solution)/shard_map/ppermute | solution.py:21
  71.7 51.8 %collective-permute-start.9 = (bf16[896,768]{1,0:T(8,128)(2,1)}, bf16[896,768]{1,0:T(8,128)(2,1)}, u32[]{:S(2)}, u32[]{:S(2)}) collective-permute-start(bf16[896,768]{1,0:T(8,128)(2,1)} %collective-permute-done.3.refs_3_.refs_4_), channel_id=1, source_target_pairs={{0,1},{1,0},{2,3},{3,2},{4,5},{5,4},{6,7},{7,6},{8,9},{9,8},{10,11... | collective-permute-start | bytes 4128776 | tf_op jit(solution)/shard_map/ppermute | solution.py:21
  72.2 35.3 %collective-permute-start.4 = (bf16[256,1024]{1,0:T(8,128)(2,1)}, bf16[256,1024]{1,0:T(8,128)(2,1)}, u32[]{:S(2)}, u32[]{:S(2)}) collective-permute-start(bf16[256,1024]{1,0:T(8,128)(2,1)} %shard_map.220.a_ref), channel_id=1, source_target_pairs={{0,4},{4,0},{8,12},{12,8},{16,20},{20,16},{24,28},{28,24},{1,5},{5... | collective-permute-start | bytes 1572872 | tf_op jit(solution)/shard_map/ppermute | solution.py:21
  88.4 34.5 %collective-permute-start.6 = (bf16[512,768]{1,0:T(8,128)(2,1)S(1)}, bf16[512,768]{1,0:T(8,128)(2,1)}, u32[]{:S(2)}, u32[]{:S(2)}) collective-permute-start(bf16[512,768]{1,0:T(8,128)(2,1)S(1)} %collective-permute-done.5.refs_2_.refs_3_), channel_id=1, source_target_pairs={{0,4},{4,0},{8,12},{12,8},{16,20},{20,16},{24,28},{28,24},{1,5},{5... | collective-permute-start | bytes 2359304 | tf_op jit(solution)/shard_map/ppermute | solution.py:21
  92.0 46.1 %collective-permute-start.14 = (bf16[1024,768]{1,0:T(8,128)(2,1)}, bf16[1024,768]{1,0:T(8,128)(2,1)}, u32[]{:S(2)}, u32[]{:S(2)}) collective-permute-start(bf16[1024,768]{1,0:T(8,128)(2,1)} %shard_map.225.refs_6_.refs_7_), channel_id=1, source_target_pairs={{0,2},{1,3},{2,0},{3,1},{4,6},{5,7},{6,4},{7,5},{8,10},{9,11},{10,... | collective-permute-start | bytes 4718600 | tf_op jit(solution)/shard_map/ppermute | solution.py:21
  122.9 23.1 %collective-permute-start.13 = (bf16[1024,768]{1,0:T(8,128)(2,1)}, bf16[1024,768]{1,0:T(8,128)(2,1)}, u32[]{:S(2)}, u32[]{:S(2)}) collective-permute-start(bf16[1024,768]{1,0:T(8,128)(2,1)} %shard_map.225.refs_6_.refs_7_), channel_id=1, source_target_pairs={{0,1},{1,0},{2,3},{3,2},{4,5},{5,4},{6,7},{7,6},{8,9},{9,8},{10,11... | collective-permute-start | bytes 4718600 | tf_op jit(solution)/shard_map/ppermute | solution.py:21
  138.1 25.9 %collective-permute-start.17 = (bf16[512,1024]{1,0:T(8,128)(2,1)}, bf16[512,1024]{1,0:T(8,128)(2,1)}, u32[]{:S(2)}, u32[]{:S(2)}) collective-permute-start(bf16[512,1024]{1,0:T(8,128)(2,1)} %shard_map.222.refs_0_), channel_id=1, source_target_pairs={{0,2},{1,3},{2,0},{3,1},{4,6},{5,7},{6,4},{7,5},{8,10},{9,11},{10,... | collective-permute-start | bytes 3145736 | tf_op jit(solution)/shard_map/ppermute | solution.py:21
  141.3 25.2 %all-to-all-start.2 = ((bf16[8,48,1024]{2,1,0:T(8,128)(2,1)}), bf16[8,48,1024]{2,1,0:T(8,128)(2,1)S(1)}, u32[]{:S(2)}, u32[]{:S(2)}) async-start(bf16[8,48,1024]{2,1,0:T(8,128)(2,1)} %bitcast.28), calls=%async_computation.2 | async-start | bytes 1572864 | tf_op jit(solution)/shard_map/all_to_all | solution.py:730
  183.8 26.9 %collective-permute-start.20 = (bf16[320,1024]{1,0:T(8,128)(2,1)S(1)}, bf16[320,1024]{1,0:T(8,128)(2,1)S(1)}, u32[]{:S(2)}, u32[]{:S(2)}) collective-permute-start(bf16[320,1024]{1,0:T(8,128)(2,1)S(1)} %copy-done.10), channel_id=1, source_target_pairs={{0,2},{1,3},{2,0},{3,1},{4,6},{5,7},{6,4},{7,5},{8,10},{9,11},{10,... | collective-permute-start | bytes 1966088 | tf_op jit(solution)/shard_map/ppermute | solution.py:21
  204.7 22.0 %collective-permute-start.21 = (bf16[256,768]{1,0:T(8,128)(2,1)}, bf16[256,768]{1,0:T(8,128)(2,1)}, u32[]{:S(2)}, u32[]{:S(2)}) collective-permute-start(bf16[256,768]{1,0:T(8,128)(2,1)} %get-tuple-element.157), channel_id=1, source_target_pairs={{0,2},{1,3},{2,0},{3,1},{4,6},{5,7},{6,4},{7,5},{8,10},{9,11},{10,... | collective-permute-start | bytes 1179656 | tf_op jit(solution)/shard_map/ppermute | solution.py:21
  205.2 21.5 %collective-permute-start.22 = (bf16[256,768]{1,0:T(8,128)(2,1)}, bf16[256,768]{1,0:T(8,128)(2,1)}, u32[]{:S(2)}, u32[]{:S(2)}) collective-permute-start(bf16[256,768]{1,0:T(8,128)(2,1)} %get-tuple-element.158), channel_id=1, source_target_pairs={{0,3},{1,2},{2,1},{3,0},{4,7},{5,6},{6,5},{7,4},{8,11},{9,10},{10,... | collective-permute-start | bytes 1179656 | tf_op jit(solution)/shard_map/ppermute | solution.py:21
  205.9 25.9 %all-to-all-start.3 = ((bf16[8,48,1024]{2,1,0:T(8,128)(2,1)}), bf16[8,48,1024]{2,1,0:T(8,128)(2,1)S(1)}, u32[]{:S(2)}, u32[]{:S(2)}) async-start(bf16[8,48,1024]{2,1,0:T(8,128)(2,1)} %bitcast.12), calls=%async_computation.3 | async-start | bytes 1572864 | tf_op jit(solution)/shard_map/all_to_all | solution.py:730
  232.8 59.5 %all-to-all-start.4 = ((bf16[8,48,3072]{2,1,0:T(8,128)(2,1)}), bf16[8,48,3072]{2,1,0:T(8,128)(2,1)}, u32[]{:S(2)}, u32[]{:S(2)}) async-start(bf16[8,48,3072]{2,1,0:T(8,128)(2,1)} %bitcast.14), calls=%async_computation.4 | async-start | bytes 4718592 | tf_op jit(solution)/shard_map/all_to_all | solution.py:730
  241.8 54.5 %collective-permute-start.34 = (bf16[320,1024]{1,0:T(8,128)(2,1)}, bf16[320,1024]{1,0:T(8,128)(2,1)}, u32[]{:S(2)}, u32[]{:S(2)}) collective-permute-start(bf16[320,1024]{1,0:T(8,128)(2,1)} %collective-permute-done.19.refs_6_.refs_2_), channel_id=1, source_target_pairs={{0,1},{1,0},{2,3},{3,2},{4,5},{5,4},{6,7},{7,6},{8,9},{9,8},{10,11... | collective-permute-start | bytes 1966088 | tf_op jit(solution)/shard_map/ppermute | solution.py:21
  249.3 46.9 %collective-permute-start.40 = (bf16[256,768]{1,0:T(8,128)(2,1)}, bf16[256,768]{1,0:T(8,128)(2,1)}, u32[]{:S(2)}, u32[]{:S(2)}) collective-permute-start(bf16[256,768]{1,0:T(8,128)(2,1)} %get-tuple-element.203), channel_id=1, source_target_pairs={{0,1},{1,0},{2,3},{3,2},{4,5},{5,4},{6,7},{7,6},{8,9},{9,8},{10,11... | collective-permute-start | bytes 1179656 | tf_op jit(solution)/shard_map/ppermute | solution.py:21
  249.4 46.8 %collective-permute-start.41 = (bf16[256,768]{1,0:T(8,128)(2,1)}, bf16[256,768]{1,0:T(8,128)(2,1)}, u32[]{:S(2)}, u32[]{:S(2)}) collective-permute-start(bf16[256,768]{1,0:T(8,128)(2,1)} %get-tuple-element.204), channel_id=1, source_target_pairs={{0,2},{1,3},{2,0},{3,1},{4,6},{5,7},{6,4},{7,5},{8,10},{9,11},{10,... | collective-permute-start | bytes 1179656 | tf_op jit(solution)/shard_map/ppermute | solution.py:21
  252.4 43.9 %collective-permute-start.42 = (bf16[256,768]{1,0:T(8,128)(2,1)}, bf16[256,768]{1,0:T(8,128)(2,1)}, u32[]{:S(2)}, u32[]{:S(2)}) collective-permute-start(bf16[256,768]{1,0:T(8,128)(2,1)} %get-tuple-element.205), channel_id=1, source_target_pairs={{0,3},{1,2},{2,1},{3,0},{4,7},{5,6},{6,5},{7,4},{8,11},{9,10},{10,... | collective-permute-start | bytes 1179656 | tf_op jit(solution)/shard_map/ppermute | solution.py:21
  259.7 42.5 %collective-permute-start.38 = (bf16[512,768]{1,0:T(8,128)(2,1)S(1)}, bf16[512,768]{1,0:T(8,128)(2,1)}, u32[]{:S(2)}, u32[]{:S(2)}) collective-permute-start(bf16[512,768]{1,0:T(8,128)(2,1)S(1)} %get-tuple-element.199), channel_id=1, source_target_pairs={{0,4},{4,0},{8,12},{12,8},{16,20},{20,16},{24,28},{28,24},{1,5},{5... | collective-permute-start | bytes 2359304 | tf_op jit(solution)/shard_map/ppermute | solution.py:21
  292.3 51.5 %all-to-all-start.5 = ((bf16[8,32,2048]{2,1,0:T(8,128)(2,1)}), bf16[8,32,2048]{2,1,0:T(8,128)(2,1)S(1)}, u32[]{:S(2)}, u32[]{:S(2)}) async-start(bf16[8,32,2048]{2,1,0:T(8,128)(2,1)} %bitcast.16), calls=%async_computation.5 | async-start | bytes 2097152 | tf_op jit(solution)/shard_map/all_to_all | solution.py:730
  302.2 25.3 %collective-permute-start.43 = (bf16[512,768]{1,0:T(8,128)(2,1)}, bf16[512,768]{1,0:T(8,128)(2,1)}, u32[]{:S(2)}, u32[]{:S(2)}) collective-permute-start(bf16[512,768]{1,0:T(8,128)(2,1)} %get-tuple-element.207), channel_id=1, source_target_pairs={{0,4},{4,0},{8,12},{12,8},{16,20},{20,16},{24,28},{28,24},{1,5},{5... | collective-permute-start | bytes 2359304 | tf_op jit(solution)/shard_map/ppermute | solution.py:21
  314.9 88.1 %collective-permute-start.28 = (bf16[2,160,3072]{2,1,0:T(8,128)(2,1)S(1)}, bf16[2,160,3072]{2,1,0:T(8,128)(2,1)}, u32[]{:S(2)}, u32[]{:S(2)}) collective-permute-start(bf16[2,160,3072]{2,1,0:T(8,128)(2,1)S(1)} %get-tuple-element.176), channel_id=1, source_target_pairs={{0,1},{1,0},{2,3},{3,2},{4,5},{5,4},{6,7},{7,6},{8,9},{9,8},{10,11... | collective-permute-start | bytes 5898248 | tf_op jit(solution)/shard_map/ppermute | solution.py:21
  327.6 27.5 %collective-permute-start.44 = (bf16[512,768]{1,0:T(8,128)(2,1)}, bf16[512,768]{1,0:T(8,128)(2,1)}, u32[]{:S(2)}, u32[]{:S(2)}) collective-permute-start(bf16[512,768]{1,0:T(8,128)(2,1)} %get-tuple-element.208), channel_id=1, source_target_pairs={{0,4},{4,0},{8,12},{12,8},{16,20},{20,16},{24,28},{28,24},{1,5},{5... | collective-permute-start | bytes 2359304 | tf_op jit(solution)/shard_map/ppermute | solution.py:21
  328.9 21.6 %collective-permute-start.45 = (bf16[256,768]{1,0:T(8,128)(2,1)S(1)}, bf16[256,768]{1,0:T(8,128)(2,1)}, u32[]{:S(2)}, u32[]{:S(2)}) collective-permute-start(bf16[256,768]{1,0:T(8,128)(2,1)S(1)} %shard_map.243.a_ref), channel_id=1, source_target_pairs={{0,16},{4,20},{8,24},{12,28},{16,0},{20,4},{24,8},{28,12},{1,17},{... | collective-permute-start | bytes 1179656 | tf_op jit(solution)/shard_map/ppermute | solution.py:21
  343.8 78.2 %all-to-all-start.6 = ((bf16[8,64,1024]{2,1,0:T(8,128)(2,1)}), bf16[8,64,1024]{2,1,0:T(8,128)(2,1)}, u32[]{:S(2)}, u32[]{:S(2)}) async-start(bf16[8,64,1024]{2,1,0:T(8,128)(2,1)} %bitcast.18), calls=%async_computation.6 | async-start | bytes 2097152 | tf_op jit(solution)/shard_map/all_to_all | solution.py:730
  355.0 32.1 %collective-permute-start.48 = (bf16[256,768]{1,0:T(8,128)(2,1)S(1)}, bf16[256,768]{1,0:T(8,128)(2,1)S(1)}, u32[]{:S(2)}, u32[]{:S(2)}) collective-permute-start(bf16[256,768]{1,0:T(8,128)(2,1)S(1)} %shard_map.246.a_ref), channel_id=1, source_target_pairs={{0,8},{4,12},{8,0},{12,4},{16,24},{20,28},{24,16},{28,20},{1,9},{5... | collective-permute-start | bytes 1179656 | tf_op jit(solution)/shard_map/ppermute | solution.py:21
  356.5 39.1 %collective-permute-start.47 = (bf16[256,768]{1,0:T(8,128)(2,1)S(1)}, bf16[256,768]{1,0:T(8,128)(2,1)S(1)}, u32[]{:S(2)}, u32[]{:S(2)}) collective-permute-start(bf16[256,768]{1,0:T(8,128)(2,1)S(1)} %get-tuple-element.216), channel_id=1, source_target_pairs={{0,8},{4,12},{8,0},{12,4},{16,24},{20,28},{24,16},{28,20},{1,9},{5... | collective-permute-start | bytes 1179656 | tf_op jit(solution)/shard_map/ppermute | solution.py:21
  358.5 37.0 %collective-permute-start.49 = (bf16[256,768]{1,0:T(8,128)(2,1)S(1)}, bf16[256,768]{1,0:T(8,128)(2,1)S(1)}, u32[]{:S(2)}, u32[]{:S(2)}) collective-permute-start(bf16[256,768]{1,0:T(8,128)(2,1)S(1)} %shard_map.247.a_ref), channel_id=1, source_target_pairs={{0,16},{4,20},{8,24},{12,28},{16,0},{20,4},{24,8},{28,12},{1,17},{... | collective-permute-start | bytes 1179656 | tf_op jit(solution)/shard_map/ppermute | solution.py:21
  395.5 24.5 %collective-permute-start.51 = (bf16[512,768]{1,0:T(8,128)(2,1)S(1)}, bf16[512,768]{1,0:T(8,128)(2,1)S(1)}, u32[]{:S(2)}, u32[]{:S(2)}) collective-permute-start(bf16[512,768]{1,0:T(8,128)(2,1)S(1)} %shard_map.249.a_ref), channel_id=1, source_target_pairs={{0,4},{4,0},{8,12},{12,8},{16,20},{20,16},{24,28},{28,24},{1,5},{5... | collective-permute-start | bytes 2359304 | tf_op jit(solution)/shard_map/ppermute | solution.py:21
  406.3 32.3 %collective-permute-start.29 = (bf16[160,3072]{1,0:T(8,128)(2,1)}, bf16[160,3072]{1,0:T(8,128)(2,1)}, u32[]{:S(2)}, u32[]{:S(2)}) collective-permute-start(bf16[160,3072]{1,0:T(8,128)(2,1)} %get-tuple-element.178), channel_id=1, source_target_pairs={{0,2},{1,3},{2,0},{3,1},{4,6},{5,7},{6,4},{7,5},{8,10},{9,11},{10,... | collective-permute-start | bytes 2949128 | tf_op jit(solution)/shard_map/ppermute | solution.py:21
  (118 other events, 1094.9 us)

commit v7 on v6

--- a/solution.py
+++ b/solution.py
@@ -326,13 +326,15 @@
     send_ref[...] = (far_ref[...] + got_ref[1].astype(F32)).astype(BF16)
 
 
-def table_out_kernel(parts, sum_ref, got_ref, out_ref):
+def table_out_kernel(parts, sum_ref, got_ref, out_ref, *bias_ref):
     rows, cols = out_ref.shape
     total = (sum_ref[...] + got_ref[...].astype(F32))[:rows]
     wide = total.shape[1] // parts
     size = cols // parts
     split = [total[:, g * wide : g * wide + size] for g in range(parts)]
-    out_ref[...] = jnp.concatenate(split, axis=1)
+    out_ref[...] = jnp.concatenate(split, axis=1) if parts > 1 else split[0]
+    for ref in bias_ref:
+        ref[...] = total[:, cols : cols + 1]
 
 
 def carry_kernel(slot_ref, got_ref, out_ref):
@@ -957,9 +959,8 @@
         return total, across(far_s)
 
     def table_end(pair, cols, parts):
-        return kernel_call(
-            functools.partial(table_out_kernel, parts), [shape((own, cols), F32)], list(pair)
-        )[0]
+        outs = [shape((own, cols), F32)] + [shape((own, 1), F32)] * (parts == 1)
+        return kernel_call(functools.partial(table_out_kernel, parts), outs, list(pair))
 
     sums = {}
 
@@ -998,16 +999,16 @@
     grad_two, _ = finish(two_parts, hidden)
     grad_one, bias_one = finish(one_parts, bias_row)
 
-    table_in = table_end(sums["table"], gates, 3)
+    (table_in,) = table_end(sums["table"], gates, 3)
     neg_ids = jnp.broadcast_to(mine[None, :], (owners, neg_own)).reshape(neg_part)
-    table_out = table_end(table_start([tg_ids, neg_ids], [got_tg_g, got_neg_g]), wide, 1)
+    table_out, table_bias = table_end(table_start([tg_ids, neg_ids], [got_tg_g, got_neg_g]), hidden, 1)
     grad_carried = kernel_call(
         carry_kernel, [shape((2, batch, hidden), F32)], [slot_pl, got_back]
     )[0]
     return (
         table_in,
-        table_out[:, :hidden],
-        table_out[:, hidden],
+        table_out,
+        table_bias[:, 0],
         grad_one,
         grad_in,
         grad_two,

time: 467 us -> 466 us (level)
  no operation moved by 1% of the time
where the time goes in v7:
time: 466 us; the launch traced here: 460 us
  waiting for transfers between devices  182 us (39%)
  Pallas kernels  134 us (29%)
  starting transfers between devices  100 us (21%)
  local copies, waits for them, and re-layouts  40.7 us (9%)
    ppermute x56, waiting for transfers between devices, swap(): return lax.ppermute(x, axis, [(i, i ^ bit) for i in range(n)])  154 us
    pallas_call x42, Pallas kernels, kernel_call(): pl.pallas_call(body, out_shape=outs, in_specs=[pl.BlockSpec(memory_space=...  134 us
    ppermute x56, starting transfers between devices, swap(): return lax.ppermute(x, axis, [(i, i ^ bit) for i in range(n)])  65.1 us
    unnamed x174, local copies, waits for them, and re-layouts  39.6 us
    all_to_all x7, starting transfers between devices, to_owners(): lax.all_to_all(x.reshape((owners, x.shape[0] // owners) + x.shape[1:]), '...  35.3 us
    all_to_all x7, waiting for transfers between devices, to_owners(): lax.all_to_all(x.reshape((owners, x.shape[0] // owners) + x.shape[1:]), '...  28.3 us
  transfers between devices with their start and end apart: 63, of which 28 were waited for; matrix products, arithmetic and copies ran while one was open for 0% of the time, Pallas kernels for 28%

profile of v7, /device:TPU:0, one launch (start us, length us, event | category | flops | bytes accessed | tf_op | source)
XLA Modules:
  0.0 460.1 jit_solution(12240553237498446557)
XLA Ops:
  12.7 6.0 %all-to-all-start = ((bf16[8,32,2048]{2,1,0:T(8,128)(2,1)}), bf16[8,32,2048]{2,1,0:T(8,128)(2,1)S(1)}, u32[]{:S(2)}, u32[]{:S(2)}) async-start(bf16[8,32,2048]{2,1,0:T(8,128)(2,1)} %bitcast.4), calls=%async_computation | async-start | bytes 2097152 | tf_op jit(solution)/shard_map/all_to_all | solution.py:732
  24.4 13.3 %collective-permute-done.1.b_ref = bf16[64,1024]{1,0:T(8,128)(2,1)S(1)} collective-permute-done((bf16[64,1024]{1,0:T(8,128)(2,1)S(1)}, bf16[64,1024]{1,0:T(8,128)(2,1)S(1)}, u32[]{:S(2)}, u32[]{:S(2)}) %collective-permute-start.1) | collective-permute-done | bytes 131104 | tf_op jit(solution)/shard_map/ppermute | solution.py:21
  37.8 5.2 %collective-permute-start.2 = (bf16[128,1024]{1,0:T(8,128)(2,1)S(1)}, bf16[128,1024]{1,0:T(8,128)(2,1)S(1)}, u32[]{:S(2)}, u32[]{:S(2)}) collective-permute-start(bf16[128,1024]{1,0:T(8,128)(2,1)S(1)} %shard_map.219.a_ref), channel_id=1, source_target_pairs={{0,16},{4,20},{8,24},{12,28},{16,0},{20,4},{24,8},{28,12},{1,17},{... | collective-permute-start | bytes 786440 | tf_op jit(solution)/shard_map/ppermute | solution.py:21
  43.0 12.1 %collective-permute-done.2.b_ref = bf16[128,1024]{1,0:T(8,128)(2,1)S(1)} collective-permute-done((bf16[128,1024]{1,0:T(8,128)(2,1)S(1)}, bf16[128,1024]{1,0:T(8,128)(2,1)S(1)}, u32[]{:S(2)}, u32[]{:S(2)}) %collective-permute-start.2) | collective-permute-done | bytes 262176 | tf_op jit(solution)/shard_map/ppermute | solution.py:21
  55.9 6.0 %shard_map.217 = (bf16[384,3072]{1,0:T(8,128)(2,1)}, s32[384,1]{1,0:T(8,128)S(1)}, s32[256,1]{1,0:T(8,128)S(1)}) custom-call(s32[1]{0:T(128)} %bitcast.2.base_ref, bf16[256,2048]{1,0:T(8,128)(2,1)S(1)} %bitcast.21, s32[384,1]{1,0:T(8,128)S(1)} %copy-done.46, s32[384,1]{1,0:T(8,128)S(1)} %copy-done.48, bf16[588,3000]{1,0:T(8,128)(2,1)} %table_ref.3), custom_call_target="tpu_custom_call" | custom-call | flops 4000000000 | bytes 6941508 | tf_op jit(solution)/shard_map/pallas_call | solution.py:42
  63.2 4.7 %all-to-all-start.1 = ((bf16[8,48,3072]{2,1,0:T(8,128)(2,1)}), bf16[8,48,3072]{2,1,0:T(8,128)(2,1)}, u32[]{:S(2)}, u32[]{:S(2)}) async-start(bf16[8,48,3072]{2,1,0:T(8,128)(2,1)} %bitcast.8), calls=%async_computation.1 | async-start | bytes 4718592 | tf_op jit(solution)/shard_map/all_to_all | solution.py:732
  74.1 14.2 %collective-permute-done.5.refs_2_.refs_3_ = bf16[512,768]{1,0:T(8,128)(2,1)S(1)} collective-permute-done((bf16[512,768]{1,0:T(8,128)(2,1)S(1)}, bf16[512,768]{1,0:T(8,128)(2,1)S(1)}, u32[]{:S(2)}, u32[]{:S(2)}) %collective-permute-start.5) | collective-permute-done | bytes 786464 | tf_op jit(solution)/shard_map/ppermute | solution.py:21
  93.7 13.8 %collective-permute-done.4.b_ref = bf16[256,1024]{1,0:T(8,128)(2,1)} collective-permute-done((bf16[256,1024]{1,0:T(8,128)(2,1)}, bf16[256,1024]{1,0:T(8,128)(2,1)}, u32[]{:S(2)}, u32[]{:S(2)}) %collective-permute-start.4) | collective-permute-done | bytes 524320 | tf_op jit(solution)/shard_map/ppermute | solution.py:21
  112.8 10.0 %collective-permute-done.6.refs_3_.refs_4_ = bf16[512,768]{1,0:T(8,128)(2,1)} collective-permute-done((bf16[512,768]{1,0:T(8,128)(2,1)S(1)}, bf16[512,768]{1,0:T(8,128)(2,1)}, u32[]{:S(2)}, u32[]{:S(2)}) %collective-permute-start.6) | collective-permute-done | bytes 786464 | tf_op jit(solution)/shard_map/ppermute | solution.py:21
  125.3 11.9 %shard_map.224 = (bf16[320,1024]{1,0:T(8,128)(2,1)S(1)}, f32[5,256,1024]{2,1,0:T(8,128)}) custom-call(s32[2]{0:T(128)S(1)} %pad_add_fusion.l_ref, f32[256,1]{1,0:T(8,128)S(1)} %reshape.149.keep_ref, s32[256,1]{1,0:T(8,128)S(1)} %copy-done.75, s32[256,1]{1,0:T(8,128)S(1)} %copy-done.18, bf16[256,2048]{1,0:T(8,128)(2,1)S(1)} %bitcast.23, ...), custom_call_target="tpu_custom_call" | custom-call | flops 12000000000 | bytes 15600648 | tf_op jit(solution)/shard_map/pallas_call | solution.py:42
  141.3 4.7 %all-to-all-start.2 = ((bf16[8,48,1024]{2,1,0:T(8,128)(2,1)}), bf16[8,48,1024]{2,1,0:T(8,128)(2,1)S(1)}, u32[]{:S(2)}, u32[]{:S(2)}) async-start(bf16[8,48,1024]{2,1,0:T(8,128)(2,1)} %bitcast.27), calls=%async_computation.2 | async-start | bytes 1572864 | tf_op jit(solution)/shard_map/all_to_all | solution.py:732
  148.3 13.0 %shard_map.226 = (bf16[320,1024]{1,0:T(8,128)(2,1)}, f32[5,256,1024]{2,1,0:T(8,128)}) custom-call(s32[2]{0:T(128)S(1)} %pad_add_fusion.l_ref, f32[256,1]{1,0:T(8,128)S(1)} %reshape.149.keep_ref, s32[256,1]{1,0:T(8,128)S(1)} %copy-done.19, bf16[256,2048]{1,0:T(8,128)(2,1)S(1)} %bitcast.24, bf16[320,1024]{1,0:T(8,128)(2,1)S(1)} %copy-done.9, ...), custom_call_target="tpu_custom_call" | custom-call | bytes 20187144 | tf_op jit(solution)/shard_map/pallas_call | solution.py:42
  168.8 11.8 %shard_map.227 = (bf16[256,512]{1,0:T(8,128)(2,1)S(1)}, bf16[256,512]{1,0:T(8,128)(2,1)S(1)}, bf16[256,512]{1,0:T(8,128)(2,1)S(1)}, bf16[256,512]{1,0:T(8,128)(2...) custom-call(f32[256,1]{1,0:T(8,128)S(1)} %div.11.valid_ref, s32[256,1]{1,0:T(8,128)S(1)} %copy-done.65, ...), custom_call_target="tpu_custom_call" | custom-call | flops 3000000000 | bytes 8521728 | tf_op jit(solution)/shard_map/pallas_call | solution.py:42
  185.3 16.3 %shard_map.228 = (f32[64,1024]{1,0:T(8,128)S(1)}, f32[256,1024]{1,0:T(8,128)}, bf16[256,768]{1,0:T(8,128)(2,1)S(1)}, bf16[256,768]{1,0:T(8,128)(2,1)S(1)}, bf16[...) custom-call(s32[2]{0:T(128)S(1)} %pad_add_fusion.l_ref, ...), custom_call_target="tpu_custom_call" | custom-call | flops 16999999488 | bytes 23331848 | tf_op jit(solution)/shard_map/pallas_call | solution.py:42
  205.8 4.7 %all-to-all-start.3 = ((bf16[8,48,1024]{2,1,0:T(8,128)(2,1)}), bf16[8,48,1024]{2,1,0:T(8,128)(2,1)S(1)}, u32[]{:S(2)}, u32[]{:S(2)}) async-start(bf16[8,48,1024]{2,1,0:T(8,128)(2,1)} %bitcast.12), calls=%async_computation.3 | async-start | bytes 1572864 | tf_op jit(solution)/shard_map/all_to_all | solution.py:732
  212.1 13.1 %shard_map.229 = (f32[64,1024]{1,0:T(8,128)S(1)}, bf16[256,3072]{1,0:T(8,128)(2,1)}, bf16[272,768]{1,0:T(8,128)(2,1)S(1)}, bf16[272,768]{1,0:T(8,128)(2,1)S(1)},...) custom-call(s32[2]{0:T(128)S(1)} %pad_add_fusion.l_ref, f32[256,1]{1,0:T(8,128)S(1)} %reshape.149.keep_ref, ...), custom_call_target="tpu_custom_call" | custom-call | flops 12999999488 | bytes 16090120 | tf_op jit(solution)/shard_map/pallas_call | solution.py:42
  232.7 5.0 %all-to-all-start.4 = ((bf16[8,48,3072]{2,1,0:T(8,128)(2,1)}), bf16[8,48,3072]{2,1,0:T(8,128)(2,1)}, u32[]{:S(2)}, u32[]{:S(2)}) async-start(bf16[8,48,3072]{2,1,0:T(8,128)(2,1)} %bitcast.14), calls=%async_computation.4 | async-start | bytes 4718592 | tf_op jit(solution)/shard_map/all_to_all | solution.py:732
  252.3 7.3 %collective-permute-done.27.refs_7_ = bf16[272,768]{1,0:T(8,128)(2,1)S(1)} collective-permute-done((bf16[272,768]{1,0:T(8,128)(2,1)S(1)}, bf16[272,768]{1,0:T(8,128)(2,1)S(1)}, u32[]{:S(2)}, u32[]{:S(2)}) %collective-permute-start.27) | collective-permute-done | bytes 417824 | tf_op jit(solution)/shard_map/ppermute | solution.py:21
  265.8 26.5 %all-to-all-done.4 = bf16[8,48,3072]{2,1,0:T(8,128)(2,1)} async-done(((bf16[8,48,3072]{2,1,0:T(8,128)(2,1)}), bf16[8,48,3072]{2,1,0:T(8,128)(2,1)}, u32[]{:S(2)}, u32[]{:S(2)}) %all-to-all-start.4) | async-done | bytes 2359328 | tf_op jit(solution)/shard_map/all_to_all | solution.py:732
  292.2 3.9 all-to-all-start.5
  296.2 5.0 %shard_map.241 = (bf16[512,768]{1,0:T(8,128)(2,1)S(1)}, bf16[512,768]{1,0:T(8,128)(2,1)}) custom-call(s32[1]{0:T(128)} %bitcast.1.l_ref, bf16[320,1024]{1,0:T(8,128)(2,1)} %get-tuple-element.151.state_ref.refs_4_.refs_0_, bf16[320,1024]{1,0:T(8,128)(2,1)S(1)} %copy-done.31, bf16[320,1024]{1,0:T(8,128)(2,1)} %collective-permute-done.19.refs_6_.refs_2_, ...), custom_call_target="tpu_custom_call" | custom-call | flops 5000000000 | bytes 5767172 | tf_op jit(solution)/shard_map/pallas_call | solution.py:42
  308.3 3.9 shard_map.231
  315.3 9.0 %collective-permute-done.39.b_ref = bf16[256,768]{1,0:T(8,128)(2,1)S(1)} collective-permute-done((bf16[256,768]{1,0:T(8,128)(2,1)S(1)}, bf16[256,768]{1,0:T(8,128)(2,1)S(1)}, u32[]{:S(2)}, u32[]{:S(2)}) %collective-permute-start.39) | collective-permute-done | bytes 393248 | tf_op jit(solution)/shard_map/ppermute | solution.py:21
  340.0 3.7 shard_map.235
  343.7 6.3 %all-to-all-start.6 = ((bf16[8,64,1024]{2,1,0:T(8,128)(2,1)}), bf16[8,64,1024]{2,1,0:T(8,128)(2,1)}, u32[]{:S(2)}, u32[]{:S(2)}) async-start(bf16[8,64,1024]{2,1,0:T(8,128)(2,1)} %bitcast.18), calls=%async_computation.6 | async-start | bytes 2097152 | tf_op jit(solution)/shard_map/all_to_all | solution.py:732
  358.4 11.4 %collective-permute-start.49 = (bf16[256,768]{1,0:T(8,128)(2,1)S(1)}, bf16[256,768]{1,0:T(8,128)(2,1)S(1)}, u32[]{:S(2)}, u32[]{:S(2)}) collective-permute-start(bf16[256,768]{1,0:T(8,128)(2,1)S(1)} %shard_map.247.a_ref), channel_id=1, source_target_pairs={{0,16},{4,20},{8,24},{12,28},{16,0},{20,4},{24,8},{28,12},{1,17},{... | collective-permute-start | bytes 1179656 | tf_op jit(solution)/shard_map/ppermute | solution.py:21
  369.8 17.2 %collective-permute-done.48.b_ref = bf16[256,768]{1,0:T(8,128)(2,1)S(1)} collective-permute-done((bf16[256,768]{1,0:T(8,128)(2,1)S(1)}, bf16[256,768]{1,0:T(8,128)(2,1)S(1)}, u32[]{:S(2)}, u32[]{:S(2)}) %collective-permute-start.48) | collective-permute-done | bytes 393248 | tf_op jit(solution)/shard_map/ppermute | solution.py:21
  387.1 8.4 %collective-permute-done.47.b_ref = bf16[256,768]{1,0:T(8,128)(2,1)S(1)} collective-permute-done((bf16[256,768]{1,0:T(8,128)(2,1)S(1)}, bf16[256,768]{1,0:T(8,128)(2,1)S(1)}, u32[]{:S(2)}, u32[]{:S(2)}) %collective-permute-start.47) | collective-permute-done | bytes 393248 | tf_op jit(solution)/shard_map/ppermute | solution.py:21
  406.7 9.0 %collective-permute-done.52.b_ref = bf16[256,768]{1,0:T(8,128)(2,1)S(1)} collective-permute-done((bf16[256,768]{1,0:T(8,128)(2,1)S(1)}, bf16[256,768]{1,0:T(8,128)(2,1)S(1)}, u32[]{:S(2)}, u32[]{:S(2)}) %collective-permute-start.52) | collective-permute-done | bytes 393248 | tf_op jit(solution)/shard_map/ppermute | solution.py:21
  426.0 5.8 %collective-permute-done.53.b_ref = bf16[256,768]{1,0:T(8,128)(2,1)} collective-permute-done((bf16[256,768]{1,0:T(8,128)(2,1)}, bf16[256,768]{1,0:T(8,128)(2,1)}, u32[]{:S(2)}, u32[]{:S(2)}) %collective-permute-start.53) | collective-permute-done | bytes 393248 | tf_op jit(solution)/shard_map/ppermute | solution.py:21
  433.0 5.5 %collective-permute-done.54.b_ref = bf16[512,768]{1,0:T(8,128)(2,1)} collective-permute-done((bf16[512,768]{1,0:T(8,128)(2,1)}, bf16[512,768]{1,0:T(8,128)(2,1)}, u32[]{:S(2)}, u32[]{:S(2)}) %collective-permute-start.54) | collective-permute-done | bytes 786464 | tf_op jit(solution)/shard_map/ppermute | solution.py:21
  449.7 6.2 %collective-permute-done.55.b_ref = bf16[512,768]{1,0:T(8,128)(2,1)S(1)} collective-permute-done((bf16[512,768]{1,0:T(8,128)(2,1)S(1)}, bf16[512,768]{1,0:T(8,128)(2,1)S(1)}, u32[]{:S(2)}, u32[]{:S(2)}) %collective-permute-start.55) | collective-permute-done | bytes 786464 | tf_op jit(solution)/shard_map/ppermute | solution.py:21
  (330 shorter events, 163.4 us)
Async XLA Ops:
  12.7 43.2 %all-to-all-start = ((bf16[8,32,2048]{2,1,0:T(8,128)(2,1)}), bf16[8,32,2048]{2,1,0:T(8,128)(2,1)S(1)}, u32[]{:S(2)}, u32[]{:S(2)}) async-start(bf16[8,32,2048]{2,1,0:T(8,128)(2,1)} %bitcast.4), calls=%async_computation | async-start | bytes 2097152 | tf_op jit(solution)/shard_map/all_to_all | solution.py:732
  18.7 44.5 %collective-permute-start.3 = (bf16[896,768]{1,0:T(8,128)(2,1)S(1)}, bf16[896,768]{1,0:T(8,128)(2,1)}, u32[]{:S(2)}, u32[]{:S(2)}) collective-permute-start(bf16[896,768]{1,0:T(8,128)(2,1)S(1)} %get-tuple-element.134), channel_id=1, source_target_pairs={{0,2},{1,3},{2,0},{3,1},{4,6},{5,7},{6,4},{7,5},{8,10},{9,11},{10,... | collective-permute-start | bytes 4128776 | tf_op jit(solution)/shard_map/ppermute | solution.py:21
  63.2 59.7 %all-to-all-start.1 = ((bf16[8,48,3072]{2,1,0:T(8,128)(2,1)}), bf16[8,48,3072]{2,1,0:T(8,128)(2,1)}, u32[]{:S(2)}, u32[]{:S(2)}) async-start(bf16[8,48,3072]{2,1,0:T(8,128)(2,1)} %bitcast.8), calls=%async_computation.1 | async-start | bytes 4718592 | tf_op jit(solution)/shard_map/all_to_all | solution.py:732
  71.7 51.8 %collective-permute-start.7 = (bf16[1024,768]{1,0:T(8,128)(2,1)}, bf16[1024,768]{1,0:T(8,128)(2,1)}, u32[]{:S(2)}, u32[]{:S(2)}) collective-permute-start(bf16[1024,768]{1,0:T(8,128)(2,1)} %get-tuple-element.122.refs_0_.refs_1_), channel_id=1, source_target_pairs={{0,1},{1,0},{2,3},{3,2},{4,5},{5,4},{6,7},{7,6},{8,9},{9,8},{10,11... | collective-permute-start | bytes 4718600 | tf_op jit(solution)/shard_map/ppermute | solution.py:21
  71.7 51.8 %collective-permute-start.9 = (bf16[896,768]{1,0:T(8,128)(2,1)}, bf16[896,768]{1,0:T(8,128)(2,1)}, u32[]{:S(2)}, u32[]{:S(2)}) collective-permute-start(bf16[896,768]{1,0:T(8,128)(2,1)} %collective-permute-done.3.refs_3_.refs_4_), channel_id=1, source_target_pairs={{0,1},{1,0},{2,3},{3,2},{4,5},{5,4},{6,7},{7,6},{8,9},{9,8},{10,11... | collective-permute-start | bytes 4128776 | tf_op jit(solution)/shard_map/ppermute | solution.py:21
  72.2 35.3 %collective-permute-start.4 = (bf16[256,1024]{1,0:T(8,128)(2,1)}, bf16[256,1024]{1,0:T(8,128)(2,1)}, u32[]{:S(2)}, u32[]{:S(2)}) collective-permute-start(bf16[256,1024]{1,0:T(8,128)(2,1)} %shard_map.220.a_ref), channel_id=1, source_target_pairs={{0,4},{4,0},{8,12},{12,8},{16,20},{20,16},{24,28},{28,24},{1,5},{5... | collective-permute-start | bytes 1572872 | tf_op jit(solution)/shard_map/ppermute | solution.py:21
  88.4 34.5 %collective-permute-start.6 = (bf16[512,768]{1,0:T(8,128)(2,1)S(1)}, bf16[512,768]{1,0:T(8,128)(2,1)}, u32[]{:S(2)}, u32[]{:S(2)}) collective-permute-start(bf16[512,768]{1,0:T(8,128)(2,1)S(1)} %collective-permute-done.5.refs_2_.refs_3_), channel_id=1, source_target_pairs={{0,4},{4,0},{8,12},{12,8},{16,20},{20,16},{24,28},{28,24},{1,5},{5... | collective-permute-start | bytes 2359304 | tf_op jit(solution)/shard_map/ppermute | solution.py:21
  91.9 46.1 %collective-permute-start.14 = (bf16[1024,768]{1,0:T(8,128)(2,1)}, bf16[1024,768]{1,0:T(8,128)(2,1)}, u32[]{:S(2)}, u32[]{:S(2)}) collective-permute-start(bf16[1024,768]{1,0:T(8,128)(2,1)} %shard_map.225.refs_6_.refs_7_), channel_id=1, source_target_pairs={{0,2},{1,3},{2,0},{3,1},{4,6},{5,7},{6,4},{7,5},{8,10},{9,11},{10,... | collective-permute-start | bytes 4718600 | tf_op jit(solution)/shard_map/ppermute | solution.py:21
  122.9 23.0 %collective-permute-start.13 = (bf16[1024,768]{1,0:T(8,128)(2,1)}, bf16[1024,768]{1,0:T(8,128)(2,1)}, u32[]{:S(2)}, u32[]{:S(2)}) collective-permute-start(bf16[1024,768]{1,0:T(8,128)(2,1)} %shard_map.225.refs_6_.refs_7_), channel_id=1, source_target_pairs={{0,1},{1,0},{2,3},{3,2},{4,5},{5,4},{6,7},{7,6},{8,9},{9,8},{10,11... | collective-permute-start | bytes 4718600 | tf_op jit(solution)/shard_map/ppermute | solution.py:21
  138.1 25.9 %collective-permute-start.17 = (bf16[512,1024]{1,0:T(8,128)(2,1)}, bf16[512,1024]{1,0:T(8,128)(2,1)}, u32[]{:S(2)}, u32[]{:S(2)}) collective-permute-start(bf16[512,1024]{1,0:T(8,128)(2,1)} %shard_map.222.refs_0_), channel_id=1, source_target_pairs={{0,2},{1,3},{2,0},{3,1},{4,6},{5,7},{6,4},{7,5},{8,10},{9,11},{10,... | collective-permute-start | bytes 3145736 | tf_op jit(solution)/shard_map/ppermute | solution.py:21
  141.3 25.2 %all-to-all-start.2 = ((bf16[8,48,1024]{2,1,0:T(8,128)(2,1)}), bf16[8,48,1024]{2,1,0:T(8,128)(2,1)S(1)}, u32[]{:S(2)}, u32[]{:S(2)}) async-start(bf16[8,48,1024]{2,1,0:T(8,128)(2,1)} %bitcast.27), calls=%async_computation.2 | async-start | bytes 1572864 | tf_op jit(solution)/shard_map/all_to_all | solution.py:732
  183.7 26.9 %collective-permute-start.20 = (bf16[320,1024]{1,0:T(8,128)(2,1)S(1)}, bf16[320,1024]{1,0:T(8,128)(2,1)S(1)}, u32[]{:S(2)}, u32[]{:S(2)}) collective-permute-start(bf16[320,1024]{1,0:T(8,128)(2,1)S(1)} %copy-done.10), channel_id=1, source_target_pairs={{0,2},{1,3},{2,0},{3,1},{4,6},{5,7},{6,4},{7,5},{8,10},{9,11},{10,... | collective-permute-start | bytes 1966088 | tf_op jit(solution)/shard_map/ppermute | solution.py:21
  204.6 22.0 %collective-permute-start.21 = (bf16[256,768]{1,0:T(8,128)(2,1)}, bf16[256,768]{1,0:T(8,128)(2,1)}, u32[]{:S(2)}, u32[]{:S(2)}) collective-permute-start(bf16[256,768]{1,0:T(8,128)(2,1)} %get-tuple-element.159), channel_id=1, source_target_pairs={{0,2},{1,3},{2,0},{3,1},{4,6},{5,7},{6,4},{7,5},{8,10},{9,11},{10,... | collective-permute-start | bytes 1179656 | tf_op jit(solution)/shard_map/ppermute | solution.py:21
  205.1 21.5 %collective-permute-start.22 = (bf16[256,768]{1,0:T(8,128)(2,1)}, bf16[256,768]{1,0:T(8,128)(2,1)}, u32[]{:S(2)}, u32[]{:S(2)}) collective-permute-start(bf16[256,768]{1,0:T(8,128)(2,1)} %get-tuple-element.160), channel_id=1, source_target_pairs={{0,3},{1,2},{2,1},{3,0},{4,7},{5,6},{6,5},{7,4},{8,11},{9,10},{10,... | collective-permute-start | bytes 1179656 | tf_op jit(solution)/shard_map/ppermute | solution.py:21
  205.8 26.0 %all-to-all-start.3 = ((bf16[8,48,1024]{2,1,0:T(8,128)(2,1)}), bf16[8,48,1024]{2,1,0:T(8,128)(2,1)S(1)}, u32[]{:S(2)}, u32[]{:S(2)}) async-start(bf16[8,48,1024]{2,1,0:T(8,128)(2,1)} %bitcast.12), calls=%async_computation.3 | async-start | bytes 1572864 | tf_op jit(solution)/shard_map/all_to_all | solution.py:732
  232.7 59.5 %all-to-all-start.4 = ((bf16[8,48,3072]{2,1,0:T(8,128)(2,1)}), bf16[8,48,3072]{2,1,0:T(8,128)(2,1)}, u32[]{:S(2)}, u32[]{:S(2)}) async-start(bf16[8,48,3072]{2,1,0:T(8,128)(2,1)} %bitcast.14), calls=%async_computation.4 | async-start | bytes 4718592 | tf_op jit(solution)/shard_map/all_to_all | solution.py:732
  241.7 54.5 %collective-permute-start.34 = (bf16[320,1024]{1,0:T(8,128)(2,1)}, bf16[320,1024]{1,0:T(8,128)(2,1)}, u32[]{:S(2)}, u32[]{:S(2)}) collective-permute-start(bf16[320,1024]{1,0:T(8,128)(2,1)} %collective-permute-done.19.refs_6_.refs_2_), channel_id=1, source_target_pairs={{0,1},{1,0},{2,3},{3,2},{4,5},{5,4},{6,7},{7,6},{8,9},{9,8},{10,11... | collective-permute-start | bytes 1966088 | tf_op jit(solution)/shard_map/ppermute | solution.py:21
  249.2 46.9 %collective-permute-start.40 = (bf16[256,768]{1,0:T(8,128)(2,1)}, bf16[256,768]{1,0:T(8,128)(2,1)}, u32[]{:S(2)}, u32[]{:S(2)}) collective-permute-start(bf16[256,768]{1,0:T(8,128)(2,1)} %get-tuple-element.207), channel_id=1, source_target_pairs={{0,1},{1,0},{2,3},{3,2},{4,5},{5,4},{6,7},{7,6},{8,9},{9,8},{10,11... | collective-permute-start | bytes 1179656 | tf_op jit(solution)/shard_map/ppermute | solution.py:21
  249.3 46.8 %collective-permute-start.41 = (bf16[256,768]{1,0:T(8,128)(2,1)}, bf16[256,768]{1,0:T(8,128)(2,1)}, u32[]{:S(2)}, u32[]{:S(2)}) collective-permute-start(bf16[256,768]{1,0:T(8,128)(2,1)} %get-tuple-element.208), channel_id=1, source_target_pairs={{0,2},{1,3},{2,0},{3,1},{4,6},{5,7},{6,4},{7,5},{8,10},{9,11},{10,... | collective-permute-start | bytes 1179656 | tf_op jit(solution)/shard_map/ppermute | solution.py:21
  252.3 43.9 %collective-permute-start.42 = (bf16[256,768]{1,0:T(8,128)(2,1)}, bf16[256,768]{1,0:T(8,128)(2,1)}, u32[]{:S(2)}, u32[]{:S(2)}) collective-permute-start(bf16[256,768]{1,0:T(8,128)(2,1)} %get-tuple-element.209), channel_id=1, source_target_pairs={{0,3},{1,2},{2,1},{3,0},{4,7},{5,6},{6,5},{7,4},{8,11},{9,10},{10,... | collective-permute-start | bytes 1179656 | tf_op jit(solution)/shard_map/ppermute | solution.py:21
  259.6 42.5 %collective-permute-start.38 = (bf16[512,768]{1,0:T(8,128)(2,1)S(1)}, bf16[512,768]{1,0:T(8,128)(2,1)}, u32[]{:S(2)}, u32[]{:S(2)}) collective-permute-start(bf16[512,768]{1,0:T(8,128)(2,1)S(1)} %get-tuple-element.203), channel_id=1, source_target_pairs={{0,4},{4,0},{8,12},{12,8},{16,20},{20,16},{24,28},{28,24},{1,5},{5... | collective-permute-start | bytes 2359304 | tf_op jit(solution)/shard_map/ppermute | solution.py:21
  292.2 51.5 %all-to-all-start.5 = ((bf16[8,32,2048]{2,1,0:T(8,128)(2,1)}), bf16[8,32,2048]{2,1,0:T(8,128)(2,1)S(1)}, u32[]{:S(2)}, u32[]{:S(2)}) async-start(bf16[8,32,2048]{2,1,0:T(8,128)(2,1)} %bitcast.16), calls=%async_computation.5 | async-start | bytes 2097152 | tf_op jit(solution)/shard_map/all_to_all | solution.py:732
  302.1 25.3 %collective-permute-start.43 = (bf16[512,768]{1,0:T(8,128)(2,1)}, bf16[512,768]{1,0:T(8,128)(2,1)}, u32[]{:S(2)}, u32[]{:S(2)}) collective-permute-start(bf16[512,768]{1,0:T(8,128)(2,1)} %get-tuple-element.211), channel_id=1, source_target_pairs={{0,4},{4,0},{8,12},{12,8},{16,20},{20,16},{24,28},{28,24},{1,5},{5... | collective-permute-start | bytes 2359304 | tf_op jit(solution)/shard_map/ppermute | solution.py:21
  314.8 88.1 %collective-permute-start.28 = (bf16[2,160,3072]{2,1,0:T(8,128)(2,1)S(1)}, bf16[2,160,3072]{2,1,0:T(8,128)(2,1)}, u32[]{:S(2)}, u32[]{:S(2)}) collective-permute-start(bf16[2,160,3072]{2,1,0:T(8,128)(2,1)S(1)} %get-tuple-element.178), channel_id=1, source_target_pairs={{0,1},{1,0},{2,3},{3,2},{4,5},{5,4},{6,7},{7,6},{8,9},{9,8},{10,11... | collective-permute-start | bytes 5898248 | tf_op jit(solution)/shard_map/ppermute | solution.py:21
  327.5 27.5 %collective-permute-start.44 = (bf16[512,768]{1,0:T(8,128)(2,1)}, bf16[512,768]{1,0:T(8,128)(2,1)}, u32[]{:S(2)}, u32[]{:S(2)}) collective-permute-start(bf16[512,768]{1,0:T(8,128)(2,1)} %get-tuple-element.212), channel_id=1, source_target_pairs={{0,4},{4,0},{8,12},{12,8},{16,20},{20,16},{24,28},{28,24},{1,5},{5... | collective-permute-start | bytes 2359304 | tf_op jit(solution)/shard_map/ppermute | solution.py:21
  328.8 21.6 %collective-permute-start.45 = (bf16[256,768]{1,0:T(8,128)(2,1)S(1)}, bf16[256,768]{1,0:T(8,128)(2,1)}, u32[]{:S(2)}, u32[]{:S(2)}) collective-permute-start(bf16[256,768]{1,0:T(8,128)(2,1)S(1)} %shard_map.243.a_ref), channel_id=1, source_target_pairs={{0,16},{4,20},{8,24},{12,28},{16,0},{20,4},{24,8},{28,12},{1,17},{... | collective-permute-start | bytes 1179656 | tf_op jit(solution)/shard_map/ppermute | solution.py:21
  343.7 78.2 %all-to-all-start.6 = ((bf16[8,64,1024]{2,1,0:T(8,128)(2,1)}), bf16[8,64,1024]{2,1,0:T(8,128)(2,1)}, u32[]{:S(2)}, u32[]{:S(2)}) async-start(bf16[8,64,1024]{2,1,0:T(8,128)(2,1)} %bitcast.18), calls=%async_computation.6 | async-start | bytes 2097152 | tf_op jit(solution)/shard_map/all_to_all | solution.py:732
  355.0 32.1 %collective-permute-start.48 = (bf16[256,768]{1,0:T(8,128)(2,1)S(1)}, bf16[256,768]{1,0:T(8,128)(2,1)S(1)}, u32[]{:S(2)}, u32[]{:S(2)}) collective-permute-start(bf16[256,768]{1,0:T(8,128)(2,1)S(1)} %shard_map.246.a_ref), channel_id=1, source_target_pairs={{0,8},{4,12},{8,0},{12,4},{16,24},{20,28},{24,16},{28,20},{1,9},{5... | collective-permute-start | bytes 1179656 | tf_op jit(solution)/shard_map/ppermute | solution.py:21
  356.4 39.1 %collective-permute-start.47 = (bf16[256,768]{1,0:T(8,128)(2,1)S(1)}, bf16[256,768]{1,0:T(8,128)(2,1)S(1)}, u32[]{:S(2)}, u32[]{:S(2)}) collective-permute-start(bf16[256,768]{1,0:T(8,128)(2,1)S(1)} %get-tuple-element.220), channel_id=1, source_target_pairs={{0,8},{4,12},{8,0},{12,4},{16,24},{20,28},{24,16},{28,20},{1,9},{5... | collective-permute-start | bytes 1179656 | tf_op jit(solution)/shard_map/ppermute | solution.py:21
  358.4 37.0 %collective-permute-start.49 = (bf16[256,768]{1,0:T(8,128)(2,1)S(1)}, bf16[256,768]{1,0:T(8,128)(2,1)S(1)}, u32[]{:S(2)}, u32[]{:S(2)}) collective-permute-start(bf16[256,768]{1,0:T(8,128)(2,1)S(1)} %shard_map.247.a_ref), channel_id=1, source_target_pairs={{0,16},{4,20},{8,24},{12,28},{16,0},{20,4},{24,8},{28,12},{1,17},{... | collective-permute-start | bytes 1179656 | tf_op jit(solution)/shard_map/ppermute | solution.py:21
  395.4 24.5 %collective-permute-start.51 = (bf16[512,768]{1,0:T(8,128)(2,1)S(1)}, bf16[512,768]{1,0:T(8,128)(2,1)S(1)}, u32[]{:S(2)}, u32[]{:S(2)}) collective-permute-start(bf16[512,768]{1,0:T(8,128)(2,1)S(1)} %shard_map.249.a_ref), channel_id=1, source_target_pairs={{0,4},{4,0},{8,12},{12,8},{16,20},{20,16},{24,28},{28,24},{1,5},{5... | collective-permute-start | bytes 2359304 | tf_op jit(solution)/shard_map/ppermute | solution.py:21
  406.2 32.3 %collective-permute-start.29 = (bf16[160,3072]{1,0:T(8,128)(2,1)}, bf16[160,3072]{1,0:T(8,128)(2,1)}, u32[]{:S(2)}, u32[]{:S(2)}) collective-permute-start(bf16[160,3072]{1,0:T(8,128)(2,1)} %get-tuple-element.180), channel_id=1, source_target_pairs={{0,2},{1,3},{2,0},{3,1},{4,6},{5,7},{6,4},{7,5},{8,10},{9,11},{10,... | collective-permute-start | bytes 2949128 | tf_op jit(solution)/shard_map/ppermute | solution.py:21
  (118 other events, 1094.7 us)
